TPU v7x, 32 devices: a whole 2x2x4 slice. The times are simulated.
32 devices in a mesh: crop: 4 (over x, core), row: 8 (over z, y).
Axes of the slice: x: 2, y: 2, z: 4, core: 2. Of those that a mesh axis runs over, the one named last changes fastest.
Arguments:
- node: bfloat16 [4, 256, 256], P('crop', 'row'), may hold values from -6 to 6
- pair: bfloat16 [4, 256, 256, 128], P('crop', 'row'), may hold values from -6 to 6
- recycle: int32 [4], P('crop'), may hold values from 0 to 3
- mask: int32 [4, 256], P('crop'), may hold values 0 or 1
- node_cot: bfloat16 [4, 256, 256], P('crop', 'row'), may hold values from -6 to 6
- pair_cot: bfloat16 [4, 256, 256, 128], P('crop', 'row'), may hold values from -6 to 6
- master: float32 [1199616], P(('crop', 'row')), may hold values from -4 to 4, as said below
- first: float32 [1199616], P(('crop', 'row')), may hold values from -0.0014648438 to 0.0014648438
- second: float32 [1199616], P(('crop', 'row')), may hold values from 1e-08 to 1e-07
Outputs:
- node_out: bfloat16 [4, 256, 256], P('crop', 'row')
- pair_out: bfloat16 [4, 256, 256, 128], P('crop', 'row')
- node_grad: bfloat16 [4, 256, 256], P('crop', 'row')
- pair_grad: bfloat16 [4, 256, 256, 128], P('crop', 'row')
- weight_grad: float32 [1199616], P(('crop', 'row'))
- bias_grad: float32 [128], replicated
- grad_norm: float32 [], replicated
- new_master: float32 [1199616], P(('crop', 'row'))
- new_first: float32 [1199616], P(('crop', 'row'))
- new_second: float32 [1199616], P(('crop', 'row'))
- new_weights: bfloat16 [1199616], P(('crop', 'row'))
Inputs may be any that keep to these rules, and one draw needn't show every extreme that they name: `master`: the parameters packed end to end in the order that the first step lists.
All inputs are finite; a program needn't handle non-finite values. No bound on the sum of `mask` on one device may be relied on, other than what follows from the above.
Results may differ from a plain program's by a relative error of at most 0.022.
Values may be sent and summed in bfloat16 or wider, within the bound.
No kernel may reach another device: no remote copies, remote signals or barrier semaphores. Data moves between devices by JAX's collectives and lax.ppermute only.
A program may use at most 384 MiB of HBM per device.

v0:
```python
import math

import jax
import jax.numpy as jnp
import numpy as np
from jax import lax
from jax.experimental import pallas as pl
from jax.experimental.pallas import tpu as pltpu
from jax.sharding import PartitionSpec as P

NODE_DIM = 256
PAIR_DIM = 128
HEADS = 8
HEAD_DIM = 32
OUTER = 32
TRI_DIM = 128
FFN_NODE = 1024
FFN_PAIR = 512
RECYCLES = 4
ADAM_STEP = 3


EPS_NORM = 1e-05
ADAM_EPS = 1e-08
BETA_ONE = 0.9
BETA_TWO = 0.95
LEARN_RATE = 0.06
WEIGHT_DECAY = 0.1
CLIP_NORM = 1.0
MASK_FILL = 1000000000.0
HIGHEST = lax.Precision.HIGHEST


def segment_list():
    heads_width = HEADS * HEAD_DIM
    entries = [
        ("embed", (RECYCLES, NODE_DIM)),
        ("gain_one", (NODE_DIM,)),
        ("w_query", (NODE_DIM, heads_width)),
        ("w_key", (NODE_DIM, heads_width)),
        ("w_value", (NODE_DIM, heads_width)),
        ("w_bias", (PAIR_DIM, HEADS)),
        ("w_attn_out", (heads_width, NODE_DIM)),
        ("gain_two", (NODE_DIM,)),
        ("w_node_up", (NODE_DIM, FFN_NODE)),
        ("w_node_down", (FFN_NODE, NODE_DIM)),
        ("gain_three", (NODE_DIM,)),
        ("w_left_node", (NODE_DIM, OUTER)),
        ("w_right_node", (NODE_DIM, OUTER)),
        ("w_outer", (OUTER * OUTER, PAIR_DIM)),
    ]
    for prefix in ("out_", "in_"):
        entries += [
            (prefix + "gain_in", (PAIR_DIM,)),
            (prefix + "w_left", (PAIR_DIM, TRI_DIM)),
            (prefix + "w_right", (PAIR_DIM, TRI_DIM)),
            (prefix + "w_gate", (PAIR_DIM, PAIR_DIM)),
            (prefix + "gain_tri", (TRI_DIM,)),
            (prefix + "w_tri_out", (TRI_DIM, PAIR_DIM)),
        ]
    entries += [
        ("gain_pair", (PAIR_DIM,)),
        ("w_pair_up", (PAIR_DIM, FFN_PAIR)),
        ("w_pair_down", (FFN_PAIR, PAIR_DIM)),
        ("bias_pair", (PAIR_DIM,)),
    ]
    return entries


def unpack(flat):
    params = {}
    offset = 0
    for entry_name, entry_shape in segment_list():
        extent = math.prod(entry_shape)
        params[entry_name] = flat[offset : offset + extent].reshape(entry_shape)
        offset += extent
    return params


LOW = jnp.bfloat16
WIDE = jnp.float32
BOTH = ("crop", "row")
TILE = 16
VMEM_LIMIT = 56 * 2**20
INV_SQRT2 = 1.0 / math.sqrt(2.0)
INV_SQRT2PI = 1.0 / math.sqrt(2.0 * math.pi)


class Layout:
    def __init__(self, crops, rows):
        self.crops, self.rows, self.wide = crops, rows, rows // crops
        self.planes = (0, 2, 1, 3) if crops == 4 else tuple(range(crops))
        self.slots = (0, 2, 1, 3) if crops == 4 else tuple(range(crops))
        self.crop_of = tuple(self.planes.index(k) for k in range(crops))
        self.high_of = tuple(self.slots.index(k) for k in range(crops))
        ident = lambda c, z, y: (c * crops + z) * self.wide + y
        spots = [
            (c, z, y) for c in range(crops) for z in range(crops) for y in range(self.wide)
        ]
        self.outward = [
            (ident(c, z, y), ident(self.slots[z], self.planes[c], y)) for c, z, y in spots
        ]
        self.homeward = [(there, here) for here, there in self.outward]
        self.groups = [
            [
                ident(self.slots[z], plane, y)
                for z in range(crops)
                for y in range(self.wide)
            ]
            for plane in range(crops)
        ]
        half = crops // 2
        self.cores = [
            [(2 * x + k) * rows + r for k in range(2)] for x in range(half) for r in range(rows)
        ]
        self.chips = [
            [(2 * x + k) * rows + r for x in range(half)] for k in range(2) for r in range(rows)
        ]


def exchange(blocks, axes, groups=None):
    return lax.all_to_all(blocks, axes, 0, 0, axis_index_groups=groups, tiled=True)


def spread(part, count, axes, groups=None):
    return exchange(jnp.broadcast_to(part[None], (count,) + part.shape), axes, groups)


def dot_nn(a, b):
    return lax.dot_general(a, b, (((1,), (0,)), ((), ())), preferred_element_type=WIDE)


def dot_nt(a, b):
    return lax.dot_general(a, b, (((1,), (1,)), ((), ())), preferred_element_type=WIDE)


def dot_tn(a, b):
    return lax.dot_general(a, b, (((0,), (0,)), ((), ())), preferred_element_type=WIDE)


def norm_parts(x):
    centered = x - jnp.mean(x, axis=0, keepdims=True)
    scale = lax.rsqrt(jnp.mean(centered * centered, axis=0, keepdims=True) + EPS_NORM)
    return centered * scale, scale


def norm_back(grad, hat, scale, gain):
    grad_gain = jnp.sum(grad * hat, axis=1, keepdims=True)
    wide = grad * gain
    inner = jnp.mean(wide * hat, axis=0, keepdims=True)
    return scale * (wide - jnp.mean(wide, axis=0, keepdims=True) - hat * inner), grad_gain


def sigmoid(x):
    return 0.5 * jnp.tanh(0.5 * x) + 0.5


def cat(ref, start, count):
    return jnp.concatenate([ref[start + t] for t in range(count)], axis=1)


def put(ref, start, count, value):
    width = value.shape[1] // count
    for t in range(count):
        ref[start + t] = value[:, t * width : (t + 1) * width]


def swapped(value):
    if value.shape[0] % TILE or value.shape[1] % TILE:
        return jnp.swapaxes(value.astype(WIDE), 0, 1).astype(LOW)
    return jnp.swapaxes(value, 0, 1)


def cell_mask(mask_ref, start, count):
    return jnp.concatenate([mask_ref[start + t] for t in range(count)], axis=1)


def send_pair(scratch, out_ref):
    parts, share = out_ref.shape[0], out_ref.shape[1] // 2
    channels = parts * share
    for side in range(2):
        value = swapped(scratch[:, side * channels : (side + 1) * channels, :])
        out_ref[:, side * share : (side + 1) * share] = value.reshape(
            (parts, share) + value.shape[1:]
        )


def take_pair(in_ref, scratch):
    parts, share = in_ref.shape[0], in_ref.shape[1] // 2
    channels = parts * share
    for side in range(2):
        value = in_ref[:, side * share : (side + 1) * share]
        value = value.reshape((channels,) + value.shape[2:])
        scratch[:, side * channels : (side + 1) * channels, :] = swapped(value)


def front(x, gain, w_sides, mask):
    hat, _ = norm_parts(x)
    normed = (hat * gain).astype(LOW)
    return (dot_nn(w_sides, normed) * mask).astype(LOW)


def gate_of(x, gain, w_gate):
    hat, _ = norm_parts(x)
    return sigmoid(dot_nn(w_gate, (hat * gain).astype(LOW)))


def post(x, mixed, gain_in, w_gate, gain_tri, w_out):
    hat, _ = norm_parts(mixed)
    update = dot_nn(w_out, (hat * gain_tri).astype(LOW))
    return x + gate_of(x, gain_in, w_gate) * update


def post_back(grad, x, mixed, gain_in, w_gate, gain_tri, w_out, w_out_back):
    hat, scale = norm_parts(mixed)
    normed = (hat * gain_tri).astype(LOW)
    update = dot_nn(w_out, normed)
    gate = gate_of(x, gain_in, w_gate)
    update_grad = (grad * gate).astype(LOW)
    gate_grad = (grad * update * (gate * (1.0 - gate))).astype(LOW)
    grad_out = dot_nt(normed, update_grad)
    mixed_grad, grad_gain = norm_back(dot_nn(w_out_back, update_grad), hat, scale, gain_tri)
    return mixed_grad.astype(LOW), gate_grad, grad_out, grad_gain


def front_back(grad, x, sides_grad, gate_grad, mask, gain, w_all_back):
    hat, scale = norm_parts(x)
    normed = (hat * gain).astype(LOW)
    sides = jnp.concatenate([sides_grad * mask.astype(LOW), gate_grad], axis=0)
    grad_w = dot_nt(normed, sides)
    x_grad, grad_gain = norm_back(dot_nn(w_all_back, sides), hat, scale, gain)
    return grad + x_grad, grad_w, grad_gain


def gelu_parts(x):
    cumulative = 0.5 * lax.erf(x * INV_SQRT2) + 0.5
    density = INV_SQRT2PI * jnp.exp(-0.5 * x * x)
    return x * cumulative, cumulative + x * density


def zero_first(*refs):
    @pl.when(pl.program_id(0) == 0)
    def _():
        for ref in refs:
            ref[...] = jnp.zeros_like(ref)


def run(body, step_rows, rows, in_arrays, in_kinds, outs, scratch, flops):
    def spec(kind, shape):
        if kind == "r":
            return pl.BlockSpec((step_rows,) + shape[1:], lambda i: (i,) + (0,) * (len(shape) - 1))
        if kind == "s":
            return pl.BlockSpec(
                shape[:-2] + (step_rows, shape[-1]),
                lambda i: (0,) * (len(shape) - 2) + (i, 0),
            )
        return pl.BlockSpec(shape, lambda i: (0,) * len(shape))

    moved = sum(a.size * a.dtype.itemsize for a in in_arrays)
    return pl.pallas_call(
        body,
        grid=(rows // step_rows,),
        in_specs=[spec(kind, a.shape) for kind, a in zip(in_kinds, in_arrays)],
        out_specs=[spec(kind, shape) for kind, shape, _ in outs],
        out_shape=[jax.ShapeDtypeStruct(shape, dtype) for _, shape, dtype in outs],
        scratch_shapes=scratch,
        compiler_params=pltpu.CompilerParams(vmem_limit_bytes=VMEM_LIMIT),
        cost_estimate=pl.CostEstimate(flops=flops, bytes_accessed=moved, transcendentals=0),
    )(*in_arrays)


def loop(count, body):
    def step(t, carry):
        body(t)
        return carry

    lax.fori_loop(0, count, step, 0)


GROUP = 2


def kernel_open(pair, table, right, mask, gain, w_sides, x_out, sides_out, scratch):
    rows = pair.shape[0]
    group = min(GROUP, rows)
    w_low = w_sides[...].T
    right_low = right[...]

    def step(t):
        at = t * group
        x = jnp.concatenate(
            [
                pair[at + k].T.astype(WIDE) + dot_nn(table[at + k], right_low)
                for k in range(group)
            ],
            axis=1,
        )
        put(x_out, at, group, x)
        put(scratch, at, group, front(x, gain[...], w_low, cell_mask(mask, at, group)))

    loop(rows // group, step)
    send_pair(scratch, sides_out)


def kernel_middle(
    mixed, x_in, mask, gain_in, w_gate, gain_tri, w_out, gain_next, w_sides, x_out, sides_out,
    arrived, scratch,
):
    rows = x_in.shape[0]
    group = min(GROUP, rows)
    arrived[...] = swapped(mixed[...])
    w_low, gate_low, out_low = w_sides[...].T, w_gate[...].T, w_out[...].T

    def step(t):
        at = t * group
        x = post(
            cat(x_in, at, group), cat(arrived, at, group).astype(WIDE),
            gain_in[...], gate_low, gain_tri[...], out_low,
        )
        put(x_out, at, group, x)
        put(scratch, at, group, front(x, gain_next[...], w_low, cell_mask(mask, at, group)))

    loop(rows // group, step)
    send_pair(scratch, sides_out)


def kernel_turn(
    mixed, x_in, cot, gain_in, w_gate, gain_tri, w_out, gain_pair, w_up, w_down, bias,
    pair_out, x_grad, gate_grad, mixed_grad, g_out, g_tri, g_up, g_down, g_pair, g_bias,
    arrived, leaving,
):
    rows = x_in.shape[0]
    group = min(GROUP, rows)
    arrived[...] = swapped(mixed[...])
    gate_low, out_low, out_back = w_gate[...].T, w_out[...].T, w_out[...]
    up_low, up_back = w_up[...].T, w_up[...]
    down_low, down_back = w_down[...].T, w_down[...]
    zero_first(g_out, g_tri, g_up, g_down, g_pair, g_bias)
    chunk = PAIR_DIM

    def step(t):
        at = t * group
        x_two = cat(x_in, at, group)
        mix = cat(arrived, at, group).astype(WIDE)
        x = post(x_two, mix, gain_in[...], gate_low, gain_tri[...], out_low)
        hat, scale = norm_parts(x)
        normed = (hat * gain_pair[...]).astype(LOW)
        cot_low = jnp.concatenate([cot[at + k].T for k in range(group)], axis=1)
        total = x + bias[...]
        normed_grad = jnp.zeros_like(x)
        for c in range(FFN_PAIR // chunk):
            part = slice(c * chunk, (c + 1) * chunk)
            act, slope = gelu_parts(dot_nn(up_low[part], normed))
            act_low = act.astype(LOW)
            total = total + dot_nn(down_low[:, part], act_low)
            hidden_grad = (dot_nn(down_back[part], cot_low) * slope).astype(LOW)
            normed_grad = normed_grad + dot_nn(up_back[:, part], hidden_grad)
            g_up[:, part] += dot_nt(normed, hidden_grad)
            g_down[part] += dot_nt(act_low, cot_low)
        total_low = total.astype(LOW)
        width = total.shape[1] // group
        for k in range(group):
            pair_out[at + k] = total_low[:, k * width : (k + 1) * width].T
        cot_wide = cot_low.astype(WIDE)
        g_bias[...] += jnp.sum(cot_wide, axis=1, keepdims=True)
        back, grad_gain = norm_back(normed_grad, hat, scale, gain_pair[...])
        g_pair[...] += grad_gain
        grad = cot_wide + back
        put(x_grad, at, group, grad)
        mix_grad, gates, grad_out, grad_tri = post_back(
            grad, x_two, mix, gain_in[...], gate_low, gain_tri[...], out_low, out_back
        )
        put(leaving, at, group, mix_grad)
        put(gate_grad, at, group, gates)
        g_out[...] += grad_out
        g_tri[...] += grad_tri

    loop(rows // group, step)
    mixed_grad[...] = swapped(leaving[...])


def kernel_return(
    sides_grad, x_after, gate_after, grad_in, mask, gain_after, w_after, mixed, x_before,
    gain_in, w_gate, gain_tri, w_out,
    x_grad, gate_grad, mixed_grad, g_after, g_gain, g_out, g_tri,
    sides, arrived, leaving,
):
    rows = x_after.shape[0]
    group = min(GROUP, rows)
    take_pair(sides_grad, sides)
    arrived[...] = swapped(mixed[...])
    gate_low, out_low, out_back = w_gate[...].T, w_out[...].T, w_out[...]
    zero_first(g_after, g_gain, g_out, g_tri)

    def step(t):
        at = t * group
        grad, grad_w, grad_gain = front_back(
            cat(grad_in, at, group), cat(x_after, at, group), cat(sides, at, group),
            cat(gate_after, at, group), cell_mask(mask, at, group), gain_after[...], w_after[...],
        )
        g_after[...] += grad_w
        g_gain[...] += grad_gain
        put(x_grad, at, group, grad)
        mix_grad, gates, grad_out, grad_tri = post_back(
            grad, cat(x_before, at, group), cat(arrived, at, group).astype(WIDE),
            gain_in[...], gate_low, gain_tri[...], out_low, out_back,
        )
        put(leaving, at, group, mix_grad)
        put(gate_grad, at, group, gates)
        g_out[...] += grad_out
        g_tri[...] += grad_tri

    loop(rows // group, step)
    mixed_grad[...] = swapped(leaving[...])


def kernel_close(
    sides_grad, x_after, gate_after, grad_in, mask, gain_after, w_after, table, right,
    pair_grad, table_grad, right_grad, g_after, g_gain, sides,
):
    rows = x_after.shape[0]
    group = min(GROUP, rows)
    take_pair(sides_grad, sides)
    zero_first(g_after, g_gain, right_grad)

    def step(t):
        at = t * group
        grad, grad_w, grad_gain = front_back(
            cat(grad_in, at, group), cat(x_after, at, group), cat(sides, at, group),
            cat(gate_after, at, group), cell_mask(mask, at, group), gain_after[...], w_after[...],
        )
        g_after[...] += grad_w
        g_gain[...] += grad_gain
        low = grad.astype(LOW)
        width = low.shape[1] // group
        for k in range(group):
            own = low[:, k * width : (k + 1) * width]
            pair_grad[at + k] = own.T
            table_grad[at + k] = dot_nn(own, right[...]).astype(LOW)
            right_grad[...] += dot_tn(table[at + k], own)

    loop(rows // group, step)


def kernel_mix(incoming, left, right, out):
    length = left.shape[-1]
    a = left[...].reshape(length, length)
    b = right[...].reshape(length, length)
    mixed = dot_tn(a, b) if incoming else dot_nt(a, b)
    out[...] = mixed.astype(LOW).reshape(out.shape)


def kernel_mix_back(incoming, grad, left, right, out):
    length = left.shape[-1]
    g = grad[...].reshape(length, length)
    a = left[...].reshape(length, length)
    b = right[...].reshape(length, length)
    block = (out.shape[0], out.shape[3], out.shape[4])
    a_grad = dot_nt(b, g) if incoming else dot_nn(g, b)
    b_grad = dot_nn(a, g) if incoming else dot_tn(g, a)
    out[:, 0, 0] = a_grad.astype(LOW).reshape(block)
    out[:, 1, 0] = b_grad.astype(LOW).reshape(block)


def mix(sides, incoming):
    parts, double, rows, length = sides.shape
    share = double // 2
    block = (parts, 1, rows, length)
    return pl.pallas_call(
        lambda *refs: kernel_mix(incoming, *refs),
        grid=(share,),
        in_specs=[
            pl.BlockSpec(block, lambda c: (0, c, 0, 0)),
            pl.BlockSpec(block, lambda c: (0, c + share, 0, 0)),
        ],
        out_specs=pl.BlockSpec(block, lambda c: (0, c, 0, 0)),
        out_shape=jax.ShapeDtypeStruct((parts, share, rows, length), LOW),
        compiler_params=pltpu.CompilerParams(vmem_limit_bytes=VMEM_LIMIT),
        cost_estimate=pl.CostEstimate(
            flops=2 * share * length**3, bytes_accessed=3 * share * length * length * 2,
            transcendentals=0,
        ),
    )(sides, sides)


def mix_back(grad, sides, incoming):
    parts, double, rows, length = sides.shape
    share = double // 2
    block = (parts, 1, rows, length)
    out = pl.pallas_call(
        lambda *refs: kernel_mix_back(incoming, *refs),
        grid=(share,),
        in_specs=[
            pl.BlockSpec(block, lambda c: (0, c, 0, 0)),
            pl.BlockSpec(block, lambda c: (0, c, 0, 0)),
            pl.BlockSpec(block, lambda c: (0, c + share, 0, 0)),
        ],
        out_specs=pl.BlockSpec((parts, 2, 1, rows, length), lambda c: (0, 0, c, 0, 0)),
        out_shape=jax.ShapeDtypeStruct((parts, 2, share, rows, length), LOW),
        compiler_params=pltpu.CompilerParams(vmem_limit_bytes=VMEM_LIMIT),
        cost_estimate=pl.CostEstimate(
            flops=4 * share * length**3, bytes_accessed=5 * share * length * length * 2,
            transcendentals=0,
        ),
    )(grad, sides, sides)
    return out.reshape(sides.shape)


def row_norm(x):
    centered = x - jnp.mean(x, axis=-1, keepdims=True)
    scale = lax.rsqrt(jnp.mean(centered * centered, axis=-1, keepdims=True) + EPS_NORM)
    return centered * scale, scale


def row_norm_back(grad, hat, scale, gain):
    grad_gain = jnp.sum(grad * hat, axis=0)
    wide = grad * gain
    inner = jnp.mean(wide * hat, axis=-1, keepdims=True)
    return scale * (wide - jnp.mean(wide, axis=-1, keepdims=True) - hat * inner), grad_gain


def low_of(x):
    return x.astype(LOW)


def local(layout, node, pair, recycle, mask, node_cot, pair_cot, master, first, second):
    crops, ranks = layout.crops, layout.rows
    devices = crops * ranks
    local_rows, length = node.shape[1], pair.shape[2]
    share = TRI_DIM // ranks
    heads_width = HEADS * HEAD_DIM
    scale_factor = HEAD_DIM ** (-0.5)
    node, pair, node_cot, pair_cot = node[0], pair[0], node_cot[0], pair_cot[0]

    crop_at, row_at = lax.axis_index("crop"), lax.axis_index("row")
    high_at, wide_at = row_at // layout.wide, row_at % layout.wide
    pick = lambda table, index: jnp.asarray(np.array(table, np.int32))[index]
    plane_crop = pick(layout.crop_of, high_at)
    plane_slot = pick(layout.high_of, crop_at) * layout.wide + wide_at

    padded = -(-master.shape[0] // 1024) * 1024
    shard = jnp.pad(low_of(master), (0, padded - master.shape[0])).reshape(-1, 128)
    shards = spread(shard, ranks, "row")
    shards = spread(shards, crops // 2, BOTH, layout.chips)
    shards = spread(shards, 2, BOTH, layout.cores)
    shards = jnp.swapaxes(shards, 0, 1).reshape(devices, padded)
    params = unpack(shards[:, : master.shape[0]].reshape(-1))
    wide = {entry_name: entry.astype(WIDE) for entry_name, entry in params.items()}
    node_all = spread(node, ranks, "row").reshape(length, NODE_DIM)
    pair_plane = lax.ppermute(pair, BOTH, layout.outward)
    cot_plane = lax.ppermute(pair_cot, BOTH, layout.outward)
    keep = mask.astype(WIDE)
    keep_plane = lax.ppermute(keep, BOTH, layout.outward)
    keep_rows = lax.dynamic_slice_in_dim(keep_plane[0], plane_slot * local_rows, local_rows, 0)
    mask_plane = (keep_rows[:, None] * keep_plane)[:, None, :]

    one_hot = (recycle[:, None] == jnp.arange(RECYCLES, dtype=jnp.int32)[None, :]).astype(WIDE)
    start_all = node_all.astype(WIDE) + jnp.matmul(one_hot, wide["embed"], precision=HIGHEST)
    hat_all, scale_all = row_norm(start_all)
    normed_all = low_of(hat_all * wide["gain_one"])
    own = lambda a: lax.dynamic_slice_in_dim(a, row_at * local_rows, local_rows, 0)
    start_node, hat_one, scale_one, normed_one = (
        own(a) for a in (start_all, hat_all, scale_all, normed_all)
    )
    query = low_of(dot_nn(normed_one, params["w_query"])).reshape(local_rows, HEADS, HEAD_DIM)
    key = low_of(dot_nn(normed_all, params["w_key"])).reshape(length, HEADS, HEAD_DIM)
    value = low_of(dot_nn(normed_all, params["w_value"])).reshape(length, HEADS, HEAD_DIM)
    pair_bias = jnp.einsum("ijd,dh->hij", pair, params["w_bias"], preferred_element_type=WIDE)
    scores = jnp.einsum("ihd,jhd->hij", query, key, preferred_element_type=WIDE) * scale_factor
    scores = scores + pair_bias + ((keep - 1.0) * MASK_FILL)[:, None, :]
    soft = jax.nn.softmax(scores, axis=-1)
    soft_low = low_of(soft)
    attended = jnp.einsum("hij,jhd->ihd", soft_low, value, preferred_element_type=WIDE)
    attended = low_of(attended.reshape(local_rows, heads_width))
    after_attn = start_node + dot_nn(attended, params["w_attn_out"])
    hat_two, scale_two = row_norm(after_attn)
    normed_two = low_of(hat_two * wide["gain_two"])
    act, slope = gelu_parts(dot_nn(normed_two, params["w_node_up"]))
    act_low = low_of(act)
    node_final = after_attn + dot_nn(act_low, params["w_node_down"])
    hat_three, scale_three = row_norm(node_final)
    normed_three = low_of(hat_three * wide["gain_three"])
    w_factors = jnp.concatenate([params["w_left_node"], params["w_right_node"]], axis=1)
    factors = low_of(dot_nn(normed_three, w_factors))

    factors_all = spread(factors, devices, BOTH)
    factors_all = lax.dynamic_slice_in_dim(factors_all, plane_crop * ranks, ranks, 0)
    left = lax.dynamic_index_in_dim(factors_all, plane_slot, 0, keepdims=False)[:, :OUTER]
    right = factors_all[:, :, OUTER:].reshape(length, OUTER)
    w_outer = params["w_outer"].reshape(OUTER, OUTER, PAIR_DIM)
    table = low_of(jnp.einsum("ip,pqe->ieq", left, w_outer, preferred_element_type=WIDE))

    column = lambda name: wide[name].reshape(-1, 1)
    sides_of = lambda prefix: jnp.concatenate(
        [params[prefix + "w_left"], params[prefix + "w_right"]], axis=1
    )
    all_of = lambda prefix: jnp.concatenate(
        [params[prefix + "w_left"], params[prefix + "w_right"], params[prefix + "w_gate"]], axis=1
    )
    tri_of = lambda prefix: (
        column(prefix + "gain_in"), params[prefix + "w_gate"], column(prefix + "gain_tri"),
        params[prefix + "w_tri_out"],
    )
    step_rows = min(TILE, local_rows)
    state = (local_rows, TRI_DIM, length)
    sides_shape = (ranks, 2 * share, local_rows, length)
    mixed_shape = (TRI_DIM, local_rows, length)
    natural = (local_rows, length, PAIR_DIM)
    buffer = lambda channels: pltpu.VMEM((step_rows, channels, length), LOW)
    trade = lambda blocks: exchange(blocks, BOTH, layout.groups)
    merge = lambda blocks: blocks.reshape(mixed_shape)
    split = lambda blocks: blocks.reshape(ranks, share, local_rows, length)
    unit = 2 * local_rows * length * PAIR_DIM * PAIR_DIM

    x_one, sides = run(
        kernel_open, step_rows, local_rows,
        (pair_plane, table, right.T, mask_plane, column("out_gain_in"), sides_of("out_")), "rrwrww",
        (("r", state, WIDE), ("s", sides_shape, LOW)), [buffer(2 * TRI_DIM)], 3 * unit,
    )
    sides_out = trade(sides)
    mixed_out = merge(trade(mix(sides_out, False)))
    x_two, sides = run(
        kernel_middle, step_rows, local_rows,
        (mixed_out, x_one, mask_plane, *tri_of("out_"), column("in_gain_in"), sides_of("in_")),
        "srr" + "wwww" + "ww",
        (("r", state, WIDE), ("s", sides_shape, LOW)),
        [buffer(TRI_DIM), buffer(2 * TRI_DIM)], 4 * unit,
    )
    sides_in = trade(sides)
    mixed_in = merge(trade(mix(sides_in, True)))
    square = (TRI_DIM, PAIR_DIM)
    gain_shape = (PAIR_DIM, 1)
    pair_final, x_grad, gate_grad, mixed_grad, g_in_out, g_in_tri, g_up, g_down, g_pair, g_bias = run(
        kernel_turn, step_rows, local_rows,
        (mixed_in, x_two, cot_plane, *tri_of("in_"), column("gain_pair"), params["w_pair_up"],
         params["w_pair_down"], column("bias_pair")),
        "srr" + "wwww" + "wwww",
        (("r", natural, LOW), ("r", state, WIDE), ("r", state, LOW), ("s", mixed_shape, LOW),
         ("a", square, WIDE), ("a", gain_shape, WIDE), ("a", (PAIR_DIM, FFN_PAIR), WIDE),
         ("a", (FFN_PAIR, PAIR_DIM), WIDE), ("a", gain_shape, WIDE), ("a", gain_shape, WIDE)),
        [buffer(TRI_DIM), buffer(TRI_DIM)], 32 * unit,
    )
    pair_out = lax.ppermute(pair_final, BOTH, layout.homeward)
    sides_grad = trade(mix_back(trade(split(mixed_grad)), sides_in, True))
    after_shape = (PAIR_DIM, 2 * TRI_DIM + PAIR_DIM)
    x_grad, gate_grad, mixed_grad, g_in_all, g_in_gain, g_out_out, g_out_tri = run(
        kernel_return, step_rows, local_rows,
        (sides_grad, x_two, gate_grad, x_grad, mask_plane, column("in_gain_in"), all_of("in_"),
         mixed_out, x_one, *tri_of("out_")),
        "srrrr" + "ww" + "sr" + "wwww",
        (("r", state, WIDE), ("r", state, LOW), ("s", mixed_shape, LOW), ("a", after_shape, WIDE),
         ("a", gain_shape, WIDE), ("a", square, WIDE), ("a", gain_shape, WIDE)),
        [buffer(2 * TRI_DIM), buffer(TRI_DIM), buffer(TRI_DIM)], 12 * unit,
    )
    sides_grad = trade(mix_back(trade(split(mixed_grad)), sides_out, False))
    pair_one_grad, table_grad, right_part, g_out_all, g_out_gain = run(
        kernel_close, step_rows, local_rows,
        (sides_grad, x_one, gate_grad, x_grad, mask_plane, column("out_gain_in"), all_of("out_"),
         table, right),
        "srrrr" + "ww" + "rw",
        (("r", natural, LOW), ("r", (local_rows, PAIR_DIM, OUTER), LOW), ("a", (OUTER, length), WIDE),
         ("a", after_shape, WIDE), ("a", gain_shape, WIDE)),
        [buffer(2 * TRI_DIM)], 8 * unit,
    )
    pair_one_home = lax.ppermute(pair_one_grad, BOTH, layout.homeward)

    left_grad = low_of(jnp.einsum("ieq,pqe->ip", table_grad, w_outer, preferred_element_type=WIDE))
    g_outer = jnp.einsum("ip,ieq->pqe", left, table_grad, preferred_element_type=WIDE)
    right_blocks = low_of(right_part.T).reshape(ranks, local_rows, OUTER)
    factor_blocks = jnp.concatenate(
        [jnp.broadcast_to(left_grad[None], right_blocks.shape), right_blocks], axis=2
    )
    factor_grads = exchange(jnp.tile(factor_blocks, (crops, 1, 1)), BOTH)
    factor_grads = factor_grads.reshape(crops, crops, layout.wide, local_rows, 2 * OUTER)
    factor_grads = lax.dynamic_index_in_dim(
        factor_grads, pick(layout.planes, crop_at), 1, keepdims=False
    ).reshape(ranks, local_rows, 2 * OUTER)
    left_rows = lax.dynamic_index_in_dim(
        factor_grads, pick(layout.slots, high_at) * layout.wide + wide_at, 0, keepdims=False
    )[:, :OUTER]
    right_rows = low_of(jnp.sum(factor_grads[:, :, OUTER:].astype(WIDE), axis=0))
    factor_rows = jnp.concatenate([left_rows, right_rows], axis=1)

    g_factors = dot_tn(normed_three, factor_rows)
    final_part, g_three = row_norm_back(
        dot_nt(factor_rows, w_factors), hat_three, scale_three, wide["gain_three"]
    )
    final_grad = node_cot.astype(WIDE) + final_part
    final_low = low_of(final_grad)
    g_node_down = dot_tn(act_low, final_low)
    hidden_grad = low_of(dot_nt(final_low, params["w_node_down"]) * slope)
    g_node_up = dot_tn(normed_two, hidden_grad)
    after_part, g_two = row_norm_back(
        dot_nt(hidden_grad, params["w_node_up"]), hat_two, scale_two, wide["gain_two"]
    )
    after_grad = final_grad + after_part
    after_low = low_of(after_grad)
    g_attn_out = dot_tn(attended, after_low)
    attended_grad = low_of(dot_nt(after_low, params["w_attn_out"]))
    attended_grad = attended_grad.reshape(local_rows, HEADS, HEAD_DIM)
    soft_grad = jnp.einsum("ihd,jhd->hij", attended_grad, value, preferred_element_type=WIDE)
    score_low = low_of(soft * (soft_grad - jnp.sum(soft_grad * soft, axis=-1, keepdims=True)))
    query_grad = jnp.einsum("hij,jhd->ihd", score_low, key, preferred_element_type=WIDE)
    key_part = jnp.einsum("hij,ihd->jhd", score_low, query, preferred_element_type=WIDE)
    value_part = jnp.einsum("hij,ihd->jhd", soft_low, attended_grad, preferred_element_type=WIDE)
    key_value = jnp.concatenate(
        [
            low_of(key_part.reshape(length, heads_width) * scale_factor),
            low_of(value_part.reshape(length, heads_width)),
        ],
        axis=1,
    )
    key_value = exchange(key_value.reshape(ranks, local_rows, 2 * heads_width), "row")
    key_value = low_of(jnp.sum(key_value.astype(WIDE), axis=0))
    query_low = low_of(query_grad.reshape(local_rows, heads_width) * scale_factor)
    g_bias_head = jnp.einsum("ijd,hij->dh", pair, score_low, preferred_element_type=WIDE)
    pair_grad = pair_one_home.astype(WIDE) + jnp.einsum(
        "hij,dh->ijd", score_low, params["w_bias"], preferred_element_type=WIDE
    )
    projections = jnp.concatenate([query_low, key_value], axis=1)
    g_projections = dot_tn(normed_one, projections)
    w_projections = jnp.concatenate([params["w_query"], params["w_key"], params["w_value"]], axis=1)
    start_part, g_one = row_norm_back(
        dot_nt(projections, w_projections), hat_one, scale_one, wide["gain_one"]
    )
    node_grad = after_grad + start_part
    g_embed = one_hot[0][:, None] * jnp.sum(node_grad, axis=0)[None, :]

    grads = {
        "embed": g_embed,
        "gain_one": g_one,
        "w_query": g_projections[:, :heads_width],
        "w_key": g_projections[:, heads_width : 2 * heads_width],
        "w_value": g_projections[:, 2 * heads_width :],
        "w_bias": g_bias_head,
        "w_attn_out": g_attn_out,
        "gain_two": g_two,
        "w_node_up": g_node_up,
        "w_node_down": g_node_down,
        "gain_three": g_three,
        "w_left_node": g_factors[:, :OUTER],
        "w_right_node": g_factors[:, OUTER:],
        "w_outer": g_outer,
        "gain_pair": g_pair,
        "w_pair_up": g_up,
        "w_pair_down": g_down,
        "bias_pair": g_bias,
    }
    for prefix, g_all, g_gain, g_tri, g_out in (
        ("out_", g_out_all, g_out_gain, g_out_tri, g_out_out),
        ("in_", g_in_all, g_in_gain, g_in_tri, g_in_out),
    ):
        grads[prefix + "gain_in"] = g_gain
        grads[prefix + "w_left"] = g_all[:, :TRI_DIM]
        grads[prefix + "w_right"] = g_all[:, TRI_DIM : 2 * TRI_DIM]
        grads[prefix + "w_gate"] = g_all[:, 2 * TRI_DIM :]
        grads[prefix + "gain_tri"] = g_tri
        grads[prefix + "w_tri_out"] = g_out
    flat_grad = jnp.concatenate(
        [low_of(grads[entry_name]).reshape(-1) for entry_name, entry_shape in segment_list()]
    )

    blocks = jnp.pad(flat_grad.reshape(devices, -1), ((0, 0), (0, padded - master.shape[0])))
    blocks = blocks.reshape(crops // 2, 2, ranks, padded // 128, 128)
    total = lambda got: low_of(jnp.sum(got.astype(WIDE), axis=0))
    blocks = total(exchange(jnp.swapaxes(blocks, 0, 1), BOTH, layout.cores))
    blocks = total(exchange(blocks, BOTH, layout.chips))
    blocks = jnp.sum(exchange(blocks, "row").astype(WIDE), axis=0)
    grad_own = blocks.reshape(-1)[: master.shape[0]]
    bias_total = jnp.sum(spread(g_bias.reshape(1, PAIR_DIM), devices, BOTH), axis=(0, 1))
    square = jnp.sum(grad_own * grad_own)
    squares = spread(jnp.full((1, 128), square), devices, BOTH)
    grad_norm = jnp.sqrt(jnp.sum(squares[:, 0, 0]))
    clipped = grad_own * (CLIP_NORM / jnp.maximum(grad_norm, CLIP_NORM))
    new_first = BETA_ONE * first + (1.0 - BETA_ONE) * clipped
    new_second = BETA_TWO * second + (1.0 - BETA_TWO) * clipped * clipped
    first_hat = new_first / (1.0 - BETA_ONE**ADAM_STEP)
    second_hat = new_second / (1.0 - BETA_TWO**ADAM_STEP)
    new_master = master - LEARN_RATE * (
        first_hat / (jnp.sqrt(second_hat) + ADAM_EPS) + WEIGHT_DECAY * master
    )
    return (
        low_of(node_final)[None],
        pair_out[None],
        low_of(node_grad)[None],
        low_of(pair_grad)[None],
        grad_own,
        bias_total,
        grad_norm,
        new_master,
        new_first,
        new_second,
        low_of(new_master),
    )


def solution(mesh):
    layout = Layout(mesh.shape["crop"], mesh.shape["row"])
    return jax.shard_map(
        lambda *arrays: local(layout, *arrays),
        mesh=mesh,
        in_specs=(
            P("crop", "row", None),
            P("crop", "row", None, None),
            P("crop"),
            P("crop", None),
            P("crop", "row", None),
            P("crop", "row", None, None),
            P(("crop", "row")),
            P(("crop", "row")),
            P(("crop", "row")),
        ),
        out_specs=(
            P("crop", "row", None),
            P("crop", "row", None, None),
            P("crop", "row", None),
            P("crop", "row", None, None),
            P(("crop", "row")),
            P(),
            P(),
            P(("crop", "row")),
            P(("crop", "row")),
            P(("crop", "row")),
            P(("crop", "row")),
        ),
        check_vma=False,
    )
```

profile of v0, /device:TPU:0, one launch (start us, length us, event | category | flops | bytes accessed | tf_op | source)
XLA Modules:
  0.0 1017.0 jit_solution(14719610209974627447)
XLA Ops:
  1.7 23.9 %all_to_all.100 = bf16[8,296,128]{2,1,0:T(8,128)(2,1)S(1)} all-to-all(bf16[8,296,128]{2,1,0:T(8,128)(2,1)S(1)} %broadcast_in_dim.31), channel_id=1, replica_groups=mesh['crop'=4,'row'=8] {'row'}, dimensions={0} | all-to-all | bytes 1212416 | tf_op jit(solution)/shard_map/all_to_all | solution.py:122
  26.8 3.6 all-to-all-start.2
  31.1 17.2 %collective-permute-start = (bf16[32,256,128]{2,1,0:T(8,128)(2,1)}, bf16[32,256,128]{2,1,0:T(8,128)(2,1)}, u32[]{:S(2)}, u32[]{:S(2)}) collective-permute-start(bf16[32,256,128]{2,1,0:T(8,128)(2,1)} %bitcast.10), channel_id=1, source_target_pairs={{0,0},{1,1},{2,16},{3,17},{4,8},{5,9},{6,24},{7,25},{8,4},{9,5},{1... | collective-permute-start | bytes 6291464 | tf_op jit(solution)/shard_map/ppermute | solution.py:550
  52.1 5.7 all_to_all.101
  58.4 3.6 all-to-all-start
  62.8 5.3 reshape.484
  68.8 4.9 slice.182
  73.7 46.5 %slice.188 = bf16[149952,8]{1,0:T(8,128)(2,1)} reshape(bf16[32,37488]{1,0:T(8,128)(2,1)S(1)} %slice.233) | data formatting | bytes 4798464 | tf_op jit(solution)/shard_map/slice | solution.py:75
  128.4 2.3 fusion.40
  138.1 15.6 %slice.196 = bf16[37488,32]{1,0:T(8,128)(2,1)} reshape(bf16[32,37488]{1,0:T(8,128)(2,1)S(1)} %slice.233) | data formatting | bytes 4798464 | tf_op jit(solution)/shard_map/slice | solution.py:75
  159.5 7.0 all-to-all-start.4
  169.9 4.4 all-to-all-done.4
  179.2 11.3 %shard_map.212 = (f32[32,128,256]{2,1,0:T(8,128)}, bf16[8,32,32,256]{3,2,1,0:T(8,128)(2,1)}) custom-call(bf16[32,256,128]{2,1,0:T(8,128)(2,1)} %collective-permute-done.pair, bf16[32,128,32]{2,1,0:T(8,128)(2,1)} %bitcast.228, bf16[32,256]{1,0:T(8,128)(2,1)} %copy.410.right, f32[32,1,256]{2,1,0:T(1,128)} %broadcast_multiply_fusion.mask, ...), custom_call_target="tpu_custom_call" | custom-call | flops 805306368 | bytes 2474496 | tf_op jit(solution)/shard_map/pallas_call | solution.py:260
  190.5 53.2 %all_to_all.102.refs_0_.refs_1_.refs_2_ = bf16[8,32,32,256]{3,2,1,0:T(8,128)(2,1)} all-to-all(bf16[8,32,32,256]{3,2,1,0:T(8,128)(2,1)} %get-tuple-element.37), channel_id=1, replica_groups={{0,1,16,17,8,9,24,25},{2,3,18,19,10,11,26,27},{4,5,20,21,12,13,28,29},{..., dimensions={0} | all-to-all | bytes 8388608 | tf_op jit(solution)/shard_map/all_to_all | solution.py:122
  243.6 11.5 %shard_map.213 = bf16[8,16,32,256]{3,2,1,0:T(8,128)(2,1)} custom-call(bf16[8,32,32,256]{3,2,1,0:T(8,128)(2,1)} %all_to_all.102.refs_0_.refs_1_.refs_2_, bf16[8,32,32,256]{3,2,1,0:T(8,128)(2,1)} %all_to_all.102.refs_0_.refs_1_.refs_2_), custom_call_target="tpu_custom_call" | custom-call | flops 536870912 | bytes 6291456 | tf_op jit(solution)/shard_map/pallas_call | solution.py:469
  255.1 3.7 all-to-all-start.6
  261.0 23.9 %all-to-all-done.6 = bf16[8,16,32,256]{3,2,1,0:T(8,128)(2,1)S(1)} async-done(((bf16[8,16,32,256]{3,2,1,0:T(8,128)(2,1)}), bf16[8,16,32,256]{3,2,1,0:T(8,128)(2,1)S(1)}, u32[]{:S(2)}, u32[]{:S(2)}) %all-to-all-start.6) | async-done | bytes 2097184 | tf_op jit(solution)/shard_map/all_to_all | solution.py:122
  286.2 15.8 %shard_map.214 = (f32[32,128,256]{2,1,0:T(8,128)}, bf16[8,32,32,256]{3,2,1,0:T(8,128)(2,1)}) custom-call(bf16[128,32,256]{2,1,0:T(8,128)(2,1)} %bitcast.220, f32[32,128,256]{2,1,0:T(8,128)} %get-tuple-element.38.x_in.x_before.x_after, f32[32,1,256]{2,1,0:T(1,128)} %broadcast_multiply_fusion.mask, f32[128,1]{1,0:T(8,128)} %copy.411.gain.gain_in.gain_after, ...), custom_call_target="tpu_custom_call" | custom-call | flops 1073741824 | bytes 6456832 | tf_op jit(solution)/shard_map/pallas_call | solution.py:260
  302.0 4.6 all-to-all-start.7
  306.6 17.2 %collective-permute-start.2 = (bf16[32,256,128]{2,1,0:T(8,128)(2,1)}, bf16[32,256,128]{2,1,0:T(8,128)(2,1)}, u32[]{:S(2)}, u32[]{:S(2)}) collective-permute-start(bf16[32,256,128]{2,1,0:T(8,128)(2,1)} %bitcast.31), channel_id=1, source_target_pairs={{0,0},{1,1},{2,16},{3,17},{4,8},{5,9},{6,24},{7,25},{8,4},{9,5},{1... | collective-permute-start | bytes 6291464 | tf_op jit(solution)/shard_map/ppermute | solution.py:551
  323.8 73.8 %all-to-all-done.7.refs_0_.refs_1_.refs_2_ = bf16[8,32,32,256]{3,2,1,0:T(8,128)(2,1)} async-done(((bf16[8,32,32,256]{3,2,1,0:T(8,128)(2,1)}), bf16[8,32,32,256]{3,2,1,0:T(8,128)(2,1)}, u32[]{:S(2)}, u32[]{:S(2)}) %all-to-all-start.7) | async-done | bytes 4194336 | tf_op jit(solution)/shard_map/all_to_all | solution.py:122
  397.7 11.5 %shard_map.215 = bf16[8,16,32,256]{3,2,1,0:T(8,128)(2,1)} custom-call(bf16[8,32,32,256]{3,2,1,0:T(8,128)(2,1)} %all-to-all-done.7.refs_0_.refs_1_.refs_2_, bf16[8,32,32,256]{3,2,1,0:T(8,128)(2,1)} %all-to-all-done.7.refs_0_.refs_1_.refs_2_), custom_call_target="tpu_custom_call" | custom-call | flops 536870912 | bytes 6291456 | tf_op jit(solution)/shard_map/pallas_call | solution.py:469
  409.1 5.3 all-to-all-start.8
  419.9 20.6 %all-to-all-done.8 = bf16[8,16,32,256]{3,2,1,0:T(8,128)(2,1)S(1)} async-done(((bf16[8,16,32,256]{3,2,1,0:T(8,128)(2,1)}), bf16[8,16,32,256]{3,2,1,0:T(8,128)(2,1)S(1)}, u32[]{:S(2)}, u32[]{:S(2)}) %all-to-all-start.8) | async-done | bytes 2097184 | tf_op jit(solution)/shard_map/all_to_all | solution.py:122
  441.8 55.3 %shard_map.216 = (bf16[32,256,128]{2,1,0:T(8,128)(2,1)}, f32[32,128,256]{2,1,0:T(8,128)}, bf16[32,128,256]{2,1,0:T(8,128)(2,1)}, bf16[128,32,256]{2,1,0:T(8,128)...) custom-call(bf16[128,32,256]{2,1,0:T(8,128)(2,1)} %bitcast.231, ...), custom_call_target="tpu_custom_call" | custom-call | flops 8589934592 | bytes 8718336 | tf_op jit(solution)/shard_map/pallas_call | solution.py:260
  497.1 30.6 %all_to_all.103.refs_0_ = bf16[8,16,32,256]{3,2,1,0:T(8,128)(2,1)} all-to-all(bf16[8,16,32,256]{3,2,1,0:T(8,128)(2,1)} %bitcast.232), channel_id=1, replica_groups={{0,1,16,17,8,9,24,25},{2,3,18,19,10,11,26,27},{4,5,20,21,12,13,28,29},{..., dimensions={0} | all-to-all | bytes 4194304 | tf_op jit(solution)/shard_map/all_to_all | solution.py:122
  527.7 12.5 %shard_map.217 = bf16[8,2,16,32,256]{4,3,2,1,0:T(8,128)(2,1)} custom-call(bf16[8,16,32,256]{3,2,1,0:T(8,128)(2,1)} %all_to_all.103.refs_0_, bf16[8,32,32,256]{3,2,1,0:T(8,128)(2,1)} %all-to-all-done.7.refs_0_.refs_1_.refs_2_, bf16[8,32,32,256]{3,2,1,0:T(8,128)(2,1)} %all-to-all-done.7.refs_0_.refs_1_.refs_2_), custom_call_target="tpu_custom_call" | custom-call | flops 1073741824 | bytes 10485760 | tf_op jit(solution)/shard_map/pallas_call | solution.py:490
  540.2 4.7 all-to-all-start.10
  545.5 47.9 %all-to-all-done.10.sides_grad = bf16[8,32,32,256]{3,2,1,0:T(8,128)(2,1)} async-done(((bf16[8,32,32,256]{3,2,1,0:T(8,128)(2,1)}), bf16[8,32,32,256]{3,2,1,0:T(8,128)(2,1)}, u32[]{:S(2)}, u32[]{:S(2)}) %all-to-all-start.10) | async-done | bytes 4194336 | tf_op jit(solution)/shard_map/all_to_all | solution.py:122
  593.5 22.9 %shard_map.218 = (f32[32,128,256]{2,1,0:T(8,128)}, bf16[32,128,256]{2,1,0:T(8,128)(2,1)}, bf16[128,32,256]{2,1,0:T(8,128)(2,1)}, f32[128,384]{1,0:T(8,128)}, f32...) custom-call(bf16[8,32,32,256]{3,2,1,0:T(8,128)(2,1)} %all-to-all-done.10.sides_grad, ...), custom_call_target="tpu_custom_call" | custom-call | flops 3221225472 | bytes 21169664 | tf_op jit(solution)/shard_map/pallas_call | solution.py:260
  616.3 3.6 all-to-all-start.11
  623.2 22.9 %all-to-all-done.11.refs_0_ = bf16[8,16,32,256]{3,2,1,0:T(8,128)(2,1)S(1)} async-done(((bf16[8,16,32,256]{3,2,1,0:T(8,128)(2,1)}), bf16[8,16,32,256]{3,2,1,0:T(8,128)(2,1)S(1)}, u32[]{:S(2)}, u32[]{:S(2)}) %all-to-all-start.11) | async-done | bytes 2097184 | tf_op jit(solution)/shard_map/all_to_all | solution.py:122
  647.3 12.4 %shard_map.219 = bf16[8,2,16,32,256]{4,3,2,1,0:T(8,128)(2,1)} custom-call(bf16[8,16,32,256]{3,2,1,0:T(8,128)(2,1)} %copy-done.1, bf16[8,32,32,256]{3,2,1,0:T(8,128)(2,1)} %all_to_all.102.refs_0_.refs_1_.refs_2_, bf16[8,32,32,256]{3,2,1,0:T(8,128)(2,1)} %all_to_all.102.refs_0_.refs_1_.refs_2_), custom_call_target="tpu_custom_call" | custom-call | flops 1073741824 | bytes 10485760 | tf_op jit(solution)/shard_map/pallas_call | solution.py:490
  659.8 4.7 all-to-all-start.12
  668.3 17.2 %collective-permute-start.3 = (bf16[32,256,128]{2,1,0:T(8,128)(2,1)}, bf16[32,256,128]{2,1,0:T(8,128)(2,1)}, u32[]{:S(2)}, u32[]{:S(2)}) collective-permute-start(bf16[32,256,128]{2,1,0:T(8,128)(2,1)} %get-tuple-element.41), channel_id=1, source_target_pairs={{0,0},{1,1},{16,2},{17,3},{8,4},{9,5},{24,6},{25,7},{4,8},{5,9},{2... | collective-permute-start | bytes 6291464 | tf_op jit(solution)/shard_map/ppermute | solution.py:643
  689.5 66.0 %all-to-all-done.12.sides_grad = bf16[8,32,32,256]{3,2,1,0:T(8,128)(2,1)} async-done(((bf16[8,32,32,256]{3,2,1,0:T(8,128)(2,1)}), bf16[8,32,32,256]{3,2,1,0:T(8,128)(2,1)}, u32[]{:S(2)}, u32[]{:S(2)}) %all-to-all-start.12) | async-done | bytes 4194336 | tf_op jit(solution)/shard_map/all_to_all | solution.py:122
  755.5 15.0 %shard_map.220 = (bf16[32,256,128]{2,1,0:T(8,128)(2,1)}, bf16[32,128,32]{2,1,0:T(8,128)(2,1)}, f32[32,256]{1,0:T(8,128)}, f32[128,384]{1,0:T(8,128)}, f32[128,1]{1,0:T(8,128)}) custom-call(bf16[8,32,32,256]{3,2,1,0:T(8,128)(2,1)} %all-to-all-done.12.sides_grad, f32[32,128,256]{2,1,0:T(8,128)} %get-tuple-element.38.x_in.x_before.x_after, ...), custom_call_target="tpu_custom_call" | custom-call | flops 2147483648 | bytes 15090176 | tf_op jit(solution)/shard_map/pallas_call | solution.py:260
  774.7 5.4 all-to-all-start.13
  781.2 17.3 %collective-permute-start.4 = (bf16[32,256,128]{2,1,0:T(8,128)(2,1)}, bf16[32,256,128]{2,1,0:T(8,128)(2,1)}, u32[]{:S(2)}, u32[]{:S(2)}) collective-permute-start(bf16[32,256,128]{2,1,0:T(8,128)(2,1)} %get-tuple-element.50), channel_id=1, source_target_pairs={{0,0},{1,1},{16,2},{17,3},{8,4},{9,5},{24,6},{25,7},{4,8},{5,9},{2... | collective-permute-start | bytes 6291464 | tf_op jit(solution)/shard_map/ppermute | solution.py:665
  809.6 3.6 all-to-all-start.14
  813.6 2.0 fusion.17
  816.1 44.4 %all-to-all-done.14 = bf16[8,32,512]{2,1,0:T(8,128)(2,1)S(1)} async-done(((bf16[8,32,512]{2,1,0:T(8,128)(2,1)}), bf16[8,32,512]{2,1,0:T(8,128)(2,1)S(1)}, u32[]{:S(2)}, u32[]{:S(2)}) %all-to-all-start.14) | async-done | bytes 262176 | tf_op jit(solution)/shard_map/all_to_all | solution.py:122
  866.7 3.2 dynamic-update-slice.2
  869.9 3.2 dynamic-update-slice.3
  873.1 3.2 dynamic-update-slice.4
  877.7 3.2 dynamic-update-slice.6
  882.3 9.1 dynamic-update-slice.8
  891.4 9.1 dynamic-update-slice.9
  904.9 5.2 dynamic-update-slice.13
  928.6 3.2 dynamic-update-slice.27
  931.8 3.1 dynamic-update-slice.28
  936.2 4.8 reshape.539
  941.4 5.7 all_to_all.104
  948.9 3.6 all-to-all-start.16
  952.6 15.8 %all-to-all-done.16 = bf16[2,8,296,128]{3,1,2,0:T(8,128)(2,1)S(1)} async-done(((bf16[2,8,296,128]{3,1,2,0:T(8,128)(2,1)}), bf16[2,8,296,128]{3,1,2,0:T(8,128)(2,1)S(1)}, u32[]{:S(2)}, u32[]{:S(2)}) %all-to-all-start.16) | async-done | bytes 1212448 | tf_op jit(solution)/shard_map/all_to_all | solution.py:122
  969.0 2.5 all-to-all-start.18
  973.1 5.5 all-to-all-done.18
  978.6 3.5 all-to-all-start.17
  982.7 3.6 fusion.36
  986.3 12.3 %all-to-all-done.17 = bf16[8,296,128]{2,1,0:T(8,128)(2,1)S(1)} async-done(((bf16[8,296,128]{2,1,0:T(8,128)(2,1)}), bf16[8,296,128]{2,1,0:T(8,128)(2,1)S(1)}, u32[]{:S(2)}, u32[]{:S(2)}) %all-to-all-start.17) | async-done | bytes 606240 | tf_op jit(solution)/shard_map/all_to_all | solution.py:122
  1000.6 2.7 all-to-all-start.19
  1003.3 4.9 fusion.1
  1008.2 2.1 all-to-all-done.19
  1012.6 3.1 copy.506
  (375 shorter events, 115.0 us)
Async XLA Ops:
  26.8 24.9 %all-to-all-start.2 = ((bf16[2,8,296,128]{3,1,2,0:T(8,128)(2,1)}), bf16[2,8,296,128]{3,1,2,0:T(8,128)(2,1)S(1)}, u32[]{:S(2)}, u32[]{:S(2)}) async-start(bf16[2,8,296,128]{3,1,2,0:T(8,128)(2,1)} %broadcast_in_dim.32), calls=%async_computation.2 | async-start | bytes 2424832 | tf_op jit(solution)/shard_map/all_to_all | solution.py:122
  30.5 20.5 %collective-permute-start.1 = (f32[1,256]{1,0:T(1,128)S(1)}, f32[1,256]{1,0:T(1,128)S(1)}, u32[]{:S(2)}, u32[]{:S(2)}) collective-permute-start(f32[1,256]{1,0:T(1,128)S(1)} %convert_element_type.258), channel_id=1, source_target_pairs={{0,0},{1,1},{2,16},{3,17},{4,8},{5,9},{6,24},{7,25},{8,4},{9,5},{1... | collective-permute-start | bytes 3080 | tf_op jit(solution)/shard_map/ppermute | solution.py:553
  31.1 148.1 %collective-permute-start = (bf16[32,256,128]{2,1,0:T(8,128)(2,1)}, bf16[32,256,128]{2,1,0:T(8,128)(2,1)}, u32[]{:S(2)}, u32[]{:S(2)}) collective-permute-start(bf16[32,256,128]{2,1,0:T(8,128)(2,1)} %bitcast.10), channel_id=1, source_target_pairs={{0,0},{1,1},{2,16},{3,17},{4,8},{5,9},{6,24},{7,25},{8,4},{9,5},{1... | collective-permute-start | bytes 6291464 | tf_op jit(solution)/shard_map/ppermute | solution.py:550
  58.4 62.6 %all-to-all-start = ((bf16[8,32,256]{2,1,0:T(8,128)(2,1)}), bf16[8,32,256]{2,1,0:T(8,128)(2,1)S(1)}, u32[]{:S(2)}, u32[]{:S(2)}) async-start(bf16[8,32,256]{2,1,0:T(8,128)(2,1)} %broadcast_in_dim.29), calls=%async_computation | async-start | bytes 262144 | tf_op jit(solution)/shard_map/all_to_all | solution.py:122
  68.8 52.7 %copy-start.69 = (f32[256]{0:T(256)}, f32[256]{0:T(256)S(1)}, u32[]{:S(2)}) copy-start(f32[256]{0:T(256)S(1)} %get-tuple-element.101) | copy-start | bytes 3076
  68.8 66.9 %copy-start.59 = (f32[256]{0:T(256)}, f32[256]{0:T(256)S(1)}, u32[]{:S(2)}) copy-start(f32[256]{0:T(256)S(1)} %get-tuple-element.100) | copy-start | bytes 3076
  68.8 88.9 %copy-start.61 = (f32[256]{0:T(256)}, f32[256]{0:T(256)S(1)}, u32[]{:S(2)}) copy-start(f32[256]{0:T(256)S(1)} %get-tuple-element.99) | copy-start | bytes 3076
  156.4 34.1 %copy-start.2 = (bf16[9372,128]{1,0:T(8,128)(2,1)}, bf16[9372,128]{1,0:T(8,128)(2,1)S(1)}, u32[]{:S(2)}) copy-start(bf16[9372,128]{1,0:T(8,128)(2,1)S(1)} %slice.202) | copy-start | bytes 7197700
  159.5 14.8 %all-to-all-start.4 = ((bf16[32,2,1024]{2,1,0:T(2,128)(2,1)}), bf16[32,2,1024]{2,1,0:T(2,128)(2,1)S(1)}, u32[]{:S(2)}, u32[]{:S(2)}) async-start(bf16[32,2,1024]{2,1,0:T(2,128)(2,1)} %reshape.576), calls=%async_computation.4 | async-start | bytes 262144 | tf_op jit(solution)/shard_map/all_to_all | solution.py:122
  178.5 65.2 %copy-start.8 = (bf16[8,32,32]{2,1,0:T(8,128)(2,1)}, bf16[8,32,32]{2,1,0:T(8,128)(2,1)S(1)}, u32[]{:S(2)}) copy-start(bf16[8,32,32]{2,1,0:T(8,128)(2,1)S(1)} %constant_dynamic-slice_fusion.3) | copy-start | bytes 49156
  255.1 29.8 %all-to-all-start.6 = ((bf16[8,16,32,256]{3,2,1,0:T(8,128)(2,1)}), bf16[8,16,32,256]{3,2,1,0:T(8,128)(2,1)S(1)}, u32[]{:S(2)}, u32[]{:S(2)}) async-start(bf16[8,16,32,256]{3,2,1,0:T(8,128)(2,1)} %shard_map.213), calls=%async_computation.6 | async-start | bytes 4194304 | tf_op jit(solution)/shard_map/all_to_all | solution.py:122
  302.0 95.6 %all-to-all-start.7 = ((bf16[8,32,32,256]{3,2,1,0:T(8,128)(2,1)}), bf16[8,32,32,256]{3,2,1,0:T(8,128)(2,1)}, u32[]{:S(2)}, u32[]{:S(2)}) async-start(bf16[8,32,32,256]{3,2,1,0:T(8,128)(2,1)} %get-tuple-element.39), calls=%async_computation.7 | async-start | bytes 8388608 | tf_op jit(solution)/shard_map/all_to_all | solution.py:122
  306.6 113.3 %collective-permute-start.2 = (bf16[32,256,128]{2,1,0:T(8,128)(2,1)}, bf16[32,256,128]{2,1,0:T(8,128)(2,1)}, u32[]{:S(2)}, u32[]{:S(2)}) collective-permute-start(bf16[32,256,128]{2,1,0:T(8,128)(2,1)} %bitcast.31), channel_id=1, source_target_pairs={{0,0},{1,1},{2,16},{3,17},{4,8},{5,9},{6,24},{7,25},{8,4},{9,5},{1... | collective-permute-start | bytes 6291464 | tf_op jit(solution)/shard_map/ppermute | solution.py:551
  409.1 31.3 %all-to-all-start.8 = ((bf16[8,16,32,256]{3,2,1,0:T(8,128)(2,1)}), bf16[8,16,32,256]{3,2,1,0:T(8,128)(2,1)S(1)}, u32[]{:S(2)}, u32[]{:S(2)}) async-start(bf16[8,16,32,256]{3,2,1,0:T(8,128)(2,1)} %shard_map.215), calls=%async_computation.8 | async-start | bytes 4194304 | tf_op jit(solution)/shard_map/all_to_all | solution.py:122
  540.2 53.3 %all-to-all-start.10 = ((bf16[8,32,32,256]{3,2,1,0:T(8,128)(2,1)}), bf16[8,32,32,256]{3,2,1,0:T(8,128)(2,1)}, u32[]{:S(2)}, u32[]{:S(2)}) async-start(bf16[8,32,32,256]{3,2,1,0:T(8,128)(2,1)} %bitcast.223), calls=%async_computation.10 | async-start | bytes 8388608 | tf_op jit(solution)/shard_map/all_to_all | solution.py:122
  616.3 29.7 %all-to-all-start.11 = ((bf16[8,16,32,256]{3,2,1,0:T(8,128)(2,1)}), bf16[8,16,32,256]{3,2,1,0:T(8,128)(2,1)S(1)}, u32[]{:S(2)}, u32[]{:S(2)}) async-start(bf16[8,16,32,256]{3,2,1,0:T(8,128)(2,1)} %bitcast.230), calls=%async_computation.11 | async-start | bytes 4194304 | tf_op jit(solution)/shard_map/all_to_all | solution.py:122
  659.7 25.8 %copy-start.53 = (f32[128,1]{1,0:T(8,128)S(1)}, f32[128,1]{1,0:T(8,128)}, u32[]{:S(2)}) copy-start(f32[128,1]{1,0:T(8,128)} %get-tuple-element.57) | copy-start | bytes 1540
  659.8 26.4 %copy-start.30 = (f32[128,1]{1,0:T(8,128)S(1)}, f32[128,1]{1,0:T(8,128)}, u32[]{:S(2)}) copy-start(f32[128,1]{1,0:T(8,128)} %get-tuple-element.62) | copy-start | bytes 1540
  659.8 26.4 %copy-start.52 = (f32[128,1]{1,0:T(8,128)S(1)}, f32[128,1]{1,0:T(8,128)}, u32[]{:S(2)}) copy-start(f32[128,1]{1,0:T(8,128)} %get-tuple-element.59) | copy-start | bytes 1540
  659.8 27.1 %copy-start.51 = (f32[128,128]{1,0:T(8,128)S(1)}, f32[128,128]{1,0:T(8,128)}, u32[]{:S(2)}) copy-start(f32[128,128]{1,0:T(8,128)} %get-tuple-element.58) | copy-start | bytes 196612
  659.8 27.7 %copy-start.28 = (f32[512,128]{1,0:T(8,128)S(1)}, f32[512,128]{1,0:T(8,128)}, u32[]{:S(2)}) copy-start(f32[512,128]{1,0:T(8,128)} %get-tuple-element.61) | copy-start | bytes 786436
  659.8 95.7 %all-to-all-start.12 = ((bf16[8,32,32,256]{3,2,1,0:T(8,128)(2,1)}), bf16[8,32,32,256]{3,2,1,0:T(8,128)(2,1)}, u32[]{:S(2)}, u32[]{:S(2)}) async-start(bf16[8,32,32,256]{3,2,1,0:T(8,128)(2,1)} %bitcast.222), calls=%async_computation.12 | async-start | bytes 8388608 | tf_op jit(solution)/shard_map/all_to_all | solution.py:122
  664.5 23.7 %copy-start.34 = (f32[128,384]{1,0:T(8,128)S(1)}, f32[128,384]{1,0:T(8,128)}, u32[]{:S(2)}) copy-start(f32[128,384]{1,0:T(8,128)} %get-tuple-element.56) | copy-start | bytes 589828
  664.5 23.7 %copy-start.54 = (f32[128,1]{1,0:T(8,128)S(1)}, f32[128,1]{1,0:T(8,128)}, u32[]{:S(2)}) copy-start(f32[128,1]{1,0:T(8,128)} %get-tuple-element.55) | copy-start | bytes 1540
  664.5 23.7 %copy-start.55 = (f32[128,1]{1,0:T(8,128)S(1)}, f32[128,1]{1,0:T(8,128)}, u32[]{:S(2)}) copy-start(f32[128,1]{1,0:T(8,128)} %get-tuple-element.53) | copy-start | bytes 1540
  668.3 314.3 %collective-permute-start.3 = (bf16[32,256,128]{2,1,0:T(8,128)(2,1)}, bf16[32,256,128]{2,1,0:T(8,128)(2,1)}, u32[]{:S(2)}, u32[]{:S(2)}) collective-permute-start(bf16[32,256,128]{2,1,0:T(8,128)(2,1)} %get-tuple-element.41), channel_id=1, source_target_pairs={{0,0},{1,1},{16,2},{17,3},{8,4},{9,5},{24,6},{25,7},{4,8},{5,9},{2... | collective-permute-start | bytes 6291464 | tf_op jit(solution)/shard_map/ppermute | solution.py:643
  770.6 28.0 %copy-start.56 = (f32[128,1]{1,0:T(8,128)S(1)}, f32[128,1]{1,0:T(8,128)}, u32[]{:S(2)}) copy-start(f32[128,1]{1,0:T(8,128)} %get-tuple-element.51) | copy-start | bytes 1540
  772.3 26.7 %copy-start.21 = (f32[32,256]{1,0:T(8,128)S(1)}, f32[32,256]{1,0:T(8,128)}, u32[]{:S(2)}) copy-start(f32[32,256]{1,0:T(8,128)} %copy-done.20) | copy-start | bytes 98308
  772.3 26.7 %copy-start.62 = (f32[256]{0:T(256)S(1)}, f32[256]{0:T(256)}, u32[]{:S(2)}) copy-start(f32[256]{0:T(256)} %copy-done.61) | copy-start | bytes 3076
  772.3 26.7 %copy-start.72 = (f32[32]{0:T(128)S(1)}, f32[32]{0:T(128)}, u32[]{:S(2)}) copy-start(f32[32]{0:T(128)} %copy-done.71) | copy-start | bytes 388
  772.3 26.7 %copy-start.75 = (f32[32]{0:T(128)S(1)}, f32[32]{0:T(128)}, u32[]{:S(2)}) copy-start(f32[32]{0:T(128)} %copy-done.74) | copy-start | bytes 388
  772.3 27.0 %copy-start.10 = (bf16[256,32]{1,0:T(8,128)(2,1)S(1)}, bf16[256,32]{1,0:T(8,128)(2,1)}, u32[]{:S(2)}) copy-start(bf16[256,32]{1,0:T(8,128)(2,1)} %copy-done.9) | copy-start | bytes 49156
  772.4 27.0 %copy-start.12 = (bf16[256,32]{1,0:T(8,128)(2,1)S(1)}, bf16[256,32]{1,0:T(8,128)(2,1)}, u32[]{:S(2)}) copy-start(bf16[256,32]{1,0:T(8,128)(2,1)} %copy-done.11) | copy-start | bytes 49156
  772.4 27.3 %copy-start.64 = (bf16[1,32,256]{2,1,0:T(8,128)(2,1)S(1)}, bf16[1,32,256]{2,1,0:T(8,128)(2,1)}, u32[]{:S(2)}) copy-start(bf16[1,32,256]{2,1,0:T(8,128)(2,1)} %param.17) | copy-start | bytes 49156
  772.4 28.0 %copy-start.19 = (f32[32,1024]{1,0:T(8,128)S(1)}, f32[32,1024]{1,0:T(8,128)}, u32[]{:S(2)}) copy-start(f32[32,1024]{1,0:T(8,128)} %copy-done.18) | copy-start | bytes 393220
  774.7 24.0 %all-to-all-start.13 = ((bf16[32,2,1024]{2,1,0:T(2,128)(2,1)}), bf16[32,2,1024]{2,1,0:T(2,128)(2,1)S(1)}, u32[]{:S(2)}, u32[]{:S(2)}) async-start(bf16[32,2,1024]{2,1,0:T(2,128)(2,1)} %reshape.578), calls=%async_computation.13 | async-start | bytes 262144 | tf_op jit(solution)/shard_map/all_to_all | solution.py:122
  781.2 222.1 %collective-permute-start.4 = (bf16[32,256,128]{2,1,0:T(8,128)(2,1)}, bf16[32,256,128]{2,1,0:T(8,128)(2,1)}, u32[]{:S(2)}, u32[]{:S(2)}) collective-permute-start(bf16[32,256,128]{2,1,0:T(8,128)(2,1)} %get-tuple-element.50), channel_id=1, source_target_pairs={{0,0},{1,1},{16,2},{17,3},{8,4},{9,5},{24,6},{25,7},{4,8},{5,9},{2... | collective-permute-start | bytes 6291464 | tf_op jit(solution)/shard_map/ppermute | solution.py:665
  809.6 50.9 %all-to-all-start.14 = ((bf16[8,32,512]{2,1,0:T(8,128)(2,1)}), bf16[8,32,512]{2,1,0:T(8,128)(2,1)S(1)}, u32[]{:S(2)}, u32[]{:S(2)}) async-start(bf16[8,32,512]{2,1,0:T(8,128)(2,1)} %pad_maximum_fusion), calls=%async_computation.14 | async-start | bytes 524288 | tf_op jit(solution)/shard_map/all_to_all | solution.py:122
  813.3 48.5 %copy-start.47 = (bf16[256,256]{1,0:T(8,128)(2,1)S(1)}, bf16[256,256]{1,0:T(8,128)(2,1)}, u32[]{:S(2)}) copy-start(bf16[256,256]{1,0:T(8,128)(2,1)} %get-tuple-element.82) | copy-start | bytes 393220
  813.3 48.5 %copy-start.48 = (bf16[256,256]{1,0:T(8,128)(2,1)S(1)}, bf16[256,256]{1,0:T(8,128)(2,1)}, u32[]{:S(2)}) copy-start(bf16[256,256]{1,0:T(8,128)(2,1)} %get-tuple-element.83) | copy-start | bytes 393220
  813.3 48.5 %copy-start.49 = (bf16[256,256]{1,0:T(8,128)(2,1)S(1)}, bf16[256,256]{1,0:T(8,128)(2,1)}, u32[]{:S(2)}) copy-start(bf16[256,256]{1,0:T(8,128)(2,1)} %get-tuple-element.84) | copy-start | bytes 393220
  813.3 48.5 %copy-start.70 = (f32[256]{0:T(256)S(1)}, f32[256]{0:T(256)}, u32[]{:S(2)}) copy-start(f32[256]{0:T(256)} %copy-done.69) | copy-start | bytes 3076
  813.5 49.4 %copy-start.89 = (f32[32]{0:T(128)S(1)}, f32[32]{0:T(128)}, u32[]{:S(2)}) copy-start(f32[32]{0:T(128)} %fusion.57) | copy-start | bytes 388
  813.5 50.9 %copy-start.90 = (f32[4]{0:T(128)S(1)}, f32[4]{0:T(128)}, u32[]{:S(2)}) copy-start(f32[4]{0:T(128)} %compare_convert_fusion) | copy-start | bytes 52
  815.9 65.0 %copy-start.88 = (bf16[256]{0:T(256)(128)(2,1)S(1)}, bf16[256]{0:T(256)(128)(2,1)}, u32[]{:S(2)}) copy-start(bf16[256]{0:T(256)(128)(2,1)} %get-tuple-element.67) | copy-start | bytes 1540
  862.9 48.6 %copy-start.46 = (bf16[16384]{0:T(1024)(128)(2,1)S(1)}, bf16[16384]{0:T(1024)(128)(2,1)}, u32[]{:S(2)}) copy-start(bf16[16384]{0:T(1024)(128)(2,1)} %get-tuple-element.113) | copy-start | bytes 98308
  862.9 50.2 %copy-start.45 = (bf16[16384]{0:T(1024)(128)(2,1)S(1)}, bf16[16384]{0:T(1024)(128)(2,1)}, u32[]{:S(2)}) copy-start(bf16[16384]{0:T(1024)(128)(2,1)} %get-tuple-element.112) | copy-start | bytes 98308
  862.9 51.8 %copy-start.44 = (bf16[16384]{0:T(1024)(128)(2,1)S(1)}, bf16[16384]{0:T(1024)(128)(2,1)}, u32[]{:S(2)}) copy-start(bf16[16384]{0:T(1024)(128)(2,1)} %get-tuple-element.111) | copy-start | bytes 98308
  862.9 53.3 %copy-start.81 = (bf16[128]{0:T(256)(128)(2,1)S(1)}, bf16[128]{0:T(256)(128)(2,1)}, u32[]{:S(2)}) copy-start(bf16[128]{0:T(256)(128)(2,1)} %get-tuple-element.134) | copy-start | bytes 772
  862.9 54.7 %copy-start.50 = (f32[128,128]{1,0:T(8,128)S(1)}, f32[128,128]{1,0:T(8,128)}, u32[]{:S(2)}) copy-start(f32[128,128]{1,0:T(8,128)} %get-tuple-element.54) | copy-start | bytes 196612
  863.0 55.3 %copy-start.80 = (bf16[128]{0:T(256)(128)(2,1)S(1)}, bf16[128]{0:T(256)(128)(2,1)}, u32[]{:S(2)}) copy-start(bf16[128]{0:T(256)(128)(2,1)} %get-tuple-element.133) | copy-start | bytes 772
  863.0 56.7 %copy-start.43 = (bf16[16384]{0:T(1024)(128)(2,1)S(1)}, bf16[16384]{0:T(1024)(128)(2,1)}, u32[]{:S(2)}) copy-start(bf16[16384]{0:T(1024)(128)(2,1)} %get-tuple-element.110) | copy-start | bytes 98308
  864.5 56.8 %copy-start.42 = (bf16[16384]{0:T(1024)(128)(2,1)S(1)}, bf16[16384]{0:T(1024)(128)(2,1)}, u32[]{:S(2)}) copy-start(bf16[16384]{0:T(1024)(128)(2,1)} %get-tuple-element.109) | copy-start | bytes 98308
  864.5 58.3 %copy-start.41 = (bf16[16384]{0:T(1024)(128)(2,1)S(1)}, bf16[16384]{0:T(1024)(128)(2,1)}, u32[]{:S(2)}) copy-start(bf16[16384]{0:T(1024)(128)(2,1)} %get-tuple-element.108) | copy-start | bytes 98308
  864.5 59.8 %copy-start.79 = (bf16[128]{0:T(256)(128)(2,1)S(1)}, bf16[128]{0:T(256)(128)(2,1)}, u32[]{:S(2)}) copy-start(bf16[128]{0:T(256)(128)(2,1)} %convert_reduce_fusion.3) | copy-start | bytes 772
  864.5 61.2 %copy-start.39 = (bf16[16384]{0:T(1024)(128)(2,1)S(1)}, bf16[16384]{0:T(1024)(128)(2,1)}, u32[]{:S(2)}) copy-start(bf16[16384]{0:T(1024)(128)(2,1)} %convert_bitcast_fusion.2) | copy-start | bytes 98308
  864.7 62.6 %copy-start.78 = (bf16[128]{0:T(256)(128)(2,1)S(1)}, bf16[128]{0:T(256)(128)(2,1)}, u32[]{:S(2)}) copy-start(bf16[128]{0:T(256)(128)(2,1)} %get-tuple-element.132) | copy-start | bytes 772
  864.7 64.0 %copy-start.15 = (bf16[16,4,8,128]{3,1,2,0:T(4,128)(2,1)S(1)}, bf16[16,4,8,128]{3,1,2,0:T(4,128)(2,1)}, u32[]{:S(2)}) copy-start(bf16[16,4,8,128]{3,1,2,0:T(4,128)(2,1)} %copy.461) | copy-start | bytes 393220
  864.8 67.1 %copy-start.14 = (bf16[65536]{0:T(1024)(128)(2,1)S(1)}, bf16[65536]{0:T(1024)(128)(2,1)}, u32[]{:S(2)}) copy-start(bf16[65536]{0:T(1024)(128)(2,1)} %convert_bitcast_fusion) | copy-start | bytes 393220
  869.9 65.0 %copy-start.77 = (bf16[128]{0:T(256)(128)(2,1)S(1)}, bf16[128]{0:T(256)(128)(2,1)}, u32[]{:S(2)}) copy-start(bf16[128]{0:T(256)(128)(2,1)} %get-tuple-element.131) | copy-start | bytes 772
  948.9 19.5 %all-to-all-start.16 = ((bf16[2,8,296,128]{3,1,2,0:T(8,128)(2,1)}), bf16[2,8,296,128]{3,1,2,0:T(8,128)(2,1)S(1)}, u32[]{:S(2)}, u32[]{:S(2)}) async-start(bf16[2,8,296,128]{3,1,2,0:T(8,128)(2,1)} %reduce_sum.266), calls=%async_computation.16 | async-start | bytes 2424832 | tf_op jit(solution)/shard_map/all_to_all | solution.py:122
  969.0 9.6 all-to-all-start.18
  978.6 20.0 %all-to-all-start.17 = ((bf16[8,296,128]{2,1,0:T(8,128)(2,1)}), bf16[8,296,128]{2,1,0:T(8,128)(2,1)S(1)}, u32[]{:S(2)}, u32[]{:S(2)}) async-start(bf16[8,296,128]{2,1,0:T(8,128)(2,1)} %copy.442), calls=%async_computation.17 | async-start | bytes 1212416 | tf_op jit(solution)/shard_map/all_to_all | solution.py:122
  1000.6 9.8 all-to-all-start.19
  (48 other events, 367.6 us)
where the time goes:
time: 1040 us; the launch traced here: 1020 us
  waiting for transfers between devices  340 us (33%)
  local copies, waits for them, and re-layouts  193 us (19%)
  Pallas kernels  168 us (16%)
  starting transfers between devices  132 us (13%)
  blocking collectives  119 us (11%)
  matrix products  28.6 us (3%)
  other arithmetic  28 us (3%)
    all_to_all x15, waiting for transfers between devices, exchange(): lax.all_to_all(blocks, axes, 0, 0, axis_index_groups=groups, tiled=True)  340 us
    pallas_call x5, Pallas kernels, run(): pl.pallas_call(body, grid=(rows // step_rows,), in_specs=[spec(kind, a.sh...  120 us
    all_to_all x5, blocking collectives, exchange(): lax.all_to_all(blocks, axes, 0, 0, axis_index_groups=groups, tiled=True)  119 us
    unnamed x228, local copies, waits for them, and re-layouts  82.9 us
    slice x11, local copies, waits for them, and re-layouts, unpack(): params[entry_name] = flat[offset:offset + extent].reshape(entry_shape)  76.9 us
    all_to_all x15, starting transfers between devices, exchange(): lax.all_to_all(blocks, axes, 0, 0, axis_index_groups=groups, tiled=True)  62.2 us
    pallas_call x2, Pallas kernels, mix_back(): pl.pallas_call(lambda *refs: kernel_mix_back(incoming, *refs), grid=(shar...  24.9 us
    pallas_call x2, Pallas kernels, mix(): pl.pallas_call(lambda *refs: kernel_mix(incoming, *refs), grid=(share,),...  22.9 us
  transfers between devices with their start and end apart: 20, of which 12 were waited for; matrix products, arithmetic and copies ran while one was open for 23% of the time, Pallas kernels for 3%

commit v1 on v0

--- a/solution.py
+++ b/solution.py
@@ -1,4 +1,5 @@
 import math
+from typing import Any, NamedTuple
 
 import jax
 import jax.numpy as jnp
@@ -31,50 +32,71 @@
 HIGHEST = lax.Precision.HIGHEST
 
 
-def segment_list():
-    heads_width = HEADS * HEAD_DIM
-    entries = [
-        ("embed", (RECYCLES, NODE_DIM)),
-        ("gain_one", (NODE_DIM,)),
-        ("w_query", (NODE_DIM, heads_width)),
-        ("w_key", (NODE_DIM, heads_width)),
-        ("w_value", (NODE_DIM, heads_width)),
-        ("w_bias", (PAIR_DIM, HEADS)),
-        ("w_attn_out", (heads_width, NODE_DIM)),
-        ("gain_two", (NODE_DIM,)),
-        ("w_node_up", (NODE_DIM, FFN_NODE)),
-        ("w_node_down", (FFN_NODE, NODE_DIM)),
-        ("gain_three", (NODE_DIM,)),
-        ("w_left_node", (NODE_DIM, OUTER)),
-        ("w_right_node", (NODE_DIM, OUTER)),
-        ("w_outer", (OUTER * OUTER, PAIR_DIM)),
-    ]
-    for prefix in ("out_", "in_"):
-        entries += [
-            (prefix + "gain_in", (PAIR_DIM,)),
-            (prefix + "w_left", (PAIR_DIM, TRI_DIM)),
-            (prefix + "w_right", (PAIR_DIM, TRI_DIM)),
-            (prefix + "w_gate", (PAIR_DIM, PAIR_DIM)),
-            (prefix + "gain_tri", (TRI_DIM,)),
-            (prefix + "w_tri_out", (TRI_DIM, PAIR_DIM)),
-        ]
-    entries += [
-        ("gain_pair", (PAIR_DIM,)),
-        ("w_pair_up", (PAIR_DIM, FFN_PAIR)),
-        ("w_pair_down", (FFN_PAIR, PAIR_DIM)),
-        ("bias_pair", (PAIR_DIM,)),
-    ]
-    return entries
-
-
-def unpack(flat):
-    params = {}
-    offset = 0
-    for entry_name, entry_shape in segment_list():
-        extent = math.prod(entry_shape)
-        params[entry_name] = flat[offset : offset + extent].reshape(entry_shape)
-        offset += extent
-    return params
+class Triangle(NamedTuple):
+    gain_in: Any
+    w_left: Any
+    w_right: Any
+    w_gate: Any
+    gain_tri: Any
+    w_tri_out: Any
+
+
+class Params(NamedTuple):
+    embed: Any
+    gain_one: Any
+    w_query: Any
+    w_key: Any
+    w_value: Any
+    w_bias: Any
+    w_attn_out: Any
+    gain_two: Any
+    w_node_up: Any
+    w_node_down: Any
+    gain_three: Any
+    w_left_node: Any
+    w_right_node: Any
+    w_outer: Any
+    outgoing: Triangle
+    incoming: Triangle
+    gain_pair: Any
+    w_pair_up: Any
+    w_pair_down: Any
+    bias_pair: Any
+
+
+LANES = 128
+HEADS_WIDTH = HEADS * HEAD_DIM
+
+
+def first_rows():
+    square = PAIR_DIM * TRI_DIM
+    triangle = Triangle(PAIR_DIM, square, square, PAIR_DIM * PAIR_DIM, TRI_DIM, square)
+    sizes = Params(
+        embed=RECYCLES * NODE_DIM,
+        gain_one=NODE_DIM,
+        w_query=NODE_DIM * HEADS_WIDTH,
+        w_key=NODE_DIM * HEADS_WIDTH,
+        w_value=NODE_DIM * HEADS_WIDTH,
+        w_bias=PAIR_DIM * HEADS,
+        w_attn_out=HEADS_WIDTH * NODE_DIM,
+        gain_two=NODE_DIM,
+        w_node_up=NODE_DIM * FFN_NODE,
+        w_node_down=FFN_NODE * NODE_DIM,
+        gain_three=NODE_DIM,
+        w_left_node=NODE_DIM * OUTER,
+        w_right_node=NODE_DIM * OUTER,
+        w_outer=OUTER * OUTER * PAIR_DIM,
+        outgoing=triangle,
+        incoming=triangle,
+        gain_pair=PAIR_DIM,
+        w_pair_up=PAIR_DIM * FFN_PAIR,
+        w_pair_down=FFN_PAIR * PAIR_DIM,
+        bias_pair=PAIR_DIM,
+    )
+    leaves, tree = jax.tree.flatten(sizes)
+    ends = np.cumsum(leaves) // LANES
+    starts = [0] + [int(end) for end in ends[:-1]]
+    return jax.tree.unflatten(tree, starts), int(ends[-1])
 
 
 LOW = jnp.bfloat16
@@ -88,28 +110,19 @@
 
 class Layout:
     def __init__(self, crops, rows):
-        self.crops, self.rows, self.wide = crops, rows, rows // crops
-        self.planes = (0, 2, 1, 3) if crops == 4 else tuple(range(crops))
-        self.slots = (0, 2, 1, 3) if crops == 4 else tuple(range(crops))
-        self.crop_of = tuple(self.planes.index(k) for k in range(crops))
-        self.high_of = tuple(self.slots.index(k) for k in range(crops))
-        ident = lambda c, z, y: (c * crops + z) * self.wide + y
-        spots = [
-            (c, z, y) for c in range(crops) for z in range(crops) for y in range(self.wide)
+        self.crops, self.rows = crops, rows
+        self.devices = crops * rows
+        self.wide = 2 ** (int(math.log2(rows)) // 2)
+        self.high = rows // self.wide
+        half = crops // 2
+        self.moves = [
+            (here, self.work_place(here))
+            for here in range(self.devices)
+            if here != self.work_place(here)
         ]
-        self.outward = [
-            (ident(c, z, y), ident(self.slots[z], self.planes[c], y)) for c, z, y in spots
+        self.groups = [
+            [self.work_place(c * rows + r) for r in range(rows)] for c in range(crops)
         ]
-        self.homeward = [(there, here) for here, there in self.outward]
-        self.groups = [
-            [
-                ident(self.slots[z], plane, y)
-                for z in range(crops)
-                for y in range(self.wide)
-            ]
-            for plane in range(crops)
-        ]
-        half = crops // 2
         self.cores = [
             [(2 * x + k) * rows + r for k in range(2)] for x in range(half) for r in range(rows)
         ]
@@ -117,6 +130,15 @@
             [(2 * x + k) * rows + r for x in range(half)] for k in range(2) for r in range(rows)
         ]
 
+    def work_place(self, here):
+        crop, row = here // self.rows, here % self.rows
+        high, wide = row // self.wide, row % self.wide
+        core = crop % 2
+        away = (high // (self.high // 2) + core) % 2
+        crop = crop + away * (1 - 2 * core)
+        high = high + away * (self.high - 1 - 2 * high)
+        return crop * self.rows + high * self.wide + wide
+
 
 def exchange(blocks, axes, groups=None):
     return lax.all_to_all(blocks, axes, 0, 0, axis_index_groups=groups, tiled=True)
@@ -153,6 +175,14 @@
 
 def sigmoid(x):
     return 0.5 * jnp.tanh(0.5 * x) + 0.5
+
+
+def column(row):
+    return jnp.broadcast_to(row, (LANES, row.shape[1])).T[:, :1]
+
+
+def row_of(values):
+    return jnp.broadcast_to(values, (values.shape[0], LANES)).T[:1]
 
 
 def cat(ref, start, count):
@@ -280,11 +310,20 @@
 GROUP = 2
 
 
+def sides_low(w):
+    return jnp.concatenate([w[:PAIR_DIM].T, w[PAIR_DIM : 2 * PAIR_DIM].T], axis=0)
+
+
+def all_back(w):
+    return jnp.concatenate([w[k * PAIR_DIM : (k + 1) * PAIR_DIM] for k in range(3)], axis=1)
+
+
 def kernel_open(pair, table, right, mask, gain, w_sides, x_out, sides_out, scratch):
     rows = pair.shape[0]
     group = min(GROUP, rows)
-    w_low = w_sides[...].T
+    w_low = sides_low(w_sides)
     right_low = right[...]
+    gain_low = column(gain[...])
 
     def step(t):
         at = t * group
@@ -296,7 +335,7 @@
             axis=1,
         )
         put(x_out, at, group, x)
-        put(scratch, at, group, front(x, gain[...], w_low, cell_mask(mask, at, group)))
+        put(scratch, at, group, front(x, gain_low, w_low, cell_mask(mask, at, group)))
 
     loop(rows // group, step)
     send_pair(scratch, sides_out)
@@ -309,16 +348,17 @@
     rows = x_in.shape[0]
     group = min(GROUP, rows)
     arrived[...] = swapped(mixed[...])
-    w_low, gate_low, out_low = w_sides[...].T, w_gate[...].T, w_out[...].T
+    w_low, gate_low, out_low = sides_low(w_sides), w_gate[...].T, w_out[...].T
+    in_col, tri_col, next_col = column(gain_in[...]), column(gain_tri[...]), column(gain_next[...])
 
     def step(t):
         at = t * group
         x = post(
             cat(x_in, at, group), cat(arrived, at, group).astype(WIDE),
-            gain_in[...], gate_low, gain_tri[...], out_low,
+            in_col, gate_low, tri_col, out_low,
         )
         put(x_out, at, group, x)
-        put(scratch, at, group, front(x, gain_next[...], w_low, cell_mask(mask, at, group)))
+        put(scratch, at, group, front(x, next_col, w_low, cell_mask(mask, at, group)))
 
     loop(rows // group, step)
     send_pair(scratch, sides_out)
@@ -335,6 +375,8 @@
     gate_low, out_low, out_back = w_gate[...].T, w_out[...].T, w_out[...]
     up_low, up_back = w_up[...].T, w_up[...]
     down_low, down_back = w_down[...].T, w_down[...]
+    in_col, tri_col = column(gain_in[...]), column(gain_tri[...])
+    pair_col, bias_col = column(gain_pair[...]), column(bias[...])
     zero_first(g_out, g_tri, g_up, g_down, g_pair, g_bias)
     chunk = PAIR_DIM
 
@@ -342,11 +384,11 @@
         at = t * group
         x_two = cat(x_in, at, group)
         mix = cat(arrived, at, group).astype(WIDE)
-        x = post(x_two, mix, gain_in[...], gate_low, gain_tri[...], out_low)
+        x = post(x_two, mix, in_col, gate_low, tri_col, out_low)
         hat, scale = norm_parts(x)
-        normed = (hat * gain_pair[...]).astype(LOW)
+        normed = (hat * pair_col).astype(LOW)
         cot_low = jnp.concatenate([cot[at + k].T for k in range(group)], axis=1)
-        total = x + bias[...]
+        total = x + bias_col
         normed_grad = jnp.zeros_like(x)
         for c in range(FFN_PAIR // chunk):
             part = slice(c * chunk, (c + 1) * chunk)
@@ -363,12 +405,12 @@
             pair_out[at + k] = total_low[:, k * width : (k + 1) * width].T
         cot_wide = cot_low.astype(WIDE)
         g_bias[...] += jnp.sum(cot_wide, axis=1, keepdims=True)
-        back, grad_gain = norm_back(normed_grad, hat, scale, gain_pair[...])
+        back, grad_gain = norm_back(normed_grad, hat, scale, pair_col)
         g_pair[...] += grad_gain
         grad = cot_wide + back
         put(x_grad, at, group, grad)
         mix_grad, gates, grad_out, grad_tri = post_back(
-            grad, x_two, mix, gain_in[...], gate_low, gain_tri[...], out_low, out_back
+            grad, x_two, mix, in_col, gate_low, tri_col, out_low, out_back
         )
         put(leaving, at, group, mix_grad)
         put(gate_grad, at, group, gates)
@@ -390,20 +432,22 @@
     take_pair(sides_grad, sides)
     arrived[...] = swapped(mixed[...])
     gate_low, out_low, out_back = w_gate[...].T, w_out[...].T, w_out[...]
+    in_col, tri_col, after_col = column(gain_in[...]), column(gain_tri[...]), column(gain_after[...])
+    after_back = all_back(w_after)
     zero_first(g_after, g_gain, g_out, g_tri)
 
     def step(t):
         at = t * group
         grad, grad_w, grad_gain = front_back(
             cat(grad_in, at, group), cat(x_after, at, group), cat(sides, at, group),
-            cat(gate_after, at, group), cell_mask(mask, at, group), gain_after[...], w_after[...],
+            cat(gate_after, at, group), cell_mask(mask, at, group), after_col, after_back,
         )
         g_after[...] += grad_w
         g_gain[...] += grad_gain
         put(x_grad, at, group, grad)
         mix_grad, gates, grad_out, grad_tri = post_back(
             grad, cat(x_before, at, group), cat(arrived, at, group).astype(WIDE),
-            gain_in[...], gate_low, gain_tri[...], out_low, out_back,
+            in_col, gate_low, tri_col, out_low, out_back,
         )
         put(leaving, at, group, mix_grad)
         put(gate_grad, at, group, gates)
@@ -421,13 +465,14 @@
     rows = x_after.shape[0]
     group = min(GROUP, rows)
     take_pair(sides_grad, sides)
+    after_col, after_back = column(gain_after[...]), all_back(w_after)
     zero_first(g_after, g_gain, right_grad)
 
     def step(t):
         at = t * group
         grad, grad_w, grad_gain = front_back(
             cat(grad_in, at, group), cat(x_after, at, group), cat(sides, at, group),
-            cat(gate_after, at, group), cell_mask(mask, at, group), gain_after[...], w_after[...],
+            cat(gate_after, at, group), cell_mask(mask, at, group), after_col, after_back,
         )
         g_after[...] += grad_w
         g_gain[...] += grad_gain
@@ -442,36 +487,42 @@
     loop(rows // group, step)
 
 
+CHANNELS = 4
+
+
 def kernel_mix(incoming, left, right, out):
-    length = left.shape[-1]
-    a = left[...].reshape(length, length)
-    b = right[...].reshape(length, length)
-    mixed = dot_tn(a, b) if incoming else dot_nt(a, b)
-    out[...] = mixed.astype(LOW).reshape(out.shape)
+    parts, count, rows, length = out.shape
+    for c in range(count):
+        a = left[:, c].reshape(length, length)
+        b = right[:, c].reshape(length, length)
+        mixed = dot_tn(a, b) if incoming else dot_nt(a, b)
+        out[:, c] = mixed.astype(LOW).reshape(parts, rows, length)
 
 
 def kernel_mix_back(incoming, grad, left, right, out):
-    length = left.shape[-1]
-    g = grad[...].reshape(length, length)
-    a = left[...].reshape(length, length)
-    b = right[...].reshape(length, length)
-    block = (out.shape[0], out.shape[3], out.shape[4])
-    a_grad = dot_nt(b, g) if incoming else dot_nn(g, b)
-    b_grad = dot_nn(a, g) if incoming else dot_tn(g, a)
-    out[:, 0, 0] = a_grad.astype(LOW).reshape(block)
-    out[:, 1, 0] = b_grad.astype(LOW).reshape(block)
+    parts, count, rows, length = grad.shape
+    for c in range(count):
+        g = grad[:, c].reshape(length, length)
+        a = left[:, c].reshape(length, length)
+        b = right[:, c].reshape(length, length)
+        a_grad = dot_nt(b, g) if incoming else dot_nn(g, b)
+        b_grad = dot_nn(a, g) if incoming else dot_tn(g, a)
+        out[:, 0, c] = a_grad.astype(LOW).reshape(parts, rows, length)
+        out[:, 1, c] = b_grad.astype(LOW).reshape(parts, rows, length)
 
 
 def mix(sides, incoming):
     parts, double, rows, length = sides.shape
     share = double // 2
-    block = (parts, 1, rows, length)
+    count = min(CHANNELS, share)
+    steps = share // count
+    block = (parts, count, rows, length)
     return pl.pallas_call(
         lambda *refs: kernel_mix(incoming, *refs),
-        grid=(share,),
+        grid=(steps,),
         in_specs=[
             pl.BlockSpec(block, lambda c: (0, c, 0, 0)),
-            pl.BlockSpec(block, lambda c: (0, c + share, 0, 0)),
+            pl.BlockSpec(block, lambda c: (0, c + steps, 0, 0)),
         ],
         out_specs=pl.BlockSpec(block, lambda c: (0, c, 0, 0)),
         out_shape=jax.ShapeDtypeStruct((parts, share, rows, length), LOW),
@@ -486,16 +537,18 @@
 def mix_back(grad, sides, incoming):
     parts, double, rows, length = sides.shape
     share = double // 2
-    block = (parts, 1, rows, length)
+    count = min(CHANNELS, share)
+    steps = share // count
+    block = (parts, count, rows, length)
     out = pl.pallas_call(
         lambda *refs: kernel_mix_back(incoming, *refs),
-        grid=(share,),
+        grid=(steps,),
         in_specs=[
             pl.BlockSpec(block, lambda c: (0, c, 0, 0)),
             pl.BlockSpec(block, lambda c: (0, c, 0, 0)),
-            pl.BlockSpec(block, lambda c: (0, c + share, 0, 0)),
+            pl.BlockSpec(block, lambda c: (0, c + steps, 0, 0)),
         ],
-        out_specs=pl.BlockSpec((parts, 2, 1, rows, length), lambda c: (0, 0, c, 0, 0)),
+        out_specs=pl.BlockSpec((parts, 2, count, rows, length), lambda c: (0, 0, c, 0, 0)),
         out_shape=jax.ShapeDtypeStruct((parts, 2, share, rows, length), LOW),
         compiler_params=pltpu.CompilerParams(vmem_limit_bytes=VMEM_LIMIT),
         cost_estimate=pl.CostEstimate(
@@ -506,6 +559,105 @@
     return out.reshape(sides.shape)
 
 
+def share_rows(share):
+    return -(-(share + 2 * LANES) // (TILE * LANES)) * TILE
+
+
+def whole(shape):
+    return pl.BlockSpec(shape, lambda *_: (0,) * len(shape))
+
+
+def one_call(body, in_arrays, outs, scratch):
+    return pl.pallas_call(
+        body,
+        in_specs=[whole(a.shape) for a in in_arrays],
+        out_specs=[whole(shape) for shape, _ in outs],
+        out_shape=[jax.ShapeDtypeStruct(shape, dtype) for shape, dtype in outs],
+        scratch_shapes=scratch,
+        grid=(1,),
+        compiler_params=pltpu.CompilerParams(vmem_limit_bytes=VMEM_LIMIT),
+    )(*in_arrays)
+
+
+def share_order(layout):
+    return [((d // layout.rows) % 2, d // (2 * layout.rows), d % layout.rows) for d in range(layout.devices)]
+
+
+def unpack(layout, shares, share):
+    at, total = first_rows()
+    height = shares.shape[3]
+    first = [share * d // LANES for d in range(layout.devices)]
+    order = share_order(layout)
+    matrices = [
+        (NODE_DIM, 3, 3 * HEADS_WIDTH), (HEADS_WIDTH, 1, NODE_DIM), (NODE_DIM, 1, FFN_NODE),
+        (FFN_NODE, 1, NODE_DIM), (PAIR_DIM, 1, FFN_PAIR),
+    ]
+    places = [at.w_query, at.w_attn_out, at.w_node_up, at.w_node_down, at.w_pair_up]
+
+    def body(shares_ref, flat_out, *rest):
+        outs, flat = rest[:-1], rest[-1]
+        for d, place in enumerate(order):
+            block = shares_ref[place].astype(WIDE)
+            if d:
+                tail = flat[first[d] : first[d] + 1]
+                flat[first[d] : first[d] + height] = block
+                flat[first[d] : first[d] + 1] = block[:1] + tail
+            else:
+                flat[:height] = block
+        flat_out[...] = flat[: flat_out.shape[0]].astype(LOW)
+        for out, place, (rows, count, width) in zip(outs, places, matrices):
+            pieces = width // count // LANES
+            for m in range(count):
+                for a in range(pieces):
+                    start = place + m * rows * pieces + a
+                    value = flat[pl.ds(start, rows, stride=pieces), :] if pieces > 1 else flat[start : start + rows]
+                    lane = (m * pieces + a) * LANES
+                    out[:, lane : lane + LANES] = value.astype(LOW)
+
+    flat_rows = -(-total // TILE) * TILE
+    return one_call(
+        body,
+        (shares,),
+        [((flat_rows, LANES), LOW)] + [((rows, width), LOW) for rows, _, width in matrices],
+        [pltpu.VMEM((first[-1] + height + TILE, LANES), WIDE)],
+    )
+
+
+def pack(layout, grads, share):
+    _, total = first_rows()
+    height = share_rows(share)
+    first = [share * d // LANES for d in range(layout.devices)]
+    order = share_order(layout)
+
+    def body(*refs):
+        ins, out, flat = refs[:-2], refs[-2], refs[-1]
+        flat[total:] = jnp.zeros((flat.shape[0] - total, LANES), WIDE)
+        for ref, (place, count, _) in zip(ins, grads):
+            if ref.shape[1] == 1:
+                flat[place : place + 1] = row_of(ref[...])
+                continue
+            rows, pieces = ref.shape[0], ref.shape[1] // count // LANES
+            for m in range(count):
+                for a in range(pieces):
+                    lane = (m * pieces + a) * LANES
+                    value = ref[:, lane : lane + LANES]
+                    start = place + m * rows * pieces + a
+                    if pieces > 1 and rows > 1:
+                        flat[pl.ds(start, rows, stride=pieces), :] = value
+                    else:
+                        flat[start : start + rows] = value
+        for d, where in enumerate(order):
+            out[where] = flat[first[d] : first[d] + height].astype(LOW)
+
+    shape = (2, layout.crops // 2, layout.rows, height, LANES)
+    return one_call(
+        body,
+        tuple(array for _, _, array in grads),
+        [(shape, LOW)],
+        [pltpu.VMEM((first[-1] + height + TILE, LANES), WIDE)],
+    )[0]
+
+
 def row_norm(x):
     centered = x - jnp.mean(x, axis=-1, keepdims=True)
     scale = lax.rsqrt(jnp.mean(centered * centered, axis=-1, keepdims=True) + EPS_NORM)
@@ -533,73 +685,84 @@
     node, pair, node_cot, pair_cot = node[0], pair[0], node_cot[0], pair_cot[0]
 
     crop_at, row_at = lax.axis_index("crop"), lax.axis_index("row")
-    high_at, wide_at = row_at // layout.wide, row_at % layout.wide
-    pick = lambda table, index: jnp.asarray(np.array(table, np.int32))[index]
-    plane_crop = pick(layout.crop_of, high_at)
-    plane_slot = pick(layout.high_of, crop_at) * layout.wide + wide_at
-
-    padded = -(-master.shape[0] // 1024) * 1024
-    shard = jnp.pad(low_of(master), (0, padded - master.shape[0])).reshape(-1, 128)
-    shards = spread(shard, ranks, "row")
+    here = crop_at * ranks + row_at
+    partner = layout.work_place(here)
+    stays = partner == here
+    work_crop, work_row = partner // ranks, partner % ranks
+    moved = lambda array: jnp.where(stays, array, lax.ppermute(array, BOTH, layout.moves))
+
+    amount = master.shape[0]
+    height = share_rows(amount)
+    offset = (here * (amount % LANES)) % LANES
+    shard = lax.dynamic_update_slice(jnp.zeros(height * LANES, LOW), low_of(master), (offset,))
+    shards = spread(shard.reshape(height, LANES), ranks, "row")
     shards = spread(shards, crops // 2, BOTH, layout.chips)
     shards = spread(shards, 2, BOTH, layout.cores)
-    shards = jnp.swapaxes(shards, 0, 1).reshape(devices, padded)
-    params = unpack(shards[:, : master.shape[0]].reshape(-1))
-    wide = {entry_name: entry.astype(WIDE) for entry_name, entry in params.items()}
+    shards = shards.reshape(2, crops // 2, ranks, height, LANES)
+    flat, w_projections, w_attn_out, w_node_up, w_node_down, w_pair_up = unpack(
+        layout, shards, amount
+    )
+    at, _ = first_rows()
+    rows_from = lambda start, count: lax.slice_in_dim(flat, start, start + count, axis=0)
+    wide_row = lambda start, count=1: rows_from(start, count).astype(WIDE).reshape(1, -1)
+    narrow = lambda start, count, width: lax.optimization_barrier(rows_from(start, count)).reshape(-1, width)
+    w_bias = narrow(at.w_bias, HEADS, HEADS)
+    w_factors = narrow(at.w_left_node, 2 * NODE_DIM * OUTER // LANES, OUTER)
+    w_factors = jnp.concatenate([w_factors[:NODE_DIM], w_factors[NODE_DIM:]], axis=1)
+    embed = rows_from(at.embed, 2 * RECYCLES).astype(WIDE).reshape(RECYCLES, NODE_DIM)
+    gain_one, gain_two, gain_three = (
+        wide_row(start, NODE_DIM // LANES) for start in (at.gain_one, at.gain_two, at.gain_three)
+    )
     node_all = spread(node, ranks, "row").reshape(length, NODE_DIM)
-    pair_plane = lax.ppermute(pair, BOTH, layout.outward)
-    cot_plane = lax.ppermute(pair_cot, BOTH, layout.outward)
+    pair_plane, cot_plane = moved(pair), moved(pair_cot)
     keep = mask.astype(WIDE)
-    keep_plane = lax.ppermute(keep, BOTH, layout.outward)
-    keep_rows = lax.dynamic_slice_in_dim(keep_plane[0], plane_slot * local_rows, local_rows, 0)
+    keep_plane = moved(keep)
+    keep_rows = lax.dynamic_slice_in_dim(keep_plane[0], work_row * local_rows, local_rows, 0)
     mask_plane = (keep_rows[:, None] * keep_plane)[:, None, :]
 
     one_hot = (recycle[:, None] == jnp.arange(RECYCLES, dtype=jnp.int32)[None, :]).astype(WIDE)
-    start_all = node_all.astype(WIDE) + jnp.matmul(one_hot, wide["embed"], precision=HIGHEST)
+    start_all = node_all.astype(WIDE) + jnp.matmul(one_hot, embed, precision=HIGHEST)
     hat_all, scale_all = row_norm(start_all)
-    normed_all = low_of(hat_all * wide["gain_one"])
+    normed_all = low_of(hat_all * gain_one)
     own = lambda a: lax.dynamic_slice_in_dim(a, row_at * local_rows, local_rows, 0)
     start_node, hat_one, scale_one, normed_one = (
         own(a) for a in (start_all, hat_all, scale_all, normed_all)
     )
-    query = low_of(dot_nn(normed_one, params["w_query"])).reshape(local_rows, HEADS, HEAD_DIM)
-    key = low_of(dot_nn(normed_all, params["w_key"])).reshape(length, HEADS, HEAD_DIM)
-    value = low_of(dot_nn(normed_all, params["w_value"])).reshape(length, HEADS, HEAD_DIM)
-    pair_bias = jnp.einsum("ijd,dh->hij", pair, params["w_bias"], preferred_element_type=WIDE)
+    query = low_of(dot_nn(normed_one, w_projections[:, :heads_width]))
+    query = query.reshape(local_rows, HEADS, HEAD_DIM)
+    key_value = low_of(dot_nn(normed_all, w_projections[:, heads_width:]))
+    key = key_value[:, :heads_width].reshape(length, HEADS, HEAD_DIM)
+    value = key_value[:, heads_width:].reshape(length, HEADS, HEAD_DIM)
+    pair_bias = jnp.einsum("ijd,dh->hij", pair, w_bias, preferred_element_type=WIDE)
     scores = jnp.einsum("ihd,jhd->hij", query, key, preferred_element_type=WIDE) * scale_factor
     scores = scores + pair_bias + ((keep - 1.0) * MASK_FILL)[:, None, :]
     soft = jax.nn.softmax(scores, axis=-1)
     soft_low = low_of(soft)
     attended = jnp.einsum("hij,jhd->ihd", soft_low, value, preferred_element_type=WIDE)
     attended = low_of(attended.reshape(local_rows, heads_width))
-    after_attn = start_node + dot_nn(attended, params["w_attn_out"])
+    after_attn = start_node + dot_nn(attended, w_attn_out)
     hat_two, scale_two = row_norm(after_attn)
-    normed_two = low_of(hat_two * wide["gain_two"])
-    act, slope = gelu_parts(dot_nn(normed_two, params["w_node_up"]))
+    normed_two = low_of(hat_two * gain_two)
+    act, slope = gelu_parts(dot_nn(normed_two, w_node_up))
     act_low = low_of(act)
-    node_final = after_attn + dot_nn(act_low, params["w_node_down"])
+    node_final = after_attn + dot_nn(act_low, w_node_down)
     hat_three, scale_three = row_norm(node_final)
-    normed_three = low_of(hat_three * wide["gain_three"])
-    w_factors = jnp.concatenate([params["w_left_node"], params["w_right_node"]], axis=1)
+    normed_three = low_of(hat_three * gain_three)
     factors = low_of(dot_nn(normed_three, w_factors))
 
     factors_all = spread(factors, devices, BOTH)
-    factors_all = lax.dynamic_slice_in_dim(factors_all, plane_crop * ranks, ranks, 0)
-    left = lax.dynamic_index_in_dim(factors_all, plane_slot, 0, keepdims=False)[:, :OUTER]
+    factors_all = lax.dynamic_slice_in_dim(factors_all, work_crop * ranks, ranks, 0)
+    left = lax.dynamic_index_in_dim(factors_all, work_row, 0, keepdims=False)[:, :OUTER]
     right = factors_all[:, :, OUTER:].reshape(length, OUTER)
-    w_outer = params["w_outer"].reshape(OUTER, OUTER, PAIR_DIM)
+    w_outer = rows_from(at.w_outer, OUTER * OUTER).reshape(OUTER, OUTER, PAIR_DIM)
     table = low_of(jnp.einsum("ip,pqe->ieq", left, w_outer, preferred_element_type=WIDE))
 
-    column = lambda name: wide[name].reshape(-1, 1)
-    sides_of = lambda prefix: jnp.concatenate(
-        [params[prefix + "w_left"], params[prefix + "w_right"]], axis=1
-    )
-    all_of = lambda prefix: jnp.concatenate(
-        [params[prefix + "w_left"], params[prefix + "w_right"], params[prefix + "w_gate"]], axis=1
-    )
-    tri_of = lambda prefix: (
-        column(prefix + "gain_in"), params[prefix + "w_gate"], column(prefix + "gain_tri"),
-        params[prefix + "w_tri_out"],
+    gain_row = lambda start: wide_row(start)
+    matrix = lambda start, rows=PAIR_DIM: rows_from(start, rows)
+    sides_of = lambda tri: matrix(tri.w_left, 2 * PAIR_DIM)
+    all_of = lambda tri: matrix(tri.w_left, 3 * PAIR_DIM)
+    tri_of = lambda tri: (
+        gain_row(tri.gain_in), matrix(tri.w_gate), gain_row(tri.gain_tri), matrix(tri.w_tri_out)
     )
     step_rows = min(TILE, local_rows)
     state = (local_rows, TRI_DIM, length)
@@ -614,14 +777,14 @@
 
     x_one, sides = run(
         kernel_open, step_rows, local_rows,
-        (pair_plane, table, right.T, mask_plane, column("out_gain_in"), sides_of("out_")), "rrwrww",
+        (pair_plane, table, right.T, mask_plane, gain_row(at.outgoing.gain_in), sides_of(at.outgoing)), "rrwrww",
         (("r", state, WIDE), ("s", sides_shape, LOW)), [buffer(2 * TRI_DIM)], 3 * unit,
     )
     sides_out = trade(sides)
     mixed_out = merge(trade(mix(sides_out, False)))
     x_two, sides = run(
         kernel_middle, step_rows, local_rows,
-        (mixed_out, x_one, mask_plane, *tri_of("out_"), column("in_gain_in"), sides_of("in_")),
+        (mixed_out, x_one, mask_plane, *tri_of(at.outgoing), gain_row(at.incoming.gain_in), sides_of(at.incoming)),
         "srr" + "wwww" + "ww",
         (("r", state, WIDE), ("s", sides_shape, LOW)),
         [buffer(TRI_DIM), buffer(2 * TRI_DIM)], 4 * unit,
@@ -632,21 +795,21 @@
     gain_shape = (PAIR_DIM, 1)
     pair_final, x_grad, gate_grad, mixed_grad, g_in_out, g_in_tri, g_up, g_down, g_pair, g_bias = run(
         kernel_turn, step_rows, local_rows,
-        (mixed_in, x_two, cot_plane, *tri_of("in_"), column("gain_pair"), params["w_pair_up"],
-         params["w_pair_down"], column("bias_pair")),
+        (mixed_in, x_two, cot_plane, *tri_of(at.incoming), gain_row(at.gain_pair), w_pair_up,
+         matrix(at.w_pair_down, FFN_PAIR), gain_row(at.bias_pair)),
         "srr" + "wwww" + "wwww",
         (("r", natural, LOW), ("r", state, WIDE), ("r", state, LOW), ("s", mixed_shape, LOW),
          ("a", square, WIDE), ("a", gain_shape, WIDE), ("a", (PAIR_DIM, FFN_PAIR), WIDE),
          ("a", (FFN_PAIR, PAIR_DIM), WIDE), ("a", gain_shape, WIDE), ("a", gain_shape, WIDE)),
         [buffer(TRI_DIM), buffer(TRI_DIM)], 32 * unit,
     )
-    pair_out = lax.ppermute(pair_final, BOTH, layout.homeward)
+    pair_out = moved(pair_final)
     sides_grad = trade(mix_back(trade(split(mixed_grad)), sides_in, True))
     after_shape = (PAIR_DIM, 2 * TRI_DIM + PAIR_DIM)
     x_grad, gate_grad, mixed_grad, g_in_all, g_in_gain, g_out_out, g_out_tri = run(
         kernel_return, step_rows, local_rows,
-        (sides_grad, x_two, gate_grad, x_grad, mask_plane, column("in_gain_in"), all_of("in_"),
-         mixed_out, x_one, *tri_of("out_")),
+        (sides_grad, x_two, gate_grad, x_grad, mask_plane, gain_row(at.incoming.gain_in), all_of(at.incoming),
+         mixed_out, x_one, *tri_of(at.outgoing)),
         "srrrr" + "ww" + "sr" + "wwww",
         (("r", state, WIDE), ("r", state, LOW), ("s", mixed_shape, LOW), ("a", after_shape, WIDE),
          ("a", gain_shape, WIDE), ("a", square, WIDE), ("a", gain_shape, WIDE)),
@@ -655,14 +818,14 @@
     sides_grad = trade(mix_back(trade(split(mixed_grad)), sides_out, False))
     pair_one_grad, table_grad, right_part, g_out_all, g_out_gain = run(
         kernel_close, step_rows, local_rows,
-        (sides_grad, x_one, gate_grad, x_grad, mask_plane, column("out_gain_in"), all_of("out_"),
+        (sides_grad, x_one, gate_grad, x_grad, mask_plane, gain_row(at.outgoing.gain_in), all_of(at.outgoing),
          table, right),
         "srrrr" + "ww" + "rw",
         (("r", natural, LOW), ("r", (local_rows, PAIR_DIM, OUTER), LOW), ("a", (OUTER, length), WIDE),
          ("a", after_shape, WIDE), ("a", gain_shape, WIDE)),
         [buffer(2 * TRI_DIM)], 8 * unit,
     )
-    pair_one_home = lax.ppermute(pair_one_grad, BOTH, layout.homeward)
+    pair_one_home = moved(pair_one_grad)
 
     left_grad = low_of(jnp.einsum("ieq,pqe->ip", table_grad, w_outer, preferred_element_type=WIDE))
     g_outer = jnp.einsum("ip,ieq->pqe", left, table_grad, preferred_element_type=WIDE)
@@ -671,32 +834,30 @@
         [jnp.broadcast_to(left_grad[None], right_blocks.shape), right_blocks], axis=2
     )
     factor_grads = exchange(jnp.tile(factor_blocks, (crops, 1, 1)), BOTH)
-    factor_grads = factor_grads.reshape(crops, crops, layout.wide, local_rows, 2 * OUTER)
-    factor_grads = lax.dynamic_index_in_dim(
-        factor_grads, pick(layout.planes, crop_at), 1, keepdims=False
-    ).reshape(ranks, local_rows, 2 * OUTER)
-    left_rows = lax.dynamic_index_in_dim(
-        factor_grads, pick(layout.slots, high_at) * layout.wide + wide_at, 0, keepdims=False
-    )[:, :OUTER]
+    left_rows = lax.dynamic_index_in_dim(factor_grads, partner, 0, keepdims=False)[:, :OUTER]
+    factor_grads = lax.dynamic_slice_in_dim(factor_grads, (crop_at // 2) * 2 * ranks, 2 * ranks, 0)
+    factor_grads = factor_grads.reshape(2, 2, ranks // 2, local_rows, 2 * OUTER)
+    factor_grads = lax.dynamic_index_in_dim(factor_grads, crop_at % 2, 1, keepdims=False)
+    factor_grads = factor_grads.reshape(ranks, local_rows, 2 * OUTER)
     right_rows = low_of(jnp.sum(factor_grads[:, :, OUTER:].astype(WIDE), axis=0))
     factor_rows = jnp.concatenate([left_rows, right_rows], axis=1)
 
     g_factors = dot_tn(normed_three, factor_rows)
     final_part, g_three = row_norm_back(
-        dot_nt(factor_rows, w_factors), hat_three, scale_three, wide["gain_three"]
+        dot_nt(factor_rows, w_factors), hat_three, scale_three, gain_three
     )
     final_grad = node_cot.astype(WIDE) + final_part
     final_low = low_of(final_grad)
     g_node_down = dot_tn(act_low, final_low)
-    hidden_grad = low_of(dot_nt(final_low, params["w_node_down"]) * slope)
+    hidden_grad = low_of(dot_nt(final_low, w_node_down) * slope)
     g_node_up = dot_tn(normed_two, hidden_grad)
     after_part, g_two = row_norm_back(
-        dot_nt(hidden_grad, params["w_node_up"]), hat_two, scale_two, wide["gain_two"]
+        dot_nt(hidden_grad, w_node_up), hat_two, scale_two, gain_two
     )
     after_grad = final_grad + after_part
     after_low = low_of(after_grad)
     g_attn_out = dot_tn(attended, after_low)
-    attended_grad = low_of(dot_nt(after_low, params["w_attn_out"]))
+    attended_grad = low_of(dot_nt(after_low, w_attn_out))
     attended_grad = attended_grad.reshape(local_rows, HEADS, HEAD_DIM)
     soft_grad = jnp.einsum("ihd,jhd->hij", attended_grad, value, preferred_element_type=WIDE)
     score_low = low_of(soft * (soft_grad - jnp.sum(soft_grad * soft, axis=-1, keepdims=True)))
@@ -715,61 +876,55 @@
     query_low = low_of(query_grad.reshape(local_rows, heads_width) * scale_factor)
     g_bias_head = jnp.einsum("ijd,hij->dh", pair, score_low, preferred_element_type=WIDE)
     pair_grad = pair_one_home.astype(WIDE) + jnp.einsum(
-        "hij,dh->ijd", score_low, params["w_bias"], preferred_element_type=WIDE
+        "hij,dh->ijd", score_low, w_bias, preferred_element_type=WIDE
     )
     projections = jnp.concatenate([query_low, key_value], axis=1)
     g_projections = dot_tn(normed_one, projections)
-    w_projections = jnp.concatenate([params["w_query"], params["w_key"], params["w_value"]], axis=1)
     start_part, g_one = row_norm_back(
-        dot_nt(projections, w_projections), hat_one, scale_one, wide["gain_one"]
+        dot_nt(projections, w_projections), hat_one, scale_one, gain_one
     )
     node_grad = after_grad + start_part
     g_embed = one_hot[0][:, None] * jnp.sum(node_grad, axis=0)[None, :]
 
-    grads = {
-        "embed": g_embed,
-        "gain_one": g_one,
-        "w_query": g_projections[:, :heads_width],
-        "w_key": g_projections[:, heads_width : 2 * heads_width],
-        "w_value": g_projections[:, 2 * heads_width :],
-        "w_bias": g_bias_head,
-        "w_attn_out": g_attn_out,
-        "gain_two": g_two,
-        "w_node_up": g_node_up,
-        "w_node_down": g_node_down,
-        "gain_three": g_three,
-        "w_left_node": g_factors[:, :OUTER],
-        "w_right_node": g_factors[:, OUTER:],
-        "w_outer": g_outer,
-        "gain_pair": g_pair,
-        "w_pair_up": g_up,
-        "w_pair_down": g_down,
-        "bias_pair": g_bias,
-    }
-    for prefix, g_all, g_gain, g_tri, g_out in (
-        ("out_", g_out_all, g_out_gain, g_out_tri, g_out_out),
-        ("in_", g_in_all, g_in_gain, g_in_tri, g_in_out),
+    as_rows = lambda array: lax.optimization_barrier(array).reshape(-1, LANES)
+    grads = [
+        (at.embed, 1, g_embed),
+        (at.gain_one, 1, g_one[None]),
+        (at.w_query, 3, g_projections),
+        (at.w_bias, 1, as_rows(g_bias_head)),
+        (at.w_attn_out, 1, g_attn_out),
+        (at.gain_two, 1, g_two[None]),
+        (at.w_node_up, 1, g_node_up),
+        (at.w_node_down, 1, g_node_down),
+        (at.gain_three, 1, g_three[None]),
+        (at.w_left_node, 1, as_rows(g_factors[:, :OUTER])),
+        (at.w_right_node, 1, as_rows(g_factors[:, OUTER:])),
+        (at.w_outer, 1, g_outer.reshape(OUTER * OUTER, PAIR_DIM)),
+        (at.gain_pair, 1, g_pair),
+        (at.w_pair_up, 1, g_up),
+        (at.w_pair_down, 1, g_down),
+        (at.bias_pair, 1, g_bias),
+    ]
+    for tri, g_all, g_gain, g_tri, g_out in (
+        (at.outgoing, g_out_all, g_out_gain, g_out_tri, g_out_out),
+        (at.incoming, g_in_all, g_in_gain, g_in_tri, g_in_out),
     ):
-        grads[prefix + "gain_in"] = g_gain
-        grads[prefix + "w_left"] = g_all[:, :TRI_DIM]
-        grads[prefix + "w_right"] = g_all[:, TRI_DIM : 2 * TRI_DIM]
-        grads[prefix + "w_gate"] = g_all[:, 2 * TRI_DIM :]
-        grads[prefix + "gain_tri"] = g_tri
-        grads[prefix + "w_tri_out"] = g_out
-    flat_grad = jnp.concatenate(
-        [low_of(grads[entry_name]).reshape(-1) for entry_name, entry_shape in segment_list()]
-    )
-
-    blocks = jnp.pad(flat_grad.reshape(devices, -1), ((0, 0), (0, padded - master.shape[0])))
-    blocks = blocks.reshape(crops // 2, 2, ranks, padded // 128, 128)
+        grads += [
+            (tri.gain_in, 1, g_gain),
+            (tri.w_left, 3, g_all),
+            (tri.gain_tri, 1, g_tri),
+            (tri.w_tri_out, 1, g_out),
+        ]
+
+    blocks = pack(layout, grads, amount)
     total = lambda got: low_of(jnp.sum(got.astype(WIDE), axis=0))
-    blocks = total(exchange(jnp.swapaxes(blocks, 0, 1), BOTH, layout.cores))
+    blocks = total(exchange(blocks, BOTH, layout.cores))
     blocks = total(exchange(blocks, BOTH, layout.chips))
     blocks = jnp.sum(exchange(blocks, "row").astype(WIDE), axis=0)
-    grad_own = blocks.reshape(-1)[: master.shape[0]]
+    grad_own = lax.dynamic_slice(blocks.reshape(-1), (offset,), (amount,))
     bias_total = jnp.sum(spread(g_bias.reshape(1, PAIR_DIM), devices, BOTH), axis=(0, 1))
-    square = jnp.sum(grad_own * grad_own)
-    squares = spread(jnp.full((1, 128), square), devices, BOTH)
+    square_own = jnp.sum(grad_own * grad_own)
+    squares = spread(jnp.full((1, LANES), square_own), devices, BOTH)
     grad_norm = jnp.sqrt(jnp.sum(squares[:, 0, 0]))
     clipped = grad_own * (CLIP_NORM / jnp.maximum(grad_norm, CLIP_NORM))
     new_first = BETA_ONE * first + (1.0 - BETA_ONE) * clipped

time: 1040 us -> 841 us (0.81); the launches traced: 1020 us -> 837 us
  blocking collectives: 119 us -> 266 us
  local copies, waits for them, and re-layouts: 193 us -> 48 us
  waiting for transfers between devices: 340 us -> 249 us
  starting transfers between devices: 132 us -> 59 us
  Pallas kernels: 168 us -> 150 us
    all_to_all x5 -> x8, blocking collectives: 119 us -> 266 us  [exchange(): lax.all_to_all(blocks, axes, 0, 0, axis_index_groups=groups, tiled=True)]
    all_to_all x15 -> x12, waiting for transfers between devices: 340 us -> 249 us  [exchange(): lax.all_to_all(blocks, axes, 0, 0, axis_index_groups=groups, tiled=True)]
    unnamed x228 -> x84, local copies, waits for them, and re-layouts: 82.9 us -> 8.75 us
    slice x13 -> x12, local copies, waits for them, and re-layouts: 77.2 us -> 13 us  [the longest x6 8.78 us: local(): lax.slice_in_dim(flat, start, start + count, axis=0)]
    ppermute x5, starting transfers between devices: 69.6 us -> 7.63 us  [local(): lax.ppermute(array, BOTH, layout.moves)]
    pallas_call x4 -> x6, Pallas kernels: 47.8 us -> 30.6 us  [the longest x2 11.8 us: mix_back(): pl.pallas_call(lambda *refs: kernel_mix_back(incoming, *refs), grid=(step...]
    reshape x16 -> x6, local copies, waits for them, and re-layouts: 17.1 us -> 2.97 us  [the longest x3 2.11 us: local(): as_rows = lambda array: lax.optimization_barrier(array).reshape(-1, LANES)]
    all_to_all x15 -> x12, starting transfers between devices: 62.2 us -> 51.4 us  [exchange(): lax.all_to_all(blocks, axes, 0, 0, axis_index_groups=groups, tiled=True)]
  transfers between devices with their start and end apart: 20 -> 17, of which waited for: 12 -> 12; matrix products, arithmetic and copies ran while one was open for 23% -> 11% of each run, Pallas kernels for 3% -> 1%
where the time goes in v1:
time: 841 us; the launch traced here: 837 us
  blocking collectives  266 us (32%)
  waiting for transfers between devices  249 us (30%)
  Pallas kernels  150 us (18%)
  starting transfers between devices  59 us (7%)
  local copies, waits for them, and re-layouts  48 us (6%)
  matrix products  31.4 us (4%)
  other arithmetic  30.1 us (4%)
    all_to_all x8, blocking collectives, exchange(): lax.all_to_all(blocks, axes, 0, 0, axis_index_groups=groups, tiled=True)  266 us
    all_to_all x12, waiting for transfers between devices, exchange(): lax.all_to_all(blocks, axes, 0, 0, axis_index_groups=groups, tiled=True)  249 us
    pallas_call x5, Pallas kernels, run(): pl.pallas_call(body, grid=(rows // step_rows,), in_specs=[spec(kind, a.sh...  119 us
    all_to_all x12, starting transfers between devices, exchange(): lax.all_to_all(blocks, axes, 0, 0, axis_index_groups=groups, tiled=True)  51.4 us
  transfers between devices with their start and end apart: 17, of which 12 were waited for; matrix products, arithmetic and copies ran while one was open for 11% of the time, Pallas kernels for 1%

profile of v1, /device:TPU:0, one launch (start us, length us, event | category | flops | bytes accessed | tf_op | source)
XLA Modules:
  0.0 837.2 jit_solution(2403802117084012949)
XLA Ops:
  2.5 24.2 %all_to_all.100 = bf16[8,304,128]{2,1,0:T(8,128)(2,1)S(1)} all-to-all(bf16[8,304,128]{2,1,0:T(8,128)(2,1)S(1)} %broadcast_in_dim.40), channel_id=1, replica_groups=mesh['crop'=4,'row'=8] {'row'}, dimensions={0} | all-to-all | bytes 1245184 | tf_op jit(solution)/shard_map/all_to_all | solution.py:144
  28.0 3.6 all-to-all-start.2
  32.3 2.0 collective-permute-start
  35.8 10.4 %all-to-all-done.2 = bf16[2,8,304,128]{3,2,1,0:T(8,128)(2,1)S(1)} async-done(((bf16[2,8,304,128]{3,2,1,0:T(8,128)(2,1)}), bf16[2,8,304,128]{3,2,1,0:T(8,128)(2,1)S(1)}, u32[]{:S(2)}, u32[]{:S(2)}) %all-to-all-start.2) | async-done | bytes 1245216 | tf_op jit(solution)/shard_map/all_to_all | solution.py:144
  46.5 6.7 all_to_all.101.shares_ref
  53.8 4.3 all-to-all-start
  58.1 4.4 shard_map.176
  66.1 21.1 %all-to-all-done = bf16[8,32,256]{2,1,0:T(8,128)(2,1)S(1)} async-done(((bf16[8,32,256]{2,1,0:T(8,128)(2,1)}), bf16[8,32,256]{2,1,0:T(8,128)(2,1)S(1)}, u32[]{:S(2)}, u32[]{:S(2)}) %all-to-all-start) | async-done | bytes 131104 | tf_op jit(solution)/shard_map/all_to_all | solution.py:144
  94.3 1.7 copy.157
  98.7 1.6 convolution_convert_fusion.3
  104.6 1.8 reshape.364
  106.4 3.3 all-to-all-start.4
  111.0 1.7 slice.127
  114.3 3.1 all-to-all-done.4
  117.4 1.8 reshape.365
  121.6 1.9 convolution_convert_fusion
  123.4 2.4 copy.163
  127.3 11.3 %shard_map.177 = (f32[32,128,256]{2,1,0:T(8,128)}, bf16[8,32,32,256]{3,2,1,0:T(8,128)(2,1)}) custom-call(bf16[32,256,128]{2,1,0:T(8,128)(2,1)} %broadcast_select_fusion.1.pair, bf16[32,128,32]{2,1,0:T(8,128)(2,1)} %bitcast.152, bf16[32,256]{1,0:T(8,128)(2,1)} %copy.164.right, f32[32,1,256]{2,1,0:T(1,128)} %broadcast_multiply_fusion.mask, ...), custom_call_target="tpu_custom_call" | custom-call | flops 805306368 | bytes 2474496 | tf_op jit(solution)/shard_map/pallas_call | solution.py:290
  138.7 53.2 %all_to_all.102.refs_0_.refs_1_.refs_2_ = bf16[8,32,32,256]{3,2,1,0:T(8,128)(2,1)} all-to-all(bf16[8,32,32,256]{3,2,1,0:T(8,128)(2,1)} %get-tuple-element.48), channel_id=1, replica_groups={{0,1,2,3,10,11,8,9},{6,7,4,5,12,13,14,15},{16,17,18,19,26,27,24,25},{22..., dimensions={0} | all-to-all | bytes 8388608 | tf_op jit(solution)/shard_map/all_to_all | solution.py:144
  191.9 4.7 shard_map.178
  196.6 30.6 %all_to_all.103 = bf16[8,16,32,256]{3,2,1,0:T(8,128)(2,1)} all-to-all(bf16[8,16,32,256]{3,2,1,0:T(8,128)(2,1)} %shard_map.178), channel_id=1, replica_groups={{0,1,2,3,10,11,8,9},{6,7,4,5,12,13,14,15},{16,17,18,19,26,27,24,25},{22..., dimensions={0} | all-to-all | bytes 4194304 | tf_op jit(solution)/shard_map/all_to_all | solution.py:144
  227.2 15.8 %shard_map.179 = (f32[32,128,256]{2,1,0:T(8,128)}, bf16[8,32,32,256]{3,2,1,0:T(8,128)(2,1)}) custom-call(bf16[128,32,256]{2,1,0:T(8,128)(2,1)} %bitcast.148, f32[32,128,256]{2,1,0:T(8,128)} %get-tuple-element.49.x_in.x_before.x_after, f32[32,1,256]{2,1,0:T(1,128)} %broadcast_multiply_fusion.mask, f32[1,128]{1,0:T(1,128)} %get-tuple-element.99.gain.gain_in.gain_after, ...), custom_call_target="tpu_custom_call" | custom-call | flops 1073741824 | bytes 6456832 | tf_op jit(solution)/shard_map/pallas_call | solution.py:290
  243.0 53.2 %all_to_all.104.refs_0_.refs_1_.refs_2_ = bf16[8,32,32,256]{3,2,1,0:T(8,128)(2,1)} all-to-all(bf16[8,32,32,256]{3,2,1,0:T(8,128)(2,1)} %get-tuple-element.50), channel_id=1, replica_groups={{0,1,2,3,10,11,8,9},{6,7,4,5,12,13,14,15},{16,17,18,19,26,27,24,25},{22..., dimensions={0} | all-to-all | bytes 8388608 | tf_op jit(solution)/shard_map/all_to_all | solution.py:144
  296.2 4.8 shard_map.180
  300.9 4.4 all-to-all-start.8
  307.9 3.1 broadcast_select_fusion.cot
  311.0 19.6 %all-to-all-done.8 = bf16[8,16,32,256]{3,2,1,0:T(8,128)(2,1)} async-done(((bf16[8,16,32,256]{3,2,1,0:T(8,128)(2,1)}), bf16[8,16,32,256]{3,2,1,0:T(8,128)(2,1)}, u32[]{:S(2)}, u32[]{:S(2)}) %all-to-all-start.8) | async-done | bytes 2097184 | tf_op jit(solution)/shard_map/all_to_all | solution.py:144
  330.6 54.1 %shard_map.181 = (bf16[32,256,128]{2,1,0:T(8,128)(2,1)}, f32[32,128,256]{2,1,0:T(8,128)}, bf16[32,128,256]{2,1,0:T(8,128)(2,1)}, bf16[128,32,256]{2,1,0:T(8,128)...) custom-call(bf16[128,32,256]{2,1,0:T(8,128)(2,1)} %bitcast.27.mixed,, ...), custom_call_target="tpu_custom_call" | custom-call | flops 8589934592 | bytes 8718336 | tf_op jit(solution)/shard_map/pallas_call | solution.py:290
  384.7 58.4 %all_to_all.105.refs_0_ = bf16[8,16,32,256]{3,2,1,0:T(8,128)(2,1)} all-to-all(bf16[8,16,32,256]{3,2,1,0:T(8,128)(2,1)} %bitcast.155), channel_id=1, replica_groups={{0,1,2,3,10,11,8,9},{6,7,4,5,12,13,14,15},{16,17,18,19,26,27,24,25},{22..., dimensions={0} | all-to-all | bytes 4194304 | tf_op jit(solution)/shard_map/all_to_all | solution.py:144
  443.1 5.9 shard_map.182
  449.1 4.6 all-to-all-start.10
  453.6 1.7 fusion.62
  455.3 46.1 %all-to-all-done.10.sides_grad = bf16[8,32,32,256]{3,2,1,0:T(8,128)(2,1)} async-done(((bf16[8,32,32,256]{3,2,1,0:T(8,128)(2,1)}), bf16[8,32,32,256]{3,2,1,0:T(8,128)(2,1)}, u32[]{:S(2)}, u32[]{:S(2)}) %all-to-all-start.10) | async-done | bytes 4194336 | tf_op jit(solution)/shard_map/all_to_all | solution.py:144
  501.4 22.9 %shard_map.183 = (f32[32,128,256]{2,1,0:T(8,128)}, bf16[32,128,256]{2,1,0:T(8,128)(2,1)}, bf16[128,32,256]{2,1,0:T(8,128)(2,1)}, f32[128,384]{1,0:T(8,128)}, f32...) custom-call(bf16[8,32,32,256]{3,2,1,0:T(8,128)(2,1)} %all-to-all-done.10.sides_grad, ...), custom_call_target="tpu_custom_call" | custom-call | flops 3221225472 | bytes 21169664 | tf_op jit(solution)/shard_map/pallas_call | solution.py:290
  524.3 30.6 %all_to_all.106.refs_0_ = bf16[8,16,32,256]{3,2,1,0:T(8,128)(2,1)} all-to-all(bf16[8,16,32,256]{3,2,1,0:T(8,128)(2,1)} %bitcast.156), channel_id=1, replica_groups={{0,1,2,3,10,11,8,9},{6,7,4,5,12,13,14,15},{16,17,18,19,26,27,24,25},{22..., dimensions={0} | all-to-all | bytes 4194304 | tf_op jit(solution)/shard_map/all_to_all | solution.py:144
  554.9 5.9 shard_map.184
  560.8 4.6 all-to-all-start.12
  566.5 46.6 %all-to-all-done.12.sides_grad = bf16[8,32,32,256]{3,2,1,0:T(8,128)(2,1)} async-done(((bf16[8,32,32,256]{3,2,1,0:T(8,128)(2,1)}), bf16[8,32,32,256]{3,2,1,0:T(8,128)(2,1)}, u32[]{:S(2)}, u32[]{:S(2)}) %all-to-all-start.12) | async-done | bytes 4194336 | tf_op jit(solution)/shard_map/all_to_all | solution.py:144
  613.1 15.1 %shard_map.185 = (bf16[32,256,128]{2,1,0:T(8,128)(2,1)}, bf16[32,128,32]{2,1,0:T(8,128)(2,1)}, f32[32,256]{1,0:T(8,128)}, f32[128,384]{1,0:T(8,128)}, f32[128,1]{1,0:T(8,128)}) custom-call(bf16[8,32,32,256]{3,2,1,0:T(8,128)(2,1)} %all-to-all-done.12.sides_grad, f32[32,128,256]{2,1,0:T(8,128)} %get-tuple-element.49.x_in.x_before.x_after, ...), custom_call_target="tpu_custom_call" | custom-call | flops 2147483648 | bytes 15090176 | tf_op jit(solution)/shard_map/pallas_call | solution.py:290
  628.2 2.4 copy.165
  635.0 1.6 copy.168
  638.2 1.8 reshape.366
  640.0 4.8 all-to-all-start.13
  646.1 2.0 collective-permute-start.3
  650.4 2.0 collective-permute-start.4
  652.6 1.8 reshape.367
  656.2 1.7 multiply_reduce_fusion.3
  663.6 2.2 fusion.8
  672.8 9.2 %all-to-all-start.14 = ((bf16[8,32,512]{2,1,0:T(8,128)(2,1)}), bf16[8,32,512]{2,1,0:T(8,128)(2,1)S(1)}, u32[]{:S(2)}, u32[]{:S(2)}) async-start(bf16[8,32,512]{2,1,0:T(8,128)(2,1)} %pad_maximum_fusion), calls=%async_computation.14 | async-start | bytes 524288 | tf_op jit(solution)/shard_map/all_to_all | solution.py:144
  684.3 63.9 %all-to-all-done.14 = bf16[8,32,512]{2,1,0:T(8,128)(2,1)S(1)} async-done(((bf16[8,32,512]{2,1,0:T(8,128)(2,1)}), bf16[8,32,512]{2,1,0:T(8,128)(2,1)S(1)}, u32[]{:S(2)}, u32[]{:S(2)}) %all-to-all-start.14) | async-done | bytes 262176 | tf_op jit(solution)/shard_map/all_to_all | solution.py:144
  751.9 1.9 fusion.31.refs_2_
  753.8 4.9 shard_map.186
  758.6 9.2 %all_to_all.107 = bf16[2,2,8,304,128]{4,3,2,1,0:T(8,128)(2,1)} all-to-all(bf16[2,2,8,304,128]{4,3,2,1,0:T(8,128)(2,1)} %shard_map.186), channel_id=1, replica_groups={{0,8},{1,9},{2,10},{3,11},{4,12},{5,13},{6,14},{7,15},{16,24},{17,25},{..., dimensions={0} | all-to-all | bytes 4980736 | tf_op jit(solution)/shard_map/all_to_all | solution.py:144
  767.9 3.5 reduce_sum.266
  771.4 3.7 all-to-all-start.16
  775.2 16.1 %all-to-all-done.16 = bf16[2,8,304,128]{3,2,1,0:T(8,128)(2,1)S(1)} async-done(((bf16[2,8,304,128]{3,2,1,0:T(8,128)(2,1)}), bf16[2,8,304,128]{3,2,1,0:T(8,128)(2,1)S(1)}, u32[]{:S(2)}, u32[]{:S(2)}) %all-to-all-start.16) | async-done | bytes 1245216 | tf_op jit(solution)/shard_map/all_to_all | solution.py:144
  792.0 2.6 all-to-all-start.18
  795.8 5.9 all-to-all-done.18
  801.7 3.5 all-to-all-start.17
  805.8 3.1 select_bitcast_fusion
  808.9 13.1 %all-to-all-done.17 = bf16[8,304,128]{2,1,0:T(8,128)(2,1)S(1)} async-done(((bf16[8,304,128]{2,1,0:T(8,128)(2,1)}), bf16[8,304,128]{2,1,0:T(8,128)(2,1)S(1)}, u32[]{:S(2)}, u32[]{:S(2)}) %all-to-all-start.17) | async-done | bytes 622624 | tf_op jit(solution)/shard_map/all_to_all | solution.py:144
  824.1 2.7 all-to-all-start.19
  826.9 4.1 fusion.1
  831.0 2.9 all-to-all-done.19
  (203 shorter events, 69.5 us)
Async XLA Ops:
  26.8 4.8 copy-start.37
  26.8 5.5 copy-start
  28.0 18.2 %all-to-all-start.2 = ((bf16[2,8,304,128]{3,2,1,0:T(8,128)(2,1)}), bf16[2,8,304,128]{3,2,1,0:T(8,128)(2,1)S(1)}, u32[]{:S(2)}, u32[]{:S(2)}) async-start(bf16[2,8,304,128]{3,2,1,0:T(8,128)(2,1)} %broadcast_in_dim.41), calls=%async_computation.2 | async-start | bytes 2490368 | tf_op jit(solution)/shard_map/all_to_all | solution.py:144
  31.6 3.3 collective-permute-start.1
  32.3 93.5 %collective-permute-start = (bf16[32,256,128]{2,1,0:T(8,128)(2,1)S(1)}, bf16[32,256,128]{2,1,0:T(8,128)(2,1)}, u32[]{:S(2)}, u32[]{:S(2)}) collective-permute-start(bf16[32,256,128]{2,1,0:T(8,128)(2,1)S(1)} %bitcast.147), channel_id=1, source_target_pairs={{4,10},{5,11},{6,8},{7,9},{8,6},{9,7},{10,4},{11,5},{20,26},{21,27... | collective-permute-start | bytes 6291464 | tf_op jit(solution)/shard_map/ppermute | solution.py:692
  46.5 6.7 copy-start.26
  53.8 33.4 %all-to-all-start = ((bf16[8,32,256]{2,1,0:T(8,128)(2,1)}), bf16[8,32,256]{2,1,0:T(8,128)(2,1)S(1)}, u32[]{:S(2)}, u32[]{:S(2)}) async-start(bf16[8,32,256]{2,1,0:T(8,128)(2,1)} %broadcast_in_dim.37), calls=%async_computation | async-start | bytes 262144 | tf_op jit(solution)/shard_map/all_to_all | solution.py:144
  62.5 28.5 %copy-start.3 = (bf16[256,768]{1,0:T(8,128)(2,1)S(1)}, bf16[256,768]{1,0:T(8,128)(2,1)}, u32[]{:S(2)}) copy-start(bf16[256,768]{1,0:T(8,128)(2,1)} %get-tuple-element.44) | copy-start | bytes 1179652
  63.8 27.4 %copy-start.27 = (f32[256]{0:T(256)}, f32[256]{0:T(256)S(1)}, u32[]{:S(2)}) copy-start(f32[256]{0:T(256)S(1)} %get-tuple-element.109) | copy-start | bytes 3076
  87.8 3.1 copy-start.15
  88.0 14.8 %copy-start.11 = (bf16[256,32]{1,0:T(8,128)(2,1)}, bf16[256,32]{1,0:T(8,128)(2,1)S(1)}, u32[]{:S(2)}) copy-start(bf16[256,32]{1,0:T(8,128)(2,1)S(1)} %slice.131) | copy-start | bytes 49156
  90.9 0.6 copy-start.7
  91.6 10.2 %copy-start.1 = (bf16[256,1024]{1,0:T(8,128)(2,1)S(1)}, bf16[256,1024]{1,0:T(8,128)(2,1)}, u32[]{:S(2)}) copy-start(bf16[256,1024]{1,0:T(8,128)(2,1)} %get-tuple-element.46) | copy-start | bytes 1572868
  93.2 9.0 %copy-start.2 = (bf16[1024,256]{1,0:T(8,128)(2,1)S(1)}, bf16[1024,256]{1,0:T(8,128)(2,1)}, u32[]{:S(2)}) copy-start(bf16[1024,256]{1,0:T(8,128)(2,1)} %get-tuple-element.47) | copy-start | bytes 1572868
  97.1 0.7 copy-start.5
  98.7 4.1 copy-start.29
  100.3 1.5 copy-start.18
  101.5 1.2 copy-start.31
  101.7 0.5 copy-start.34
  102.5 1.3 copy-start.33
  102.8 1.1 copy-start.36
  106.4 11.0 %all-to-all-start.4 = ((bf16[32,2,1024]{2,1,0:T(2,128)(2,1)}), bf16[32,2,1024]{2,1,0:T(2,128)(2,1)}, u32[]{:S(2)}, u32[]{:S(2)}) async-start(bf16[32,2,1024]{2,1,0:T(2,128)(2,1)} %reshape.364), calls=%async_computation.4 | async-start | bytes 262144 | tf_op jit(solution)/shard_map/all_to_all | solution.py:144
  120.2 7.2 copy-start.10
  300.9 29.6 %all-to-all-start.8 = ((bf16[8,16,32,256]{3,2,1,0:T(8,128)(2,1)}), bf16[8,16,32,256]{3,2,1,0:T(8,128)(2,1)}, u32[]{:S(2)}, u32[]{:S(2)}) async-start(bf16[8,16,32,256]{3,2,1,0:T(8,128)(2,1)} %shard_map.180), calls=%async_computation.8 | async-start | bytes 4194304 | tf_op jit(solution)/shard_map/all_to_all | solution.py:144
  305.3 2.6 collective-permute-start.2
  449.1 52.3 %all-to-all-start.10 = ((bf16[8,32,32,256]{3,2,1,0:T(8,128)(2,1)}), bf16[8,32,32,256]{3,2,1,0:T(8,128)(2,1)}, u32[]{:S(2)}, u32[]{:S(2)}) async-start(bf16[8,32,32,256]{3,2,1,0:T(8,128)(2,1)} %bitcast.151), calls=%async_computation.10 | async-start | bytes 8388608 | tf_op jit(solution)/shard_map/all_to_all | solution.py:144
  560.8 52.3 %all-to-all-start.12 = ((bf16[8,32,32,256]{3,2,1,0:T(8,128)(2,1)}), bf16[8,32,32,256]{3,2,1,0:T(8,128)(2,1)}, u32[]{:S(2)}, u32[]{:S(2)}) async-start(bf16[8,32,32,256]{3,2,1,0:T(8,128)(2,1)} %bitcast.150), calls=%async_computation.12 | async-start | bytes 8388608 | tf_op jit(solution)/shard_map/all_to_all | solution.py:144
  633.4 22.7 %copy-start.12 = (bf16[256,32]{1,0:T(8,128)(2,1)S(1)}, bf16[256,32]{1,0:T(8,128)(2,1)}, u32[]{:S(2)}) copy-start(bf16[256,32]{1,0:T(8,128)(2,1)} %copy-done.11) | copy-start | bytes 49156
  633.4 22.7 %copy-start.25 = (f32[256]{0:T(256)S(1)}, f32[256]{0:T(256)}, u32[]{:S(2)}) copy-start(f32[256]{0:T(256)} %get-tuple-element.107) | copy-start | bytes 3076
  640.0 12.5 %all-to-all-start.13 = ((bf16[32,2,1024]{2,1,0:T(2,128)(2,1)}), bf16[32,2,1024]{2,1,0:T(2,128)(2,1)}, u32[]{:S(2)}, u32[]{:S(2)}) async-start(bf16[32,2,1024]{2,1,0:T(2,128)(2,1)} %reshape.366), calls=%async_computation.13 | async-start | bytes 262144 | tf_op jit(solution)/shard_map/all_to_all | solution.py:144
  646.1 159.7 %collective-permute-start.3 = (bf16[32,256,128]{2,1,0:T(8,128)(2,1)}, bf16[32,256,128]{2,1,0:T(8,128)(2,1)}, u32[]{:S(2)}, u32[]{:S(2)}) collective-permute-start(bf16[32,256,128]{2,1,0:T(8,128)(2,1)} %get-tuple-element.53), channel_id=1, source_target_pairs={{4,10},{5,11},{6,8},{7,9},{8,6},{9,7},{10,4},{11,5},{20,26},{21,27... | collective-permute-start | bytes 6291464 | tf_op jit(solution)/shard_map/ppermute | solution.py:692
  649.3 13.3 %copy-start.32 = (f32[32]{0:T(128)S(1)}, f32[32]{0:T(128)}, u32[]{:S(2)}) copy-start(f32[32]{0:T(128)} %copy-done.31) | copy-start | bytes 388
  649.3 14.3 %copy-start.30 = (f32[8,32]{1,0:T(8,128)S(1)}, f32[8,32]{1,0:T(8,128)}, u32[]{:S(2)}) copy-start(f32[8,32]{1,0:T(8,128)} %copy-done.29) | copy-start | bytes 3076
  650.4 176.4 %collective-permute-start.4 = (bf16[32,256,128]{2,1,0:T(8,128)(2,1)}, bf16[32,256,128]{2,1,0:T(8,128)(2,1)}, u32[]{:S(2)}, u32[]{:S(2)}) collective-permute-start(bf16[32,256,128]{2,1,0:T(8,128)(2,1)} %get-tuple-element.62), channel_id=1, source_target_pairs={{4,10},{5,11},{6,8},{7,9},{8,6},{9,7},{10,4},{11,5},{20,26},{21,27... | collective-permute-start | bytes 6291464 | tf_op jit(solution)/shard_map/ppermute | solution.py:692
  654.4 8.9 %copy-start.14 = (bf16[256,256]{1,0:T(8,128)(2,1)S(1)}, bf16[256,256]{1,0:T(8,128)(2,1)}, u32[]{:S(2)}) copy-start(bf16[256,256]{1,0:T(8,128)(2,1)} %get-tuple-element.45) | copy-start | bytes 393220
  661.0 4.8 copy-start.6
  661.0 4.7 copy-start.23
  665.8 1.1 copy-start.13
  665.8 1.2 copy-start.35
  666.3 2.1 copy-start.24
  666.8 4.6 copy-start.22
  669.4 12.6 %copy-start.19 = (bf16[8,32,32]{2,1,0:T(8,128)(2,1)S(1)}, bf16[8,32,32]{2,1,0:T(8,128)(2,1)}, u32[]{:S(2)}) copy-start(bf16[8,32,32]{2,1,0:T(8,128)(2,1)} %copy-done.18) | copy-start | bytes 49156
  671.5 76.7 %copy-start.4 = (bf16[256,768]{1,0:T(8,128)(2,1)S(1)}, bf16[256,768]{1,0:T(8,128)(2,1)}, u32[]{:S(2)}) copy-start(bf16[256,768]{1,0:T(8,128)(2,1)} %get-tuple-element.44) | copy-start | bytes 1179652
  671.5 76.7 %copy-start.28 = (f32[256]{0:T(256)S(1)}, f32[256]{0:T(256)}, u32[]{:S(2)}) copy-start(f32[256]{0:T(256)} %copy-done.27) | copy-start | bytes 3076
  671.7 78.0 %copy-start.38 = (f32[32]{0:T(128)S(1)}, f32[32]{0:T(128)}, u32[]{:S(2)}) copy-start(f32[32]{0:T(128)} %fusion.47) | copy-start | bytes 388
  671.8 79.5 %copy-start.39 = (f32[4]{0:T(128)S(1)}, f32[4]{0:T(128)}, u32[]{:S(2)}) copy-start(f32[4]{0:T(128)} %compare_convert_fusion) | copy-start | bytes 52
  672.8 75.3 %all-to-all-start.14 = ((bf16[8,32,512]{2,1,0:T(8,128)(2,1)}), bf16[8,32,512]{2,1,0:T(8,128)(2,1)S(1)}, u32[]{:S(2)}, u32[]{:S(2)}) async-start(bf16[8,32,512]{2,1,0:T(8,128)(2,1)} %pad_maximum_fusion), calls=%async_computation.14 | async-start | bytes 524288 | tf_op jit(solution)/shard_map/all_to_all | solution.py:144
  771.3 3.8 copy-start.17
  771.4 20.0 %all-to-all-start.16 = ((bf16[2,8,304,128]{3,2,1,0:T(8,128)(2,1)}), bf16[2,8,304,128]{3,2,1,0:T(8,128)(2,1)S(1)}, u32[]{:S(2)}, u32[]{:S(2)}) async-start(bf16[2,8,304,128]{3,2,1,0:T(8,128)(2,1)} %reduce_sum.266), calls=%async_computation.16 | async-start | bytes 2490368 | tf_op jit(solution)/shard_map/all_to_all | solution.py:144
  792.0 9.7 %all-to-all-start.18 = ((f32[32,1,128]{2,1,0:T(1,128)}), f32[32,1,128]{2,1,0:T(1,128)S(1)}, u32[]{:S(2)}, u32[]{:S(2)}) async-start(f32[32,1,128]{2,1,0:T(1,128)} %broadcast_in_dim.53), calls=%async_computation.18 | async-start | bytes 32768 | tf_op jit(solution)/shard_map/all_to_all | solution.py:144
  801.7 20.3 %all-to-all-start.17 = ((bf16[8,304,128]{2,1,0:T(8,128)(2,1)}), bf16[8,304,128]{2,1,0:T(8,128)(2,1)S(1)}, u32[]{:S(2)}, u32[]{:S(2)}) async-start(bf16[8,304,128]{2,1,0:T(8,128)(2,1)} %reduce_sum.267), calls=%async_computation.17 | async-start | bytes 1245184 | tf_op jit(solution)/shard_map/all_to_all | solution.py:144
  805.8 21.1 %copy-start.16 = (bf16[128,8]{1,0:T(8,128)(2,1)S(1)}, bf16[128,8]{1,0:T(8,128)(2,1)}, u32[]{:S(2)}) copy-start(bf16[128,8]{1,0:T(8,128)(2,1)} %copy-done.15) | copy-start | bytes 6148
  822.8 12.4 %copy-start.9 = (f32[37488]{0:T(1024)}, f32[37488]{0:T(1024)S(1)}, u32[]{:S(2)}) copy-start(f32[37488]{0:T(1024)S(1)} %get-tuple-element.89) | copy-start | bytes 449860
  824.1 9.8 %all-to-all-start.19 = ((f32[32,1,128]{2,1,0:T(1,128)}), f32[32,1,128]{2,1,0:T(1,128)S(1)}, u32[]{:S(2)}, u32[]{:S(2)}) async-start(f32[32,1,128]{2,1,0:T(1,128)} %broadcast_in_dim_broadcast_in_dim_broadcast_in_dim.3), calls=%async_computation.19 | async-start | bytes 32768 | tf_op jit(solution)/shard_map/all_to_all | solution.py:144
  826.8 8.4 %copy-start.8 = (f32[37488]{0:T(1024)S(1)}, f32[37488]{0:T(1024)}, u32[]{:S(2)}) copy-start(f32[37488]{0:T(1024)} %param.15) | copy-start | bytes 449860
  826.8 8.4 %copy-start.20 = (f32[37488]{0:T(1024)S(1)}, f32[37488]{0:T(1024)}, u32[]{:S(2)}) copy-start(f32[37488]{0:T(1024)} %param.16) | copy-start | bytes 449860
  826.8 8.4 %copy-start.21 = (f32[37488]{0:T(1024)S(1)}, f32[37488]{0:T(1024)}, u32[]{:S(2)}) copy-start(f32[37488]{0:T(1024)} %param.17) | copy-start | bytes 449860

commit v2 on v1

v2 whole, which is shorter than its diff:
```python
import math
from typing import Any, NamedTuple

import jax
import jax.numpy as jnp
import numpy as np
from jax import lax
from jax.experimental import pallas as pl
from jax.experimental.pallas import tpu as pltpu
from jax.sharding import PartitionSpec as P

NODE_DIM = 256
PAIR_DIM = 128
HEADS = 8
HEAD_DIM = 32
OUTER = 32
TRI_DIM = 128
FFN_NODE = 1024
FFN_PAIR = 512
RECYCLES = 4
ADAM_STEP = 3


EPS_NORM = 1e-05
ADAM_EPS = 1e-08
BETA_ONE = 0.9
BETA_TWO = 0.95
LEARN_RATE = 0.06
WEIGHT_DECAY = 0.1
CLIP_NORM = 1.0
MASK_FILL = 1000000000.0
HIGHEST = lax.Precision.HIGHEST


class Triangle(NamedTuple):
    gain_in: Any
    w_left: Any
    w_right: Any
    w_gate: Any
    gain_tri: Any
    w_tri_out: Any


class Params(NamedTuple):
    embed: Any
    gain_one: Any
    w_query: Any
    w_key: Any
    w_value: Any
    w_bias: Any
    w_attn_out: Any
    gain_two: Any
    w_node_up: Any
    w_node_down: Any
    gain_three: Any
    w_left_node: Any
    w_right_node: Any
    w_outer: Any
    outgoing: Triangle
    incoming: Triangle
    gain_pair: Any
    w_pair_up: Any
    w_pair_down: Any
    bias_pair: Any


LANES = 128
HEADS_WIDTH = HEADS * HEAD_DIM


def first_rows():
    square = PAIR_DIM * TRI_DIM
    triangle = Triangle(PAIR_DIM, square, square, PAIR_DIM * PAIR_DIM, TRI_DIM, square)
    sizes = Params(
        embed=RECYCLES * NODE_DIM,
        gain_one=NODE_DIM,
        w_query=NODE_DIM * HEADS_WIDTH,
        w_key=NODE_DIM * HEADS_WIDTH,
        w_value=NODE_DIM * HEADS_WIDTH,
        w_bias=PAIR_DIM * HEADS,
        w_attn_out=HEADS_WIDTH * NODE_DIM,
        gain_two=NODE_DIM,
        w_node_up=NODE_DIM * FFN_NODE,
        w_node_down=FFN_NODE * NODE_DIM,
        gain_three=NODE_DIM,
        w_left_node=NODE_DIM * OUTER,
        w_right_node=NODE_DIM * OUTER,
        w_outer=OUTER * OUTER * PAIR_DIM,
        outgoing=triangle,
        incoming=triangle,
        gain_pair=PAIR_DIM,
        w_pair_up=PAIR_DIM * FFN_PAIR,
        w_pair_down=FFN_PAIR * PAIR_DIM,
        bias_pair=PAIR_DIM,
    )
    leaves, tree = jax.tree.flatten(sizes)
    ends = np.cumsum(leaves) // LANES
    starts = [0] + [int(end) for end in ends[:-1]]
    return jax.tree.unflatten(tree, starts), int(ends[-1])


LOW = jnp.bfloat16
WIDE = jnp.float32
BOTH = ("crop", "row")
TILE = 16
VMEM_LIMIT = 56 * 2**20
INV_SQRT2 = 1.0 / math.sqrt(2.0)
INV_SQRT2PI = 1.0 / math.sqrt(2.0 * math.pi)


class Layout:
    def __init__(self, crops, rows):
        self.crops, self.rows = crops, rows
        self.devices = crops * rows
        self.wide = 2 ** (int(math.log2(rows)) // 2)
        self.high = rows // self.wide
        half = crops // 2
        self.moves = [
            (here, self.work_place(here))
            for here in range(self.devices)
            if here != self.work_place(here)
        ]
        self.groups = [
            [self.work_place(c * rows + r) for r in range(rows)] for c in range(crops)
        ]
        self.cores = [
            [(2 * x + k) * rows + r for k in range(2)] for x in range(half) for r in range(rows)
        ]
        self.chips = [
            [(2 * x + k) * rows + r for x in range(half)] for k in range(2) for r in range(rows)
        ]

    def work_place(self, here):
        crop, row = here // self.rows, here % self.rows
        high, wide = row // self.wide, row % self.wide
        core = crop % 2
        away = (high // (self.high // 2) + core) % 2
        crop = crop + away * (1 - 2 * core)
        high = high + away * (self.high - 1 - 2 * high)
        return crop * self.rows + high * self.wide + wide


def exchange(blocks, axes, groups=None):
    return lax.all_to_all(blocks, axes, 0, 0, axis_index_groups=groups, tiled=True)


def spread(part, count, axes, groups=None):
    return exchange(jnp.broadcast_to(part[None], (count,) + part.shape), axes, groups)


def dot_nn(a, b):
    return lax.dot_general(a, b, (((1,), (0,)), ((), ())), preferred_element_type=WIDE)


def dot_nt(a, b):
    return lax.dot_general(a, b, (((1,), (1,)), ((), ())), preferred_element_type=WIDE)


def dot_tn(a, b):
    return lax.dot_general(a, b, (((0,), (0,)), ((), ())), preferred_element_type=WIDE)


def norm_parts(x):
    centered = x - jnp.mean(x, axis=0, keepdims=True)
    scale = lax.rsqrt(jnp.mean(centered * centered, axis=0, keepdims=True) + EPS_NORM)
    return centered * scale, scale


def norm_back(grad, hat, scale, gain):
    grad_gain = jnp.sum(grad * hat, axis=1, keepdims=True)
    wide = grad * gain
    inner = jnp.mean(wide * hat, axis=0, keepdims=True)
    return scale * (wide - jnp.mean(wide, axis=0, keepdims=True) - hat * inner), grad_gain


def sigmoid(x):
    return 0.5 * jnp.tanh(0.5 * x) + 0.5


EMBED = slice(0, 8)
GAIN_ONE, GAIN_TWO, GAIN_THREE = slice(8, 10), slice(10, 12), slice(12, 14)
OUT_GAIN, OUT_TRI, IN_GAIN, IN_TRI = (slice(k, k + 1) for k in range(14, 18))
PAIR_GAIN, PAIR_BIAS = slice(18, 19), slice(19, 20)


def column(row):
    return jnp.broadcast_to(row, (LANES, row.shape[1])).T[:, :1]


def row_of(values):
    return jnp.broadcast_to(values, (values.shape[0], LANES)).T[:1]


def cat(ref):
    return jnp.concatenate([ref[t] for t in range(ref.shape[0])], axis=1)


def put(ref, value):
    count = ref.shape[0]
    width = value.shape[1] // count
    for t in range(count):
        ref[t] = value[:, t * width : (t + 1) * width].astype(ref.dtype)


def swapped(value):
    if value.shape[0] % TILE or value.shape[1] % TILE:
        return jnp.swapaxes(value.astype(WIDE), 0, 1).astype(LOW)
    return jnp.swapaxes(value, 0, 1)


def send_pair(scratch, out_ref):
    parts, share = out_ref.shape[0], out_ref.shape[1] // 2
    channels = parts * share
    for side in range(2):
        value = swapped(scratch[:, side * channels : (side + 1) * channels, :])
        out_ref[:, side * share : (side + 1) * share] = value.reshape(
            (parts, share) + value.shape[1:]
        )


def take_pair(in_ref, scratch):
    parts, share = in_ref.shape[0], in_ref.shape[1] // 2
    channels = parts * share
    for side in range(2):
        value = in_ref[:, side * share : (side + 1) * share]
        value = value.reshape((channels,) + value.shape[2:])
        scratch[:, side * channels : (side + 1) * channels, :] = swapped(value)


def front(x, gain, w_all, mask, x_out, hat_out, scale_out, gate_out, sides):
    hat, scale = norm_parts(x)
    all_three = dot_nn(w_all, (hat * gain).astype(LOW))
    channels = 2 * TRI_DIM
    put(sides, all_three[:channels] * mask)
    put(x_out, x)
    put(hat_out, hat)
    put(scale_out, scale)
    put(gate_out, sigmoid(all_three[channels:]))


def triangle_update(mixed, gain, w_out):
    hat, scale = norm_parts(mixed)
    normed = (hat * gain).astype(LOW)
    return hat, scale, normed, dot_nn(w_out, normed)


def post_back(grad, gate, hat, scale, normed, update, gain, w_out_back):
    update_grad = (grad * gate).astype(LOW)
    gate_grad = (grad * update * (gate * (1.0 - gate))).astype(LOW)
    grad_out = dot_nt(normed, update_grad)
    mixed_grad, grad_gain = norm_back(dot_nn(w_out_back, update_grad), hat, scale, gain)
    return mixed_grad, gate_grad, grad_out, grad_gain


def front_back(grad, hat, scale, sides_grad, gate_grad, mask, gain, w_all_back):
    normed = (hat * gain).astype(LOW)
    sides = jnp.concatenate([sides_grad * mask.astype(LOW), gate_grad], axis=0)
    grad_w = dot_nt(normed, sides)
    x_grad, grad_gain = norm_back(dot_nn(w_all_back, sides), hat, scale, gain)
    return grad + x_grad, grad_w, grad_gain


def gelu_parts(x):
    cumulative = 0.5 * lax.erf(x * INV_SQRT2) + 0.5
    density = INV_SQRT2PI * jnp.exp(-0.5 * x * x)
    return x * cumulative, cumulative + x * density


def zero_first(*refs):
    @pl.when((pl.program_id(0) == 0) & (pl.program_id(1) == 0))
    def _():
        for ref in refs:
            ref[...] = jnp.zeros_like(ref)


def run(body, step, extent, in_arrays, in_kinds, outs, scratch, flops):
    def spec(kind, shape):
        lead = (0,) * len(shape)
        block, at = {
            "r": (step[:1] + shape[1:-1] + step[1:], lambda c, r: (r,) + lead[2:] + (c,)),
            "n": (step + shape[2:], lambda c, r: (r, c) + lead[2:]),
            "s": (shape[:-2] + step, lambda c, r: lead[2:] + (r, c)),
            "c": (shape[:-1] + step[1:], lambda c, r: lead[1:] + (c,)),
            "t": (step[:1] + shape[1:], lambda c, r: (r,) + lead[1:]),
            "p": ((1,) + step[:1] + shape[2:], lambda c, r: (c, r) + lead[2:]),
            "q": (step[1:] + shape[1:], lambda c, r: (c,) + lead[1:]),
            "w": (shape, lambda c, r: lead),
        }[kind]
        return pl.BlockSpec(block, at)

    moved = sum(a.size * a.dtype.itemsize for a in in_arrays)
    return pl.pallas_call(
        body,
        grid=(extent[1] // step[1], extent[0] // step[0]),
        in_specs=[spec(kind, a.shape) for kind, a in zip(in_kinds, in_arrays)],
        out_specs=[spec(kind, shape) for kind, shape, _ in outs],
        out_shape=[jax.ShapeDtypeStruct(shape, dtype) for _, shape, dtype in outs],
        scratch_shapes=scratch,
        compiler_params=pltpu.CompilerParams(vmem_limit_bytes=VMEM_LIMIT),
        cost_estimate=pl.CostEstimate(flops=flops, bytes_accessed=moved, transcendentals=0),
    )(*in_arrays)


def all_low(w):
    return jnp.concatenate([w[k * PAIR_DIM : (k + 1) * PAIR_DIM].T for k in range(3)], axis=0)


def all_back(w):
    return jnp.concatenate([w[k * PAIR_DIM : (k + 1) * PAIR_DIM] for k in range(3)], axis=1)


def kernel_open(
    pair, table, right, mask, vectors, w_all, x_out, hat_out, scale_out, gate_out, sides_out, sides
):
    right_low = right[...]
    x = jnp.concatenate(
        [pair[t].T.astype(WIDE) + dot_tn(table[t], right_low) for t in range(pair.shape[0])],
        axis=1,
    )
    front(
        x, column(vectors[OUT_GAIN]), all_low(w_all), cat(mask), x_out, hat_out, scale_out, gate_out, sides
    )
    send_pair(sides, sides_out)


def kernel_middle(
    mixed, x_in, gate_in, mask, vectors, w_out, w_all,
    x_out, hat_out, scale_out, gate_out, sides_out, arrived, sides,
):
    arrived[...] = swapped(mixed[...])
    *_, update = triangle_update(cat(arrived).astype(WIDE), column(vectors[OUT_TRI]), w_out[...].T)
    x = cat(x_in) + cat(gate_in).astype(WIDE) * update
    front(
        x, column(vectors[IN_GAIN]), all_low(w_all), cat(mask),
        x_out, hat_out, scale_out, gate_out, sides,
    )
    send_pair(sides, sides_out)


def kernel_turn(
    mixed, x_in, gate_in, cot, vectors, w_out, w_up, w_down,
    pair_out, x_grad, gate_grad, mixed_grad, g_out, g_tri, g_up, g_down, g_pair, g_bias,
    arrived, leaving,
):
    rows = x_in.shape[0]
    arrived[...] = swapped(mixed[...])
    up_low, up_back = w_up[...].T, w_up[...]
    down_low, down_back = w_down[...].T, w_down[...]
    tri_col, pair_col = column(vectors[IN_TRI]), column(vectors[PAIR_GAIN])
    zero_first(g_out, g_tri, g_up, g_down, g_pair, g_bias)
    chunk = PAIR_DIM

    gate = cat(gate_in).astype(WIDE)
    mix_parts = triangle_update(cat(arrived).astype(WIDE), tri_col, w_out[...].T)
    x = cat(x_in) + gate * mix_parts[-1]
    hat, scale = norm_parts(x)
    normed = (hat * pair_col).astype(LOW)
    cot_low = jnp.concatenate([cot[t].T for t in range(rows)], axis=1)
    total = x + column(vectors[PAIR_BIAS])
    normed_grad = jnp.zeros_like(x)
    for c in range(FFN_PAIR // chunk):
        part = slice(c * chunk, (c + 1) * chunk)
        act, slope = gelu_parts(dot_nn(up_low[part], normed))
        act_low = act.astype(LOW)
        total = total + dot_nn(down_low[:, part], act_low)
        hidden_grad = (dot_nn(down_back[part], cot_low) * slope).astype(LOW)
        normed_grad = normed_grad + dot_nn(up_back[:, part], hidden_grad)
        g_up[:, part] += dot_nt(normed, hidden_grad)
        g_down[part] += dot_nt(act_low, cot_low)
    total_low = total.astype(LOW)
    width = total.shape[1] // rows
    for t in range(rows):
        pair_out[t] = total_low[:, t * width : (t + 1) * width].T
    cot_wide = cot_low.astype(WIDE)
    g_bias[...] += jnp.sum(cot_wide, axis=1, keepdims=True)
    back, grad_gain = norm_back(normed_grad, hat, scale, pair_col)
    g_pair[...] += grad_gain
    grad = cot_wide + back
    put(x_grad, grad)
    mix_grad, gates, grad_out, grad_tri = post_back(grad, gate, *mix_parts, tri_col, w_out[...])
    put(leaving, mix_grad)
    put(gate_grad, gates)
    g_out[...] += grad_out
    g_tri[...] += grad_tri
    mixed_grad[...] = swapped(leaving[...])


def kernel_return(
    sides_grad, hat_after, scale_after, gate_after, grad_in, mask, vectors, w_after,
    mixed, gate_in, w_out,
    x_grad, gate_grad, mixed_grad, g_after, g_gain, g_out, g_tri,
    sides, arrived, leaving,
):
    take_pair(sides_grad, sides)
    arrived[...] = swapped(mixed[...])
    tri_col = column(vectors[OUT_TRI])
    zero_first(g_after, g_gain, g_out, g_tri)
    grad, grad_w, grad_gain = front_back(
        cat(grad_in), cat(hat_after).astype(WIDE), cat(scale_after), cat(sides), cat(gate_after),
        cat(mask), column(vectors[IN_GAIN]), all_back(w_after),
    )
    g_after[...] += grad_w
    g_gain[...] += grad_gain
    put(x_grad, grad)
    mix_parts = triangle_update(cat(arrived).astype(WIDE), tri_col, w_out[...].T)
    mix_grad, gates, grad_out, grad_tri = post_back(
        grad, cat(gate_in).astype(WIDE), *mix_parts, tri_col, w_out[...]
    )
    put(leaving, mix_grad)
    put(gate_grad, gates)
    g_out[...] += grad_out
    g_tri[...] += grad_tri
    mixed_grad[...] = swapped(leaving[...])


def kernel_close(
    sides_grad, hat_after, scale_after, gate_after, grad_in, mask, vectors, w_after,
    table, right,
    pair_grad, table_grad, right_grad, g_after, g_gain, sides,
):
    take_pair(sides_grad, sides)
    zero_first(g_after, g_gain)

    @pl.when(pl.program_id(1) == 0)
    def _():
        right_grad[...] = jnp.zeros_like(right_grad)

    grad, grad_w, grad_gain = front_back(
        cat(grad_in), cat(hat_after).astype(WIDE), cat(scale_after), cat(sides), cat(gate_after),
        cat(mask), column(vectors[OUT_GAIN]), all_back(w_after),
    )
    g_after[...] += grad_w
    g_gain[...] += grad_gain
    low = grad.astype(LOW)
    rows = table.shape[0]
    width = low.shape[1] // rows
    for t in range(rows):
        own = low[:, t * width : (t + 1) * width]
        pair_grad[t] = own.T
        table_grad[0, t] = dot_nt(right[...], own)
        right_grad[...] += dot_nn(table[t], own)


CHANNELS = 4


def kernel_mix(incoming, left, right, out):
    parts, count, rows, length = out.shape
    for c in range(count):
        a = left[:, c].reshape(length, length)
        b = right[:, c].reshape(length, length)
        mixed = dot_tn(a, b) if incoming else dot_nt(a, b)
        out[:, c] = mixed.astype(LOW).reshape(parts, rows, length)


def kernel_mix_back(incoming, grad, left, right, out):
    parts, count, rows, length = grad.shape
    for c in range(count):
        g = grad[:, c].reshape(length, length)
        a = left[:, c].reshape(length, length)
        b = right[:, c].reshape(length, length)
        a_grad = dot_nt(b, g) if incoming else dot_nn(g, b)
        b_grad = dot_nn(a, g) if incoming else dot_tn(g, a)
        out[:, 0, c] = a_grad.astype(LOW).reshape(parts, rows, length)
        out[:, 1, c] = b_grad.astype(LOW).reshape(parts, rows, length)


def mix(sides, incoming):
    parts, double, rows, length = sides.shape
    share = double // 2
    count = min(CHANNELS, share)
    steps = share // count
    block = (parts, count, rows, length)
    return pl.pallas_call(
        lambda *refs: kernel_mix(incoming, *refs),
        grid=(steps,),
        in_specs=[
            pl.BlockSpec(block, lambda c: (0, c, 0, 0)),
            pl.BlockSpec(block, lambda c: (0, c + steps, 0, 0)),
        ],
        out_specs=pl.BlockSpec(block, lambda c: (0, c, 0, 0)),
        out_shape=jax.ShapeDtypeStruct((parts, share, rows, length), LOW),
        compiler_params=pltpu.CompilerParams(vmem_limit_bytes=VMEM_LIMIT),
        cost_estimate=pl.CostEstimate(
            flops=2 * share * length**3, bytes_accessed=3 * share * length * length * 2,
            transcendentals=0,
        ),
    )(sides, sides)


def mix_back(grad, sides, incoming):
    parts, double, rows, length = sides.shape
    share = double // 2
    count = min(CHANNELS, share)
    steps = share // count
    block = (parts, count, rows, length)
    out = pl.pallas_call(
        lambda *refs: kernel_mix_back(incoming, *refs),
        grid=(steps,),
        in_specs=[
            pl.BlockSpec(block, lambda c: (0, c, 0, 0)),
            pl.BlockSpec(block, lambda c: (0, c, 0, 0)),
            pl.BlockSpec(block, lambda c: (0, c + steps, 0, 0)),
        ],
        out_specs=pl.BlockSpec((parts, 2, count, rows, length), lambda c: (0, 0, c, 0, 0)),
        out_shape=jax.ShapeDtypeStruct((parts, 2, share, rows, length), LOW),
        compiler_params=pltpu.CompilerParams(vmem_limit_bytes=VMEM_LIMIT),
        cost_estimate=pl.CostEstimate(
            flops=4 * share * length**3, bytes_accessed=5 * share * length * length * 2,
            transcendentals=0,
        ),
    )(grad, sides, sides)
    return out.reshape(sides.shape)


def share_rows(share):
    return -(-(share + 2 * LANES) // (TILE * LANES)) * TILE


def whole(shape):
    return pl.BlockSpec(shape, lambda *_: (0,) * len(shape))


def one_call(body, scalars, in_arrays, outs, scratch=()):
    return pl.pallas_call(
        body,
        in_specs=[pl.BlockSpec(memory_space=pltpu.SMEM)] * len(scalars)
        + [whole(a.shape) for a in in_arrays],
        out_specs=[whole(shape) for shape, _ in outs],
        out_shape=[jax.ShapeDtypeStruct(shape, dtype) for shape, dtype in outs],
        scratch_shapes=list(scratch),
        grid=(1,),
        compiler_params=pltpu.CompilerParams(vmem_limit_bytes=VMEM_LIMIT),
    )(*scalars, *in_arrays)


def lane_in(shape, start, width):
    lane = lax.broadcasted_iota(jnp.int32, shape, 1)
    return (lane >= start) & (lane < start + width)


def rolled(value, shift):
    shift %= LANES
    return pltpu.roll(value, shift, 1) if shift else value


def share_order(layout):
    return [((d // layout.rows) % 2, d // (2 * layout.rows), d % layout.rows) for d in range(layout.devices)]


def unpack(layout, shares, share):
    at, _ = first_rows()
    height = shares.shape[3]
    first = [share * d // LANES for d in range(layout.devices)]
    order = share_order(layout)
    matrices = [
        (at.w_query, NODE_DIM, 3, 3 * HEADS_WIDTH),
        (at.w_attn_out, HEADS_WIDTH, 1, NODE_DIM),
        (at.w_node_up, NODE_DIM, 1, FFN_NODE),
        (at.w_node_down, FFN_NODE, 1, NODE_DIM),
        (at.w_outer, OUTER * OUTER, 1, PAIR_DIM),
        (at.outgoing.w_left, 3 * PAIR_DIM, 1, TRI_DIM),
        (at.outgoing.w_tri_out, TRI_DIM, 1, PAIR_DIM),
        (at.incoming.w_left, 3 * PAIR_DIM, 1, TRI_DIM),
        (at.incoming.w_tri_out, TRI_DIM, 1, PAIR_DIM),
        (at.w_pair_up, PAIR_DIM, 1, FFN_PAIR),
        (at.w_pair_down, FFN_PAIR, 1, PAIR_DIM),
    ]
    small = [(at.embed, 8), (at.gain_one, 2), (at.gain_two, 2), (at.gain_three, 2)]
    small += [
        (start, 1)
        for start in (
            at.outgoing.gain_in, at.outgoing.gain_tri, at.incoming.gain_in, at.incoming.gain_tri,
            at.gain_pair, at.bias_pair,
        )
    ]

    def body(shares_ref, vectors, bias_out, factors_out, *rest):
        outs, flat, narrow = rest[:-2], rest[-2], rest[-1]
        for d, place in enumerate(order):
            block = shares_ref[place].astype(WIDE)
            if d:
                tail = flat[first[d] : first[d] + 1]
                flat[first[d] : first[d] + height] = block
                flat[first[d] : first[d] + 1] = block[:1] + tail
            else:
                flat[:height] = block
        row = 0
        vectors[...] = jnp.zeros_like(vectors)
        for start, count in small:
            vectors[row : row + count] = flat[start : start + count]
            row += count
        for out, (place, rows, count, width) in zip(outs, matrices):
            pieces = width // count // LANES
            for m in range(count):
                for a in range(pieces):
                    start = place + m * rows * pieces + a
                    value = (
                        flat[pl.ds(start, rows, stride=pieces), :]
                        if pieces > 1
                        else flat[start : start + rows]
                    )
                    lane = (m * pieces + a) * LANES
                    out[:, lane : lane + LANES] = value.astype(LOW)
        per_row = LANES // HEADS
        shape = (HEADS, LANES)
        value = flat[at.w_bias : at.w_bias + HEADS]
        for a in range(per_row):
            kept = jnp.where(lane_in(shape, 0, HEADS), rolled(value, -HEADS * a), 0.0)
            narrow[pl.ds(a, HEADS, stride=per_row), :] = kept
        bias_out[...] = narrow[:PAIR_DIM].astype(LOW)
        per_row = LANES // OUTER
        count = NODE_DIM // per_row
        shape = (count, LANES)
        left, right = (flat[start : start + count] for start in (at.w_left_node, at.w_right_node))
        for a in range(per_row):
            kept = jnp.where(lane_in(shape, 0, OUTER), rolled(left, -OUTER * a), 0.0)
            kept += jnp.where(lane_in(shape, OUTER, OUTER), rolled(right, OUTER - OUTER * a), 0.0)
            narrow[pl.ds(a, count, stride=per_row), :] = kept
        factors_out[...] = narrow[...].astype(LOW)

    return one_call(
        body,
        (),
        (shares,),
        [((24, LANES), WIDE), ((PAIR_DIM, LANES), LOW), ((NODE_DIM, LANES), LOW)]
        + [((rows, width), LOW) for _, rows, _, width in matrices],
        [pltpu.VMEM((first[-1] + height + TILE, LANES), WIDE), pltpu.VMEM((NODE_DIM, LANES), WIDE)],
    )


def pack(layout, share, recycle, grads, node_parts):
    at, total = first_rows()
    height = share_rows(share)
    first = [share * d // LANES for d in range(layout.devices)]
    order = share_order(layout)
    many = len(grads)

    def body(recycle_ref, *refs):
        ins, rest = refs[:many], refs[many:]
        (
            arrived, query_low, start, normed_one, after_grad, vectors, w_projections,
            act_low, final_low, normed_two, hidden_grad, attended, after_low, g_factors,
            out, node_grad_out, flat, narrow,
        ) = rest

        def store(place, count, value):
            rows, pieces = value.shape[0], value.shape[1] // count // LANES
            for m in range(count):
                for a in range(pieces):
                    lane = (m * pieces + a) * LANES
                    begin = place + m * rows * pieces + a
                    part = value[:, lane : lane + LANES]
                    if pieces > 1 and rows > 1:
                        flat[pl.ds(begin, rows, stride=pieces), :] = part
                    else:
                        flat[begin : begin + rows] = part

        flat[total:] = jnp.zeros((flat.shape[0] - total, LANES), WIDE)
        for ref, (place, count, _) in zip(ins, grads):
            store(place, count, row_of(ref[...]) if ref.shape[1] == 1 else ref[...])
        store(at.w_node_down, 1, dot_tn(act_low[...], final_low[...]))
        store(at.w_node_up, 1, dot_tn(normed_two[...], hidden_grad[...]))
        store(at.w_attn_out, 1, dot_tn(attended[...], after_low[...]))
        per_row = LANES // OUTER
        count = NODE_DIM // per_row
        narrow[...] = g_factors[...]
        left = jnp.zeros((count, LANES), WIDE)
        right = left
        for a in range(per_row):
            piece = narrow[pl.ds(a, count, stride=per_row), :]
            inside = lane_in(piece.shape, OUTER * a, OUTER)
            left = jnp.where(inside, rolled(piece, OUTER * a), left)
            right = jnp.where(inside, rolled(piece, OUTER * a - OUTER), right)
        store(at.w_left_node, 1, left)
        store(at.w_right_node, 1, right)

        key_value = jnp.sum(arrived[...].astype(WIDE), axis=0).astype(LOW)
        projections = jnp.concatenate([query_low[...], key_value], axis=1)
        store(at.w_query, 3, dot_tn(normed_one[...], projections))
        hat, scale = row_norm(start[...])
        part, grad_gain = row_norm_back(
            dot_nt(projections, w_projections[...]), hat, scale, vector(vectors, GAIN_ONE)
        )
        node_grad = after_grad[...] + part
        node_grad_out[...] = node_grad.astype(LOW)
        store(at.gain_one, 1, grad_gain)
        flat[at.embed : at.embed + 2 * RECYCLES] = jnp.zeros((2 * RECYCLES, LANES), WIDE)
        column_sum = jnp.sum(node_grad, axis=0, keepdims=True)
        for a in range(NODE_DIM // LANES):
            place = at.embed + (NODE_DIM // LANES) * recycle_ref[0] + a
            flat[pl.ds(place, 1), :] = column_sum[:, a * LANES : (a + 1) * LANES]
        for d, where in enumerate(order):
            out[where] = flat[first[d] : first[d] + height].astype(LOW)

    shape = (2, layout.crops // 2, layout.rows, height, LANES)
    return one_call(
        body,
        (recycle,),
        tuple(array for _, _, array in grads) + tuple(node_parts),
        [(shape, LOW), (node_parts[2].shape, LOW)],
        [pltpu.VMEM((first[-1] + height + TILE, LANES), WIDE), pltpu.VMEM((NODE_DIM, LANES), WIDE)],
    )


def row_norm(x):
    centered = x - jnp.mean(x, axis=-1, keepdims=True)
    scale = lax.rsqrt(jnp.mean(centered * centered, axis=-1, keepdims=True) + EPS_NORM)
    return centered * scale, scale


def row_norm_back(grad, hat, scale, gain):
    grad_gain = jnp.sum(grad * hat, axis=0, keepdims=True)
    wide = grad * gain
    inner = jnp.mean(wide * hat, axis=-1, keepdims=True)
    return scale * (wide - jnp.mean(wide, axis=-1, keepdims=True) - hat * inner), grad_gain


def vector(ref, rows):
    return jnp.concatenate([ref[r : r + 1] for r in range(rows.start, rows.stop)], axis=1)


def by_head(value):
    return jnp.concatenate(
        [
            jnp.where(lane_in(value.shape, h * HEAD_DIM, HEAD_DIM), value, 0.0)
            for h in range(HEADS)
        ],
        axis=0,
    )


def head_sum(value):
    rows = value.shape[0] // HEADS
    parts = [value[h * rows : (h + 1) * rows] for h in range(HEADS)]
    return sum(
        jnp.where(lane_in(part.shape, h * HEAD_DIM, HEAD_DIM), part, 0.0)
        for h, part in enumerate(parts)
    )


SCORE_SCALE = HEAD_DIM ** (-0.5)
KEEP_LANE = 2 * OUTER


def node_forward(
    recycle, node_ref, all_ref, bias_ref, keep, keep_rows, vectors, w_projections, w_attn_out, w_up, w_down,
    w_factors,
    node_out, factors_out, start_out, normed_one, soft_out, heads_out, key_out, value_out,
    attended_out, after_out, act_out, slope_out, final_out, flat,
):
    pieces = NODE_DIM // LANES
    length = all_ref.shape[0] // pieces
    embed = jnp.concatenate(
        [vectors[pl.ds(pieces * recycle[0] + a, 1), :] for a in range(pieces)], axis=1
    )
    flat[...] = all_ref[...].astype(WIDE)
    all_rows = jnp.concatenate(
        [flat[pl.ds(a, length, stride=pieces), :] for a in range(pieces)], axis=1
    )
    gain = vector(vectors, GAIN_ONE)
    normed_all = (row_norm(all_rows + embed)[0] * gain).astype(LOW)
    start = node_ref[...].astype(WIDE) + embed
    normed = (row_norm(start)[0] * gain).astype(LOW)
    start_out[...] = start
    normed_one[...] = normed
    query = dot_nn(normed, w_projections[:, :HEADS_WIDTH]).astype(LOW).astype(WIDE)
    heads = by_head(query).astype(LOW)
    key_value = dot_nn(normed_all, w_projections[:, HEADS_WIDTH:]).astype(LOW)
    key, value = key_value[:, :HEADS_WIDTH], key_value[:, HEADS_WIDTH:]
    heads_out[...] = heads
    key_out[...] = key
    value_out[...] = value
    scores = dot_nt(heads, key) * SCORE_SCALE + bias_ref[...] + (keep[...] - 1.0) * MASK_FILL
    powers = jnp.exp(scores - jnp.max(scores, axis=-1, keepdims=True))
    soft = powers / jnp.sum(powers, axis=-1, keepdims=True)
    soft_out[...] = soft
    attended = head_sum(dot_nn(soft.astype(LOW), value)).astype(LOW)
    attended_out[...] = attended
    after = start + dot_nn(attended, w_attn_out[...])
    after_out[...] = after
    normed = (row_norm(after)[0] * vector(vectors, GAIN_TWO)).astype(LOW)
    act, slope = gelu_parts(dot_nn(normed, w_up[...]))
    act_out[...] = act.astype(LOW)
    slope_out[...] = slope
    final = after + dot_nn(act.astype(LOW), w_down[...])
    final_out[...] = final
    node_out[...] = final.astype(LOW)
    normed = (row_norm(final)[0] * vector(vectors, GAIN_THREE)).astype(LOW)
    factors = dot_nn(normed, w_factors[...])
    factors = jnp.where(lane_in(factors.shape, KEEP_LANE, 1), keep_rows[...], factors).astype(LOW)
    factors_out[...] = jnp.broadcast_to(factors[None], factors_out.shape)


def node_backward(
    sources, factor_ref, cot, vectors, soft_ref, heads, key, value, after_ref, slope, final_ref,
    w_attn_out, w_up, w_down, w_factors,
    key_value_out, query_out, score_out, after_grad_out, final_low_out, normed_two_out,
    hidden_out, after_low_out, g_factors, g_two, g_three,
):
    ranks = key_value_out.shape[0]
    left = factor_ref[sources[0]].astype(WIDE)
    right = sum(factor_ref[sources[1 + r]].astype(WIDE) for r in range(ranks))
    rows = jnp.where(lane_in(left.shape, 0, OUTER), left, right).astype(LOW)
    hat, scale = row_norm(final_ref[...])
    gain = vector(vectors, GAIN_THREE)
    g_factors[...] = dot_tn((hat * gain).astype(LOW), rows)
    part, g_three[...] = row_norm_back(dot_nt(rows, w_factors[...]), hat, scale, gain)
    final_grad = cot[...].astype(WIDE) + part
    final_low = final_grad.astype(LOW)
    final_low_out[...] = final_low
    hidden_grad = (dot_nt(final_low, w_down[...]) * slope[...]).astype(LOW)
    hidden_out[...] = hidden_grad
    hat, scale = row_norm(after_ref[...])
    gain = vector(vectors, GAIN_TWO)
    normed_two_out[...] = (hat * gain).astype(LOW)
    part, g_two[...] = row_norm_back(dot_nt(hidden_grad, w_up[...]), hat, scale, gain)
    after_grad = final_grad + part
    after_grad_out[...] = after_grad
    after_low = after_grad.astype(LOW)
    after_low_out[...] = after_low
    attended_grad = dot_nt(after_low, w_attn_out[...]).astype(LOW).astype(WIDE)
    grad_heads = by_head(attended_grad).astype(LOW)
    soft = soft_ref[...]
    soft_grad = dot_nt(grad_heads, value[...])
    score_grad = soft * (soft_grad - jnp.sum(soft_grad * soft, axis=-1, keepdims=True))
    score_low = score_grad.astype(LOW)
    score_out[...] = score_low
    key_part = (dot_tn(score_low, heads[...]) * SCORE_SCALE).astype(LOW)
    value_part = dot_tn(soft.astype(LOW), grad_heads).astype(LOW)
    local_rows = cot.shape[0]
    for r in range(ranks):
        span = slice(r * local_rows, (r + 1) * local_rows)
        key_value_out[r, :, :HEADS_WIDTH] = key_part[span]
        key_value_out[r, :, HEADS_WIDTH:] = value_part[span]
    query_out[...] = (head_sum(dot_nn(score_low, key[...])) * SCORE_SCALE).astype(LOW)


def outer_tables(
    sources, factors, w_outer, table_out, right_out, left_out, mask_out, w_wide, steps
):
    local_rows = left_out.shape[0]
    ranks = right_out.shape[1] // local_rows
    left_low = factors[sources[0]][:, :OUTER]
    left_out[...] = left_low
    right = jnp.concatenate([factors[sources[1 + r]].astype(WIDE) for r in range(ranks)], axis=0)
    turned = right.T
    right_out[...] = turned[OUTER : 2 * OUTER].astype(LOW)
    own_keep = factors[sources[0]][:, KEEP_LANE : KEEP_LANE + 1].astype(WIDE)
    mask_out[:, 0, :] = own_keep * turned[KEEP_LANE : KEEP_LANE + 1]
    w_wide[...] = w_outer[...].astype(WIDE)
    for q in range(OUTER):
        w_q = w_wide[pl.ds(q, OUTER, stride=OUTER), :].astype(LOW)
        steps[q] = dot_nn(left_low, w_q)
    table_out[...] = jnp.swapaxes(steps[...], 0, 1).astype(LOW)


def outer_backward(table_grad, right_grad, left, w_outer, factors_out, g_outer, w_wide, steps):
    crops, ranks, local_rows, _ = factors_out.shape
    steps[...] = jnp.swapaxes(jnp.sum(table_grad[...], axis=0), 0, 1)
    w_wide[...] = w_outer[...].astype(WIDE)
    left_grad = jnp.zeros((local_rows, OUTER), WIDE)
    for q in range(OUTER):
        grad_q = steps[q].astype(LOW)
        w_q = w_wide[pl.ds(q, OUTER, stride=OUTER), :].astype(LOW)
        left_grad = left_grad + dot_nt(grad_q, w_q)
        g_outer[pl.ds(q, OUTER, stride=OUTER), :] = dot_tn(left[...], grad_q)
    right_rows = right_grad[...].T
    for r in range(ranks):
        block = jnp.concatenate(
            [
                left_grad,
                right_rows[r * local_rows : (r + 1) * local_rows],
                jnp.zeros((local_rows, LANES - 2 * OUTER), WIDE),
            ],
            axis=1,
        ).astype(LOW)
        for c in range(crops):
            factors_out[c, r] = block


def low_of(x):
    return x.astype(LOW)


def local(layout, node, pair, recycle, mask, node_cot, pair_cot, master, first, second):
    crops, ranks = layout.crops, layout.rows
    devices = crops * ranks
    local_rows, length = node.shape[1], pair.shape[2]
    share = TRI_DIM // ranks
    node, pair, node_cot, pair_cot = node[0], pair[0], node_cot[0], pair_cot[0]

    crop_at, row_at = lax.axis_index("crop"), lax.axis_index("row")
    here = crop_at * ranks + row_at
    partner = layout.work_place(here)
    stays = partner == here
    work_crop, work_row = partner // ranks, partner % ranks
    moved = lambda array: jnp.where(stays, array, lax.ppermute(array, BOTH, layout.moves))

    at, _ = first_rows()

    amount = master.shape[0]
    height = share_rows(amount)
    offset = (here * (amount % LANES)) % LANES
    shard = lax.dynamic_update_slice(jnp.zeros(height * LANES, LOW), low_of(master), (offset,))
    node_rows = local_rows * NODE_DIM // LANES
    shards = jnp.concatenate([shard.reshape(height, LANES), node.reshape(-1, LANES)], axis=0)
    shards = spread(shards, ranks, "row").reshape(ranks, -1, LANES)
    shards, pair = lax.optimization_barrier((shards, pair))
    node_all = shards[:, height:].reshape(-1, LANES)
    shards = shards[:, :height].reshape(-1, LANES)
    shards = spread(shards, crops // 2, BOTH, layout.chips)
    shards = spread(shards, 2, BOTH, layout.cores)
    shards = shards.reshape(2, crops // 2, ranks, height, LANES)
    (
        vectors, w_bias, w_factors, w_projections, w_attn_out, w_node_up, w_node_down, w_outer,
        w_out_all, w_out_end, w_in_all, w_in_end, w_pair_up, w_pair_down,
    ) = unpack(layout, shards, amount)
    pair_plane = moved(pair)
    keep = mask.astype(WIDE)
    keep_rows = lax.dynamic_slice_in_dim(keep[0], row_at * local_rows, local_rows, 0)[:, None]

    pair_bias = jnp.einsum("ijd,dh->hij", pair, w_bias[:, :HEADS], preferred_element_type=WIDE)
    rows_low = lambda width: ((local_rows, width), LOW)
    rows_wide = lambda width: ((local_rows, width), WIDE)
    by_heads = (HEADS * local_rows, length)
    (
        node_out, factors, start, normed_one, soft, heads, key, value, attended, after, act_low,
        slope, node_final,
    ) = one_call(
        node_forward,
        (recycle,),
        (node, node_all, pair_bias.reshape(by_heads), keep, keep_rows, vectors, w_projections, w_attn_out,
         w_node_up, w_node_down, w_factors),
        [rows_low(NODE_DIM), ((devices, local_rows, LANES), LOW), rows_wide(NODE_DIM),
         rows_low(NODE_DIM), (by_heads, WIDE), (by_heads[:1] + (HEADS_WIDTH,), LOW),
         ((length, HEADS_WIDTH), LOW), ((length, HEADS_WIDTH), LOW), rows_low(HEADS_WIDTH),
         rows_wide(NODE_DIM), rows_low(FFN_NODE), rows_wide(FFN_NODE), rows_wide(NODE_DIM)],
        [pltpu.VMEM(node_all.shape, WIDE)],
    )

    factors = exchange(factors, BOTH)
    factors, pair_cot = lax.optimization_barrier((factors, pair_cot))
    everyone = jnp.arange(ranks, dtype=jnp.int32)
    sources = jnp.concatenate([partner[None], work_crop * ranks + everyone]).astype(jnp.int32)
    table, right, left, mask_plane = one_call(
        outer_tables,
        (sources,),
        (factors, w_outer),
        [((local_rows, OUTER, PAIR_DIM), LOW), ((OUTER, length), LOW), ((local_rows, OUTER), LOW),
         ((local_rows, 1, length), WIDE)],
        [pltpu.VMEM((OUTER * OUTER, PAIR_DIM), WIDE), pltpu.VMEM((OUTER, local_rows, PAIR_DIM), WIDE)],
    )

    step = (min(TILE, local_rows), min(LANES, length))
    extent = (local_rows, length)
    pieces = length // step[1]
    state = (local_rows, TRI_DIM, length)
    line = (local_rows, 1, length)
    sides_shape = (ranks, 2 * share, local_rows, length)
    mixed_shape = (TRI_DIM, local_rows, length)
    natural = (local_rows, length, PAIR_DIM)
    buffer = lambda channels: pltpu.VMEM((step[0], channels, step[1]), LOW)
    trade = lambda blocks: exchange(blocks, BOTH, layout.groups)
    merge = lambda blocks: blocks.reshape(mixed_shape)
    split = lambda blocks: blocks.reshape(ranks, share, local_rows, length)
    unit = 2 * local_rows * length * PAIR_DIM * PAIR_DIM
    front_outs = (
        ("r", state, WIDE), ("r", state, LOW), ("r", line, WIDE), ("r", state, LOW),
        ("s", sides_shape, LOW),
    )
    square = (TRI_DIM, PAIR_DIM)
    gain_shape = (PAIR_DIM, 1)
    after_shape = (PAIR_DIM, 2 * TRI_DIM + PAIR_DIM)

    x_one, hat_tri_out, scale_tri_out, gate_tri_out, sides = run(
        kernel_open, step, extent,
        (pair_plane, table, right, mask_plane, vectors, w_out_all),
        "ntcrww", front_outs, [buffer(2 * TRI_DIM)], 4 * unit,
    )
    sides_out, cot_plane = lax.optimization_barrier((trade(sides), moved(pair_cot)))
    mixed_out = merge(trade(mix(sides_out, False)))
    x_two, hat_tri_in, scale_tri_in, gate_tri_in, sides = run(
        kernel_middle, step, extent,
        (mixed_out, x_one, gate_tri_out, mask_plane, vectors, w_out_end, w_in_all), "srrrwww", front_outs, [buffer(TRI_DIM), buffer(2 * TRI_DIM)], 5 * unit,
    )
    sides_in = trade(sides)
    mixed_in = merge(trade(mix(sides_in, True)))
    pair_final, x_grad, gate_grad, mixed_grad, g_in_out, g_in_tri, g_up, g_down, g_pair, g_bias = run(
        kernel_turn, step, extent,
        (mixed_in, x_two, gate_tri_in, cot_plane, vectors, w_in_end, w_pair_up, w_pair_down),
        "srrnwwww",
        (("n", natural, LOW), ("r", state, WIDE), ("r", state, LOW), ("s", mixed_shape, LOW),
         ("w", square, WIDE), ("w", gain_shape, WIDE), ("w", (PAIR_DIM, FFN_PAIR), WIDE),
         ("w", (FFN_PAIR, PAIR_DIM), WIDE), ("w", gain_shape, WIDE), ("w", gain_shape, WIDE)),
        [buffer(TRI_DIM), buffer(TRI_DIM)], 32 * unit,
    )
    sides_grad = trade(mix_back(trade(split(mixed_grad)), sides_in, True))
    sides_grad, pair_out = lax.optimization_barrier((sides_grad, moved(pair_final)))
    x_grad, gate_grad, mixed_grad, g_in_all, g_in_gain, g_out_out, g_out_tri = run(
        kernel_return, step, extent,
        (sides_grad, hat_tri_in, scale_tri_in, gate_grad, x_grad, mask_plane,
         vectors, w_in_all, mixed_out, gate_tri_out, w_out_end),
        "srrrrrwwsrw",
        (("r", state, WIDE), ("r", state, LOW), ("s", mixed_shape, LOW), ("w", after_shape, WIDE),
         ("w", gain_shape, WIDE), ("w", square, WIDE), ("w", gain_shape, WIDE)),
        [buffer(2 * TRI_DIM), buffer(TRI_DIM), buffer(TRI_DIM)], 12 * unit,
    )
    sides_grad = trade(mix_back(trade(split(mixed_grad)), sides_out, False))
    pair_one_grad, table_grad, right_part, g_out_all, g_out_gain = run(
        kernel_close, step, extent,
        (sides_grad, hat_tri_out, scale_tri_out, gate_grad, x_grad, mask_plane,
         vectors, w_out_all, table, right),
        "srrrrrwwtc",
        (("n", natural, LOW), ("p", (pieces, local_rows, OUTER, PAIR_DIM), WIDE),
         ("c", (OUTER, length), WIDE), ("w", after_shape, WIDE), ("w", gain_shape, WIDE)),
        [buffer(2 * TRI_DIM)], 8 * unit,
    )

    factor_grads, g_outer = one_call(
        outer_backward,
        (),
        (table_grad, right_part, left, w_outer),
        [((crops, ranks, local_rows, LANES), LOW), ((OUTER * OUTER, PAIR_DIM), WIDE)],
        [pltpu.VMEM((OUTER * OUTER, PAIR_DIM), WIDE), pltpu.VMEM((OUTER, local_rows, PAIR_DIM), WIDE)],
    )
    factor_grads = exchange(factor_grads.reshape(devices, local_rows, LANES), BOTH)

    workers = layout.work_place(crop_at * ranks + everyone)
    sources = jnp.concatenate([partner[None], workers]).astype(jnp.int32)
    (
        key_value, query_low, score_low, after_grad, final_low, normed_two, hidden_grad, after_low,
        g_factors, g_two, g_three,
    ) = one_call(
        node_backward,
        (sources,),
        (factor_grads, node_cot, vectors, soft, heads, key, value, after, slope, node_final,
         w_attn_out, w_node_up, w_node_down, w_factors),
        [((ranks, local_rows, 2 * HEADS_WIDTH), LOW), rows_low(HEADS_WIDTH), (by_heads, LOW),
         rows_wide(NODE_DIM), rows_low(NODE_DIM), rows_low(NODE_DIM), rows_low(FFN_NODE),
         rows_low(NODE_DIM), ((NODE_DIM, LANES), WIDE), ((1, NODE_DIM), WIDE), ((1, NODE_DIM), WIDE)],
    )
    key_value = exchange(key_value, "row")
    key_value, pair_one_grad = lax.optimization_barrier((key_value, pair_one_grad))
    pair_one_home = moved(pair_one_grad)
    score_low = score_low.reshape(HEADS, local_rows, length)
    g_bias_head = jnp.einsum("ijd,hij->dh", pair, score_low, preferred_element_type=WIDE)
    grads = [
        (at.w_bias, 1, lax.optimization_barrier(g_bias_head).reshape(-1, LANES)),
        (at.gain_two, 1, g_two),
        (at.gain_three, 1, g_three),
        (at.w_outer, 1, g_outer),
        (at.gain_pair, 1, g_pair),
        (at.w_pair_up, 1, g_up),
        (at.w_pair_down, 1, g_down),
        (at.bias_pair, 1, g_bias),
    ]
    for tri, g_all, g_gain, g_tri, g_out in (
        (at.outgoing, g_out_all, g_out_gain, g_out_tri, g_out_out),
        (at.incoming, g_in_all, g_in_gain, g_in_tri, g_in_out),
    ):
        grads += [
            (tri.gain_in, 1, g_gain),
            (tri.w_left, 3, g_all),
            (tri.gain_tri, 1, g_tri),
            (tri.w_tri_out, 1, g_out),
        ]

    blocks, node_grad = pack(
        layout, amount, recycle, grads,
        (key_value, query_low, start, normed_one, after_grad, vectors, w_projections, act_low,
         final_low, normed_two, hidden_grad, attended, after_low, g_factors),
    )
    total = lambda got: low_of(jnp.sum(got.astype(WIDE), axis=0))
    blocks = total(exchange(blocks, BOTH, layout.cores))
    blocks = total(exchange(blocks, BOTH, layout.chips))
    blocks = jnp.sum(exchange(blocks, "row").astype(WIDE), axis=0)
    blocks, pair_one_home = lax.optimization_barrier((blocks, pair_one_home))
    grad_own = lax.dynamic_slice(blocks.reshape(-1), (offset,), (amount,))
    pair_grad = pair_one_home.astype(WIDE) + jnp.einsum(
        "hij,dh->ijd", score_low, w_bias[:, :HEADS], preferred_element_type=WIDE
    )
    square_own = jnp.broadcast_to(jnp.sum(grad_own * grad_own), (1, LANES))
    last = jnp.concatenate([g_bias.reshape(1, LANES), square_own], axis=0)
    last = jnp.sum(spread(last, devices, BOTH).reshape(devices, 2, LANES), axis=0)
    bias_total = last[0]
    grad_norm = jnp.sqrt(last[1, 0])
    clipped = grad_own * (CLIP_NORM / jnp.maximum(grad_norm, CLIP_NORM))
    new_first = BETA_ONE * first + (1.0 - BETA_ONE) * clipped
    new_second = BETA_TWO * second + (1.0 - BETA_TWO) * clipped * clipped
    first_hat = new_first / (1.0 - BETA_ONE**ADAM_STEP)
    second_hat = new_second / (1.0 - BETA_TWO**ADAM_STEP)
    new_master = master - LEARN_RATE * (
        first_hat / (jnp.sqrt(second_hat) + ADAM_EPS) + WEIGHT_DECAY * master
    )
    return (
        node_out[None],
        pair_out[None],
        node_grad[None],
        low_of(pair_grad)[None],
        grad_own,
        bias_total,
        grad_norm,
        new_master,
        new_first,
        new_second,
        low_of(new_master),
    )


def solution(mesh):
    layout = Layout(mesh.shape["crop"], mesh.shape["row"])
    return jax.shard_map(
        lambda *arrays: local(layout, *arrays),
        mesh=mesh,
        in_specs=(
            P("crop", "row", None),
            P("crop", "row", None, None),
            P("crop"),
            P("crop", None),
            P("crop", "row", None),
            P("crop", "row", None, None),
            P(("crop", "row")),
            P(("crop", "row")),
            P(("crop", "row")),
        ),
        out_specs=(
            P("crop", "row", None),
            P("crop", "row", None, None),
            P("crop", "row", None),
            P("crop", "row", None, None),
            P(("crop", "row")),
            P(),
            P(),
            P(("crop", "row")),
            P(("crop", "row")),
            P(("crop", "row")),
            P(("crop", "row")),
        ),
        check_vma=False,
    )
```

time: 841 us -> 688 us (0.82)
  waiting for transfers between devices: 249 us -> 142 us
  blocking collectives: 266 us -> 351 us
  local copies, waits for them, and re-layouts: 48 us -> 11 us
  Pallas kernels: 150 us -> 119 us
  starting transfers between devices: 59 us -> 31.7 us
  matrix products: 31.4 us -> 5.6 us
  other arithmetic: 30.1 us -> 21.2 us
    all_to_all x12 -> x7, waiting for transfers between devices: 249 us -> 142 us  [exchange(): lax.all_to_all(blocks, axes, 0, 0, axis_index_groups=groups, tiled=True)]
    all_to_all x8 -> x11, blocking collectives: 266 us -> 351 us  [exchange(): lax.all_to_all(blocks, axes, 0, 0, axis_index_groups=groups, tiled=True)]
    pallas_call x7 -> x11, Pallas kernels: 128 us -> 97.9 us  [the longest x5 76.8 us: run(): pl.pallas_call(body, grid=(extent[1] // step[1], extent[0] // step[0]), i...]
    dot_general x28 -> x2, matrix products: 31 us -> 4.3 us  [the longest x1 2.88 us: local(): jnp.einsum('hij,dh->ijd', score_low, w_bias[:, :HEADS], preferred_element...]
    all_to_all x12 -> x7, starting transfers between devices: 51.4 us -> 26.1 us  [exchange(): lax.all_to_all(blocks, axes, 0, 0, axis_index_groups=groups, tiled=True)]
    slice x14 -> x3, local copies, waits for them, and re-layouts: 13.9 us -> 2.13 us  [the longest x1 1.57 us: local(): node_all = shards[:, height:].reshape(-1, LANES)]
  transfers between devices with their start and end apart: 17 -> 11, of which waited for: 12 -> 7; matrix products, arithmetic and copies ran while one was open for 11% -> 4% of each run, Pallas kernels for 1% -> 2%
where the time goes in v2:
time: 688 us; the launch traced here: 685 us
  blocking collectives  351 us (51%)
  waiting for transfers between devices  142 us (21%)
  Pallas kernels  119 us (17%)
  starting transfers between devices  31.7 us (5%)
  other arithmetic  21.2 us (3%)
  local copies, waits for them, and re-layouts  11 us (2%)
    all_to_all x11, blocking collectives, exchange(): lax.all_to_all(blocks, axes, 0, 0, axis_index_groups=groups, tiled=True)  351 us
    all_to_all x7, waiting for transfers between devices, exchange(): lax.all_to_all(blocks, axes, 0, 0, axis_index_groups=groups, tiled=True)  142 us
    pallas_call x5, Pallas kernels, run(): pl.pallas_call(body, grid=(extent[1] // step[1], extent[0] // step[0]), i...  76.8 us
    all_to_all x7, starting transfers between devices, exchange(): lax.all_to_all(blocks, axes, 0, 0, axis_index_groups=groups, tiled=True)  26.1 us
    pallas_call x6, Pallas kernels, one_call(): pl.pallas_call(body, in_specs=[pl.BlockSpec(memory_space=pltpu.SMEM)] * l...  21.1 us
  transfers between devices with their start and end apart: 11, of which 7 were waited for; matrix products, arithmetic and copies ran while one was open for 4% of the time, Pallas kernels for 2%

profile of v2, /device:TPU:0, one launch (start us, length us, event | category | flops | bytes accessed | tf_op | source)
XLA Modules:
  0.0 685.3 jit_solution(9764872750189030037)
XLA Ops:
  0.7 0.9 reshape_squeeze.3
  1.5 0.9 convert_element_type.22
  2.5 0.8 dynamic_update_slice.3
  3.5 26.5 %all_to_all.90 = bf16[8,368,128]{2,1,0:T(8,128)(2,1)S(1)} all-to-all(bf16[8,368,128]{2,1,0:T(8,128)(2,1)S(1)} %broadcast_in_dim.49), channel_id=1, replica_groups=mesh['crop'=4,'row'=8] {'row'}, dimensions={0} | all-to-all | bytes 1507328 | tf_op jit(solution)/shard_map/all_to_all | solution.py:144
  30.0 2.0 collective-permute-start
  32.0 1.1 broadcast_in_dim.51
  33.2 3.6 all-to-all-start.1
  38.2 1.6 slice.16
  39.8 13.9 %all-to-all-done.1 = bf16[2,2432,128]{2,1,0:T(8,128)(2,1)S(1)} async-done(((bf16[2,2432,128]{2,1,0:T(8,128)(2,1)}), bf16[2,2432,128]{2,1,0:T(8,128)(2,1)S(1)}, u32[]{:S(2)}, u32[]{:S(2)}) %all-to-all-start.1) | async-done | bytes 1245216 | tf_op jit(solution)/shard_map/all_to_all | solution.py:144
  54.0 6.7 all_to_all.91
  60.7 3.5 shard_map.176
  64.1 1.4 fusion.6
  65.5 0.8 copy.42
  66.4 4.2 shard_map.177
  70.5 2.6 all-to-all-start.3
  73.9 11.4 %all-to-all-done.3.factors = bf16[32,32,128]{2,1,0:T(8,128)(2,1)S(1)} async-done(((bf16[32,32,128]{2,1,0:T(8,128)(2,1)}), bf16[32,32,128]{2,1,0:T(8,128)(2,1)S(1)}, u32[]{:S(2)}, u32[]{:S(2)}) %all-to-all-start.3) | async-done | bytes 262176 | tf_op jit(solution)/shard_map/all_to_all | solution.py:144
  85.2 0.7 copy-done.2
  85.9 2.2 shard_map.178
  88.1 1.5 broadcast_select_fusion.3.pair
  89.7 8.9 %shard_map.179 = (f32[32,128,256]{2,1,0:T(8,128)}, bf16[32,128,256]{2,1,0:T(8,128)(2,1)}, f32[32,1,256]{2,1,0:T(1,128)}, bf16[32,128,256]{2,1,0:T(8,128)(2,1)}, bf16[8,32,32,256]{3,2,1,0:T(8,128)(2,1)}) custom-call(bf16[32,256,128]{2,1,0:T(8,128)(2,1)} %broadcast_select_fusion.3.pair, bf16[32,32,128]{2,1,0:T(8,128)(2,1)} %get-tuple-element.114.table, ...), custom_call_target="tpu_custom_call" | custom-call | flops 1073741824 | bytes 2519040 | tf_op jit(solution)/shard_map/pallas_call | solution.py:292
  98.6 4.8 all-to-all-start.4
  103.3 0.8 collective-permute-start.1
  104.1 3.1 broadcast_select_fusion.2.cot
  107.3 44.9 %all-to-all-done.4.refs_0_.refs_1_.refs_2_ = bf16[8,32,32,256]{3,2,1,0:T(8,128)(2,1)} async-done(((bf16[8,32,32,256]{3,2,1,0:T(8,128)(2,1)}), bf16[8,32,32,256]{3,2,1,0:T(8,128)(2,1)}, u32[]{:S(2)}, u32[]{:S(2)}) %all-to-all-start.4) | async-done | bytes 4194336 | tf_op jit(solution)/shard_map/all_to_all | solution.py:144
  152.1 4.7 shard_map.180
  156.9 54.0 %all_to_all.92 = bf16[8,16,32,256]{3,2,1,0:T(8,128)(2,1)} all-to-all(bf16[8,16,32,256]{3,2,1,0:T(8,128)(2,1)} %shard_map.180), channel_id=1, replica_groups={{0,1,2,3,10,11,8,9},{6,7,4,5,12,13,14,15},{16,17,18,19,26,27,24,25},{22..., dimensions={0} | all-to-all | bytes 4194304 | tf_op jit(solution)/shard_map/all_to_all | solution.py:144
  210.9 11.0 %shard_map.181 = (f32[32,128,256]{2,1,0:T(8,128)}, bf16[32,128,256]{2,1,0:T(8,128)(2,1)}, f32[32,1,256]{2,1,0:T(1,128)}, bf16[32,128,256]{2,1,0:T(8,128)(2,1)}, bf16[8,32,32,256]{3,2,1,0:T(8,128)(2,1)}) custom-call(bf16[128,32,256]{2,1,0:T(8,128)(2,1)} %bitcast.40, f32[32,128,256]{2,1,0:T(8,128)} %get-tuple-element.121.x_in, ...), custom_call_target="tpu_custom_call" | custom-call | flops 1342177280 | bytes 8564736 | tf_op jit(solution)/shard_map/pallas_call | solution.py:292
  221.9 53.2 %all_to_all.93.refs_0_.refs_1_.refs_2_ = bf16[8,32,32,256]{3,2,1,0:T(8,128)(2,1)} all-to-all(bf16[8,32,32,256]{3,2,1,0:T(8,128)(2,1)} %get-tuple-element.125), channel_id=1, replica_groups={{0,1,2,3,10,11,8,9},{6,7,4,5,12,13,14,15},{16,17,18,19,26,27,24,25},{22..., dimensions={0} | all-to-all | bytes 8388608 | tf_op jit(solution)/shard_map/all_to_all | solution.py:144
  275.1 4.8 shard_map.182
  279.9 30.6 %all_to_all.94 = bf16[8,16,32,256]{3,2,1,0:T(8,128)(2,1)} all-to-all(bf16[8,16,32,256]{3,2,1,0:T(8,128)(2,1)} %shard_map.182), channel_id=1, replica_groups={{0,1,2,3,10,11,8,9},{6,7,4,5,12,13,14,15},{16,17,18,19,26,27,24,25},{22..., dimensions={0} | all-to-all | bytes 4194304 | tf_op jit(solution)/shard_map/all_to_all | solution.py:144
  310.5 31.4 %shard_map.183 = (bf16[32,256,128]{2,1,0:T(8,128)(2,1)}, f32[32,128,256]{2,1,0:T(8,128)}, bf16[32,128,256]{2,1,0:T(8,128)(2,1)}, bf16[128,32,256]{2,1,0:T(8,128)...) custom-call(bf16[128,32,256]{2,1,0:T(8,128)(2,1)} %bitcast.53, ...), custom_call_target="tpu_custom_call" | custom-call | flops 8589934592 | bytes 10792960 | tf_op jit(solution)/shard_map/pallas_call | solution.py:292
  341.9 30.6 %all_to_all.95.refs_0_ = bf16[8,16,32,256]{3,2,1,0:T(8,128)(2,1)} all-to-all(bf16[8,16,32,256]{3,2,1,0:T(8,128)(2,1)} %bitcast.54), channel_id=1, replica_groups={{0,1,2,3,10,11,8,9},{6,7,4,5,12,13,14,15},{16,17,18,19,26,27,24,25},{22..., dimensions={0} | all-to-all | bytes 4194304 | tf_op jit(solution)/shard_map/all_to_all | solution.py:144
  372.5 5.9 shard_map.184
  378.5 4.6 all-to-all-start.9
  383.1 0.8 collective-permute-start.2
  383.9 3.1 broadcast_select_fusion.1
  387.0 43.8 %all-to-all-done.9.sides_grad = bf16[8,32,32,256]{3,2,1,0:T(8,128)(2,1)} async-done(((bf16[8,32,32,256]{3,2,1,0:T(8,128)(2,1)}), bf16[8,32,32,256]{3,2,1,0:T(8,128)(2,1)}, u32[]{:S(2)}, u32[]{:S(2)}) %all-to-all-start.9) | async-done | bytes 4194336 | tf_op jit(solution)/shard_map/all_to_all | solution.py:144
  430.8 14.7 %shard_map.185 = (f32[32,128,256]{2,1,0:T(8,128)}, bf16[32,128,256]{2,1,0:T(8,128)(2,1)}, bf16[128,32,256]{2,1,0:T(8,128)(2,1)}, f32[128,384]{1,0:T(8,128)}, f32...) custom-call(bf16[8,32,32,256]{3,2,1,0:T(8,128)(2,1)} %all-to-all-done.9.sides_grad, ...), custom_call_target="tpu_custom_call" | custom-call | flops 3221225472 | bytes 16986112 | tf_op jit(solution)/shard_map/pallas_call | solution.py:292
  445.6 53.9 %all_to_all.96.refs_0_ = bf16[8,16,32,256]{3,2,1,0:T(8,128)(2,1)} all-to-all(bf16[8,16,32,256]{3,2,1,0:T(8,128)(2,1)} %bitcast.55), channel_id=1, replica_groups={{0,1,2,3,10,11,8,9},{6,7,4,5,12,13,14,15},{16,17,18,19,26,27,24,25},{22..., dimensions={0} | all-to-all | bytes 4194304 | tf_op jit(solution)/shard_map/all_to_all | solution.py:144
  499.5 5.9 shard_map.186
  505.4 53.2 %all_to_all.97.sides_grad = bf16[8,32,32,256]{3,2,1,0:T(8,128)(2,1)} all-to-all(bf16[8,32,32,256]{3,2,1,0:T(8,128)(2,1)} %bitcast.47), channel_id=1, replica_groups={{0,1,2,3,10,11,8,9},{6,7,4,5,12,13,14,15},{16,17,18,19,26,27,24,25},{22..., dimensions={0} | all-to-all | bytes 8388608 | tf_op jit(solution)/shard_map/all_to_all | solution.py:144
  558.6 10.8 %shard_map.187 = (bf16[32,256,128]{2,1,0:T(8,128)(2,1)}, f32[2,32,32,128]{3,2,1,0:T(8,128)}, f32[32,256]{1,0:T(8,128)}, f32[128,384]{1,0:T(8,128)}, f32[128,1]{1,0:T(8,128)}) custom-call(bf16[8,32,32,256]{3,2,1,0:T(8,128)(2,1)} %all_to_all.97.sides_grad, bf16[32,128,256]{2,1,0:T(8,128)(2,1)} %get-tuple-element.141.hat_after, ...), custom_call_target="tpu_custom_call" | custom-call | flops 2147483648 | bytes 13037568 | tf_op jit(solution)/shard_map/pallas_call | solution.py:292
  569.3 3.1 shard_map.188
  572.4 4.0 all-to-all-start.12
  577.1 10.0 %all-to-all-done.12.factor_ref = bf16[32,32,128]{2,1,0:T(8,128)(2,1)S(1)} async-done(((bf16[32,32,128]{2,1,0:T(8,128)(2,1)}), bf16[32,32,128]{2,1,0:T(8,128)(2,1)S(1)}, u32[]{:S(2)}, u32[]{:S(2)}) %all-to-all-start.12) | async-done | bytes 262176 | tf_op jit(solution)/shard_map/all_to_all | solution.py:144
  587.1 0.7 copy-done.3
  587.8 3.9 shard_map.189
  591.7 13.2 %all_to_all.98.refs_16_ = bf16[8,32,512]{2,1,0:T(8,128)(2,1)} all-to-all(bf16[8,32,512]{2,1,0:T(8,128)(2,1)} %get-tuple-element.172), channel_id=1, replica_groups=mesh['crop'=4,'row'=8] {'row'}, dimensions={0} | all-to-all | bytes 524288 | tf_op jit(solution)/shard_map/all_to_all | solution.py:144
  604.9 2.0 collective-permute-start.3
  606.9 1.3 convolution_bitcast_fusion
  609.0 4.3 shard_map.190
  613.3 9.9 %all_to_all.99 = bf16[2,2,8,304,128]{4,3,2,1,0:T(8,128)(2,1)} all-to-all(bf16[2,2,8,304,128]{4,3,2,1,0:T(8,128)(2,1)} %get-tuple-element.187), channel_id=1, replica_groups={{0,8},{1,9},{2,10},{3,11},{4,12},{5,13},{6,14},{7,15},{16,24},{17,25},{..., dimensions={0} | all-to-all | bytes 4980736 | tf_op jit(solution)/shard_map/all_to_all | solution.py:144
  623.2 2.2 reduce_sum.51
  625.4 18.8 %all_to_all.100 = bf16[2,8,304,128]{3,2,1,0:T(8,128)(2,1)S(1)} all-to-all(bf16[2,8,304,128]{3,2,1,0:T(8,128)(2,1)S(1)} %reduce_sum.51), channel_id=1, replica_groups={{0,16},{1,17},{2,18},{3,19},{4,20},{5,21},{6,22},{7,23},{8,24},{9,25},{..., dimensions={0} | all-to-all | bytes 2490368 | tf_op jit(solution)/shard_map/all_to_all | solution.py:144
  644.2 1.2 reduce_sum.52
  645.4 4.0 all-to-all-start.16
  649.5 2.9 fusion.2
  652.4 15.5 %all-to-all-done.16 = bf16[8,304,128]{2,1,0:T(8,128)(2,1)S(1)} async-done(((bf16[8,304,128]{2,1,0:T(8,128)(2,1)}), bf16[8,304,128]{2,1,0:T(8,128)(2,1)S(1)}, u32[]{:S(2)}, u32[]{:S(2)}) %all-to-all-start.16) | async-done | bytes 622624 | tf_op jit(solution)/shard_map/all_to_all | solution.py:144
  667.9 1.8 broadcast_select_fusion
  669.7 0.7 multiply_reduce_fusion
  671.7 2.6 all-to-all-start.17
  674.4 4.2 fusion
  678.6 2.9 all-to-all-done.17
  683.4 0.9 fusion.13
  (49 shorter events, 5.9 us)
Async XLA Ops:
  0.6 29.4 %copy-start = (bf16[1,32,256,128]{3,2,1,0:T(8,128)(2,1)S(1)}, bf16[1,32,256,128]{3,2,1,0:T(8,128)(2,1)}, u32[]{:S(2)}) copy-start(bf16[1,32,256,128]{3,2,1,0:T(8,128)(2,1)} %param.10) | copy-start | bytes 6291460
  30.0 2.0 copy-start.1
  30.0 58.1 %collective-permute-start = (bf16[32,256,128]{2,1,0:T(8,128)(2,1)S(1)}, bf16[32,256,128]{2,1,0:T(8,128)(2,1)}, u32[]{:S(2)}, u32[]{:S(2)}) collective-permute-start(bf16[32,256,128]{2,1,0:T(8,128)(2,1)S(1)} %bitcast.42), channel_id=1, source_target_pairs={{4,10},{5,11},{6,8},{7,9},{8,6},{9,7},{10,4},{11,5},{20,26},{21,27... | collective-permute-start | bytes 6291464 | tf_op jit(solution)/shard_map/ppermute | solution.py:898
  32.0 5.4 copy-start.12
  33.2 20.5 %all-to-all-start.1 = ((bf16[2,2432,128]{2,1,0:T(8,128)(2,1)}), bf16[2,2432,128]{2,1,0:T(8,128)(2,1)S(1)}, u32[]{:S(2)}, u32[]{:S(2)}) async-start(bf16[2,2432,128]{2,1,0:T(8,128)(2,1)} %broadcast_in_dim.51), calls=%async_computation.1 | async-start | bytes 2490368 | tf_op jit(solution)/shard_map/all_to_all | solution.py:144
  37.5 23.2 %copy-start.11 = (f32[1,256]{1,0:T(1,128)}, f32[1,256]{1,0:T(1,128)S(1)}, u32[]{:S(2)}) copy-start(f32[1,256]{1,0:T(1,128)S(1)} %convert_element_type.23.keep) | copy-start | bytes 3076
  70.5 14.7 %all-to-all-start.3 = ((bf16[32,32,128]{2,1,0:T(8,128)(2,1)}), bf16[32,32,128]{2,1,0:T(8,128)(2,1)S(1)}, u32[]{:S(2)}, u32[]{:S(2)}) async-start(bf16[32,32,128]{2,1,0:T(8,128)(2,1)} %get-tuple-element.111), calls=%async_computation.3 | async-start | bytes 524288 | tf_op jit(solution)/shard_map/all_to_all | solution.py:144
  85.2 0.7 copy-start.2
  98.6 53.6 %all-to-all-start.4 = ((bf16[8,32,32,256]{3,2,1,0:T(8,128)(2,1)}), bf16[8,32,32,256]{3,2,1,0:T(8,128)(2,1)}, u32[]{:S(2)}, u32[]{:S(2)}) async-start(bf16[8,32,32,256]{3,2,1,0:T(8,128)(2,1)} %get-tuple-element.118), calls=%async_computation.4 | async-start | bytes 8388608 | tf_op jit(solution)/shard_map/all_to_all | solution.py:144
  103.3 0.8 collective-permute-start.1
  378.5 52.4 %all-to-all-start.9 = ((bf16[8,32,32,256]{3,2,1,0:T(8,128)(2,1)}), bf16[8,32,32,256]{3,2,1,0:T(8,128)(2,1)}, u32[]{:S(2)}, u32[]{:S(2)}) async-start(bf16[8,32,32,256]{3,2,1,0:T(8,128)(2,1)} %bitcast.46), calls=%async_computation.9 | async-start | bytes 8388608 | tf_op jit(solution)/shard_map/all_to_all | solution.py:144
  383.1 0.8 collective-permute-start.2
  572.4 14.6 %all-to-all-start.12 = ((bf16[32,32,128]{2,1,0:T(8,128)(2,1)}), bf16[32,32,128]{2,1,0:T(8,128)(2,1)S(1)}, u32[]{:S(2)}, u32[]{:S(2)}) async-start(bf16[32,32,128]{2,1,0:T(8,128)(2,1)} %bitcast.62), calls=%async_computation.12 | async-start | bytes 524288 | tf_op jit(solution)/shard_map/all_to_all | solution.py:144
  587.1 0.7 copy-start.3
  604.9 63.1 %collective-permute-start.3 = (bf16[32,256,128]{2,1,0:T(8,128)(2,1)}, bf16[32,256,128]{2,1,0:T(8,128)(2,1)}, u32[]{:S(2)}, u32[]{:S(2)}) collective-permute-start(bf16[32,256,128]{2,1,0:T(8,128)(2,1)} %get-tuple-element.188), channel_id=1, source_target_pairs={{4,10},{5,11},{6,8},{7,9},{8,6},{9,7},{10,4},{11,5},{20,26},{21,27... | collective-permute-start | bytes 6291464 | tf_op jit(solution)/shard_map/ppermute | solution.py:898
  644.2 5.2 copy-start.7
  644.2 5.3 copy-start.6
  644.2 5.3 copy-start.10
  645.4 22.4 %all-to-all-start.16 = ((bf16[8,304,128]{2,1,0:T(8,128)(2,1)}), bf16[8,304,128]{2,1,0:T(8,128)(2,1)S(1)}, u32[]{:S(2)}, u32[]{:S(2)}) async-start(bf16[8,304,128]{2,1,0:T(8,128)(2,1)} %reduce_sum.52), calls=%async_computation.16 | async-start | bytes 1245184 | tf_op jit(solution)/shard_map/all_to_all | solution.py:144
  670.5 12.8 %copy-start.5 = (f32[37488]{0:T(1024)}, f32[37488]{0:T(1024)S(1)}, u32[]{:S(2)}) copy-start(f32[37488]{0:T(1024)S(1)} %get-tuple-element.196) | copy-start | bytes 449860
  671.7 9.8 %all-to-all-start.17 = ((f32[32,2,128]{2,1,0:T(2,128)}), f32[32,2,128]{2,1,0:T(2,128)S(1)}, u32[]{:S(2)}, u32[]{:S(2)}) async-start(f32[32,2,128]{2,1,0:T(2,128)} %broadcast_in_dim.59), calls=%async_computation.17 | async-start | bytes 65536 | tf_op jit(solution)/shard_map/all_to_all | solution.py:144
  674.3 9.0 %copy-start.4 = (f32[37488]{0:T(1024)S(1)}, f32[37488]{0:T(1024)}, u32[]{:S(2)}) copy-start(f32[37488]{0:T(1024)} %param.15) | copy-start | bytes 449860
  674.3 9.0 %copy-start.8 = (f32[37488]{0:T(1024)S(1)}, f32[37488]{0:T(1024)}, u32[]{:S(2)}) copy-start(f32[37488]{0:T(1024)} %param.16) | copy-start | bytes 449860
  674.3 9.0 %copy-start.9 = (f32[37488]{0:T(1024)S(1)}, f32[37488]{0:T(1024)}, u32[]{:S(2)}) copy-start(f32[37488]{0:T(1024)} %param.17) | copy-start | bytes 449860

commit v3 on v2

--- a/solution.py
+++ b/solution.py
@@ -126,6 +126,7 @@
         self.cores = [
             [(2 * x + k) * rows + r for k in range(2)] for x in range(half) for r in range(rows)
         ]
+        self.slabs = [[2 * x * rows + k for k in range(2 * rows)] for x in range(half)]
         self.chips = [
             [(2 * x + k) * rows + r for x in range(half)] for k in range(2) for r in range(rows)
         ]
@@ -161,9 +162,15 @@
 
 
 def norm_parts(x):
-    centered = x - jnp.mean(x, axis=0, keepdims=True)
+    hat, _, scale = norm_all(x)
+    return hat, scale
+
+
+def norm_all(x):
+    mean = jnp.mean(x, axis=0, keepdims=True)
+    centered = x - mean
     scale = lax.rsqrt(jnp.mean(centered * centered, axis=0, keepdims=True) + EPS_NORM)
-    return centered * scale, scale
+    return centered * scale, mean, scale
 
 
 def norm_back(grad, hat, scale, gain):
@@ -227,13 +234,13 @@
         scratch[:, side * channels : (side + 1) * channels, :] = swapped(value)
 
 
-def front(x, gain, w_all, mask, x_out, hat_out, scale_out, gate_out, sides):
-    hat, scale = norm_parts(x)
+def front(x, gain, w_all, mask, x_out, mean_out, scale_out, gate_out, sides):
+    hat, mean, scale = norm_all(x)
     all_three = dot_nn(w_all, (hat * gain).astype(LOW))
     channels = 2 * TRI_DIM
     put(sides, all_three[:channels] * mask)
     put(x_out, x)
-    put(hat_out, hat)
+    put(mean_out, mean)
     put(scale_out, scale)
     put(gate_out, sigmoid(all_three[channels:]))
 
@@ -252,7 +259,8 @@
     return mixed_grad, gate_grad, grad_out, grad_gain
 
 
-def front_back(grad, hat, scale, sides_grad, gate_grad, mask, gain, w_all_back):
+def front_back(grad, x, mean, scale, sides_grad, gate_grad, mask, gain, w_all_back):
+    hat = (x - mean) * scale
     normed = (hat * gain).astype(LOW)
     sides = jnp.concatenate([sides_grad * mask.astype(LOW), gate_grad], axis=0)
     grad_w = dot_nt(normed, sides)
@@ -266,17 +274,23 @@
     return x * cumulative, cumulative + x * density
 
 
-def zero_first(*refs):
+def zero_first(*refs, earlier=()):
     @pl.when((pl.program_id(0) == 0) & (pl.program_id(1) == 0))
     def _():
-        for ref in refs:
-            ref[...] = jnp.zeros_like(ref)
-
-
-def run(body, step, extent, in_arrays, in_kinds, outs, scratch, flops):
+        for k, ref in enumerate(refs):
+            ref[...] = earlier[k][...] if earlier else jnp.zeros_like(ref)
+
+
+def run(body, step, extent, in_arrays, in_kinds, outs, scratch, flops, skip=0, aliases={}):
     def spec(kind, shape):
         lead = (0,) * len(shape)
+        if kind == "m":
+            return pl.BlockSpec(memory_space=pltpu.SMEM)
+        if kind == "x":
+            return pl.BlockSpec(memory_space=pl.ANY)
         block, at = {
+            "R": (step[:1] + shape[1:-1] + step[1:], lambda c, r: (r + skip,) + lead[2:] + (c,)),
+            "N": (step + shape[2:], lambda c, r: (r + skip, c) + lead[2:]),
             "r": (step[:1] + shape[1:-1] + step[1:], lambda c, r: (r,) + lead[2:] + (c,)),
             "n": (step + shape[2:], lambda c, r: (r, c) + lead[2:]),
             "s": (shape[:-2] + step, lambda c, r: lead[2:] + (r, c)),
@@ -296,6 +310,7 @@
         out_specs=[spec(kind, shape) for kind, shape, _ in outs],
         out_shape=[jax.ShapeDtypeStruct(shape, dtype) for _, shape, dtype in outs],
         scratch_shapes=scratch,
+        input_output_aliases=aliases,
         compiler_params=pltpu.CompilerParams(vmem_limit_bytes=VMEM_LIMIT),
         cost_estimate=pl.CostEstimate(flops=flops, bytes_accessed=moved, transcendentals=0),
     )(*in_arrays)
@@ -310,49 +325,54 @@
 
 
 def kernel_open(
-    pair, table, right, mask, vectors, w_all, x_out, hat_out, scale_out, gate_out, sides_out, sides
+    stays, pair, pair_home, table, right, mask, vectors, w_all, x_out, mean_out, scale_out, gate_out, sides_out, sides
 ):
     right_low = right[...]
+    at_home = stays[0] == 1
     x = jnp.concatenate(
-        [pair[t].T.astype(WIDE) + dot_tn(table[t], right_low) for t in range(pair.shape[0])],
+        [
+            jnp.where(at_home, pair_home[t], pair[t]).T.astype(WIDE) + dot_tn(table[t], right_low)
+            for t in range(pair.shape[0])
+        ],
         axis=1,
     )
     front(
-        x, column(vectors[OUT_GAIN]), all_low(w_all), cat(mask), x_out, hat_out, scale_out, gate_out, sides
+        x, column(vectors[OUT_GAIN]), all_low(w_all), cat(mask), x_out, mean_out, scale_out, gate_out,
+        sides,
     )
     send_pair(sides, sides_out)
 
 
 def kernel_middle(
     mixed, x_in, gate_in, mask, vectors, w_out, w_all,
-    x_out, hat_out, scale_out, gate_out, sides_out, arrived, sides,
+    x_out, mean_out, scale_out, gate_out, sides_out, arrived, sides,
 ):
     arrived[...] = swapped(mixed[...])
     *_, update = triangle_update(cat(arrived).astype(WIDE), column(vectors[OUT_TRI]), w_out[...].T)
-    x = cat(x_in) + cat(gate_in).astype(WIDE) * update
+    x = cat(x_in).astype(WIDE) + cat(gate_in).astype(WIDE) * update
     front(
         x, column(vectors[IN_GAIN]), all_low(w_all), cat(mask),
-        x_out, hat_out, scale_out, gate_out, sides,
+        x_out, mean_out, scale_out, gate_out, sides,
     )
     send_pair(sides, sides_out)
 
 
-def kernel_turn(
-    mixed, x_in, gate_in, cot, vectors, w_out, w_up, w_down,
-    pair_out, x_grad, gate_grad, mixed_grad, g_out, g_tri, g_up, g_down, g_pair, g_bias,
-    arrived, leaving,
-):
+def kernel_turn(mixed, x_in, gate_in, cot, vectors, w_out, w_up, w_down, *rest):
+    (
+        pair_out, x_grad, gate_grad, mixed_grad, g_out, g_tri, g_up, g_down, g_pair, g_bias,
+        arrived, leaving,
+    ) = rest[-12:]
     rows = x_in.shape[0]
     arrived[...] = swapped(mixed[...])
     up_low, up_back = w_up[...].T, w_up[...]
     down_low, down_back = w_down[...].T, w_down[...]
     tri_col, pair_col = column(vectors[IN_TRI]), column(vectors[PAIR_GAIN])
-    zero_first(g_out, g_tri, g_up, g_down, g_pair, g_bias)
+    zero_first(g_out, g_tri, g_up, g_down, g_pair, g_bias, earlier=rest[3:-12])
     chunk = PAIR_DIM
 
     gate = cat(gate_in).astype(WIDE)
     mix_parts = triangle_update(cat(arrived).astype(WIDE), tri_col, w_out[...].T)
-    x = cat(x_in) + gate * mix_parts[-1]
+    x = cat(x_in).astype(WIDE) + gate * mix_parts[-1]
     hat, scale = norm_parts(x)
     normed = (hat * pair_col).astype(LOW)
     cot_low = jnp.concatenate([cot[t].T for t in range(rows)], axis=1)
@@ -386,7 +406,7 @@
 
 
 def kernel_return(
-    sides_grad, hat_after, scale_after, gate_after, grad_in, mask, vectors, w_after,
+    sides_grad, x_after, mean_after, scale_after, gate_after, grad_in, mask, vectors, w_after,
     mixed, gate_in, w_out,
     x_grad, gate_grad, mixed_grad, g_after, g_gain, g_out, g_tri,
     sides, arrived, leaving,
@@ -396,7 +416,8 @@
     tri_col = column(vectors[OUT_TRI])
     zero_first(g_after, g_gain, g_out, g_tri)
     grad, grad_w, grad_gain = front_back(
-        cat(grad_in), cat(hat_after).astype(WIDE), cat(scale_after), cat(sides), cat(gate_after),
+        cat(grad_in).astype(WIDE), cat(x_after).astype(WIDE), cat(mean_after), cat(scale_after),
+        cat(sides), cat(gate_after),
         cat(mask), column(vectors[IN_GAIN]), all_back(w_after),
     )
     g_after[...] += grad_w
@@ -414,7 +435,7 @@
 
 
 def kernel_close(
-    sides_grad, hat_after, scale_after, gate_after, grad_in, mask, vectors, w_after,
+    sides_grad, x_after, mean_after, scale_after, gate_after, grad_in, mask, vectors, w_after,
     table, right,
     pair_grad, table_grad, right_grad, g_after, g_gain, sides,
 ):
@@ -426,7 +447,8 @@
         right_grad[...] = jnp.zeros_like(right_grad)
 
     grad, grad_w, grad_gain = front_back(
-        cat(grad_in), cat(hat_after).astype(WIDE), cat(scale_after), cat(sides), cat(gate_after),
+        cat(grad_in).astype(WIDE), cat(x_after).astype(WIDE), cat(mean_after), cat(scale_after),
+        cat(sides), cat(gate_after),
         cat(mask), column(vectors[OUT_GAIN]), all_back(w_after),
     )
     g_after[...] += grad_w
@@ -441,22 +463,26 @@
         right_grad[...] += dot_nn(table[t], own)
 
 
-CHANNELS = 4
-
-
-def kernel_mix(incoming, left, right, out):
-    parts, count, rows, length = out.shape
+CHANNELS = 8
+
+
+def kernel_mix(incoming, left, right, *outs):
+    parts, count, rows, length = left.shape
+    part = rows // len(outs)
     for c in range(count):
         a = left[:, c].reshape(length, length)
         b = right[:, c].reshape(length, length)
         mixed = dot_tn(a, b) if incoming else dot_nt(a, b)
-        out[:, c] = mixed.astype(LOW).reshape(parts, rows, length)
-
-
-def kernel_mix_back(incoming, grad, left, right, out):
-    parts, count, rows, length = grad.shape
+        mixed = mixed.astype(LOW).reshape(parts, rows, length)
+        for k, out in enumerate(outs):
+            out[:, c] = mixed[:, k * part : (k + 1) * part]
+
+
+def kernel_mix_back(incoming, *refs):
+    *grads, left, right, out = refs
+    parts, count, rows, length = left.shape
     for c in range(count):
-        g = grad[:, c].reshape(length, length)
+        g = jnp.concatenate([grad[:, c] for grad in grads], axis=1).reshape(length, length)
         a = left[:, c].reshape(length, length)
         b = right[:, c].reshape(length, length)
         a_grad = dot_nt(b, g) if incoming else dot_nn(g, b)
@@ -465,12 +491,13 @@
         out[:, 1, c] = b_grad.astype(LOW).reshape(parts, rows, length)
 
 
-def mix(sides, incoming):
+def mix(sides, incoming, pieces=1):
     parts, double, rows, length = sides.shape
     share = double // 2
     count = min(CHANNELS, share)
     steps = share // count
     block = (parts, count, rows, length)
+    part = (parts, count, rows // pieces, length)
     return pl.pallas_call(
         lambda *refs: kernel_mix(incoming, *refs),
         grid=(steps,),
@@ -478,8 +505,8 @@
             pl.BlockSpec(block, lambda c: (0, c, 0, 0)),
             pl.BlockSpec(block, lambda c: (0, c + steps, 0, 0)),
         ],
-        out_specs=pl.BlockSpec(block, lambda c: (0, c, 0, 0)),
-        out_shape=jax.ShapeDtypeStruct((parts, share, rows, length), LOW),
+        out_specs=[pl.BlockSpec(part, lambda c: (0, c, 0, 0))] * pieces,
+        out_shape=[jax.ShapeDtypeStruct((parts, share) + part[2:], LOW)] * pieces,
         compiler_params=pltpu.CompilerParams(vmem_limit_bytes=VMEM_LIMIT),
         cost_estimate=pl.CostEstimate(
             flops=2 * share * length**3, bytes_accessed=3 * share * length * length * 2,
@@ -488,17 +515,18 @@
     )(sides, sides)
 
 
-def mix_back(grad, sides, incoming):
+def mix_back(grads, sides, incoming):
     parts, double, rows, length = sides.shape
     share = double // 2
     count = min(CHANNELS, share)
     steps = share // count
     block = (parts, count, rows, length)
+    part = (parts, count, rows // len(grads), length)
     out = pl.pallas_call(
         lambda *refs: kernel_mix_back(incoming, *refs),
         grid=(steps,),
-        in_specs=[
-            pl.BlockSpec(block, lambda c: (0, c, 0, 0)),
+        in_specs=[pl.BlockSpec(part, lambda c: (0, c, 0, 0))] * len(grads)
+        + [
             pl.BlockSpec(block, lambda c: (0, c, 0, 0)),
             pl.BlockSpec(block, lambda c: (0, c + steps, 0, 0)),
         ],
@@ -509,7 +537,7 @@
             flops=4 * share * length**3, bytes_accessed=5 * share * length * length * 2,
             transcendentals=0,
         ),
-    )(grad, sides, sides)
+    )(*grads, sides, sides)
     return out.reshape(sides.shape)
 
 
@@ -629,19 +657,19 @@
     )
 
 
-def pack(layout, share, recycle, grads, node_parts):
+def pack(layout, share, scalars, grads, node_parts):
     at, total = first_rows()
     height = share_rows(share)
     first = [share * d // LANES for d in range(layout.devices)]
     order = share_order(layout)
     many = len(grads)
 
-    def body(recycle_ref, *refs):
+    def body(scalar_ref, *refs):
         ins, rest = refs[:many], refs[many:]
         (
-            arrived, query_low, start, normed_one, after_grad, vectors, w_projections,
+            key_value, query_low, start, normed_own, normed_all, after_grad, vectors, w_projections,
             act_low, final_low, normed_two, hidden_grad, attended, after_low, g_factors,
-            out, node_grad_out, flat, narrow,
+            out, node_parts_out, flat, narrow, steps,
         ) = rest
 
         def store(place, count, value):
@@ -675,20 +703,24 @@
         store(at.w_left_node, 1, left)
         store(at.w_right_node, 1, right)
 
-        key_value = jnp.sum(arrived[...].astype(WIDE), axis=0).astype(LOW)
-        projections = jnp.concatenate([query_low[...], key_value], axis=1)
-        store(at.w_query, 3, dot_tn(normed_one[...], projections))
+        store(at.w_query, 1, dot_tn(normed_own[...], query_low[...]))
+        store(at.w_key, 2, dot_tn(normed_all[...], key_value[...]))
+        steps[...] = dot_nt(key_value[...], w_projections[:, HEADS_WIDTH:])
+        local_rows = query_low.shape[0]
+        own = pl.ds(pl.multiple_of(scalar_ref[1] * local_rows, local_rows), local_rows)
+        steps[own, :] += dot_nt(query_low[...], w_projections[:, :HEADS_WIDTH])
         hat, scale = row_norm(start[...])
-        part, grad_gain = row_norm_back(
-            dot_nt(projections, w_projections[...]), hat, scale, vector(vectors, GAIN_ONE)
-        )
-        node_grad = after_grad[...] + part
-        node_grad_out[...] = node_grad.astype(LOW)
+        part, grad_gain = row_norm_back(steps[...], hat, scale, vector(vectors, GAIN_ONE))
+        for r in range(node_parts_out.shape[0]):
+            for a in range(NODE_DIM // LANES):
+                piece = part[r * local_rows : (r + 1) * local_rows, a * LANES : (a + 1) * LANES]
+                node_parts_out[r, a * local_rows : (a + 1) * local_rows] = piece.astype(LOW)
         store(at.gain_one, 1, grad_gain)
         flat[at.embed : at.embed + 2 * RECYCLES] = jnp.zeros((2 * RECYCLES, LANES), WIDE)
-        column_sum = jnp.sum(node_grad, axis=0, keepdims=True)
+        column_sum = jnp.sum(after_grad[...], axis=0, keepdims=True)
+        column_sum += jnp.sum(part, axis=0, keepdims=True)
         for a in range(NODE_DIM // LANES):
-            place = at.embed + (NODE_DIM // LANES) * recycle_ref[0] + a
+            place = at.embed + (NODE_DIM // LANES) * scalar_ref[0] + a
             flat[pl.ds(place, 1), :] = column_sum[:, a * LANES : (a + 1) * LANES]
         for d, where in enumerate(order):
             out[where] = flat[first[d] : first[d] + height].astype(LOW)
@@ -696,10 +728,14 @@
     shape = (2, layout.crops // 2, layout.rows, height, LANES)
     return one_call(
         body,
-        (recycle,),
+        (scalars,),
         tuple(array for _, _, array in grads) + tuple(node_parts),
-        [(shape, LOW), (node_parts[2].shape, LOW)],
-        [pltpu.VMEM((first[-1] + height + TILE, LANES), WIDE), pltpu.VMEM((NODE_DIM, LANES), WIDE)],
+        [(shape, LOW), ((layout.rows, node_parts[1].shape[0] * NODE_DIM // LANES, LANES), LOW)],
+        [
+            pltpu.VMEM((first[-1] + height + TILE, LANES), WIDE),
+            pltpu.VMEM((NODE_DIM, LANES), WIDE),
+            pltpu.VMEM(node_parts[2].shape, WIDE),
+        ],
     )
 
 
@@ -746,7 +782,7 @@
 def node_forward(
     recycle, node_ref, all_ref, bias_ref, keep, keep_rows, vectors, w_projections, w_attn_out, w_up, w_down,
     w_factors,
-    node_out, factors_out, start_out, normed_one, soft_out, heads_out, key_out, value_out,
+    node_out, factors_out, start_out, normed_own, normed_out, soft_out, heads_out, key_out, value_out,
     attended_out, after_out, act_out, slope_out, final_out, flat,
 ):
     pieces = NODE_DIM // LANES
@@ -759,11 +795,13 @@
         [flat[pl.ds(a, length, stride=pieces), :] for a in range(pieces)], axis=1
     )
     gain = vector(vectors, GAIN_ONE)
-    normed_all = (row_norm(all_rows + embed)[0] * gain).astype(LOW)
+    start_all = all_rows + embed
+    normed_all = (row_norm(start_all)[0] * gain).astype(LOW)
+    start_out[...] = start_all
+    normed_out[...] = normed_all
     start = node_ref[...].astype(WIDE) + embed
     normed = (row_norm(start)[0] * gain).astype(LOW)
-    start_out[...] = start
-    normed_one[...] = normed
+    normed_own[...] = normed
     query = dot_nn(normed, w_projections[:, :HEADS_WIDTH]).astype(LOW).astype(WIDE)
     heads = by_head(query).astype(LOW)
     key_value = dot_nn(normed_all, w_projections[:, HEADS_WIDTH:]).astype(LOW)
@@ -798,7 +836,7 @@
     key_value_out, query_out, score_out, after_grad_out, final_low_out, normed_two_out,
     hidden_out, after_low_out, g_factors, g_two, g_three,
 ):
-    ranks = key_value_out.shape[0]
+    ranks = key_value_out.shape[0] // cot.shape[0]
     left = factor_ref[sources[0]].astype(WIDE)
     right = sum(factor_ref[sources[1 + r]].astype(WIDE) for r in range(ranks))
     rows = jnp.where(lane_in(left.shape, 0, OUTER), left, right).astype(LOW)
@@ -826,13 +864,9 @@
     score_grad = soft * (soft_grad - jnp.sum(soft_grad * soft, axis=-1, keepdims=True))
     score_low = score_grad.astype(LOW)
     score_out[...] = score_low
-    key_part = (dot_tn(score_low, heads[...]) * SCORE_SCALE).astype(LOW)
-    value_part = dot_tn(soft.astype(LOW), grad_heads).astype(LOW)
-    local_rows = cot.shape[0]
-    for r in range(ranks):
-        span = slice(r * local_rows, (r + 1) * local_rows)
-        key_value_out[r, :, :HEADS_WIDTH] = key_part[span]
-        key_value_out[r, :, HEADS_WIDTH:] = value_part[span]
+    key_part = dot_tn(score_low, heads[...]) * SCORE_SCALE
+    key_value_out[:, :HEADS_WIDTH] = key_part.astype(LOW)
+    key_value_out[:, HEADS_WIDTH:] = dot_tn(soft.astype(LOW), grad_heads).astype(LOW)
     query_out[...] = (head_sum(dot_nn(score_low, key[...])) * SCORE_SCALE).astype(LOW)
 
 
@@ -916,7 +950,7 @@
         vectors, w_bias, w_factors, w_projections, w_attn_out, w_node_up, w_node_down, w_outer,
         w_out_all, w_out_end, w_in_all, w_in_end, w_pair_up, w_pair_down,
     ) = unpack(layout, shards, amount)
-    pair_plane = moved(pair)
+    pair_plane = lax.ppermute(pair, BOTH, layout.moves)
     keep = mask.astype(WIDE)
     keep_rows = lax.dynamic_slice_in_dim(keep[0], row_at * local_rows, local_rows, 0)[:, None]
 
@@ -925,24 +959,25 @@
     rows_wide = lambda width: ((local_rows, width), WIDE)
     by_heads = (HEADS * local_rows, length)
     (
-        node_out, factors, start, normed_one, soft, heads, key, value, attended, after, act_low,
+        node_out, factors, start_all, normed_own, normed_all, soft, heads, key, value, attended, after, act_low,
         slope, node_final,
     ) = one_call(
         node_forward,
         (recycle,),
         (node, node_all, pair_bias.reshape(by_heads), keep, keep_rows, vectors, w_projections, w_attn_out,
          w_node_up, w_node_down, w_factors),
-        [rows_low(NODE_DIM), ((devices, local_rows, LANES), LOW), rows_wide(NODE_DIM),
-         rows_low(NODE_DIM), (by_heads, WIDE), (by_heads[:1] + (HEADS_WIDTH,), LOW),
+        [rows_low(NODE_DIM), ((2 * ranks, local_rows, LANES), LOW), ((length, NODE_DIM), WIDE),
+         rows_low(NODE_DIM), ((length, NODE_DIM), LOW), (by_heads, WIDE), (by_heads[:1] + (HEADS_WIDTH,), LOW),
          ((length, HEADS_WIDTH), LOW), ((length, HEADS_WIDTH), LOW), rows_low(HEADS_WIDTH),
          rows_wide(NODE_DIM), rows_low(FFN_NODE), rows_wide(FFN_NODE), rows_wide(NODE_DIM)],
         [pltpu.VMEM(node_all.shape, WIDE)],
     )
 
-    factors = exchange(factors, BOTH)
+    factors = exchange(factors, BOTH, layout.slabs)
     factors, pair_cot = lax.optimization_barrier((factors, pair_cot))
     everyone = jnp.arange(ranks, dtype=jnp.int32)
-    sources = jnp.concatenate([partner[None], work_crop * ranks + everyone]).astype(jnp.int32)
+    slab = 2 * ranks
+    sources = jnp.concatenate([partner[None], work_crop * ranks + everyone]).astype(jnp.int32) % slab
     table, right, left, mask_plane = one_call(
         outer_tables,
         (sources,),
@@ -962,56 +997,66 @@
     natural = (local_rows, length, PAIR_DIM)
     buffer = lambda channels: pltpu.VMEM((step[0], channels, step[1]), LOW)
     trade = lambda blocks: exchange(blocks, BOTH, layout.groups)
-    merge = lambda blocks: blocks.reshape(mixed_shape)
-    split = lambda blocks: blocks.reshape(ranks, share, local_rows, length)
+    merge = lambda blocks: blocks.reshape((TRI_DIM,) + blocks.shape[2:])
+    split = lambda blocks: blocks.reshape((ranks, share) + blocks.shape[1:])
     unit = 2 * local_rows * length * PAIR_DIM * PAIR_DIM
     front_outs = (
-        ("r", state, WIDE), ("r", state, LOW), ("r", line, WIDE), ("r", state, LOW),
+        ("r", state, LOW), ("r", line, WIDE), ("r", line, WIDE), ("r", state, LOW),
         ("s", sides_shape, LOW),
     )
     square = (TRI_DIM, PAIR_DIM)
     gain_shape = (PAIR_DIM, 1)
     after_shape = (PAIR_DIM, 2 * TRI_DIM + PAIR_DIM)
 
-    x_one, hat_tri_out, scale_tri_out, gate_tri_out, sides = run(
+    x_one, mean_tri_out, scale_tri_out, gate_tri_out, sides = run(
         kernel_open, step, extent,
-        (pair_plane, table, right, mask_plane, vectors, w_out_all),
-        "ntcrww", front_outs, [buffer(2 * TRI_DIM)], 4 * unit,
+        (stays.astype(jnp.int32)[None], pair_plane, pair, table, right, mask_plane, vectors, w_out_all),
+        "mnntcrww", front_outs, [buffer(2 * TRI_DIM)], 4 * unit,
     )
     sides_out, cot_plane = lax.optimization_barrier((trade(sides), moved(pair_cot)))
-    mixed_out = merge(trade(mix(sides_out, False)))
-    x_two, hat_tri_in, scale_tri_in, gate_tri_in, sides = run(
+    mixed_out = merge(trade(mix(sides_out, False)[0]))
+    x_two, mean_tri_in, scale_tri_in, gate_tri_in, sides = run(
         kernel_middle, step, extent,
         (mixed_out, x_one, gate_tri_out, mask_plane, vectors, w_out_end, w_in_all), "srrrwww", front_outs, [buffer(TRI_DIM), buffer(2 * TRI_DIM)], 5 * unit,
     )
     sides_in = trade(sides)
-    mixed_in = merge(trade(mix(sides_in, True)))
-    pair_final, x_grad, gate_grad, mixed_grad, g_in_out, g_in_tri, g_up, g_down, g_pair, g_bias = run(
-        kernel_turn, step, extent,
-        (mixed_in, x_two, gate_tri_in, cot_plane, vectors, w_in_end, w_pair_up, w_pair_down),
-        "srrnwwww",
-        (("n", natural, LOW), ("r", state, WIDE), ("r", state, LOW), ("s", mixed_shape, LOW),
-         ("w", square, WIDE), ("w", gain_shape, WIDE), ("w", (PAIR_DIM, FFN_PAIR), WIDE),
-         ("w", (FFN_PAIR, PAIR_DIM), WIDE), ("w", gain_shape, WIDE), ("w", gain_shape, WIDE)),
-        [buffer(TRI_DIM), buffer(TRI_DIM)], 32 * unit,
-    )
-    sides_grad = trade(mix_back(trade(split(mixed_grad)), sides_in, True))
+    turns = 2 if local_rows % (2 * TILE) == 0 else 1
+    turn_rows = local_rows // turns
+    mixed_in = [merge(trade(piece)) for piece in mix(sides_in, True, turns)]
+    turned, grads_in = (), []
+    for k in range(turns):
+        turned = run(
+            kernel_turn, step, (turn_rows, length),
+            (mixed_in[k], x_two, gate_tri_in, cot_plane, vectors, w_in_end, w_pair_up, w_pair_down,
+             *turned),
+            "sRRNwwww" + ("xxxwwwwww" if k else ""),
+            (("N", natural, LOW), ("R", state, LOW), ("R", state, LOW),
+             ("s", (TRI_DIM, turn_rows, length), LOW),
+             ("w", square, WIDE), ("w", gain_shape, WIDE), ("w", (PAIR_DIM, FFN_PAIR), WIDE),
+             ("w", (FFN_PAIR, PAIR_DIM), WIDE), ("w", gain_shape, WIDE), ("w", gain_shape, WIDE)),
+            [buffer(TRI_DIM), buffer(TRI_DIM)], 32 * unit // turns,
+            skip=k * turn_rows // step[0], aliases={8: 0, 9: 1, 10: 2} if k else {},
+        )
+        turned = list(turned)
+        grads_in.append(trade(split(turned.pop(3))))
+    pair_final, x_grad, gate_grad, g_in_out, g_in_tri, g_up, g_down, g_pair, g_bias = turned
+    sides_grad = trade(mix_back(grads_in, sides_in, True))
     sides_grad, pair_out = lax.optimization_barrier((sides_grad, moved(pair_final)))
     x_grad, gate_grad, mixed_grad, g_in_all, g_in_gain, g_out_out, g_out_tri = run(
         kernel_return, step, extent,
-        (sides_grad, hat_tri_in, scale_tri_in, gate_grad, x_grad, mask_plane,
+        (sides_grad, x_two, mean_tri_in, scale_tri_in, gate_grad, x_grad, mask_plane,
          vectors, w_in_all, mixed_out, gate_tri_out, w_out_end),
-        "srrrrrwwsrw",
-        (("r", state, WIDE), ("r", state, LOW), ("s", mixed_shape, LOW), ("w", after_shape, WIDE),
+        "srrrrrrwwsrw",
+        (("r", state, LOW), ("r", state, LOW), ("s", mixed_shape, LOW), ("w", after_shape, WIDE),
          ("w", gain_shape, WIDE), ("w", square, WIDE), ("w", gain_shape, WIDE)),
         [buffer(2 * TRI_DIM), buffer(TRI_DIM), buffer(TRI_DIM)], 12 * unit,
     )
-    sides_grad = trade(mix_back(trade(split(mixed_grad)), sides_out, False))
+    sides_grad = trade(mix_back([trade(split(mixed_grad))], sides_out, False))
     pair_one_grad, table_grad, right_part, g_out_all, g_out_gain = run(
         kernel_close, step, extent,
-        (sides_grad, hat_tri_out, scale_tri_out, gate_grad, x_grad, mask_plane,
+        (sides_grad, x_one, mean_tri_out, scale_tri_out, gate_grad, x_grad, mask_plane,
          vectors, w_out_all, table, right),
-        "srrrrrwwtc",
+        "srrrrrrwwtc",
         (("n", natural, LOW), ("p", (pieces, local_rows, OUTER, PAIR_DIM), WIDE),
          ("c", (OUTER, length), WIDE), ("w", after_shape, WIDE), ("w", gain_shape, WIDE)),
         [buffer(2 * TRI_DIM)], 8 * unit,
@@ -1021,13 +1066,14 @@
         outer_backward,
         (),
         (table_grad, right_part, left, w_outer),
-        [((crops, ranks, local_rows, LANES), LOW), ((OUTER * OUTER, PAIR_DIM), WIDE)],
+        [((2, ranks, local_rows, LANES), LOW), ((OUTER * OUTER, PAIR_DIM), WIDE)],
         [pltpu.VMEM((OUTER * OUTER, PAIR_DIM), WIDE), pltpu.VMEM((OUTER, local_rows, PAIR_DIM), WIDE)],
     )
-    factor_grads = exchange(factor_grads.reshape(devices, local_rows, LANES), BOTH)
+    factor_grads = exchange(factor_grads.reshape(slab, local_rows, LANES), BOTH, layout.slabs)
+    factor_grads, pair_one_grad = lax.optimization_barrier((factor_grads, pair_one_grad))
 
     workers = layout.work_place(crop_at * ranks + everyone)
-    sources = jnp.concatenate([partner[None], workers]).astype(jnp.int32)
+    sources = jnp.concatenate([partner[None], workers]).astype(jnp.int32) % slab
     (
         key_value, query_low, score_low, after_grad, final_low, normed_two, hidden_grad, after_low,
         g_factors, g_two, g_three,
@@ -1036,17 +1082,16 @@
         (sources,),
         (factor_grads, node_cot, vectors, soft, heads, key, value, after, slope, node_final,
          w_attn_out, w_node_up, w_node_down, w_factors),
-        [((ranks, local_rows, 2 * HEADS_WIDTH), LOW), rows_low(HEADS_WIDTH), (by_heads, LOW),
+        [((length, 2 * HEADS_WIDTH), LOW), rows_low(HEADS_WIDTH), (by_heads, LOW),
          rows_wide(NODE_DIM), rows_low(NODE_DIM), rows_low(NODE_DIM), rows_low(FFN_NODE),
          rows_low(NODE_DIM), ((NODE_DIM, LANES), WIDE), ((1, NODE_DIM), WIDE), ((1, NODE_DIM), WIDE)],
     )
-    key_value = exchange(key_value, "row")
-    key_value, pair_one_grad = lax.optimization_barrier((key_value, pair_one_grad))
-    pair_one_home = moved(pair_one_grad)
     score_low = score_low.reshape(HEADS, local_rows, length)
     g_bias_head = jnp.einsum("ijd,hij->dh", pair, score_low, preferred_element_type=WIDE)
+    g_bias_head = lax.optimization_barrier(g_bias_head).reshape(-1, LANES)
+    pair_one_away = lax.ppermute(pair_one_grad, BOTH, layout.moves)
     grads = [
-        (at.w_bias, 1, lax.optimization_barrier(g_bias_head).reshape(-1, LANES)),
+        (at.w_bias, 1, g_bias_head),
         (at.gain_two, 1, g_two),
         (at.gain_three, 1, g_three),
         (at.w_outer, 1, g_outer),
@@ -1066,20 +1111,24 @@
             (tri.w_tri_out, 1, g_out),
         ]
 
-    blocks, node_grad = pack(
-        layout, amount, recycle, grads,
-        (key_value, query_low, start, normed_one, after_grad, vectors, w_projections, act_low,
-         final_low, normed_two, hidden_grad, attended, after_low, g_factors),
+    blocks, node_blocks = pack(
+        layout, amount, jnp.concatenate([recycle, row_at.astype(jnp.int32)[None]]), grads,
+        (key_value, query_low, start_all, normed_own, normed_all, after_grad, vectors,
+         w_projections, act_low, final_low, normed_two, hidden_grad, attended, after_low, g_factors),
     )
     total = lambda got: low_of(jnp.sum(got.astype(WIDE), axis=0))
     blocks = total(exchange(blocks, BOTH, layout.cores))
     blocks = total(exchange(blocks, BOTH, layout.chips))
-    blocks = jnp.sum(exchange(blocks, "row").astype(WIDE), axis=0)
-    blocks, pair_one_home = lax.optimization_barrier((blocks, pair_one_home))
+    blocks = exchange(jnp.concatenate([blocks, node_blocks], axis=1), "row")
+    pair_grad = jnp.where(stays, pair_one_grad, pair_one_away).astype(WIDE) + jnp.einsum(
+        "hij,dh->ijd", score_low, w_bias[:, :HEADS], preferred_element_type=WIDE
+    )
+    blocks, pair_grad = lax.optimization_barrier((blocks, low_of(pair_grad)))
+    blocks = jnp.sum(blocks.astype(WIDE), axis=0)
+    node_parts = jnp.split(blocks[height:], NODE_DIM // LANES)
+    node_grad = low_of(after_grad + jnp.concatenate(node_parts, axis=1))
+    blocks = blocks[:height]
     grad_own = lax.dynamic_slice(blocks.reshape(-1), (offset,), (amount,))
-    pair_grad = pair_one_home.astype(WIDE) + jnp.einsum(
-        "hij,dh->ijd", score_low, w_bias[:, :HEADS], preferred_element_type=WIDE
-    )
     square_own = jnp.broadcast_to(jnp.sum(grad_own * grad_own), (1, LANES))
     last = jnp.concatenate([g_bias.reshape(1, LANES), square_own], axis=0)
     last = jnp.sum(spread(last, devices, BOTH).reshape(devices, 2, LANES), axis=0)
@@ -1097,7 +1146,7 @@
         node_out[None],
         pair_out[None],
         node_grad[None],
-        low_of(pair_grad)[None],
+        pair_grad[None],
         grad_own,
         bias_total,
         grad_norm,

time: 688 us -> 655 us (0.952)
  blocking collectives: 351 us -> 326 us
  other arithmetic: 21.2 us -> 10.9 us
  waiting for transfers between devices: 142 us -> 133 us
    all_to_all x11, blocking collectives: 351 us -> 326 us  [exchange(): lax.all_to_all(blocks, axes, 0, 0, axis_index_groups=groups, tiled=True)]
    all_to_all x7 -> x8, waiting for transfers between devices: 142 us -> 133 us  [exchange(): lax.all_to_all(blocks, axes, 0, 0, axis_index_groups=groups, tiled=True)]
    all_to_all x7 -> x8, starting transfers between devices: 26.1 us -> 31.4 us  [exchange(): lax.all_to_all(blocks, axes, 0, 0, axis_index_groups=groups, tiled=True)]
    pallas_call x5 -> x6, Pallas kernels: 76.8 us -> 78.5 us  [run(): pl.pallas_call(body, grid=(extent[1] // step[1], extent[0] // step[0]), i...]
  transfers between devices with their start and end apart: 11 -> 12, of which waited for: 7 -> 6; matrix products, arithmetic and copies ran while one was open for 4% -> 3% of each run, Pallas kernels for 2% -> 8%
where the time goes in v3:
time: 655 us; the launch traced here: 646 us
  blocking collectives  326 us (50%)
  waiting for transfers between devices  133 us (20%)
  Pallas kernels  117 us (18%)
  starting transfers between devices  37.1 us (6%)
  other arithmetic  10.9 us (2%)
  local copies, waits for them, and re-layouts  10.3 us (2%)
  matrix products  6.87 us (1%)
    all_to_all x11, blocking collectives, exchange(): lax.all_to_all(blocks, axes, 0, 0, axis_index_groups=groups, tiled=True)  326 us
    all_to_all x8, waiting for transfers between devices, exchange(): lax.all_to_all(blocks, axes, 0, 0, axis_index_groups=groups, tiled=True)  133 us
    pallas_call x6, Pallas kernels, run(): pl.pallas_call(body, grid=(extent[1] // step[1], extent[0] // step[0]), i...  78.5 us
    all_to_all x8, starting transfers between devices, exchange(): lax.all_to_all(blocks, axes, 0, 0, axis_index_groups=groups, tiled=True)  31.4 us
    pallas_call x6, Pallas kernels, one_call(): pl.pallas_call(body, in_specs=[pl.BlockSpec(memory_space=pltpu.SMEM)] * l...  21.7 us
  transfers between devices with their start and end apart: 12, of which 6 were waited for; matrix products, arithmetic and copies ran while one was open for 3% of the time, Pallas kernels for 8%

profile of v3, /device:TPU:0, one launch (start us, length us, event | category | flops | bytes accessed | tf_op | source)
XLA Modules:
  0.0 645.8 jit_solution(9713105907991783149)
XLA Ops:
  0.7 0.9 reshape_squeeze.3
  1.6 0.9 convert_element_type.26
  2.5 0.8 dynamic_update_slice.3
  3.5 26.5 %all_to_all.95 = bf16[8,368,128]{2,1,0:T(8,128)(2,1)S(1)} all-to-all(bf16[8,368,128]{2,1,0:T(8,128)(2,1)S(1)} %broadcast_in_dim.57), channel_id=1, replica_groups=mesh['crop'=4,'row'=8] {'row'}, dimensions={0} | all-to-all | bytes 1507328 | tf_op jit(solution)/shard_map/all_to_all | solution.py:145
  30.0 2.0 collective-permute-start
  32.1 1.1 broadcast_in_dim.59
  33.2 3.6 all-to-all-start.1
  37.6 0.7 copy.46.keep_rows
  38.3 1.6 slice.22
  39.9 13.9 %all-to-all-done.1 = bf16[2,2432,128]{2,1,0:T(8,128)(2,1)S(1)} async-done(((bf16[2,2432,128]{2,1,0:T(8,128)(2,1)}), bf16[2,2432,128]{2,1,0:T(8,128)(2,1)S(1)}, u32[]{:S(2)}, u32[]{:S(2)}) %all-to-all-start.1) | async-done | bytes 1245216 | tf_op jit(solution)/shard_map/all_to_all | solution.py:145
  54.1 6.7 %all_to_all.96 = bf16[2,2,2432,128]{3,2,1,0:T(8,128)(2,1)} all-to-all(bf16[2,2,2432,128]{3,2,1,0:T(8,128)(2,1)S(1)} %broadcast_in_dim.60), channel_id=1, replica_groups={{0,8},{1,9},{2,10},{3,11},{4,12},{5,13},{6,14},{7,15},{16,24},{17,25},{..., dimensions={0} | all-to-all | bytes 4980736 | tf_op jit(solution)/shard_map/all_to_all | solution.py:145
  60.8 3.5 shard_map.176
  64.3 1.4 fusion.8
  65.7 0.8 copy.45
  66.5 4.2 shard_map.177
  70.7 3.5 all-to-all-start.3
  74.4 0.7 and_select_fusion
  75.1 6.8 %all-to-all-done.3.factors = bf16[16,32,128]{2,1,0:T(8,128)(2,1)S(1)} async-done(((bf16[16,32,128]{2,1,0:T(8,128)(2,1)}), bf16[16,32,128]{2,1,0:T(8,128)(2,1)S(1)}, u32[]{:S(2)}, u32[]{:S(2)}) %all-to-all-start.3) | async-done | bytes 131104 | tf_op jit(solution)/shard_map/all_to_all | solution.py:145
  81.9 0.7 copy-done.10
  82.5 2.2 shard_map.178
  84.7 9.0 %shard_map.179 = (bf16[32,128,256]{2,1,0:T(8,128)(2,1)}, f32[32,1,256]{2,1,0:T(1,128)}, f32[32,1,256]{2,1,0:T(1,128)}, bf16[32,128,256]{2,1,0:T(8,128)(2,1)}, bf16[8,32,32,256]{3,2,1,0:T(8,128)(2,1)}) custom-call(s32[1]{0:T(128)} %bitcast.10.stays, bf16[32,256,128]{2,1,0:T(8,128)(2,1)} %collective-permute-done.pair, bf16[32,256,128]{2,1,0:T(8,128)(2,1)} %bitcast.45, ...), custom_call_target="tpu_custom_call" | custom-call | flops 1073741824 | bytes 4616196 | tf_op jit(solution)/shard_map/pallas_call | solution.py:306
  93.8 4.7 all-to-all-start.4
  98.5 0.8 collective-permute-start.1
  99.3 1.5 broadcast_select_fusion.1.cot
  100.8 45.4 %all-to-all-done.4.refs_0_.refs_1_.refs_2_ = bf16[8,32,32,256]{3,2,1,0:T(8,128)(2,1)} async-done(((bf16[8,32,32,256]{3,2,1,0:T(8,128)(2,1)}), bf16[8,32,32,256]{3,2,1,0:T(8,128)(2,1)}, u32[]{:S(2)}, u32[]{:S(2)}) %all-to-all-start.4) | async-done | bytes 4194336 | tf_op jit(solution)/shard_map/all_to_all | solution.py:145
  146.2 3.6 shard_map.180
  149.8 53.8 %all_to_all.97 = bf16[8,16,32,256]{3,2,1,0:T(8,128)(2,1)} all-to-all(bf16[8,16,32,256]{3,2,1,0:T(8,128)(2,1)} %shard_map.180), channel_id=1, replica_groups={{0,1,2,3,10,11,8,9},{6,7,4,5,12,13,14,15},{16,17,18,19,26,27,24,25},{22..., dimensions={0} | all-to-all | bytes 4194304 | tf_op jit(solution)/shard_map/all_to_all | solution.py:145
  203.6 9.9 %shard_map.181 = (bf16[32,128,256]{2,1,0:T(8,128)(2,1)}, f32[32,1,256]{2,1,0:T(1,128)}, f32[32,1,256]{2,1,0:T(1,128)}, bf16[32,128,256]{2,1,0:T(8,128)(2,1)}, bf16[8,32,32,256]{3,2,1,0:T(8,128)(2,1)}) custom-call(bf16[128,32,256]{2,1,0:T(8,128)(2,1)} %bitcast.49, bf16[32,128,256]{2,1,0:T(8,128)(2,1)} %get-tuple-element.134.x_in.x_after, ...), custom_call_target="tpu_custom_call" | custom-call | flops 1342177280 | bytes 6467584 | tf_op jit(solution)/shard_map/pallas_call | solution.py:306
  213.5 53.2 %all_to_all.98.refs_0_.refs_1_.refs_2_.refs_3_ = bf16[8,32,32,256]{3,2,1,0:T(8,128)(2,1)} all-to-all(bf16[8,32,32,256]{3,2,1,0:T(8,128)(2,1)} %get-tuple-element.138), channel_id=1, replica_groups={{0,1,2,3,10,11,8,9},{6,7,4,5,12,13,14,15},{16,17,18,19,26,27,24,25},{22..., dimensions={0} | all-to-all | bytes 8388608 | tf_op jit(solution)/shard_map/all_to_all | solution.py:145
  266.7 3.7 shard_map.182
  270.4 19.2 %all_to_all.99 = bf16[8,16,16,256]{3,2,1,0:T(8,128)(2,1)} all-to-all(bf16[8,16,16,256]{3,2,1,0:T(8,128)(2,1)} %get-tuple-element.139), channel_id=1, replica_groups={{0,1,2,3,10,11,8,9},{6,7,4,5,12,13,14,15},{16,17,18,19,26,27,24,25},{22..., dimensions={0} | all-to-all | bytes 2097152 | tf_op jit(solution)/shard_map/all_to_all | solution.py:145
  289.7 3.7 all-to-all-start.9
  293.4 17.0 %shard_map.183 = (bf16[32,256,128]{2,1,0:T(8,128)(2,1)}, bf16[32,128,256]{2,1,0:T(8,128)(2,1)}, bf16[32,128,256]{2,1,0:T(8,128)(2,1)}, bf16[128,16,256]{2,1,0:T(...) custom-call(bf16[128,16,256]{2,1,0:T(8,128)(2,1)} %bitcast.64, ...), custom_call_target="tpu_custom_call" | custom-call | flops 4294967296 | bytes 7647232 | tf_op jit(solution)/shard_map/pallas_call | solution.py:306
  310.5 4.4 all-to-all-start.8
  314.9 17.3 %shard_map.184 = (bf16[32,256,128]{2,1,0:T(8,128)(2,1)}, bf16[32,128,256]{2,1,0:T(8,128)(2,1)}, bf16[32,128,256]{2,1,0:T(8,128)(2,1)}, bf16[128,16,256]{2,1,0:T(...) custom-call(bf16[128,16,256]{2,1,0:T(8,128)(2,1)} %bitcast.61, ...), custom_call_target="tpu_custom_call", output_to_operand_aliasing={{0}: (8, {}), {1}: (9, {}), {2}: (10, {})} | custom-call | flops 4294967296 | bytes 14530048 | tf_op jit(solution)/shard_map/pallas_call | solution.py:306
  332.2 19.3 %all_to_all.100.refs_1_ = bf16[8,16,16,256]{3,2,1,0:T(8,128)(2,1)} all-to-all(bf16[8,16,16,256]{3,2,1,0:T(8,128)(2,1)} %bitcast.63), channel_id=1, replica_groups={{0,1,2,3,10,11,8,9},{6,7,4,5,12,13,14,15},{16,17,18,19,26,27,24,25},{22..., dimensions={0} | all-to-all | bytes 2097152 | tf_op jit(solution)/shard_map/all_to_all | solution.py:145
  351.6 4.9 shard_map.185
  356.5 4.7 all-to-all-start.11
  361.2 0.8 collective-permute-start.2
  362.0 1.5 broadcast_select_fusion
  363.5 45.4 %all-to-all-done.11.sides_grad = bf16[8,32,32,256]{3,2,1,0:T(8,128)(2,1)} async-done(((bf16[8,32,32,256]{3,2,1,0:T(8,128)(2,1)}), bf16[8,32,32,256]{3,2,1,0:T(8,128)(2,1)}, u32[]{:S(2)}, u32[]{:S(2)}) %all-to-all-start.11) | async-done | bytes 4194336 | tf_op jit(solution)/shard_map/all_to_all | solution.py:145
  408.9 14.8 %shard_map.186 = (bf16[32,128,256]{2,1,0:T(8,128)(2,1)}, bf16[32,128,256]{2,1,0:T(8,128)(2,1)}, bf16[128,32,256]{2,1,0:T(8,128)(2,1)}, f32[128,384]{1,0:T(8,128)...) custom-call(bf16[8,32,32,256]{3,2,1,0:T(8,128)(2,1)} %all-to-all-done.11.sides_grad, ...), custom_call_target="tpu_custom_call" | custom-call | flops 3221225472 | bytes 14921728 | tf_op jit(solution)/shard_map/pallas_call | solution.py:306
  423.7 54.9 %all_to_all.101.refs_0_ = bf16[8,16,32,256]{3,2,1,0:T(8,128)(2,1)} all-to-all(bf16[8,16,32,256]{3,2,1,0:T(8,128)(2,1)} %bitcast.59), channel_id=1, replica_groups={{0,1,2,3,10,11,8,9},{6,7,4,5,12,13,14,15},{16,17,18,19,26,27,24,25},{22..., dimensions={0} | all-to-all | bytes 4194304 | tf_op jit(solution)/shard_map/all_to_all | solution.py:145
  478.6 4.8 shard_map.187
  483.5 53.4 %all_to_all.102.sides_grad = bf16[8,32,32,256]{3,2,1,0:T(8,128)(2,1)} all-to-all(bf16[8,32,32,256]{3,2,1,0:T(8,128)(2,1)} %bitcast.52), channel_id=1, replica_groups={{0,1,2,3,10,11,8,9},{6,7,4,5,12,13,14,15},{16,17,18,19,26,27,24,25},{22..., dimensions={0} | all-to-all | bytes 8388608 | tf_op jit(solution)/shard_map/all_to_all | solution.py:145
  536.9 10.4 %shard_map.188 = (bf16[32,256,128]{2,1,0:T(8,128)(2,1)}, f32[2,32,32,128]{3,2,1,0:T(8,128)}, f32[32,256]{1,0:T(8,128)}, f32[128,384]{1,0:T(8,128)}, f32[128,1]{1,0:T(8,128)}) custom-call(bf16[8,32,32,256]{3,2,1,0:T(8,128)(2,1)} %all_to_all.102.sides_grad, bf16[32,128,256]{2,1,0:T(8,128)(2,1)} %get-tuple-element.134.x_in.x_after, ...), custom_call_target="tpu_custom_call" | custom-call | flops 2147483648 | bytes 10973184 | tf_op jit(solution)/shard_map/pallas_call | solution.py:306
  547.4 3.2 shard_map.189
  550.6 11.8 %all_to_all.103.factor_ref = bf16[16,32,128]{2,1,0:T(8,128)(2,1)} all-to-all(bf16[16,32,128]{2,1,0:T(8,128)(2,1)} %bitcast.69), channel_id=1, replica_groups={{0,1,2,3,4,5,6,7,8,9,10,11,12,13,14,15},{16,17,18,19,20,21,22,23,24,25,..., dimensions={0} | all-to-all | bytes 262144 | tf_op jit(solution)/shard_map/all_to_all | solution.py:145
  562.4 2.1 collective-permute-start.3
  565.1 3.9 shard_map.190
  568.9 1.3 convolution_bitcast_fusion
  570.3 0.7 reshape.94.refs_0_
  571.0 4.7 shard_map.191
  575.7 7.6 %all_to_all.104 = bf16[2,2,8,304,128]{4,3,2,1,0:T(8,128)(2,1)S(1)} all-to-all(bf16[2,2,8,304,128]{4,3,2,1,0:T(8,128)(2,1)} %get-tuple-element.212), channel_id=1, replica_groups={{0,8},{1,9},{2,10},{3,11},{4,12},{5,13},{6,14},{7,15},{16,24},{17,25},{..., dimensions={0} | all-to-all | bytes 4980736 | tf_op jit(solution)/shard_map/all_to_all | solution.py:145
  583.3 1.8 reduce_sum.51
  585.1 20.0 %all_to_all.105 = bf16[2,8,304,128]{3,2,1,0:T(8,128)(2,1)S(1)} all-to-all(bf16[2,8,304,128]{3,2,1,0:T(8,128)(2,1)} %reduce_sum.51), channel_id=1, replica_groups={{0,16},{1,17},{2,18},{3,19},{4,20},{5,21},{6,22},{7,23},{8,24},{9,25},{..., dimensions={0} | all-to-all | bytes 2490368 | tf_op jit(solution)/shard_map/all_to_all | solution.py:145
  605.6 0.9 pad_maximum_fusion
  606.5 4.1 all-to-all-start.17
  610.8 4.1 add_convert_fusion
  614.9 14.6 %all-to-all-done.17 = bf16[8,368,128]{2,1,0:T(8,128)(2,1)S(1)} async-done(((bf16[8,368,128]{2,1,0:T(8,128)(2,1)}), bf16[8,368,128]{2,1,0:T(8,128)(2,1)S(1)}, u32[]{:S(2)}, u32[]{:S(2)}) %all-to-all-start.17) | async-done | bytes 753696 | tf_op jit(solution)/shard_map/all_to_all | solution.py:145
  629.7 0.7 multiply_reduce_fusion
  631.7 2.7 all-to-all-start.18
  635.0 6.6 %all-to-all-done.18 = f32[32,2,128]{2,1,0:T(2,128)S(1)} async-done(((f32[32,2,128]{2,1,0:T(2,128)}), f32[32,2,128]{2,1,0:T(2,128)S(1)}, u32[]{:S(2)}, u32[]{:S(2)}) %all-to-all-start.18) | async-done | bytes 32800 | tf_op jit(solution)/shard_map/all_to_all | solution.py:145
  643.4 0.9 fusion.18
  (65 shorter events, 5.1 us)
Async XLA Ops:
  0.6 29.4 %copy-start = (bf16[1,32,256,128]{3,2,1,0:T(8,128)(2,1)S(1)}, bf16[1,32,256,128]{3,2,1,0:T(8,128)(2,1)}, u32[]{:S(2)}) copy-start(bf16[1,32,256,128]{3,2,1,0:T(8,128)(2,1)} %param.10) | copy-start | bytes 6291460
  30.0 2.1 copy-start.3
  30.0 54.7 %collective-permute-start = (bf16[32,256,128]{2,1,0:T(8,128)(2,1)S(1)}, bf16[32,256,128]{2,1,0:T(8,128)(2,1)}, u32[]{:S(2)}, u32[]{:S(2)}) collective-permute-start(bf16[32,256,128]{2,1,0:T(8,128)(2,1)S(1)} %bitcast.46), channel_id=1, source_target_pairs={{4,10},{5,11},{6,8},{7,9},{8,6},{9,7},{10,4},{11,5},{20,26},{21,27... | collective-permute-start | bytes 6291464 | tf_op jit(solution)/shard_map/ppermute | solution.py:953
  32.1 5.4 copy-start.18
  33.2 20.6 %all-to-all-start.1 = ((bf16[2,2432,128]{2,1,0:T(8,128)(2,1)}), bf16[2,2432,128]{2,1,0:T(8,128)(2,1)S(1)}, u32[]{:S(2)}, u32[]{:S(2)}) async-start(bf16[2,2432,128]{2,1,0:T(8,128)(2,1)} %broadcast_in_dim.59), calls=%async_computation.1 | async-start | bytes 2490368 | tf_op jit(solution)/shard_map/all_to_all | solution.py:145
  37.5 23.3 %copy-start.17 = (f32[1,256]{1,0:T(1,128)}, f32[1,256]{1,0:T(1,128)S(1)}, u32[]{:S(2)}) copy-start(f32[1,256]{1,0:T(1,128)S(1)} %convert_element_type.27.keep) | copy-start | bytes 3076
  70.7 11.1 %all-to-all-start.3 = ((bf16[16,32,128]{2,1,0:T(8,128)(2,1)}), bf16[16,32,128]{2,1,0:T(8,128)(2,1)S(1)}, u32[]{:S(2)}, u32[]{:S(2)}) async-start(bf16[16,32,128]{2,1,0:T(8,128)(2,1)} %get-tuple-element.124), calls=%async_computation.3 | async-start | bytes 262144 | tf_op jit(solution)/shard_map/all_to_all | solution.py:145
  81.9 0.7 copy-start.10
  93.8 4.7 copy-start.4
  93.8 52.5 %all-to-all-start.4 = ((bf16[8,32,32,256]{3,2,1,0:T(8,128)(2,1)}), bf16[8,32,32,256]{3,2,1,0:T(8,128)(2,1)}, u32[]{:S(2)}, u32[]{:S(2)}) async-start(bf16[8,32,32,256]{3,2,1,0:T(8,128)(2,1)} %get-tuple-element.131), calls=%async_computation.4 | async-start | bytes 8388608 | tf_op jit(solution)/shard_map/all_to_all | solution.py:145
  98.5 0.8 collective-permute-start.1
  289.7 20.8 %all-to-all-start.9 = ((bf16[8,16,16,256]{3,2,1,0:T(8,128)(2,1)}), bf16[8,16,16,256]{3,2,1,0:T(8,128)(2,1)S(1)}, u32[]{:S(2)}, u32[]{:S(2)}) async-start(bf16[8,16,16,256]{3,2,1,0:T(8,128)(2,1)} %get-tuple-element.147), calls=%async_computation.9 | async-start | bytes 2097152 | tf_op jit(solution)/shard_map/all_to_all | solution.py:145
  310.5 4.4 copy-start.6
  310.5 21.7 %all-to-all-start.8 = ((bf16[8,16,16,256]{3,2,1,0:T(8,128)(2,1)}), bf16[8,16,16,256]{3,2,1,0:T(8,128)(2,1)S(1)}, u32[]{:S(2)}, u32[]{:S(2)}) async-start(bf16[8,16,16,256]{3,2,1,0:T(8,128)(2,1)} %bitcast.62), calls=%async_computation.8 | async-start | bytes 2097152 | tf_op jit(solution)/shard_map/all_to_all | solution.py:145
  332.2 19.4 %copy-start.2 = (bf16[8,16,16,256]{3,2,1,0:T(8,128)(2,1)}, bf16[8,16,16,256]{3,2,1,0:T(8,128)(2,1)S(1)}, u32[]{:S(2)}) copy-start(bf16[8,16,16,256]{3,2,1,0:T(8,128)(2,1)S(1)} %all-to-all-done.8.refs_0_) | copy-start | bytes 3145732
  356.5 4.7 copy-start.5
  356.5 52.5 %all-to-all-start.11 = ((bf16[8,32,32,256]{3,2,1,0:T(8,128)(2,1)}), bf16[8,32,32,256]{3,2,1,0:T(8,128)(2,1)}, u32[]{:S(2)}, u32[]{:S(2)}) async-start(bf16[8,32,32,256]{3,2,1,0:T(8,128)(2,1)} %bitcast.51), calls=%async_computation.11 | async-start | bytes 8388608 | tf_op jit(solution)/shard_map/all_to_all | solution.py:145
  361.2 0.8 collective-permute-start.2
  547.4 21.6 %copy-start.1 = (bf16[1,32,256,128]{3,2,1,0:T(8,128)(2,1)S(1)}, bf16[1,32,256,128]{3,2,1,0:T(8,128)(2,1)}, u32[]{:S(2)}) copy-start(bf16[1,32,256,128]{3,2,1,0:T(8,128)(2,1)} %param.10) | copy-start | bytes 6291460
  562.4 48.3 %collective-permute-start.3 = (bf16[32,256,128]{2,1,0:T(8,128)(2,1)}, bf16[32,256,128]{2,1,0:T(8,128)(2,1)}, u32[]{:S(2)}, u32[]{:S(2)}) collective-permute-start(bf16[32,256,128]{2,1,0:T(8,128)(2,1)} %get-tuple-element.214), channel_id=1, source_target_pairs={{4,10},{5,11},{6,8},{7,9},{8,6},{9,7},{10,4},{11,5},{20,26},{21,27... | collective-permute-start | bytes 6291464 | tf_op jit(solution)/shard_map/ppermute | solution.py:1092
  585.1 20.5 %copy-start.16 = (bf16[8,64,128]{2,1,0:T(8,128)(2,1)S(1)}, bf16[8,64,128]{2,1,0:T(8,128)(2,1)}, u32[]{:S(2)}) copy-start(bf16[8,64,128]{2,1,0:T(8,128)(2,1)} %get-tuple-element.213) | copy-start | bytes 393220
  605.1 5.5 copy-start.11
  605.1 5.7 copy-start.9
  605.1 5.7 copy-start.14
  606.5 23.0 %all-to-all-start.17 = ((bf16[8,368,128]{2,1,0:T(8,128)(2,1)}), bf16[8,368,128]{2,1,0:T(8,128)(2,1)S(1)}, u32[]{:S(2)}, u32[]{:S(2)}) async-start(bf16[8,368,128]{2,1,0:T(8,128)(2,1)} %pad_maximum_fusion), calls=%async_computation.17 | async-start | bytes 1507328 | tf_op jit(solution)/shard_map/all_to_all | solution.py:145
  610.7 23.7 %copy-start.15 = (f32[32,256]{1,0:T(8,128)S(1)}, f32[32,256]{1,0:T(8,128)}, u32[]{:S(2)}) copy-start(f32[32,256]{1,0:T(8,128)} %get-tuple-element.183.refs_21_) | copy-start | bytes 98308
  610.7 32.7 %copy-start.7 = (f32[37488]{0:T(1024)S(1)}, f32[37488]{0:T(1024)}, u32[]{:S(2)}) copy-start(f32[37488]{0:T(1024)} %param.15) | copy-start | bytes 449860
  610.7 32.7 %copy-start.12 = (f32[37488]{0:T(1024)S(1)}, f32[37488]{0:T(1024)}, u32[]{:S(2)}) copy-start(f32[37488]{0:T(1024)} %param.16) | copy-start | bytes 449860
  610.8 32.7 %copy-start.13 = (f32[37488]{0:T(1024)S(1)}, f32[37488]{0:T(1024)}, u32[]{:S(2)}) copy-start(f32[37488]{0:T(1024)} %param.17) | copy-start | bytes 449860
  630.4 13.9 %copy-start.8 = (f32[37488]{0:T(1024)}, f32[37488]{0:T(1024)S(1)}, u32[]{:S(2)}) copy-start(f32[37488]{0:T(1024)S(1)} %get-tuple-element.222) | copy-start | bytes 449860
  631.7 9.9 %all-to-all-start.18 = ((f32[32,2,128]{2,1,0:T(2,128)}), f32[32,2,128]{2,1,0:T(2,128)S(1)}, u32[]{:S(2)}, u32[]{:S(2)}) async-start(f32[32,2,128]{2,1,0:T(2,128)} %broadcast_in_dim.70), calls=%async_computation.18 | async-start | bytes 65536 | tf_op jit(solution)/shard_map/all_to_all | solution.py:145

commit v4 on v3

--- a/solution.py
+++ b/solution.py
@@ -120,6 +120,11 @@
             for here in range(self.devices)
             if here != self.work_place(here)
         ]
+        high_of = lambda here: here % rows // self.wide
+        self.near = [
+            (here, there) for here, there in self.moves if abs(high_of(here) - high_of(there)) == 1
+        ]
+        self.far = [move for move in self.moves if move not in self.near]
         self.groups = [
             [self.work_place(c * rows + r) for r in range(rows)] for c in range(crops)
         ]
@@ -929,7 +934,9 @@
     partner = layout.work_place(here)
     stays = partner == here
     work_crop, work_row = partner // ranks, partner % ranks
-    moved = lambda array: jnp.where(stays, array, lax.ppermute(array, BOTH, layout.moves))
+    near = lambda array: lax.ppermute(array, BOTH, layout.near)
+    far = lambda array: lax.ppermute(array, BOTH, layout.far)
+    settled = lambda own, close, *pieces: jnp.where(stays, own, close + jnp.concatenate(pieces))
 
     at, _ = first_rows()
 
@@ -974,7 +981,8 @@
     )
 
     factors = exchange(factors, BOTH, layout.slabs)
-    factors, pair_cot = lax.optimization_barrier((factors, pair_cot))
+    cot_first, cot_last = jnp.split(pair_cot, 2)
+    factors, cot_first, pair_plane = lax.optimization_barrier((factors, cot_first, pair_plane))
     everyone = jnp.arange(ranks, dtype=jnp.int32)
     slab = 2 * ranks
     sources = jnp.concatenate([partner[None], work_crop * ranks + everyone]).astype(jnp.int32) % slab
@@ -1013,13 +1021,18 @@
         (stays.astype(jnp.int32)[None], pair_plane, pair, table, right, mask_plane, vectors, w_out_all),
         "mnntcrww", front_outs, [buffer(2 * TRI_DIM)], 4 * unit,
     )
-    sides_out, cot_plane = lax.optimization_barrier((trade(sides), moved(pair_cot)))
+    sides, cot_first, pair_cot = lax.optimization_barrier((sides, far(cot_first), pair_cot))
+    sides_out, cot_near = lax.optimization_barrier((trade(sides), near(pair_cot)))
     mixed_out = merge(trade(mix(sides_out, False)[0]))
+    mixed_out, cot_last = lax.optimization_barrier((mixed_out, cot_last))
     x_two, mean_tri_in, scale_tri_in, gate_tri_in, sides = run(
         kernel_middle, step, extent,
         (mixed_out, x_one, gate_tri_out, mask_plane, vectors, w_out_end, w_in_all), "srrrwww", front_outs, [buffer(TRI_DIM), buffer(2 * TRI_DIM)], 5 * unit,
     )
-    sides_in = trade(sides)
+    sides, cot_last = lax.optimization_barrier((sides, far(cot_last)))
+    sides_in, cot_plane = lax.optimization_barrier(
+        (trade(sides), settled(pair_cot, cot_near, cot_first, cot_last))
+    )
     turns = 2 if local_rows % (2 * TILE) == 0 else 1
     turn_rows = local_rows // turns
     mixed_in = [merge(trade(piece)) for piece in mix(sides_in, True, turns)]
@@ -1038,10 +1051,16 @@
             skip=k * turn_rows // step[0], aliases={8: 0, 9: 1, 10: 2} if k else {},
         )
         turned = list(turned)
-        grads_in.append(trade(split(turned.pop(3))))
+        mixed_grad = turned.pop(3)
+        if k:
+            grads_in[-1], mixed_grad = lax.optimization_barrier((grads_in[-1], mixed_grad))
+        grads_in.append(trade(split(mixed_grad)))
     pair_final, x_grad, gate_grad, g_in_out, g_in_tri, g_up, g_down, g_pair, g_bias = turned
     sides_grad = trade(mix_back(grads_in, sides_in, True))
-    sides_grad, pair_out = lax.optimization_barrier((sides_grad, moved(pair_final)))
+    out_first, out_last = jnp.split(pair_final, 2)
+    sides_grad, out_near, out_first = lax.optimization_barrier(
+        (sides_grad, near(pair_final), out_first)
+    )
     x_grad, gate_grad, mixed_grad, g_in_all, g_in_gain, g_out_out, g_out_tri = run(
         kernel_return, step, extent,
         (sides_grad, x_two, mean_tri_in, scale_tri_in, gate_grad, x_grad, mask_plane,
@@ -1051,7 +1070,9 @@
          ("w", gain_shape, WIDE), ("w", square, WIDE), ("w", gain_shape, WIDE)),
         [buffer(2 * TRI_DIM), buffer(TRI_DIM), buffer(TRI_DIM)], 12 * unit,
     )
+    mixed_grad, out_first = lax.optimization_barrier((mixed_grad, far(out_first)))
     sides_grad = trade(mix_back([trade(split(mixed_grad))], sides_out, False))
+    sides_grad, out_last = lax.optimization_barrier((sides_grad, out_last))
     pair_one_grad, table_grad, right_part, g_out_all, g_out_gain = run(
         kernel_close, step, extent,
         (sides_grad, x_one, mean_tri_out, scale_tri_out, gate_grad, x_grad, mask_plane,
@@ -1069,6 +1090,8 @@
         [((2, ranks, local_rows, LANES), LOW), ((OUTER * OUTER, PAIR_DIM), WIDE)],
         [pltpu.VMEM((OUTER * OUTER, PAIR_DIM), WIDE), pltpu.VMEM((OUTER, local_rows, PAIR_DIM), WIDE)],
     )
+    factor_grads, out_last = lax.optimization_barrier((factor_grads, far(out_last)))
+    pair_out = settled(pair_final, out_near, out_first, out_last)
     factor_grads = exchange(factor_grads.reshape(slab, local_rows, LANES), BOTH, layout.slabs)
     factor_grads, pair_one_grad = lax.optimization_barrier((factor_grads, pair_one_grad))
 
@@ -1118,7 +1141,8 @@
     )
     total = lambda got: low_of(jnp.sum(got.astype(WIDE), axis=0))
     blocks = total(exchange(blocks, BOTH, layout.cores))
-    blocks = total(exchange(blocks, BOTH, layout.chips))
+    blocks, pair_out = lax.optimization_barrier((exchange(blocks, BOTH, layout.chips), pair_out))
+    blocks = total(blocks)
     blocks = exchange(jnp.concatenate([blocks, node_blocks], axis=1), "row")
     pair_grad = jnp.where(stays, pair_one_grad, pair_one_away).astype(WIDE) + jnp.einsum(
         "hij,dh->ijd", score_low, w_bias[:, :HEADS], preferred_element_type=WIDE

time: 655 us -> 630 us (0.962)
  blocking collectives: 326 us -> 214 us
  waiting for transfers between devices: 133 us -> 190 us
  starting transfers between devices: 37.1 us -> 59.2 us
    all_to_all x11 -> x9, blocking collectives: 326 us -> 214 us  [exchange(): lax.all_to_all(blocks, axes, 0, 0, axis_index_groups=groups, tiled=True)]
    all_to_all x8 -> x10, waiting for transfers between devices: 133 us -> 190 us  [exchange(): lax.all_to_all(blocks, axes, 0, 0, axis_index_groups=groups, tiled=True)]
    all_to_all x8 -> x10, starting transfers between devices: 31.4 us -> 46.2 us  [exchange(): lax.all_to_all(blocks, axes, 0, 0, axis_index_groups=groups, tiled=True)]
    ppermute x2 -> x6, starting transfers between devices: 1.59 us -> 8.99 us  [the longest x4 5 us: local(): far = lambda array: lax.ppermute(array, BOTH, layout.far)]
  transfers between devices with their start and end apart: 12 -> 18, of which waited for: 6 -> 8; matrix products, arithmetic and copies ran while one was open for 3% -> 5% of each run, Pallas kernels for 8% -> 16%
where the time goes in v4:
time: 630 us; the launch traced here: 620 us
  blocking collectives  214 us (34%)
  waiting for transfers between devices  190 us (30%)
  Pallas kernels  117 us (19%)
  starting transfers between devices  59.2 us (9%)
  other arithmetic  16.2 us (3%)
  local copies, waits for them, and re-layouts  13.9 us (2%)
    all_to_all x9, blocking collectives, exchange(): lax.all_to_all(blocks, axes, 0, 0, axis_index_groups=groups, tiled=True)  214 us
    all_to_all x10, waiting for transfers between devices, exchange(): lax.all_to_all(blocks, axes, 0, 0, axis_index_groups=groups, tiled=True)  190 us
    pallas_call x6, Pallas kernels, run(): pl.pallas_call(body, grid=(extent[1] // step[1], extent[0] // step[0]), i...  78.6 us
    all_to_all x10, starting transfers between devices, exchange(): lax.all_to_all(blocks, axes, 0, 0, axis_index_groups=groups, tiled=True)  46.2 us
    pallas_call x6, Pallas kernels, one_call(): pl.pallas_call(body, in_specs=[pl.BlockSpec(memory_space=pltpu.SMEM)] * l...  21.6 us
  transfers between devices with their start and end apart: 18, of which 8 were waited for; matrix products, arithmetic and copies ran while one was open for 5% of the time, Pallas kernels for 16%

profile of v4, /device:TPU:0, one launch (start us, length us, event | category | flops | bytes accessed | tf_op | source)
XLA Modules:
  0.0 620.3 jit_solution(13339124309174010890)
XLA Ops:
  0.7 0.9 reshape_squeeze.3
  1.6 0.9 convert_element_type.26
  2.5 0.8 dynamic_update_slice.3
  3.5 26.5 %all_to_all.95 = bf16[8,368,128]{2,1,0:T(8,128)(2,1)S(1)} all-to-all(bf16[8,368,128]{2,1,0:T(8,128)(2,1)S(1)} %broadcast_in_dim.57), channel_id=1, replica_groups=mesh['crop'=4,'row'=8] {'row'}, dimensions={0} | all-to-all | bytes 1507328 | tf_op jit(solution)/shard_map/all_to_all | solution.py:150
  30.0 2.0 collective-permute-start
  32.0 1.1 broadcast_in_dim.59
  33.2 3.6 all-to-all-start.1
  38.2 1.6 slice.24
  39.8 13.9 %all-to-all-done.1 = bf16[2,2432,128]{2,1,0:T(8,128)(2,1)S(1)} async-done(((bf16[2,2432,128]{2,1,0:T(8,128)(2,1)}), bf16[2,2432,128]{2,1,0:T(8,128)(2,1)S(1)}, u32[]{:S(2)}, u32[]{:S(2)}) %all-to-all-start.1) | async-done | bytes 1245216 | tf_op jit(solution)/shard_map/all_to_all | solution.py:150
  54.0 6.7 %all_to_all.96 = bf16[2,2,2432,128]{3,2,1,0:T(8,128)(2,1)} all-to-all(bf16[2,2,2432,128]{3,2,1,0:T(8,128)(2,1)S(1)} %broadcast_in_dim.60), channel_id=1, replica_groups={{0,8},{1,9},{2,10},{3,11},{4,12},{5,13},{6,14},{7,15},{16,24},{17,25},{..., dimensions={0} | all-to-all | bytes 4980736 | tf_op jit(solution)/shard_map/all_to_all | solution.py:150
  60.7 3.5 shard_map.176
  64.1 1.4 fusion.10
  66.4 4.2 shard_map.177
  70.6 3.5 all-to-all-start.3
  74.2 3.1 slice_bitcast_fusion
  77.3 4.6 all-to-all-done.3.factors
  83.4 2.2 shard_map.178
  85.6 9.0 %shard_map.179 = (bf16[32,128,256]{2,1,0:T(8,128)(2,1)}, f32[32,1,256]{2,1,0:T(1,128)}, f32[32,1,256]{2,1,0:T(1,128)}, bf16[32,128,256]{2,1,0:T(8,128)(2,1)}, bf16[8,32,32,256]{3,2,1,0:T(8,128)(2,1)}) custom-call(s32[1]{0:T(128)} %bitcast.12.stays, bf16[32,256,128]{2,1,0:T(8,128)(2,1)} %collective-permute-done.pair, bf16[32,256,128]{2,1,0:T(8,128)(2,1)} %bitcast.49, ...), custom_call_target="tpu_custom_call" | custom-call | flops 1073741824 | bytes 4616196 | tf_op jit(solution)/shard_map/pallas_call | solution.py:311
  94.7 7.8 %all-to-all-start.4 = ((bf16[8,32,32,256]{3,2,1,0:T(8,128)(2,1)}), bf16[8,32,32,256]{3,2,1,0:T(8,128)(2,1)}, u32[]{:S(2)}, u32[]{:S(2)}) async-start(bf16[8,32,32,256]{3,2,1,0:T(8,128)(2,1)} %get-tuple-element.155), calls=%async_computation.4 | async-start | bytes 8388608 | tf_op jit(solution)/shard_map/all_to_all | solution.py:150
  102.5 2.0 collective-permute-start.2
  104.5 46.8 %all-to-all-done.4.refs_0_.refs_1_.refs_2_ = bf16[8,32,32,256]{3,2,1,0:T(8,128)(2,1)} async-done(((bf16[8,32,32,256]{3,2,1,0:T(8,128)(2,1)}), bf16[8,32,32,256]{3,2,1,0:T(8,128)(2,1)}, u32[]{:S(2)}, u32[]{:S(2)}) %all-to-all-start.4) | async-done | bytes 4194336 | tf_op jit(solution)/shard_map/all_to_all | solution.py:150
  151.3 3.6 shard_map.180
  154.9 30.7 %all_to_all.97 = bf16[8,16,32,256]{3,2,1,0:T(8,128)(2,1)} all-to-all(bf16[8,16,32,256]{3,2,1,0:T(8,128)(2,1)} %shard_map.180), channel_id=1, replica_groups={{0,1,2,3,10,11,8,9},{6,7,4,5,12,13,14,15},{16,17,18,19,26,27,24,25},{22..., dimensions={0} | all-to-all | bytes 4194304 | tf_op jit(solution)/shard_map/all_to_all | solution.py:150
  185.6 1.6 collective-permute-start.3
  187.3 10.0 %shard_map.181 = (bf16[32,128,256]{2,1,0:T(8,128)(2,1)}, f32[32,1,256]{2,1,0:T(1,128)}, f32[32,1,256]{2,1,0:T(1,128)}, bf16[32,128,256]{2,1,0:T(8,128)(2,1)}, bf16[8,32,32,256]{3,2,1,0:T(8,128)(2,1)}) custom-call(bf16[128,32,256]{2,1,0:T(8,128)(2,1)} %bitcast.53, bf16[32,128,256]{2,1,0:T(8,128)(2,1)} %get-tuple-element.159.x_in.x_after, ...), custom_call_target="tpu_custom_call" | custom-call | flops 1342177280 | bytes 6467584 | tf_op jit(solution)/shard_map/pallas_call | solution.py:311
  197.2 8.0 %all-to-all-start.6 = ((bf16[8,32,32,256]{3,2,1,0:T(8,128)(2,1)}), bf16[8,32,32,256]{3,2,1,0:T(8,128)(2,1)}, u32[]{:S(2)}, u32[]{:S(2)}) async-start(bf16[8,32,32,256]{3,2,1,0:T(8,128)(2,1)} %get-tuple-element.165), calls=%async_computation.6 | async-start | bytes 8388608 | tf_op jit(solution)/shard_map/all_to_all | solution.py:150
  205.3 3.5 fusion.cot
  208.7 45.4 %all-to-all-done.6.refs_0_.refs_1_.refs_2_.refs_3_ = bf16[8,32,32,256]{3,2,1,0:T(8,128)(2,1)} async-done(((bf16[8,32,32,256]{3,2,1,0:T(8,128)(2,1)}), bf16[8,32,32,256]{3,2,1,0:T(8,128)(2,1)}, u32[]{:S(2)}, u32[]{:S(2)}) %all-to-all-start.6) | async-done | bytes 4194336 | tf_op jit(solution)/shard_map/all_to_all | solution.py:150
  254.1 3.7 shard_map.182
  257.8 19.2 %all_to_all.98 = bf16[8,16,16,256]{3,2,1,0:T(8,128)(2,1)} all-to-all(bf16[8,16,16,256]{3,2,1,0:T(8,128)(2,1)} %get-tuple-element.170), channel_id=1, replica_groups={{0,1,2,3,10,11,8,9},{6,7,4,5,12,13,14,15},{16,17,18,19,26,27,24,25},{22..., dimensions={0} | all-to-all | bytes 2097152 | tf_op jit(solution)/shard_map/all_to_all | solution.py:150
  277.0 3.7 all-to-all-start.9
  280.7 17.0 %shard_map.183 = (bf16[32,256,128]{2,1,0:T(8,128)(2,1)}, bf16[32,128,256]{2,1,0:T(8,128)(2,1)}, bf16[32,128,256]{2,1,0:T(8,128)(2,1)}, bf16[128,16,256]{2,1,0:T(...) custom-call(bf16[128,16,256]{2,1,0:T(8,128)(2,1)} %bitcast.68, ...), custom_call_target="tpu_custom_call" | custom-call | flops 4294967296 | bytes 7647232 | tf_op jit(solution)/shard_map/pallas_call | solution.py:311
  297.8 4.4 all-to-all-start.8
  302.2 17.4 %shard_map.184 = (bf16[32,256,128]{2,1,0:T(8,128)(2,1)}, bf16[32,128,256]{2,1,0:T(8,128)(2,1)}, bf16[32,128,256]{2,1,0:T(8,128)(2,1)}, bf16[128,16,256]{2,1,0:T(...) custom-call(bf16[128,16,256]{2,1,0:T(8,128)(2,1)} %bitcast.65, ...), custom_call_target="tpu_custom_call", output_to_operand_aliasing={{0}: (8, {}), {1}: (9, {}), {2}: (10, {})} | custom-call | flops 4294967296 | bytes 14530048 | tf_op jit(solution)/shard_map/pallas_call | solution.py:311
  319.6 19.3 %all_to_all.99.refs_1_ = bf16[8,16,16,256]{3,2,1,0:T(8,128)(2,1)} all-to-all(bf16[8,16,16,256]{3,2,1,0:T(8,128)(2,1)} %bitcast.67), channel_id=1, replica_groups={{0,1,2,3,10,11,8,9},{6,7,4,5,12,13,14,15},{16,17,18,19,26,27,24,25},{22..., dimensions={0} | all-to-all | bytes 2097152 | tf_op jit(solution)/shard_map/all_to_all | solution.py:150
  338.9 4.9 shard_map.185
  343.8 4.7 all-to-all-start.11
  348.5 2.0 collective-permute-start.4
  350.5 1.2 fusion.22
  351.7 44.6 %all-to-all-done.11.sides_grad = bf16[8,32,32,256]{3,2,1,0:T(8,128)(2,1)} async-done(((bf16[8,32,32,256]{3,2,1,0:T(8,128)(2,1)}), bf16[8,32,32,256]{3,2,1,0:T(8,128)(2,1)}, u32[]{:S(2)}, u32[]{:S(2)}) %all-to-all-start.11) | async-done | bytes 4194336 | tf_op jit(solution)/shard_map/all_to_all | solution.py:150
  397.0 14.8 %shard_map.186 = (bf16[32,128,256]{2,1,0:T(8,128)(2,1)}, bf16[32,128,256]{2,1,0:T(8,128)(2,1)}, bf16[128,32,256]{2,1,0:T(8,128)(2,1)}, f32[128,384]{1,0:T(8,128)...) custom-call(bf16[8,32,32,256]{3,2,1,0:T(8,128)(2,1)} %all-to-all-done.11.sides_grad, ...), custom_call_target="tpu_custom_call" | custom-call | flops 3221225472 | bytes 14921728 | tf_op jit(solution)/shard_map/pallas_call | solution.py:311
  411.9 35.4 %all_to_all.100.refs_0_ = bf16[8,16,32,256]{3,2,1,0:T(8,128)(2,1)} all-to-all(bf16[8,16,32,256]{3,2,1,0:T(8,128)(2,1)} %bitcast.62), channel_id=1, replica_groups={{0,1,2,3,10,11,8,9},{6,7,4,5,12,13,14,15},{16,17,18,19,26,27,24,25},{22..., dimensions={0} | all-to-all | bytes 4194304 | tf_op jit(solution)/shard_map/all_to_all | solution.py:150
  447.3 4.9 shard_map.187
  452.2 53.2 %all_to_all.101.sides_grad = bf16[8,32,32,256]{3,2,1,0:T(8,128)(2,1)} all-to-all(bf16[8,32,32,256]{3,2,1,0:T(8,128)(2,1)} %bitcast.56), channel_id=1, replica_groups={{0,1,2,3,10,11,8,9},{6,7,4,5,12,13,14,15},{16,17,18,19,26,27,24,25},{22..., dimensions={0} | all-to-all | bytes 8388608 | tf_op jit(solution)/shard_map/all_to_all | solution.py:150
  505.4 1.9 collective-permute-start.6
  507.3 10.4 %shard_map.188 = (bf16[32,256,128]{2,1,0:T(8,128)(2,1)}, f32[2,32,32,128]{3,2,1,0:T(8,128)}, f32[32,256]{1,0:T(8,128)}, f32[128,384]{1,0:T(8,128)}, f32[128,1]{1,0:T(8,128)}) custom-call(bf16[8,32,32,256]{3,2,1,0:T(8,128)(2,1)} %all_to_all.101.sides_grad, bf16[32,128,256]{2,1,0:T(8,128)(2,1)} %get-tuple-element.159.x_in.x_after, ...), custom_call_target="tpu_custom_call" | custom-call | flops 2147483648 | bytes 10973184 | tf_op jit(solution)/shard_map/pallas_call | solution.py:311
  517.7 3.2 shard_map.189
  521.0 14.9 %all_to_all.102.factor_ref = bf16[16,32,128]{2,1,0:T(8,128)(2,1)} all-to-all(bf16[16,32,128]{2,1,0:T(8,128)(2,1)} %bitcast.73), channel_id=1, replica_groups={{0,1,2,3,4,5,6,7,8,9,10,11,12,13,14,15},{16,17,18,19,20,21,22,23,24,25,..., dimensions={0} | all-to-all | bytes 262144 | tf_op jit(solution)/shard_map/all_to_all | solution.py:150
  535.9 2.0 collective-permute-start.7
  538.5 3.8 shard_map.190
  542.4 1.3 convolution_bitcast_fusion
  544.5 4.6 shard_map.191
  549.1 7.6 %all_to_all.103 = bf16[2,2,8,304,128]{4,3,2,1,0:T(8,128)(2,1)S(1)} all-to-all(bf16[2,2,8,304,128]{4,3,2,1,0:T(8,128)(2,1)} %get-tuple-element.249), channel_id=1, replica_groups={{0,8},{1,9},{2,10},{3,11},{4,12},{5,13},{6,14},{7,15},{16,24},{17,25},{..., dimensions={0} | all-to-all | bytes 4980736 | tf_op jit(solution)/shard_map/all_to_all | solution.py:150
  556.8 1.8 reduce_sum.51
  558.6 3.7 all-to-all-start.16
  562.3 3.8 fusion.1
  566.1 12.5 %all-to-all-done.16 = bf16[2,8,304,128]{3,2,1,0:T(8,128)(2,1)S(1)} async-done(((bf16[2,8,304,128]{3,2,1,0:T(8,128)(2,1)}), bf16[2,8,304,128]{3,2,1,0:T(8,128)(2,1)S(1)}, u32[]{:S(2)}, u32[]{:S(2)}) %all-to-all-start.16) | async-done | bytes 1245216 | tf_op jit(solution)/shard_map/all_to_all | solution.py:150
  579.1 2.0 pad_maximum_fusion
  581.1 4.0 all-to-all-start.17
  585.3 3.3 add_convert_fusion
  588.6 15.5 %all-to-all-done.17 = bf16[8,368,128]{2,1,0:T(8,128)(2,1)S(1)} async-done(((bf16[8,368,128]{2,1,0:T(8,128)(2,1)}), bf16[8,368,128]{2,1,0:T(8,128)(2,1)S(1)}, u32[]{:S(2)}, u32[]{:S(2)}) %all-to-all-start.17) | async-done | bytes 753696 | tf_op jit(solution)/shard_map/all_to_all | solution.py:150
  606.2 2.7 all-to-all-start.18
  609.5 6.6 %all-to-all-done.18 = f32[32,2,128]{2,1,0:T(2,128)S(1)} async-done(((f32[32,2,128]{2,1,0:T(2,128)}), f32[32,2,128]{2,1,0:T(2,128)S(1)}, u32[]{:S(2)}, u32[]{:S(2)}) %all-to-all-start.18) | async-done | bytes 32800 | tf_op jit(solution)/shard_map/all_to_all | solution.py:150
  617.9 0.9 fusion.20
  (81 shorter events, 10.1 us)
Async XLA Ops:
  0.6 29.4 %copy-start = (bf16[1,32,256,128]{3,2,1,0:T(8,128)(2,1)S(1)}, bf16[1,32,256,128]{3,2,1,0:T(8,128)(2,1)}, u32[]{:S(2)}) copy-start(bf16[1,32,256,128]{3,2,1,0:T(8,128)(2,1)} %param.10) | copy-start | bytes 6291460
  30.0 2.0 copy-start.6
  30.0 51.9 %collective-permute-start = (bf16[32,256,128]{2,1,0:T(8,128)(2,1)S(1)}, bf16[32,256,128]{2,1,0:T(8,128)(2,1)}, u32[]{:S(2)}, u32[]{:S(2)}) collective-permute-start(bf16[32,256,128]{2,1,0:T(8,128)(2,1)S(1)} %bitcast.50), channel_id=1, source_target_pairs={{4,10},{5,11},{6,8},{7,9},{8,6},{9,7},{10,4},{11,5},{20,26},{21,27... | collective-permute-start | bytes 6291464 | tf_op jit(solution)/shard_map/ppermute | solution.py:960
  32.0 5.4 copy-start.20
  33.2 20.5 %all-to-all-start.1 = ((bf16[2,2432,128]{2,1,0:T(8,128)(2,1)}), bf16[2,2432,128]{2,1,0:T(8,128)(2,1)S(1)}, u32[]{:S(2)}, u32[]{:S(2)}) async-start(bf16[2,2432,128]{2,1,0:T(8,128)(2,1)} %broadcast_in_dim.59), calls=%async_computation.1 | async-start | bytes 2490368 | tf_op jit(solution)/shard_map/all_to_all | solution.py:150
  37.4 23.2 %copy-start.19 = (f32[1,256]{1,0:T(1,128)}, f32[1,256]{1,0:T(1,128)S(1)}, u32[]{:S(2)}) copy-start(f32[1,256]{1,0:T(1,128)S(1)} %convert_element_type.27.keep) | copy-start | bytes 3076
  70.6 11.2 %all-to-all-start.3 = ((bf16[16,32,128]{2,1,0:T(8,128)(2,1)}), bf16[16,32,128]{2,1,0:T(8,128)(2,1)S(1)}, u32[]{:S(2)}, u32[]{:S(2)}) async-start(bf16[16,32,128]{2,1,0:T(8,128)(2,1)} %get-tuple-element.145), calls=%async_computation.3 | async-start | bytes 262144 | tf_op jit(solution)/shard_map/all_to_all | solution.py:150
  81.9 1.6 copy-start.14
  81.9 12.8 %collective-permute-start.1 = (bf16[16,256,128]{2,1,0:T(8,128)(2,1)}, bf16[16,256,128]{2,1,0:T(8,128)(2,1)S(1)}, u32[]{:S(2)}, u32[]{:S(2)}) collective-permute-start(bf16[16,256,128]{2,1,0:T(8,128)(2,1)} %get-tuple-element.154), channel_id=1, source_target_pairs={{6,8},{7,9},{8,6},{9,7},{22,24},{23,25},{24,22},{25,23}} | collective-permute-start | bytes 3145736 | tf_op jit(solution)/shard_map/ppermute | solution.py:938
  94.6 7.8 %copy-start.2 = (bf16[1,32,256,128]{3,2,1,0:T(8,128)(2,1)S(1)}, bf16[1,32,256,128]{3,2,1,0:T(8,128)(2,1)}, u32[]{:S(2)}) copy-start(bf16[1,32,256,128]{3,2,1,0:T(8,128)(2,1)} %param.14) | copy-start | bytes 6291460
  94.7 56.6 %all-to-all-start.4 = ((bf16[8,32,32,256]{3,2,1,0:T(8,128)(2,1)}), bf16[8,32,32,256]{3,2,1,0:T(8,128)(2,1)}, u32[]{:S(2)}, u32[]{:S(2)}) async-start(bf16[8,32,32,256]{3,2,1,0:T(8,128)(2,1)} %get-tuple-element.155), calls=%async_computation.4 | async-start | bytes 8388608 | tf_op jit(solution)/shard_map/all_to_all | solution.py:150
  102.5 2.0 collective-permute-start.2
  154.9 30.7 %copy-start.10 = (bf16[16,256,128]{2,1,0:T(8,128)(2,1)S(1)}, bf16[16,256,128]{2,1,0:T(8,128)(2,1)}, u32[]{:S(2)}) copy-start(bf16[16,256,128]{2,1,0:T(8,128)(2,1)} %get-tuple-element.164) | copy-start | bytes 3145732
  185.6 11.6 %collective-permute-start.3 = (bf16[16,256,128]{2,1,0:T(8,128)(2,1)S(1)}, bf16[16,256,128]{2,1,0:T(8,128)(2,1)}, u32[]{:S(2)}, u32[]{:S(2)}) collective-permute-start(bf16[16,256,128]{2,1,0:T(8,128)(2,1)S(1)} %copy-done.10), channel_id=1, source_target_pairs={{6,8},{7,9},{8,6},{9,7},{22,24},{23,25},{24,22},{25,23}} | collective-permute-start | bytes 3145736 | tf_op jit(solution)/shard_map/ppermute | solution.py:938
  197.2 56.8 %all-to-all-start.6 = ((bf16[8,32,32,256]{3,2,1,0:T(8,128)(2,1)}), bf16[8,32,32,256]{3,2,1,0:T(8,128)(2,1)}, u32[]{:S(2)}, u32[]{:S(2)}) async-start(bf16[8,32,32,256]{3,2,1,0:T(8,128)(2,1)} %get-tuple-element.165), calls=%async_computation.6 | async-start | bytes 8388608 | tf_op jit(solution)/shard_map/all_to_all | solution.py:150
  277.0 20.8 %all-to-all-start.9 = ((bf16[8,16,16,256]{3,2,1,0:T(8,128)(2,1)}), bf16[8,16,16,256]{3,2,1,0:T(8,128)(2,1)S(1)}, u32[]{:S(2)}, u32[]{:S(2)}) async-start(bf16[8,16,16,256]{3,2,1,0:T(8,128)(2,1)} %get-tuple-element.178), calls=%async_computation.9 | async-start | bytes 2097152 | tf_op jit(solution)/shard_map/all_to_all | solution.py:150
  297.8 4.4 copy-start.9
  297.8 21.8 %all-to-all-start.8 = ((bf16[8,16,16,256]{3,2,1,0:T(8,128)(2,1)}), bf16[8,16,16,256]{3,2,1,0:T(8,128)(2,1)S(1)}, u32[]{:S(2)}, u32[]{:S(2)}) async-start(bf16[8,16,16,256]{3,2,1,0:T(8,128)(2,1)} %bitcast.66), calls=%async_computation.8 | async-start | bytes 2097152 | tf_op jit(solution)/shard_map/all_to_all | solution.py:150
  319.6 19.3 %copy-start.5 = (bf16[8,16,16,256]{3,2,1,0:T(8,128)(2,1)}, bf16[8,16,16,256]{3,2,1,0:T(8,128)(2,1)S(1)}, u32[]{:S(2)}) copy-start(bf16[8,16,16,256]{3,2,1,0:T(8,128)(2,1)S(1)} %all-to-all-done.8.refs_0_) | copy-start | bytes 3145732
  343.8 4.7 copy-start.3
  343.8 52.5 %all-to-all-start.11 = ((bf16[8,32,32,256]{3,2,1,0:T(8,128)(2,1)}), bf16[8,32,32,256]{3,2,1,0:T(8,128)(2,1)}, u32[]{:S(2)}, u32[]{:S(2)}) async-start(bf16[8,32,32,256]{3,2,1,0:T(8,128)(2,1)} %bitcast.55), calls=%async_computation.11 | async-start | bytes 8388608 | tf_op jit(solution)/shard_map/all_to_all | solution.py:150
  348.5 3.1 collective-permute-start.4
  396.3 15.5 %collective-permute-start.5 = (bf16[16,256,128]{2,1,0:T(8,128)(2,1)}, bf16[16,256,128]{2,1,0:T(8,128)(2,1)S(1)}, u32[]{:S(2)}, u32[]{:S(2)}) collective-permute-start(bf16[16,256,128]{2,1,0:T(8,128)(2,1)} %get-tuple-element.198), channel_id=1, source_target_pairs={{6,8},{7,9},{8,6},{9,7},{22,24},{23,25},{24,22},{25,23}} | collective-permute-start | bytes 3145736 | tf_op jit(solution)/shard_map/ppermute | solution.py:938
  411.8 35.4 %copy-start.8 = (bf16[16,256,128]{2,1,0:T(8,128)(2,1)}, bf16[16,256,128]{2,1,0:T(8,128)(2,1)S(1)}, u32[]{:S(2)}) copy-start(bf16[16,256,128]{2,1,0:T(8,128)(2,1)S(1)} %collective-permute-done.5) | copy-start | bytes 3145732
  505.4 15.6 %collective-permute-start.6 = (bf16[16,256,128]{2,1,0:T(8,128)(2,1)S(1)}, bf16[16,256,128]{2,1,0:T(8,128)(2,1)}, u32[]{:S(2)}, u32[]{:S(2)}) collective-permute-start(bf16[16,256,128]{2,1,0:T(8,128)(2,1)S(1)} %get-tuple-element.209), channel_id=1, source_target_pairs={{6,8},{7,9},{8,6},{9,7},{22,24},{23,25},{24,22},{25,23}} | collective-permute-start | bytes 3145736 | tf_op jit(solution)/shard_map/ppermute | solution.py:938
  517.7 24.7 %copy-start.1 = (bf16[1,32,256,128]{3,2,1,0:T(8,128)(2,1)S(1)}, bf16[1,32,256,128]{3,2,1,0:T(8,128)(2,1)}, u32[]{:S(2)}) copy-start(bf16[1,32,256,128]{3,2,1,0:T(8,128)(2,1)} %param.10) | copy-start | bytes 6291460
  535.9 49.4 %collective-permute-start.7 = (bf16[32,256,128]{2,1,0:T(8,128)(2,1)}, bf16[32,256,128]{2,1,0:T(8,128)(2,1)}, u32[]{:S(2)}, u32[]{:S(2)}) collective-permute-start(bf16[32,256,128]{2,1,0:T(8,128)(2,1)} %get-tuple-element.256), channel_id=1, source_target_pairs={{4,10},{5,11},{6,8},{7,9},{8,6},{9,7},{10,4},{11,5},{20,26},{21,27... | collective-permute-start | bytes 6291464 | tf_op jit(solution)/shard_map/ppermute | solution.py:1115
  558.6 3.8 copy-start.4
  558.6 20.0 %all-to-all-start.16 = ((bf16[2,8,304,128]{3,2,1,0:T(8,128)(2,1)}), bf16[2,8,304,128]{3,2,1,0:T(8,128)(2,1)S(1)}, u32[]{:S(2)}, u32[]{:S(2)}) async-start(bf16[2,8,304,128]{3,2,1,0:T(8,128)(2,1)} %reduce_sum.51), calls=%async_computation.16 | async-start | bytes 2490368 | tf_op jit(solution)/shard_map/all_to_all | solution.py:150
  566.1 19.0 %copy-start.15 = (f32[128,1]{1,0:T(8,128)S(1)}, f32[128,1]{1,0:T(8,128)}, u32[]{:S(2)}) copy-start(f32[128,1]{1,0:T(8,128)} %get-tuple-element.227.refs_7_) | copy-start | bytes 1540
  566.1 19.2 %copy-start.13 = (bf16[256,256]{1,0:T(8,128)(2,1)S(1)}, bf16[256,256]{1,0:T(8,128)(2,1)}, u32[]{:S(2)}) copy-start(bf16[256,256]{1,0:T(8,128)(2,1)} %get-tuple-element.220) | copy-start | bytes 393220
  579.1 6.2 %copy-start.7 = (bf16[32,256,128]{2,1,0:T(8,128)(2,1)S(1)}, bf16[32,256,128]{2,1,0:T(8,128)(2,1)}, u32[]{:S(2)}) copy-start(bf16[32,256,128]{2,1,0:T(8,128)(2,1)} %get-tuple-element.256) | copy-start | bytes 6291460
  581.1 23.0 %all-to-all-start.17 = ((bf16[8,368,128]{2,1,0:T(8,128)(2,1)}), bf16[8,368,128]{2,1,0:T(8,128)(2,1)S(1)}, u32[]{:S(2)}, u32[]{:S(2)}) async-start(bf16[8,368,128]{2,1,0:T(8,128)(2,1)} %pad_maximum_fusion), calls=%async_computation.17 | async-start | bytes 1507328 | tf_op jit(solution)/shard_map/all_to_all | solution.py:150
  585.2 23.7 %copy-start.18 = (f32[32,256]{1,0:T(8,128)S(1)}, f32[32,256]{1,0:T(8,128)}, u32[]{:S(2)}) copy-start(f32[32,256]{1,0:T(8,128)} %get-tuple-element.241.refs_21_) | copy-start | bytes 98308
  585.2 32.7 %copy-start.11 = (f32[37488]{0:T(1024)S(1)}, f32[37488]{0:T(1024)}, u32[]{:S(2)}) copy-start(f32[37488]{0:T(1024)} %param.15) | copy-start | bytes 449860
  585.2 32.7 %copy-start.16 = (f32[37488]{0:T(1024)S(1)}, f32[37488]{0:T(1024)}, u32[]{:S(2)}) copy-start(f32[37488]{0:T(1024)} %param.16) | copy-start | bytes 449860
  585.3 32.7 %copy-start.17 = (f32[37488]{0:T(1024)S(1)}, f32[37488]{0:T(1024)}, u32[]{:S(2)}) copy-start(f32[37488]{0:T(1024)} %param.17) | copy-start | bytes 449860
  604.9 13.9 %copy-start.12 = (f32[37488]{0:T(1024)}, f32[37488]{0:T(1024)S(1)}, u32[]{:S(2)}) copy-start(f32[37488]{0:T(1024)S(1)} %get-tuple-element.264) | copy-start | bytes 449860
  606.2 9.9 %all-to-all-start.18 = ((f32[32,2,128]{2,1,0:T(2,128)}), f32[32,2,128]{2,1,0:T(2,128)S(1)}, u32[]{:S(2)}, u32[]{:S(2)}) async-start(f32[32,2,128]{2,1,0:T(2,128)} %broadcast_in_dim.70), calls=%async_computation.18 | async-start | bytes 65536 | tf_op jit(solution)/shard_map/all_to_all | solution.py:150

commit v5 on v4

--- a/solution.py
+++ b/solution.py
@@ -1,4 +1,5 @@
 import math
+from functools import partial
 from typing import Any, NamedTuple
 
 import jax
@@ -104,6 +105,7 @@
 BOTH = ("crop", "row")
 TILE = 16
 VMEM_LIMIT = 56 * 2**20
+SMALL_LIMIT = 28 * 2**20
 INV_SQRT2 = 1.0 / math.sqrt(2.0)
 INV_SQRT2PI = 1.0 / math.sqrt(2.0 * math.pi)
 
@@ -279,11 +281,11 @@
     return x * cumulative, cumulative + x * density
 
 
-def zero_first(*refs, earlier=()):
+def zero_first(*refs):
     @pl.when((pl.program_id(0) == 0) & (pl.program_id(1) == 0))
     def _():
-        for k, ref in enumerate(refs):
-            ref[...] = earlier[k][...] if earlier else jnp.zeros_like(ref)
+        for ref in refs:
+            ref[...] = jnp.zeros_like(ref)
 
 
 def run(body, step, extent, in_arrays, in_kinds, outs, scratch, flops, skip=0, aliases={}):
@@ -362,17 +364,17 @@
     send_pair(sides, sides_out)
 
 
-def kernel_turn(mixed, x_in, gate_in, cot, vectors, w_out, w_up, w_down, *rest):
-    (
-        pair_out, x_grad, gate_grad, mixed_grad, g_out, g_tri, g_up, g_down, g_pair, g_bias,
-        arrived, leaving,
-    ) = rest[-12:]
+def kernel_turn(sums, mixed, x_in, gate_in, cot, vectors, w_out, w_up, w_down, *rest):
+    if sums:
+        g_out, g_tri, g_up, g_down, g_pair, g_bias, arrived = rest
+        zero_first(g_out, g_tri, g_up, g_down, g_pair, g_bias)
+    else:
+        pair_out, x_grad, gate_grad, mixed_grad, arrived, leaving = rest[-6:]
     rows = x_in.shape[0]
     arrived[...] = swapped(mixed[...])
     up_low, up_back = w_up[...].T, w_up[...]
     down_low, down_back = w_down[...].T, w_down[...]
     tri_col, pair_col = column(vectors[IN_TRI]), column(vectors[PAIR_GAIN])
-    zero_first(g_out, g_tri, g_up, g_down, g_pair, g_bias, earlier=rest[3:-12])
     chunk = PAIR_DIM
 
     gate = cat(gate_in).astype(WIDE)
@@ -387,55 +389,63 @@
         part = slice(c * chunk, (c + 1) * chunk)
         act, slope = gelu_parts(dot_nn(up_low[part], normed))
         act_low = act.astype(LOW)
-        total = total + dot_nn(down_low[:, part], act_low)
         hidden_grad = (dot_nn(down_back[part], cot_low) * slope).astype(LOW)
         normed_grad = normed_grad + dot_nn(up_back[:, part], hidden_grad)
-        g_up[:, part] += dot_nt(normed, hidden_grad)
-        g_down[part] += dot_nt(act_low, cot_low)
+        if sums:
+            g_up[:, part] += dot_nt(normed, hidden_grad)
+            g_down[part] += dot_nt(act_low, cot_low)
+        else:
+            total = total + dot_nn(down_low[:, part], act_low)
+    cot_wide = cot_low.astype(WIDE)
+    back, grad_pair = norm_back(normed_grad, hat, scale, pair_col)
+    grad = cot_wide + back
+    mix_grad, gates, grad_out, grad_tri = post_back(grad, gate, *mix_parts, tri_col, w_out[...])
+    if sums:
+        g_bias[...] += jnp.sum(cot_wide, axis=1, keepdims=True)
+        g_pair[...] += grad_pair
+        g_out[...] += grad_out
+        g_tri[...] += grad_tri
+        return
     total_low = total.astype(LOW)
     width = total.shape[1] // rows
     for t in range(rows):
         pair_out[t] = total_low[:, t * width : (t + 1) * width].T
-    cot_wide = cot_low.astype(WIDE)
-    g_bias[...] += jnp.sum(cot_wide, axis=1, keepdims=True)
-    back, grad_gain = norm_back(normed_grad, hat, scale, pair_col)
-    g_pair[...] += grad_gain
-    grad = cot_wide + back
     put(x_grad, grad)
-    mix_grad, gates, grad_out, grad_tri = post_back(grad, gate, *mix_parts, tri_col, w_out[...])
     put(leaving, mix_grad)
     put(gate_grad, gates)
-    g_out[...] += grad_out
-    g_tri[...] += grad_tri
     mixed_grad[...] = swapped(leaving[...])
 
 
 def kernel_return(
-    sides_grad, x_after, mean_after, scale_after, gate_after, grad_in, mask, vectors, w_after,
-    mixed, gate_in, w_out,
-    x_grad, gate_grad, mixed_grad, g_after, g_gain, g_out, g_tri,
-    sides, arrived, leaving,
+    sums, sides_grad, x_after, mean_after, scale_after, gate_after, grad_in, mask, vectors, w_after,
+    mixed, gate_in, w_out, *rest,
 ):
+    if sums:
+        g_after, g_gain, g_out, g_tri, sides, arrived = rest
+        zero_first(g_after, g_gain, g_out, g_tri)
+    else:
+        x_grad, gate_grad, mixed_grad, sides, arrived, leaving = rest
     take_pair(sides_grad, sides)
     arrived[...] = swapped(mixed[...])
     tri_col = column(vectors[OUT_TRI])
-    zero_first(g_after, g_gain, g_out, g_tri)
     grad, grad_w, grad_gain = front_back(
         cat(grad_in).astype(WIDE), cat(x_after).astype(WIDE), cat(mean_after), cat(scale_after),
         cat(sides), cat(gate_after),
         cat(mask), column(vectors[IN_GAIN]), all_back(w_after),
     )
-    g_after[...] += grad_w
-    g_gain[...] += grad_gain
-    put(x_grad, grad)
     mix_parts = triangle_update(cat(arrived).astype(WIDE), tri_col, w_out[...].T)
     mix_grad, gates, grad_out, grad_tri = post_back(
         grad, cat(gate_in).astype(WIDE), *mix_parts, tri_col, w_out[...]
     )
+    if sums:
+        g_after[...] += grad_w
+        g_gain[...] += grad_gain
+        g_out[...] += grad_out
+        g_tri[...] += grad_tri
+        return
+    put(x_grad, grad)
     put(leaving, mix_grad)
     put(gate_grad, gates)
-    g_out[...] += grad_out
-    g_tri[...] += grad_tri
     mixed_grad[...] = swapped(leaving[...])
 
 
@@ -554,7 +564,7 @@
     return pl.BlockSpec(shape, lambda *_: (0,) * len(shape))
 
 
-def one_call(body, scalars, in_arrays, outs, scratch=()):
+def one_call(body, scalars, in_arrays, outs, scratch=(), limit=VMEM_LIMIT):
     return pl.pallas_call(
         body,
         in_specs=[pl.BlockSpec(memory_space=pltpu.SMEM)] * len(scalars)
@@ -563,7 +573,7 @@
         out_shape=[jax.ShapeDtypeStruct(shape, dtype) for shape, dtype in outs],
         scratch_shapes=list(scratch),
         grid=(1,),
-        compiler_params=pltpu.CompilerParams(vmem_limit_bytes=VMEM_LIMIT),
+        compiler_params=pltpu.CompilerParams(vmem_limit_bytes=limit),
     )(*scalars, *in_arrays)
 
 
@@ -741,6 +751,7 @@
             pltpu.VMEM((NODE_DIM, LANES), WIDE),
             pltpu.VMEM(node_parts[2].shape, WIDE),
         ],
+        SMALL_LIMIT,
     )
 
 
@@ -1036,42 +1047,54 @@
     turns = 2 if local_rows % (2 * TILE) == 0 else 1
     turn_rows = local_rows // turns
     mixed_in = [merge(trade(piece)) for piece in mix(sides_in, True, turns)]
-    turned, grads_in = (), []
+    turned, grads_in = [], []
+    ends = (vectors, w_in_end, w_pair_up, w_pair_down)
     for k in range(turns):
-        turned = run(
-            kernel_turn, step, (turn_rows, length),
-            (mixed_in[k], x_two, gate_tri_in, cot_plane, vectors, w_in_end, w_pair_up, w_pair_down,
-             *turned),
-            "sRRNwwww" + ("xxxwwwwww" if k else ""),
+        *turned, mixed_grad = run(
+            partial(kernel_turn, False), step, (turn_rows, length),
+            (mixed_in[k], x_two, gate_tri_in, cot_plane, *ends, *turned),
+            "sRRNwwww" + "xxx" * (k > 0),
             (("N", natural, LOW), ("R", state, LOW), ("R", state, LOW),
-             ("s", (TRI_DIM, turn_rows, length), LOW),
-             ("w", square, WIDE), ("w", gain_shape, WIDE), ("w", (PAIR_DIM, FFN_PAIR), WIDE),
-             ("w", (FFN_PAIR, PAIR_DIM), WIDE), ("w", gain_shape, WIDE), ("w", gain_shape, WIDE)),
-            [buffer(TRI_DIM), buffer(TRI_DIM)], 32 * unit // turns,
+             ("s", (TRI_DIM, turn_rows, length), LOW)),
+            [buffer(TRI_DIM), buffer(TRI_DIM)], 24 * unit // turns,
             skip=k * turn_rows // step[0], aliases={8: 0, 9: 1, 10: 2} if k else {},
         )
-        turned = list(turned)
-        mixed_grad = turned.pop(3)
         if k:
             grads_in[-1], mixed_grad = lax.optimization_barrier((grads_in[-1], mixed_grad))
         grads_in.append(trade(split(mixed_grad)))
-    pair_final, x_grad, gate_grad, g_in_out, g_in_tri, g_up, g_down, g_pair, g_bias = turned
+    pair_final, x_grad, gate_grad = turned
     sides_grad = trade(mix_back(grads_in, sides_in, True))
+    sums = run(
+        partial(kernel_turn, True), step, extent,
+        (jnp.concatenate(mixed_in, axis=1), x_two, gate_tri_in, cot_plane, *ends), "srrnwwww",
+        (("w", square, WIDE), ("w", gain_shape, WIDE), ("w", (PAIR_DIM, FFN_PAIR), WIDE),
+         ("w", (FFN_PAIR, PAIR_DIM), WIDE), ("w", gain_shape, WIDE), ("w", gain_shape, WIDE)),
+        [buffer(TRI_DIM)], 28 * unit,
+    )
+    sides_grad, *sums = lax.optimization_barrier((sides_grad, *sums))
+    g_in_out, g_in_tri, g_up, g_down, g_pair, g_bias = sums
     out_first, out_last = jnp.split(pair_final, 2)
     sides_grad, out_near, out_first = lax.optimization_barrier(
         (sides_grad, near(pair_final), out_first)
     )
-    x_grad, gate_grad, mixed_grad, g_in_all, g_in_gain, g_out_out, g_out_tri = run(
-        kernel_return, step, extent,
-        (sides_grad, x_two, mean_tri_in, scale_tri_in, gate_grad, x_grad, mask_plane,
-         vectors, w_in_all, mixed_out, gate_tri_out, w_out_end),
-        "srrrrrrwwsrw",
-        (("r", state, LOW), ("r", state, LOW), ("s", mixed_shape, LOW), ("w", after_shape, WIDE),
-         ("w", gain_shape, WIDE), ("w", square, WIDE), ("w", gain_shape, WIDE)),
-        [buffer(2 * TRI_DIM), buffer(TRI_DIM), buffer(TRI_DIM)], 12 * unit,
+    backs = (sides_grad, x_two, mean_tri_in, scale_tri_in, gate_grad, x_grad, mask_plane,
+             vectors, w_in_all, mixed_out, gate_tri_out, w_out_end)
+    x_grad, gate_grad, mixed_grad = run(
+        partial(kernel_return, False), step, extent, backs, "srrrrrrwwsrw",
+        (("r", state, LOW), ("r", state, LOW), ("s", mixed_shape, LOW)),
+        [buffer(2 * TRI_DIM), buffer(TRI_DIM), buffer(TRI_DIM)], 8 * unit,
     )
     mixed_grad, out_first = lax.optimization_barrier((mixed_grad, far(out_first)))
-    sides_grad = trade(mix_back([trade(split(mixed_grad))], sides_out, False))
+    mixed_grad = trade(split(mixed_grad))
+    sums = run(
+        partial(kernel_return, True), step, extent, backs, "srrrrrrwwsrw",
+        (("w", after_shape, WIDE), ("w", gain_shape, WIDE), ("w", square, WIDE),
+         ("w", gain_shape, WIDE)),
+        [buffer(2 * TRI_DIM), buffer(TRI_DIM)], 12 * unit,
+    )
+    mixed_grad, *sums = lax.optimization_barrier((mixed_grad, *sums))
+    g_in_all, g_in_gain, g_out_out, g_out_tri = sums
+    sides_grad = trade(mix_back([mixed_grad], sides_out, False))
     sides_grad, out_last = lax.optimization_barrier((sides_grad, out_last))
     pair_one_grad, table_grad, right_part, g_out_all, g_out_gain = run(
         kernel_close, step, extent,

time: 630 us -> 623 us (0.989)
  blocking collectives: 214 us -> 178 us
  Pallas kernels: 117 us -> 146 us
  waiting for transfers between devices: 190 us -> 175 us
  starting transfers between devices: 59.2 us -> 68.3 us
    all_to_all x9 -> x8, blocking collectives: 214 us -> 178 us  [exchange(): lax.all_to_all(blocks, axes, 0, 0, axis_index_groups=groups, tiled=True)]
    pallas_call x6 -> x8, Pallas kernels: 78.6 us -> 110 us  [run(): pl.pallas_call(body, grid=(extent[1] // step[1], extent[0] // step[0]), i...]
    all_to_all x10 -> x11, waiting for transfers between devices: 190 us -> 175 us  [exchange(): lax.all_to_all(blocks, axes, 0, 0, axis_index_groups=groups, tiled=True)]
    all_to_all x10 -> x11, starting transfers between devices: 46.2 us -> 55.4 us  [exchange(): lax.all_to_all(blocks, axes, 0, 0, axis_index_groups=groups, tiled=True)]
  transfers between devices with their start and end apart: 18 -> 19, of which waited for: 8 -> 9; matrix products, arithmetic and copies ran while one was open for 5% -> 5% of each run, Pallas kernels for 16% -> 21%
where the time goes in v5:
time: 623 us; the launch traced here: 614 us
  blocking collectives  178 us (29%)
  waiting for transfers between devices  175 us (28%)
  Pallas kernels  146 us (23%)
  starting transfers between devices  68.3 us (11%)
  other arithmetic  19.1 us (3%)
  local copies, waits for them, and re-layouts  16.7 us (3%)
    all_to_all x8, blocking collectives, exchange(): lax.all_to_all(blocks, axes, 0, 0, axis_index_groups=groups, tiled=True)  178 us
    all_to_all x11, waiting for transfers between devices, exchange(): lax.all_to_all(blocks, axes, 0, 0, axis_index_groups=groups, tiled=True)  175 us
    pallas_call x8, Pallas kernels, run(): pl.pallas_call(body, grid=(extent[1] // step[1], extent[0] // step[0]), i...  110 us
    all_to_all x11, starting transfers between devices, exchange(): lax.all_to_all(blocks, axes, 0, 0, axis_index_groups=groups, tiled=True)  55.4 us
    pallas_call x6, Pallas kernels, one_call(): pl.pallas_call(body, in_specs=[pl.BlockSpec(memory_space=pltpu.SMEM)] * l...  19 us
  transfers between devices with their start and end apart: 19, of which 9 were waited for; matrix products, arithmetic and copies ran while one was open for 5% of the time, Pallas kernels for 21%

profile of v5, /device:TPU:0, one launch (start us, length us, event | category | flops | bytes accessed | tf_op | source)
XLA Modules:
  0.0 613.6 jit_solution(2490881484086235967)
XLA Ops:
  3.5 26.5 %all_to_all.95 = bf16[8,368,128]{2,1,0:T(8,128)(2,1)S(1)} all-to-all(bf16[8,368,128]{2,1,0:T(8,128)(2,1)S(1)} %broadcast_in_dim.57), channel_id=1, replica_groups=mesh['crop'=4,'row'=8] {'row'}, dimensions={0} | all-to-all | bytes 1507328 | tf_op jit(solution)/shard_map/all_to_all | solution.py:152
  30.0 2.0 collective-permute-start
  33.1 3.6 all-to-all-start.1
  38.2 1.6 slice.24
  39.8 13.8 %all-to-all-done.1 = bf16[2,2432,128]{2,1,0:T(8,128)(2,1)S(1)} async-done(((bf16[2,2432,128]{2,1,0:T(8,128)(2,1)}), bf16[2,2432,128]{2,1,0:T(8,128)(2,1)S(1)}, u32[]{:S(2)}, u32[]{:S(2)}) %all-to-all-start.1) | async-done | bytes 1245216 | tf_op jit(solution)/shard_map/all_to_all | solution.py:152
  53.9 6.7 %all_to_all.96 = bf16[2,2,2432,128]{3,2,1,0:T(8,128)(2,1)} all-to-all(bf16[2,2,2432,128]{3,2,1,0:T(8,128)(2,1)S(1)} %broadcast_in_dim.60), channel_id=1, replica_groups={{0,8},{1,9},{2,10},{3,11},{4,12},{5,13},{6,14},{7,15},{16,24},{17,25},{..., dimensions={0} | all-to-all | bytes 4980736 | tf_op jit(solution)/shard_map/all_to_all | solution.py:152
  60.6 3.5 shard_map.176
  64.1 1.4 fusion.10
  66.3 4.2 shard_map.177
  70.5 3.5 all-to-all-start.3
  74.1 3.1 slice_bitcast_fusion
  77.2 4.7 all-to-all-done.3.factors
  83.4 2.2 shard_map.178
  85.6 9.0 %shard_map.179 = (bf16[32,128,256]{2,1,0:T(8,128)(2,1)}, f32[32,1,256]{2,1,0:T(1,128)}, f32[32,1,256]{2,1,0:T(1,128)}, bf16[32,128,256]{2,1,0:T(8,128)(2,1)}, bf16[8,32,32,256]{3,2,1,0:T(8,128)(2,1)}) custom-call(s32[1]{0:T(128)} %bitcast.12.stays, bf16[32,256,128]{2,1,0:T(8,128)(2,1)} %collective-permute-done.pair, bf16[32,256,128]{2,1,0:T(8,128)(2,1)} %bitcast.52, ...), custom_call_target="tpu_custom_call" | custom-call | flops 1073741824 | bytes 4616196 | tf_op jit(solution)/shard_map/pallas_call | solution.py:313
  94.6 7.8 %all-to-all-start.4 = ((bf16[8,32,32,256]{3,2,1,0:T(8,128)(2,1)}), bf16[8,32,32,256]{3,2,1,0:T(8,128)(2,1)}, u32[]{:S(2)}, u32[]{:S(2)}) async-start(bf16[8,32,32,256]{3,2,1,0:T(8,128)(2,1)} %get-tuple-element.161), calls=%async_computation.4 | async-start | bytes 8388608 | tf_op jit(solution)/shard_map/all_to_all | solution.py:152
  102.5 2.0 collective-permute-start.2
  104.4 46.8 %all-to-all-done.4.refs_0_.refs_1_.refs_2_ = bf16[8,32,32,256]{3,2,1,0:T(8,128)(2,1)} async-done(((bf16[8,32,32,256]{3,2,1,0:T(8,128)(2,1)}), bf16[8,32,32,256]{3,2,1,0:T(8,128)(2,1)}, u32[]{:S(2)}, u32[]{:S(2)}) %all-to-all-start.4) | async-done | bytes 4194336 | tf_op jit(solution)/shard_map/all_to_all | solution.py:152
  151.3 3.6 shard_map.180
  154.9 30.7 %all_to_all.97 = bf16[8,16,32,256]{3,2,1,0:T(8,128)(2,1)} all-to-all(bf16[8,16,32,256]{3,2,1,0:T(8,128)(2,1)} %shard_map.180), channel_id=1, replica_groups={{0,1,2,3,10,11,8,9},{6,7,4,5,12,13,14,15},{16,17,18,19,26,27,24,25},{22..., dimensions={0} | all-to-all | bytes 4194304 | tf_op jit(solution)/shard_map/all_to_all | solution.py:152
  185.6 1.7 collective-permute-start.3
  187.3 9.9 %shard_map.181 = (bf16[32,128,256]{2,1,0:T(8,128)(2,1)}, f32[32,1,256]{2,1,0:T(1,128)}, f32[32,1,256]{2,1,0:T(1,128)}, bf16[32,128,256]{2,1,0:T(8,128)(2,1)}, bf16[8,32,32,256]{3,2,1,0:T(8,128)(2,1)}) custom-call(bf16[128,32,256]{2,1,0:T(8,128)(2,1)} %bitcast.49, bf16[32,128,256]{2,1,0:T(8,128)(2,1)} %get-tuple-element.165.x_in.x_after, ...), custom_call_target="tpu_custom_call" | custom-call | flops 1342177280 | bytes 6467584 | tf_op jit(solution)/shard_map/pallas_call | solution.py:313
  197.2 8.0 %all-to-all-start.6 = ((bf16[8,32,32,256]{3,2,1,0:T(8,128)(2,1)}), bf16[8,32,32,256]{3,2,1,0:T(8,128)(2,1)}, u32[]{:S(2)}, u32[]{:S(2)}) async-start(bf16[8,32,32,256]{3,2,1,0:T(8,128)(2,1)} %get-tuple-element.171), calls=%async_computation.6 | async-start | bytes 8388608 | tf_op jit(solution)/shard_map/all_to_all | solution.py:152
  205.2 3.5 fusion.cot
  208.7 45.3 %all-to-all-done.6.refs_0_.refs_1_.refs_2_.refs_3_ = bf16[8,32,32,256]{3,2,1,0:T(8,128)(2,1)} async-done(((bf16[8,32,32,256]{3,2,1,0:T(8,128)(2,1)}), bf16[8,32,32,256]{3,2,1,0:T(8,128)(2,1)}, u32[]{:S(2)}, u32[]{:S(2)}) %all-to-all-start.6) | async-done | bytes 4194336 | tf_op jit(solution)/shard_map/all_to_all | solution.py:152
  254.0 3.7 shard_map.182
  257.7 19.2 %all_to_all.98 = bf16[8,16,16,256]{3,2,1,0:T(8,128)(2,1)} all-to-all(bf16[8,16,16,256]{3,2,1,0:T(8,128)(2,1)} %get-tuple-element.176), channel_id=1, replica_groups={{0,1,2,3,10,11,8,9},{6,7,4,5,12,13,14,15},{16,17,18,19,26,27,24,25},{22..., dimensions={0} | all-to-all | bytes 2097152 | tf_op jit(solution)/shard_map/all_to_all | solution.py:152
  276.9 3.7 all-to-all-start.9
  280.7 14.7 %shard_map.183 = (bf16[32,256,128]{2,1,0:T(8,128)(2,1)}, bf16[32,128,256]{2,1,0:T(8,128)(2,1)}, bf16[32,128,256]{2,1,0:T(8,128)(2,1)}, bf16[128,16,256]{2,1,0:T(8,128)(2,1)}) custom-call(bf16[128,16,256]{2,1,0:T(8,128)(2,1)} %bitcast.63, bf16[32,128,256]{2,1,0:T(8,128)(2,1)} %get-tuple-element.177.x_in.x_after, ...), custom_call_target="tpu_custom_call" | custom-call | flops 3221225472 | bytes 7647232 | tf_op jit(solution)/shard_map/pallas_call | solution.py:313
  295.3 4.1 all-to-all-start.8
  299.5 14.6 %shard_map.184 = (bf16[32,256,128]{2,1,0:T(8,128)(2,1)}, bf16[32,128,256]{2,1,0:T(8,128)(2,1)}, bf16[32,128,256]{2,1,0:T(8,128)(2,1)}, bf16[128,16,256]{2,1,0:T(8,128)(2,1)}) custom-call(bf16[128,16,256]{2,1,0:T(8,128)(2,1)} %bitcast.59, ...), custom_call_target="tpu_custom_call", output_to_operand_aliasing={{0}: (8, {}), {1}: (9, {}), {2}: (10, {})} | custom-call | flops 3221225472 | bytes 13938688 | tf_op jit(solution)/shard_map/pallas_call | solution.py:313
  314.1 19.3 %all_to_all.99.refs_1_ = bf16[8,16,16,256]{3,2,1,0:T(8,128)(2,1)} all-to-all(bf16[8,16,16,256]{3,2,1,0:T(8,128)(2,1)} %bitcast.71), channel_id=1, replica_groups={{0,1,2,3,10,11,8,9},{6,7,4,5,12,13,14,15},{16,17,18,19,26,27,24,25},{22..., dimensions={0} | all-to-all | bytes 2097152 | tf_op jit(solution)/shard_map/all_to_all | solution.py:152
  333.4 4.9 shard_map.185
  338.3 5.0 all-to-all-start.11
  343.4 2.0 collective-permute-start.4
  345.4 3.0 pad_maximum_fusion.mixed
  348.3 1.2 fusion.22
  349.5 26.2 %shard_map.186 = (f32[128,128]{1,0:T(8,128)}, f32[128,1]{1,0:T(8,128)}, f32[128,512]{1,0:T(8,128)}, f32[512,128]{1,0:T(8,128)}, f32[128,1]{1,0:T(8,128)}, /*index=5*/f32[128,1]{1,0:T(8,128)}) custom-call(bf16[128,32,256]{2,1,0:T(8,128)(2,1)} %pad_maximum_fusion.mixed, bf16[32,128,256]{2,1,0:T(8,128)(2,1)} %get-tuple-element.177.x_in.x_after, ...), custom_call_target="tpu_custom_call" | custom-call | flops 7516192768 | bytes 8695808 | tf_op jit(solution)/shard_map/pallas_call | solution.py:313
  375.7 15.4 %all-to-all-done.11.sides_grad = bf16[8,32,32,256]{3,2,1,0:T(8,128)(2,1)} async-done(((bf16[8,32,32,256]{3,2,1,0:T(8,128)(2,1)}), bf16[8,32,32,256]{3,2,1,0:T(8,128)(2,1)}, u32[]{:S(2)}, u32[]{:S(2)}) %all-to-all-start.11) | async-done | bytes 4194336 | tf_op jit(solution)/shard_map/all_to_all | solution.py:152
  391.1 1.6 collective-permute-start.5
  392.8 12.9 %shard_map.187 = (bf16[32,128,256]{2,1,0:T(8,128)(2,1)}, bf16[32,128,256]{2,1,0:T(8,128)(2,1)}, bf16[128,32,256]{2,1,0:T(8,128)(2,1)}) custom-call(bf16[8,32,32,256]{3,2,1,0:T(8,128)(2,1)} %all-to-all-done.11.sides_grad, bf16[32,128,256]{2,1,0:T(8,128)(2,1)} %get-tuple-element.177.x_in.x_after, f32[32,1,256]{2,1,0:T(1,128)} %get-tuple-element.200.mean_after, ...), custom_call_target="tpu_custom_call" | custom-call | flops 2147483648 | bytes 14921728 | tf_op jit(solution)/shard_map/pallas_call | solution.py:313
  405.6 8.2 %all-to-all-start.12 = ((bf16[8,16,32,256]{3,2,1,0:T(8,128)(2,1)}), bf16[8,16,32,256]{3,2,1,0:T(8,128)(2,1)S(1)}, u32[]{:S(2)}, u32[]{:S(2)}) async-start(bf16[8,16,32,256]{3,2,1,0:T(8,128)(2,1)} %bitcast.67), calls=%async_computation.12 | async-start | bytes 4194304 | tf_op jit(solution)/shard_map/all_to_all | solution.py:152
  413.8 12.1 %shard_map.188 = (f32[128,384]{1,0:T(8,128)}, f32[128,1]{1,0:T(8,128)}, f32[128,128]{1,0:T(8,128)}, f32[128,1]{1,0:T(8,128)}) custom-call(bf16[8,32,32,256]{3,2,1,0:T(8,128)(2,1)} %all-to-all-done.11.sides_grad, bf16[32,128,256]{2,1,0:T(8,128)(2,1)} %get-tuple-element.177.x_in.x_after, f32[32,1,256]{2,1,0:T(1,128)} %get-tuple-element.200.mean_after, ...), custom_call_target="tpu_custom_call" | custom-call | flops 3221225472 | bytes 14921728 | tf_op jit(solution)/shard_map/pallas_call | solution.py:313
  425.9 14.0 %all-to-all-done.12.refs_0_ = bf16[8,16,32,256]{3,2,1,0:T(8,128)(2,1)S(1)} async-done(((bf16[8,16,32,256]{3,2,1,0:T(8,128)(2,1)}), bf16[8,16,32,256]{3,2,1,0:T(8,128)(2,1)S(1)}, u32[]{:S(2)}, u32[]{:S(2)}) %all-to-all-start.12) | async-done | bytes 2097184 | tf_op jit(solution)/shard_map/all_to_all | solution.py:152
  439.9 1.3 copy-done.37
  441.2 4.9 shard_map.189
  446.1 53.2 %all_to_all.100.sides_grad = bf16[8,32,32,256]{3,2,1,0:T(8,128)(2,1)} all-to-all(bf16[8,32,32,256]{3,2,1,0:T(8,128)(2,1)} %bitcast.57), channel_id=1, replica_groups={{0,1,2,3,10,11,8,9},{6,7,4,5,12,13,14,15},{16,17,18,19,26,27,24,25},{22..., dimensions={0} | all-to-all | bytes 8388608 | tf_op jit(solution)/shard_map/all_to_all | solution.py:152
  500.2 10.4 %shard_map.190 = (bf16[32,256,128]{2,1,0:T(8,128)(2,1)}, f32[2,32,32,128]{3,2,1,0:T(8,128)}, f32[32,256]{1,0:T(8,128)}, f32[128,384]{1,0:T(8,128)}, f32[128,1]{1,0:T(8,128)}) custom-call(bf16[8,32,32,256]{3,2,1,0:T(8,128)(2,1)} %all_to_all.100.sides_grad, bf16[32,128,256]{2,1,0:T(8,128)(2,1)} %get-tuple-element.165.x_in.x_after, ...), custom_call_target="tpu_custom_call" | custom-call | flops 2147483648 | bytes 10973184 | tf_op jit(solution)/shard_map/pallas_call | solution.py:313
  510.7 3.2 shard_map.191
  513.9 16.1 %all_to_all.101.factor_ref = bf16[16,32,128]{2,1,0:T(8,128)(2,1)} all-to-all(bf16[16,32,128]{2,1,0:T(8,128)(2,1)} %bitcast.76), channel_id=1, replica_groups={{0,1,2,3,4,5,6,7,8,9,10,11,12,13,14,15},{16,17,18,19,20,21,22,23,24,25,..., dimensions={0} | all-to-all | bytes 262144 | tf_op jit(solution)/shard_map/all_to_all | solution.py:152
  530.0 2.0 collective-permute-start.7
  532.8 4.0 shard_map.192
  536.8 1.4 convolution_bitcast_fusion
  540.7 1.9 shard_map.193
  542.5 6.5 %all_to_all.102 = bf16[2,2,8,304,128]{4,3,2,1,0:T(8,128)(2,1)S(1)} all-to-all(bf16[2,2,8,304,128]{4,3,2,1,0:T(8,128)(2,1)S(1)} %get-tuple-element.261), channel_id=1, replica_groups={{0,8},{1,9},{2,10},{3,11},{4,12},{5,13},{6,14},{7,15},{16,24},{17,25},{..., dimensions={0} | all-to-all | bytes 4980736 | tf_op jit(solution)/shard_map/all_to_all | solution.py:152
  549.0 1.8 reduce_sum.51
  550.8 4.6 all-to-all-start.16
  555.4 3.8 fusion.1
  559.2 12.6 %all-to-all-done.16 = bf16[2,8,304,128]{3,2,1,0:T(8,128)(2,1)} async-done(((bf16[2,8,304,128]{3,2,1,0:T(8,128)(2,1)}), bf16[2,8,304,128]{3,2,1,0:T(8,128)(2,1)}, u32[]{:S(2)}, u32[]{:S(2)}) %all-to-all-start.16) | async-done | bytes 1245216 | tf_op jit(solution)/shard_map/all_to_all | solution.py:152
  571.8 1.6 reduce_sum.52
  574.3 4.0 all-to-all-start.17
  578.5 3.3 add_convert_fusion
  581.8 15.5 %all-to-all-done.17 = bf16[8,368,128]{2,1,0:T(8,128)(2,1)S(1)} async-done(((bf16[8,368,128]{2,1,0:T(8,128)(2,1)}), bf16[8,368,128]{2,1,0:T(8,128)(2,1)S(1)}, u32[]{:S(2)}, u32[]{:S(2)}) %all-to-all-start.17) | async-done | bytes 753696 | tf_op jit(solution)/shard_map/all_to_all | solution.py:152
  599.4 2.7 all-to-all-start.18
  602.7 6.6 %all-to-all-done.18 = f32[32,2,128]{2,1,0:T(2,128)S(1)} async-done(((f32[32,2,128]{2,1,0:T(2,128)}), f32[32,2,128]{2,1,0:T(2,128)S(1)}, u32[]{:S(2)}, u32[]{:S(2)}) %all-to-all-start.18) | async-done | bytes 32800 | tf_op jit(solution)/shard_map/all_to_all | solution.py:152
  (147 shorter events, 16.8 us)
Async XLA Ops:
  0.6 29.4 %copy-start.31 = (bf16[1,32,256,128]{3,2,1,0:T(8,128)(2,1)S(1)}, bf16[1,32,256,128]{3,2,1,0:T(8,128)(2,1)}, u32[]{:S(2)}) copy-start(bf16[1,32,256,128]{3,2,1,0:T(8,128)(2,1)} %param.10) | copy-start | bytes 6291460
  30.0 2.0 copy-start.40
  30.0 51.9 %collective-permute-start = (bf16[32,256,128]{2,1,0:T(8,128)(2,1)S(1)}, bf16[32,256,128]{2,1,0:T(8,128)(2,1)}, u32[]{:S(2)}, u32[]{:S(2)}) collective-permute-start(bf16[32,256,128]{2,1,0:T(8,128)(2,1)S(1)} %bitcast.53), channel_id=1, source_target_pairs={{4,10},{5,11},{6,8},{7,9},{8,6},{9,7},{10,4},{11,5},{20,26},{21,27... | collective-permute-start | bytes 6291464 | tf_op jit(solution)/shard_map/ppermute | solution.py:971
  32.0 5.4 copy-start.51
  33.1 20.5 %all-to-all-start.1 = ((bf16[2,2432,128]{2,1,0:T(8,128)(2,1)}), bf16[2,2432,128]{2,1,0:T(8,128)(2,1)S(1)}, u32[]{:S(2)}, u32[]{:S(2)}) async-start(bf16[2,2432,128]{2,1,0:T(8,128)(2,1)} %broadcast_in_dim.59), calls=%async_computation.1 | async-start | bytes 2490368 | tf_op jit(solution)/shard_map/all_to_all | solution.py:152
  37.4 23.2 %copy-start.50 = (f32[1,256]{1,0:T(1,128)}, f32[1,256]{1,0:T(1,128)S(1)}, u32[]{:S(2)}) copy-start(f32[1,256]{1,0:T(1,128)S(1)} %convert_element_type.27.keep) | copy-start | bytes 3076
  70.5 11.3 %all-to-all-start.3 = ((bf16[16,32,128]{2,1,0:T(8,128)(2,1)}), bf16[16,32,128]{2,1,0:T(8,128)(2,1)S(1)}, u32[]{:S(2)}, u32[]{:S(2)}) async-start(bf16[16,32,128]{2,1,0:T(8,128)(2,1)} %get-tuple-element.151), calls=%async_computation.3 | async-start | bytes 262144 | tf_op jit(solution)/shard_map/all_to_all | solution.py:152
  81.9 12.8 %collective-permute-start.1 = (bf16[16,256,128]{2,1,0:T(8,128)(2,1)}, bf16[16,256,128]{2,1,0:T(8,128)(2,1)S(1)}, u32[]{:S(2)}, u32[]{:S(2)}) collective-permute-start(bf16[16,256,128]{2,1,0:T(8,128)(2,1)} %get-tuple-element.160), channel_id=1, source_target_pairs={{6,8},{7,9},{8,6},{9,7},{22,24},{23,25},{24,22},{25,23}} | collective-permute-start | bytes 3145736 | tf_op jit(solution)/shard_map/ppermute | solution.py:949
  94.6 7.8 %copy-start.38 = (bf16[1,32,256,128]{3,2,1,0:T(8,128)(2,1)S(1)}, bf16[1,32,256,128]{3,2,1,0:T(8,128)(2,1)}, u32[]{:S(2)}) copy-start(bf16[1,32,256,128]{3,2,1,0:T(8,128)(2,1)} %param.14) | copy-start | bytes 6291460
  94.6 56.6 %all-to-all-start.4 = ((bf16[8,32,32,256]{3,2,1,0:T(8,128)(2,1)}), bf16[8,32,32,256]{3,2,1,0:T(8,128)(2,1)}, u32[]{:S(2)}, u32[]{:S(2)}) async-start(bf16[8,32,32,256]{3,2,1,0:T(8,128)(2,1)} %get-tuple-element.161), calls=%async_computation.4 | async-start | bytes 8388608 | tf_op jit(solution)/shard_map/all_to_all | solution.py:152
  102.5 2.0 collective-permute-start.2
  154.9 30.7 %copy-start.43 = (bf16[16,256,128]{2,1,0:T(8,128)(2,1)S(1)}, bf16[16,256,128]{2,1,0:T(8,128)(2,1)}, u32[]{:S(2)}) copy-start(bf16[16,256,128]{2,1,0:T(8,128)(2,1)} %get-tuple-element.170) | copy-start | bytes 3145732
  185.6 11.6 %collective-permute-start.3 = (bf16[16,256,128]{2,1,0:T(8,128)(2,1)S(1)}, bf16[16,256,128]{2,1,0:T(8,128)(2,1)}, u32[]{:S(2)}, u32[]{:S(2)}) collective-permute-start(bf16[16,256,128]{2,1,0:T(8,128)(2,1)S(1)} %copy-done.43), channel_id=1, source_target_pairs={{6,8},{7,9},{8,6},{9,7},{22,24},{23,25},{24,22},{25,23}} | collective-permute-start | bytes 3145736 | tf_op jit(solution)/shard_map/ppermute | solution.py:949
  197.2 56.8 %all-to-all-start.6 = ((bf16[8,32,32,256]{3,2,1,0:T(8,128)(2,1)}), bf16[8,32,32,256]{3,2,1,0:T(8,128)(2,1)}, u32[]{:S(2)}, u32[]{:S(2)}) async-start(bf16[8,32,32,256]{3,2,1,0:T(8,128)(2,1)} %get-tuple-element.171), calls=%async_computation.6 | async-start | bytes 8388608 | tf_op jit(solution)/shard_map/all_to_all | solution.py:152
  276.9 18.4 %all-to-all-start.9 = ((bf16[8,16,16,256]{3,2,1,0:T(8,128)(2,1)}), bf16[8,16,16,256]{3,2,1,0:T(8,128)(2,1)S(1)}, u32[]{:S(2)}, u32[]{:S(2)}) async-start(bf16[8,16,16,256]{3,2,1,0:T(8,128)(2,1)} %get-tuple-element.184), calls=%async_computation.9 | async-start | bytes 2097152 | tf_op jit(solution)/shard_map/all_to_all | solution.py:152
  295.3 4.2 copy-start.35
  295.3 18.8 %all-to-all-start.8 = ((bf16[8,16,16,256]{3,2,1,0:T(8,128)(2,1)}), bf16[8,16,16,256]{3,2,1,0:T(8,128)(2,1)S(1)}, u32[]{:S(2)}, u32[]{:S(2)}) async-start(bf16[8,16,16,256]{3,2,1,0:T(8,128)(2,1)} %bitcast.70), calls=%async_computation.8 | async-start | bytes 2097152 | tf_op jit(solution)/shard_map/all_to_all | solution.py:152
  314.1 19.3 %copy-start.39 = (bf16[8,16,16,256]{3,2,1,0:T(8,128)(2,1)}, bf16[8,16,16,256]{3,2,1,0:T(8,128)(2,1)S(1)}, u32[]{:S(2)}) copy-start(bf16[8,16,16,256]{3,2,1,0:T(8,128)(2,1)S(1)} %all-to-all-done.8.refs_0_) | copy-start | bytes 3145732
  338.3 5.1 copy-start.33
  338.3 7.1 %copy-start.36 = (bf16[8,16,16,256]{3,2,1,0:T(8,128)(2,1)S(1)}, bf16[8,16,16,256]{3,2,1,0:T(8,128)(2,1)}, u32[]{:S(2)}) copy-start(bf16[8,16,16,256]{3,2,1,0:T(8,128)(2,1)} %copy-done.35) | copy-start | bytes 3145732
  338.3 52.8 %all-to-all-start.11 = ((bf16[8,32,32,256]{3,2,1,0:T(8,128)(2,1)}), bf16[8,32,32,256]{3,2,1,0:T(8,128)(2,1)}, u32[]{:S(2)}, u32[]{:S(2)}) async-start(bf16[8,32,32,256]{3,2,1,0:T(8,128)(2,1)} %bitcast.56), calls=%async_computation.11 | async-start | bytes 8388608 | tf_op jit(solution)/shard_map/all_to_all | solution.py:152
  343.4 47.8 %collective-permute-start.4 = (bf16[32,256,128]{2,1,0:T(8,128)(2,1)S(1)}, bf16[32,256,128]{2,1,0:T(8,128)(2,1)}, u32[]{:S(2)}, u32[]{:S(2)}) collective-permute-start(bf16[32,256,128]{2,1,0:T(8,128)(2,1)S(1)} %copy-done.33), channel_id=1, source_target_pairs={{4,10},{5,11},{10,4},{11,5},{20,26},{21,27},{26,20},{27,21}} | collective-permute-start | bytes 6291464 | tf_op jit(solution)/shard_map/ppermute | solution.py:948
  391.1 14.5 %collective-permute-start.5 = (bf16[16,256,128]{2,1,0:T(8,128)(2,1)}, bf16[16,256,128]{2,1,0:T(8,128)(2,1)}, u32[]{:S(2)}, u32[]{:S(2)}) collective-permute-start(bf16[16,256,128]{2,1,0:T(8,128)(2,1)} %get-tuple-element.205), channel_id=1, source_target_pairs={{6,8},{7,9},{8,6},{9,7},{22,24},{23,25},{24,22},{25,23}} | collective-permute-start | bytes 3145736 | tf_op jit(solution)/shard_map/ppermute | solution.py:949
  405.6 34.2 %all-to-all-start.12 = ((bf16[8,16,32,256]{3,2,1,0:T(8,128)(2,1)}), bf16[8,16,32,256]{3,2,1,0:T(8,128)(2,1)S(1)}, u32[]{:S(2)}, u32[]{:S(2)}) async-start(bf16[8,16,32,256]{3,2,1,0:T(8,128)(2,1)} %bitcast.67), calls=%async_computation.12 | async-start | bytes 4194304 | tf_op jit(solution)/shard_map/all_to_all | solution.py:152
  499.3 14.7 %collective-permute-start.6 = (bf16[16,256,128]{2,1,0:T(8,128)(2,1)S(1)}, bf16[16,256,128]{2,1,0:T(8,128)(2,1)S(1)}, u32[]{:S(2)}, u32[]{:S(2)}) collective-permute-start(bf16[16,256,128]{2,1,0:T(8,128)(2,1)S(1)} %get-tuple-element.221), channel_id=1, source_target_pairs={{6,8},{7,9},{8,6},{9,7},{22,24},{23,25},{24,22},{25,23}} | collective-permute-start | bytes 3145736 | tf_op jit(solution)/shard_map/ppermute | solution.py:949
  510.7 26.2 %copy-start.32 = (bf16[1,32,256,128]{3,2,1,0:T(8,128)(2,1)S(1)}, bf16[1,32,256,128]{3,2,1,0:T(8,128)(2,1)}, u32[]{:S(2)}) copy-start(bf16[1,32,256,128]{3,2,1,0:T(8,128)(2,1)} %param.10) | copy-start | bytes 6291460
  513.9 18.6 %copy-start.42 = (bf16[16,256,128]{2,1,0:T(8,128)(2,1)}, bf16[16,256,128]{2,1,0:T(8,128)(2,1)S(1)}, u32[]{:S(2)}) copy-start(bf16[16,256,128]{2,1,0:T(8,128)(2,1)S(1)} %collective-permute-done.6) | copy-start | bytes 3145732
  530.0 48.5 %collective-permute-start.7 = (bf16[32,256,128]{2,1,0:T(8,128)(2,1)}, bf16[32,256,128]{2,1,0:T(8,128)(2,1)}, u32[]{:S(2)}, u32[]{:S(2)}) collective-permute-start(bf16[32,256,128]{2,1,0:T(8,128)(2,1)} %get-tuple-element.268), channel_id=1, source_target_pairs={{4,10},{5,11},{6,8},{7,9},{8,6},{9,7},{10,4},{11,5},{20,26},{21,27... | collective-permute-start | bytes 6291464 | tf_op jit(solution)/shard_map/ppermute | solution.py:1138
  532.6 5.9 copy-start
  532.6 5.9 copy-start.1
  532.6 5.9 copy-start.2
  532.6 5.9 copy-start.3
  532.6 5.9 copy-start.4
  532.6 5.9 copy-start.5
  532.6 5.9 copy-start.7
  532.6 5.9 copy-start.8
  532.6 5.9 copy-start.9
  532.6 5.9 copy-start.11
  532.7 5.9 copy-start.13
  532.7 5.9 copy-start.14
  532.7 5.9 copy-start.15
  532.7 5.9 copy-start.16
  532.7 5.9 copy-start.17
  532.7 5.9 copy-start.18
  532.7 5.9 copy-start.19
  532.7 5.9 copy-start.20
  532.7 5.9 copy-start.22
  532.7 5.9 copy-start.23
  536.7 1.9 copy-start.6
  536.8 1.9 copy-start.10
  536.8 1.9 copy-start.12
  536.8 1.9 copy-start.21
  536.8 1.9 copy-start.24
  536.8 1.9 copy-start.25
  550.8 4.6 copy-start.34
  550.8 21.0 %all-to-all-start.16 = ((bf16[2,8,304,128]{3,2,1,0:T(8,128)(2,1)}), bf16[2,8,304,128]{3,2,1,0:T(8,128)(2,1)}, u32[]{:S(2)}, u32[]{:S(2)}) async-start(bf16[2,8,304,128]{3,2,1,0:T(8,128)(2,1)} %reduce_sum.51), calls=%async_computation.16 | async-start | bytes 2490368 | tf_op jit(solution)/shard_map/all_to_all | solution.py:152
  559.2 19.3 %copy-start.41 = (bf16[32,256,128]{2,1,0:T(8,128)(2,1)S(1)}, bf16[32,256,128]{2,1,0:T(8,128)(2,1)}, u32[]{:S(2)}) copy-start(bf16[32,256,128]{2,1,0:T(8,128)(2,1)} %get-tuple-element.268) | copy-start | bytes 6291460
  559.2 19.3 %copy-start.46 = (bf16[256,256]{1,0:T(8,128)(2,1)S(1)}, bf16[256,256]{1,0:T(8,128)(2,1)}, u32[]{:S(2)}) copy-start(bf16[256,256]{1,0:T(8,128)(2,1)} %get-tuple-element.232) | copy-start | bytes 393220
  574.3 23.0 %all-to-all-start.17 = ((bf16[8,368,128]{2,1,0:T(8,128)(2,1)}), bf16[8,368,128]{2,1,0:T(8,128)(2,1)S(1)}, u32[]{:S(2)}, u32[]{:S(2)}) async-start(bf16[8,368,128]{2,1,0:T(8,128)(2,1)} %pad_maximum_fusion.1), calls=%async_computation.17 | async-start | bytes 1507328 | tf_op jit(solution)/shard_map/all_to_all | solution.py:152
  578.4 32.7 %copy-start.44 = (f32[37488]{0:T(1024)S(1)}, f32[37488]{0:T(1024)}, u32[]{:S(2)}) copy-start(f32[37488]{0:T(1024)} %param.15) | copy-start | bytes 449860
  578.5 32.7 %copy-start.48 = (f32[37488]{0:T(1024)S(1)}, f32[37488]{0:T(1024)}, u32[]{:S(2)}) copy-start(f32[37488]{0:T(1024)} %param.16) | copy-start | bytes 449860
  578.5 32.7 %copy-start.49 = (f32[37488]{0:T(1024)S(1)}, f32[37488]{0:T(1024)}, u32[]{:S(2)}) copy-start(f32[37488]{0:T(1024)} %param.17) | copy-start | bytes 449860
  598.2 13.9 %copy-start.45 = (f32[37488]{0:T(1024)}, f32[37488]{0:T(1024)S(1)}, u32[]{:S(2)}) copy-start(f32[37488]{0:T(1024)S(1)} %get-tuple-element.276) | copy-start | bytes 449860
  599.4 9.9 %all-to-all-start.18 = ((f32[32,2,128]{2,1,0:T(2,128)}), f32[32,2,128]{2,1,0:T(2,128)S(1)}, u32[]{:S(2)}, u32[]{:S(2)}) async-start(f32[32,2,128]{2,1,0:T(2,128)} %broadcast_in_dim.70), calls=%async_computation.18 | async-start | bytes 65536 | tf_op jit(solution)/shard_map/all_to_all | solution.py:152
  (7 other events, 8.6 us)

commit v6 on v5

--- a/solution.py
+++ b/solution.py
@@ -281,6 +281,20 @@
     return x * cumulative, cumulative + x * density
 
 
+FEW = 4
+
+
+def few_rows(piece, *refs):
+    rows = refs[0].shape[0]
+    few = min(FEW, rows)
+
+    def step(t, carry):
+        piece(*(ref.at[pl.ds(t * few, few)] for ref in refs))
+        return carry
+
+    lax.fori_loop(0, rows // few, step, 0)
+
+
 def zero_first(*refs):
     @pl.when((pl.program_id(0) == 0) & (pl.program_id(1) == 0))
     def _():
@@ -370,50 +384,56 @@
         zero_first(g_out, g_tri, g_up, g_down, g_pair, g_bias)
     else:
         pair_out, x_grad, gate_grad, mixed_grad, arrived, leaving = rest[-6:]
-    rows = x_in.shape[0]
     arrived[...] = swapped(mixed[...])
     up_low, up_back = w_up[...].T, w_up[...]
     down_low, down_back = w_down[...].T, w_down[...]
     tri_col, pair_col = column(vectors[IN_TRI]), column(vectors[PAIR_GAIN])
     chunk = PAIR_DIM
 
-    gate = cat(gate_in).astype(WIDE)
-    mix_parts = triangle_update(cat(arrived).astype(WIDE), tri_col, w_out[...].T)
-    x = cat(x_in).astype(WIDE) + gate * mix_parts[-1]
-    hat, scale = norm_parts(x)
-    normed = (hat * pair_col).astype(LOW)
-    cot_low = jnp.concatenate([cot[t].T for t in range(rows)], axis=1)
-    total = x + column(vectors[PAIR_BIAS])
-    normed_grad = jnp.zeros_like(x)
-    for c in range(FFN_PAIR // chunk):
-        part = slice(c * chunk, (c + 1) * chunk)
-        act, slope = gelu_parts(dot_nn(up_low[part], normed))
-        act_low = act.astype(LOW)
-        hidden_grad = (dot_nn(down_back[part], cot_low) * slope).astype(LOW)
-        normed_grad = normed_grad + dot_nn(up_back[:, part], hidden_grad)
+    def piece(x_in, gate_in, cot, arrived):
+        rows = x_in.shape[0]
+        gate = cat(gate_in).astype(WIDE)
+        mix_parts = triangle_update(cat(arrived).astype(WIDE), tri_col, w_out[...].T)
+        x = cat(x_in).astype(WIDE) + gate * mix_parts[-1]
+        hat, scale = norm_parts(x)
+        normed = (hat * pair_col).astype(LOW)
+        cot_low = jnp.concatenate([cot[t].T for t in range(rows)], axis=1)
+        total = x + column(vectors[PAIR_BIAS])
+        normed_grad = jnp.zeros_like(x)
+        for c in range(FFN_PAIR // chunk):
+            part = slice(c * chunk, (c + 1) * chunk)
+            act, slope = gelu_parts(dot_nn(up_low[part], normed))
+            act_low = act.astype(LOW)
+            hidden_grad = (dot_nn(down_back[part], cot_low) * slope).astype(LOW)
+            normed_grad = normed_grad + dot_nn(up_back[:, part], hidden_grad)
+            if sums:
+                g_up[:, part] += dot_nt(normed, hidden_grad)
+                g_down[part] += dot_nt(act_low, cot_low)
+            else:
+                total = total + dot_nn(down_low[:, part], act_low)
+        cot_wide = cot_low.astype(WIDE)
+        back, grad_pair = norm_back(normed_grad, hat, scale, pair_col)
+        grad = cot_wide + back
+        mix_grad, gates, grad_out, grad_tri = post_back(grad, gate, *mix_parts, tri_col, w_out[...])
         if sums:
-            g_up[:, part] += dot_nt(normed, hidden_grad)
-            g_down[part] += dot_nt(act_low, cot_low)
-        else:
-            total = total + dot_nn(down_low[:, part], act_low)
-    cot_wide = cot_low.astype(WIDE)
-    back, grad_pair = norm_back(normed_grad, hat, scale, pair_col)
-    grad = cot_wide + back
-    mix_grad, gates, grad_out, grad_tri = post_back(grad, gate, *mix_parts, tri_col, w_out[...])
+            g_bias[...] += jnp.sum(cot_wide, axis=1, keepdims=True)
+            g_pair[...] += grad_pair
+            g_out[...] += grad_out
+            g_tri[...] += grad_tri
+            return
+        total_low = total.astype(LOW)
+        width = total.shape[1] // rows
+        for t in range(rows):
+            pair_out[t] = total_low[:, t * width : (t + 1) * width].T
+        put(x_grad, grad)
+        put(leaving, mix_grad)
+        put(gate_grad, gates)
+
     if sums:
-        g_bias[...] += jnp.sum(cot_wide, axis=1, keepdims=True)
-        g_pair[...] += grad_pair
-        g_out[...] += grad_out
-        g_tri[...] += grad_tri
-        return
-    total_low = total.astype(LOW)
-    width = total.shape[1] // rows
-    for t in range(rows):
-        pair_out[t] = total_low[:, t * width : (t + 1) * width].T
-    put(x_grad, grad)
-    put(leaving, mix_grad)
-    put(gate_grad, gates)
-    mixed_grad[...] = swapped(leaving[...])
+        few_rows(piece, x_in, gate_in, cot, arrived)
+    else:
+        piece(x_in, gate_in, cot, arrived)
+        mixed_grad[...] = swapped(leaving[...])
 
 
 def kernel_return(
@@ -428,25 +448,36 @@
     take_pair(sides_grad, sides)
     arrived[...] = swapped(mixed[...])
     tri_col = column(vectors[OUT_TRI])
-    grad, grad_w, grad_gain = front_back(
-        cat(grad_in).astype(WIDE), cat(x_after).astype(WIDE), cat(mean_after), cat(scale_after),
-        cat(sides), cat(gate_after),
-        cat(mask), column(vectors[IN_GAIN]), all_back(w_after),
-    )
-    mix_parts = triangle_update(cat(arrived).astype(WIDE), tri_col, w_out[...].T)
-    mix_grad, gates, grad_out, grad_tri = post_back(
-        grad, cat(gate_in).astype(WIDE), *mix_parts, tri_col, w_out[...]
-    )
+    after_col, after_back = column(vectors[IN_GAIN]), all_back(w_after)
+
+    def piece(
+        grad_in, x_after, mean_after, scale_after, sides, gate_after, mask, arrived, gate_in
+    ):
+        grad, grad_w, grad_gain = front_back(
+            cat(grad_in).astype(WIDE), cat(x_after).astype(WIDE), cat(mean_after), cat(scale_after),
+            cat(sides), cat(gate_after),
+            cat(mask), after_col, after_back,
+        )
+        mix_parts = triangle_update(cat(arrived).astype(WIDE), tri_col, w_out[...].T)
+        mix_grad, gates, grad_out, grad_tri = post_back(
+            grad, cat(gate_in).astype(WIDE), *mix_parts, tri_col, w_out[...]
+        )
+        if sums:
+            g_after[...] += grad_w
+            g_gain[...] += grad_gain
+            g_out[...] += grad_out
+            g_tri[...] += grad_tri
+            return
+        put(x_grad, grad)
+        put(leaving, mix_grad)
+        put(gate_grad, gates)
+
+    parts = (grad_in, x_after, mean_after, scale_after, sides, gate_after, mask, arrived, gate_in)
     if sums:
-        g_after[...] += grad_w
-        g_gain[...] += grad_gain
-        g_out[...] += grad_out
-        g_tri[...] += grad_tri
-        return
-    put(x_grad, grad)
-    put(leaving, mix_grad)
-    put(gate_grad, gates)
-    mixed_grad[...] = swapped(leaving[...])
+        few_rows(piece, *parts)
+    else:
+        piece(*parts)
+        mixed_grad[...] = swapped(leaving[...])
 
 
 def kernel_close(

time: 623 us -> 624 us (level)
  Pallas kernels: 146 us -> 165 us
  waiting for transfers between devices: 175 us -> 156 us
    all_to_all x11, waiting for transfers between devices: 175 us -> 156 us  [exchange(): lax.all_to_all(blocks, axes, 0, 0, axis_index_groups=groups, tiled=True)]
    pallas_call x8, Pallas kernels: 110 us -> 129 us  [run(): pl.pallas_call(body, grid=(extent[1] // step[1], extent[0] // step[0]), i...]
  transfers between devices with their start and end apart: 19 -> 19, of which waited for: 9 -> 9; matrix products, arithmetic and copies ran while one was open for 5% -> 5% of each run, Pallas kernels for 21% -> 24%
where the time goes in v6:
time: 624 us; the launch traced here: 614 us
  blocking collectives  178 us (29%)
  Pallas kernels  165 us (26%)
  waiting for transfers between devices  156 us (25%)
  starting transfers between devices  68.3 us (11%)
  other arithmetic  19.1 us (3%)
  local copies, waits for them, and re-layouts  16.7 us (3%)
    all_to_all x8, blocking collectives, exchange(): lax.all_to_all(blocks, axes, 0, 0, axis_index_groups=groups, tiled=True)  178 us
    all_to_all x11, waiting for transfers between devices, exchange(): lax.all_to_all(blocks, axes, 0, 0, axis_index_groups=groups, tiled=True)  156 us
    pallas_call x8, Pallas kernels, run(): pl.pallas_call(body, grid=(extent[1] // step[1], extent[0] // step[0]), i...  129 us
    all_to_all x11, starting transfers between devices, exchange(): lax.all_to_all(blocks, axes, 0, 0, axis_index_groups=groups, tiled=True)  55.4 us
    pallas_call x6, Pallas kernels, one_call(): pl.pallas_call(body, in_specs=[pl.BlockSpec(memory_space=pltpu.SMEM)] * l...  19 us
  transfers between devices with their start and end apart: 19, of which 9 were waited for; matrix products, arithmetic and copies ran while one was open for 5% of the time, Pallas kernels for 24%

profile of v6, /device:TPU:0, one launch (start us, length us, event | category | flops | bytes accessed | tf_op | source)
XLA Modules:
  0.0 613.8 jit_solution(3054211452456807089)
XLA Ops:
  3.5 26.5 %all_to_all.95 = bf16[8,368,128]{2,1,0:T(8,128)(2,1)S(1)} all-to-all(bf16[8,368,128]{2,1,0:T(8,128)(2,1)S(1)} %broadcast_in_dim.57), channel_id=1, replica_groups=mesh['crop'=4,'row'=8] {'row'}, dimensions={0} | all-to-all | bytes 1507328 | tf_op jit(solution)/shard_map/all_to_all | solution.py:152
  30.0 2.0 collective-permute-start
  33.1 3.6 all-to-all-start.1
  38.2 1.6 slice.24
  39.8 13.8 %all-to-all-done.1 = bf16[2,2432,128]{2,1,0:T(8,128)(2,1)S(1)} async-done(((bf16[2,2432,128]{2,1,0:T(8,128)(2,1)}), bf16[2,2432,128]{2,1,0:T(8,128)(2,1)S(1)}, u32[]{:S(2)}, u32[]{:S(2)}) %all-to-all-start.1) | async-done | bytes 1245216 | tf_op jit(solution)/shard_map/all_to_all | solution.py:152
  53.9 6.7 %all_to_all.96 = bf16[2,2,2432,128]{3,2,1,0:T(8,128)(2,1)} all-to-all(bf16[2,2,2432,128]{3,2,1,0:T(8,128)(2,1)S(1)} %broadcast_in_dim.60), channel_id=1, replica_groups={{0,8},{1,9},{2,10},{3,11},{4,12},{5,13},{6,14},{7,15},{16,24},{17,25},{..., dimensions={0} | all-to-all | bytes 4980736 | tf_op jit(solution)/shard_map/all_to_all | solution.py:152
  60.6 3.5 shard_map.176
  64.1 1.4 fusion.10
  66.3 4.2 shard_map.177
  70.5 3.5 all-to-all-start.3
  74.1 3.1 slice_bitcast_fusion
  77.2 4.7 all-to-all-done.3.factors
  83.4 2.2 shard_map.178
  85.6 9.0 %shard_map.179 = (bf16[32,128,256]{2,1,0:T(8,128)(2,1)}, f32[32,1,256]{2,1,0:T(1,128)}, f32[32,1,256]{2,1,0:T(1,128)}, bf16[32,128,256]{2,1,0:T(8,128)(2,1)}, bf16[8,32,32,256]{3,2,1,0:T(8,128)(2,1)}) custom-call(s32[1]{0:T(128)} %bitcast.12.stays, bf16[32,256,128]{2,1,0:T(8,128)(2,1)} %collective-permute-done.pair, bf16[32,256,128]{2,1,0:T(8,128)(2,1)} %bitcast.52, ...), custom_call_target="tpu_custom_call" | custom-call | flops 1073741824 | bytes 4616196 | tf_op jit(solution)/shard_map/pallas_call | solution.py:327
  94.6 7.8 %all-to-all-start.4 = ((bf16[8,32,32,256]{3,2,1,0:T(8,128)(2,1)}), bf16[8,32,32,256]{3,2,1,0:T(8,128)(2,1)}, u32[]{:S(2)}, u32[]{:S(2)}) async-start(bf16[8,32,32,256]{3,2,1,0:T(8,128)(2,1)} %get-tuple-element.161), calls=%async_computation.4 | async-start | bytes 8388608 | tf_op jit(solution)/shard_map/all_to_all | solution.py:152
  102.5 2.0 collective-permute-start.2
  104.4 46.8 %all-to-all-done.4.refs_0_.refs_1_.refs_2_ = bf16[8,32,32,256]{3,2,1,0:T(8,128)(2,1)} async-done(((bf16[8,32,32,256]{3,2,1,0:T(8,128)(2,1)}), bf16[8,32,32,256]{3,2,1,0:T(8,128)(2,1)}, u32[]{:S(2)}, u32[]{:S(2)}) %all-to-all-start.4) | async-done | bytes 4194336 | tf_op jit(solution)/shard_map/all_to_all | solution.py:152
  151.3 3.6 shard_map.180
  154.9 30.7 %all_to_all.97 = bf16[8,16,32,256]{3,2,1,0:T(8,128)(2,1)} all-to-all(bf16[8,16,32,256]{3,2,1,0:T(8,128)(2,1)} %shard_map.180), channel_id=1, replica_groups={{0,1,2,3,10,11,8,9},{6,7,4,5,12,13,14,15},{16,17,18,19,26,27,24,25},{22..., dimensions={0} | all-to-all | bytes 4194304 | tf_op jit(solution)/shard_map/all_to_all | solution.py:152
  185.6 1.7 collective-permute-start.3
  187.3 9.9 %shard_map.181 = (bf16[32,128,256]{2,1,0:T(8,128)(2,1)}, f32[32,1,256]{2,1,0:T(1,128)}, f32[32,1,256]{2,1,0:T(1,128)}, bf16[32,128,256]{2,1,0:T(8,128)(2,1)}, bf16[8,32,32,256]{3,2,1,0:T(8,128)(2,1)}) custom-call(bf16[128,32,256]{2,1,0:T(8,128)(2,1)} %bitcast.49, bf16[32,128,256]{2,1,0:T(8,128)(2,1)} %get-tuple-element.165.x_in.x_after, ...), custom_call_target="tpu_custom_call" | custom-call | flops 1342177280 | bytes 6467584 | tf_op jit(solution)/shard_map/pallas_call | solution.py:327
  197.2 8.0 %all-to-all-start.6 = ((bf16[8,32,32,256]{3,2,1,0:T(8,128)(2,1)}), bf16[8,32,32,256]{3,2,1,0:T(8,128)(2,1)}, u32[]{:S(2)}, u32[]{:S(2)}) async-start(bf16[8,32,32,256]{3,2,1,0:T(8,128)(2,1)} %get-tuple-element.171), calls=%async_computation.6 | async-start | bytes 8388608 | tf_op jit(solution)/shard_map/all_to_all | solution.py:152
  205.2 3.5 fusion.cot
  208.7 45.3 %all-to-all-done.6.refs_0_.refs_1_.refs_2_.refs_3_ = bf16[8,32,32,256]{3,2,1,0:T(8,128)(2,1)} async-done(((bf16[8,32,32,256]{3,2,1,0:T(8,128)(2,1)}), bf16[8,32,32,256]{3,2,1,0:T(8,128)(2,1)}, u32[]{:S(2)}, u32[]{:S(2)}) %all-to-all-start.6) | async-done | bytes 4194336 | tf_op jit(solution)/shard_map/all_to_all | solution.py:152
  254.0 3.7 shard_map.182
  257.7 19.2 %all_to_all.98 = bf16[8,16,16,256]{3,2,1,0:T(8,128)(2,1)} all-to-all(bf16[8,16,16,256]{3,2,1,0:T(8,128)(2,1)} %get-tuple-element.176), channel_id=1, replica_groups={{0,1,2,3,10,11,8,9},{6,7,4,5,12,13,14,15},{16,17,18,19,26,27,24,25},{22..., dimensions={0} | all-to-all | bytes 2097152 | tf_op jit(solution)/shard_map/all_to_all | solution.py:152
  276.9 3.7 all-to-all-start.9
  280.7 14.7 %shard_map.183 = (bf16[32,256,128]{2,1,0:T(8,128)(2,1)}, bf16[32,128,256]{2,1,0:T(8,128)(2,1)}, bf16[32,128,256]{2,1,0:T(8,128)(2,1)}, bf16[128,16,256]{2,1,0:T(8,128)(2,1)}) custom-call(bf16[128,16,256]{2,1,0:T(8,128)(2,1)} %bitcast.63, bf16[32,128,256]{2,1,0:T(8,128)(2,1)} %get-tuple-element.177.x_in.x_after, ...), custom_call_target="tpu_custom_call" | custom-call | flops 3221225472 | bytes 7647232 | tf_op jit(solution)/shard_map/pallas_call | solution.py:327
  295.3 4.1 all-to-all-start.8
  299.5 14.6 %shard_map.184 = (bf16[32,256,128]{2,1,0:T(8,128)(2,1)}, bf16[32,128,256]{2,1,0:T(8,128)(2,1)}, bf16[32,128,256]{2,1,0:T(8,128)(2,1)}, bf16[128,16,256]{2,1,0:T(8,128)(2,1)}) custom-call(bf16[128,16,256]{2,1,0:T(8,128)(2,1)} %bitcast.59, ...), custom_call_target="tpu_custom_call", output_to_operand_aliasing={{0}: (8, {}), {1}: (9, {}), {2}: (10, {})} | custom-call | flops 3221225472 | bytes 13938688 | tf_op jit(solution)/shard_map/pallas_call | solution.py:327
  314.1 19.3 %all_to_all.99.refs_1_ = bf16[8,16,16,256]{3,2,1,0:T(8,128)(2,1)} all-to-all(bf16[8,16,16,256]{3,2,1,0:T(8,128)(2,1)} %bitcast.71), channel_id=1, replica_groups={{0,1,2,3,10,11,8,9},{6,7,4,5,12,13,14,15},{16,17,18,19,26,27,24,25},{22..., dimensions={0} | all-to-all | bytes 2097152 | tf_op jit(solution)/shard_map/all_to_all | solution.py:152
  333.4 4.9 shard_map.185
  338.3 5.0 all-to-all-start.11
  343.4 2.0 collective-permute-start.4
  345.4 3.0 pad_maximum_fusion.mixed
  348.3 1.2 fusion.22
  349.5 39.4 %shard_map.186 = (f32[128,128]{1,0:T(8,128)}, f32[128,1]{1,0:T(8,128)}, f32[128,512]{1,0:T(8,128)}, f32[512,128]{1,0:T(8,128)}, f32[128,1]{1,0:T(8,128)}, /*index=5*/f32[128,1]{1,0:T(8,128)}) custom-call(bf16[128,32,256]{2,1,0:T(8,128)(2,1)} %pad_maximum_fusion.mixed, bf16[32,128,256]{2,1,0:T(8,128)(2,1)} %get-tuple-element.177.x_in.x_after, ...), custom_call_target="tpu_custom_call" | custom-call | flops 7516192768 | bytes 8695808 | tf_op jit(solution)/shard_map/pallas_call | solution.py:327
  388.9 2.2 all-to-all-done.11.sides_grad
  391.1 1.6 collective-permute-start.5
  392.8 12.9 %shard_map.187 = (bf16[32,128,256]{2,1,0:T(8,128)(2,1)}, bf16[32,128,256]{2,1,0:T(8,128)(2,1)}, bf16[128,32,256]{2,1,0:T(8,128)(2,1)}) custom-call(bf16[8,32,32,256]{3,2,1,0:T(8,128)(2,1)} %all-to-all-done.11.sides_grad, bf16[32,128,256]{2,1,0:T(8,128)(2,1)} %get-tuple-element.177.x_in.x_after, f32[32,1,256]{2,1,0:T(1,128)} %get-tuple-element.200.mean_after, ...), custom_call_target="tpu_custom_call" | custom-call | flops 2147483648 | bytes 14921728 | tf_op jit(solution)/shard_map/pallas_call | solution.py:327
  405.6 8.2 %all-to-all-start.12 = ((bf16[8,16,32,256]{3,2,1,0:T(8,128)(2,1)}), bf16[8,16,32,256]{3,2,1,0:T(8,128)(2,1)S(1)}, u32[]{:S(2)}, u32[]{:S(2)}) async-start(bf16[8,16,32,256]{3,2,1,0:T(8,128)(2,1)} %bitcast.67), calls=%async_computation.12 | async-start | bytes 4194304 | tf_op jit(solution)/shard_map/all_to_all | solution.py:152
  413.8 17.9 %shard_map.188 = (f32[128,384]{1,0:T(8,128)}, f32[128,1]{1,0:T(8,128)}, f32[128,128]{1,0:T(8,128)}, f32[128,1]{1,0:T(8,128)}) custom-call(bf16[8,32,32,256]{3,2,1,0:T(8,128)(2,1)} %all-to-all-done.11.sides_grad, bf16[32,128,256]{2,1,0:T(8,128)(2,1)} %get-tuple-element.177.x_in.x_after, f32[32,1,256]{2,1,0:T(1,128)} %get-tuple-element.200.mean_after, ...), custom_call_target="tpu_custom_call" | custom-call | flops 3221225472 | bytes 14921728 | tf_op jit(solution)/shard_map/pallas_call | solution.py:327
  431.8 8.1 %all-to-all-done.12.refs_0_ = bf16[8,16,32,256]{3,2,1,0:T(8,128)(2,1)S(1)} async-done(((bf16[8,16,32,256]{3,2,1,0:T(8,128)(2,1)}), bf16[8,16,32,256]{3,2,1,0:T(8,128)(2,1)S(1)}, u32[]{:S(2)}, u32[]{:S(2)}) %all-to-all-start.12) | async-done | bytes 2097184 | tf_op jit(solution)/shard_map/all_to_all | solution.py:152
  439.9 1.3 copy-done.37
  441.2 4.9 shard_map.189
  446.1 53.2 %all_to_all.100.sides_grad = bf16[8,32,32,256]{3,2,1,0:T(8,128)(2,1)} all-to-all(bf16[8,32,32,256]{3,2,1,0:T(8,128)(2,1)} %bitcast.57), channel_id=1, replica_groups={{0,1,2,3,10,11,8,9},{6,7,4,5,12,13,14,15},{16,17,18,19,26,27,24,25},{22..., dimensions={0} | all-to-all | bytes 8388608 | tf_op jit(solution)/shard_map/all_to_all | solution.py:152
  500.0 10.4 %shard_map.190 = (bf16[32,256,128]{2,1,0:T(8,128)(2,1)}, f32[2,32,32,128]{3,2,1,0:T(8,128)}, f32[32,256]{1,0:T(8,128)}, f32[128,384]{1,0:T(8,128)}, f32[128,1]{1,0:T(8,128)}) custom-call(bf16[8,32,32,256]{3,2,1,0:T(8,128)(2,1)} %all_to_all.100.sides_grad, bf16[32,128,256]{2,1,0:T(8,128)(2,1)} %get-tuple-element.165.x_in.x_after, ...), custom_call_target="tpu_custom_call" | custom-call | flops 2147483648 | bytes 10973184 | tf_op jit(solution)/shard_map/pallas_call | solution.py:327
  510.4 3.2 shard_map.191
  513.7 16.3 %all_to_all.101.factor_ref = bf16[16,32,128]{2,1,0:T(8,128)(2,1)} all-to-all(bf16[16,32,128]{2,1,0:T(8,128)(2,1)} %bitcast.76), channel_id=1, replica_groups={{0,1,2,3,4,5,6,7,8,9,10,11,12,13,14,15},{16,17,18,19,20,21,22,23,24,25,..., dimensions={0} | all-to-all | bytes 262144 | tf_op jit(solution)/shard_map/all_to_all | solution.py:152
  530.0 2.2 collective-permute-start.7
  533.0 4.0 shard_map.192
  537.1 1.4 convolution_bitcast_fusion
  540.9 1.9 shard_map.193
  542.8 6.5 %all_to_all.102 = bf16[2,2,8,304,128]{4,3,2,1,0:T(8,128)(2,1)S(1)} all-to-all(bf16[2,2,8,304,128]{4,3,2,1,0:T(8,128)(2,1)S(1)} %get-tuple-element.261), channel_id=1, replica_groups={{0,8},{1,9},{2,10},{3,11},{4,12},{5,13},{6,14},{7,15},{16,24},{17,25},{..., dimensions={0} | all-to-all | bytes 4980736 | tf_op jit(solution)/shard_map/all_to_all | solution.py:152
  549.3 1.8 reduce_sum.51
  551.1 4.6 all-to-all-start.16
  555.7 3.8 fusion.1
  559.5 12.6 %all-to-all-done.16 = bf16[2,8,304,128]{3,2,1,0:T(8,128)(2,1)} async-done(((bf16[2,8,304,128]{3,2,1,0:T(8,128)(2,1)}), bf16[2,8,304,128]{3,2,1,0:T(8,128)(2,1)}, u32[]{:S(2)}, u32[]{:S(2)}) %all-to-all-start.16) | async-done | bytes 1245216 | tf_op jit(solution)/shard_map/all_to_all | solution.py:152
  572.0 1.6 reduce_sum.52
  574.6 4.0 all-to-all-start.17
  578.8 3.3 add_convert_fusion
  582.1 15.5 %all-to-all-done.17 = bf16[8,368,128]{2,1,0:T(8,128)(2,1)S(1)} async-done(((bf16[8,368,128]{2,1,0:T(8,128)(2,1)}), bf16[8,368,128]{2,1,0:T(8,128)(2,1)S(1)}, u32[]{:S(2)}, u32[]{:S(2)}) %all-to-all-start.17) | async-done | bytes 753696 | tf_op jit(solution)/shard_map/all_to_all | solution.py:152
  599.7 2.7 all-to-all-start.18
  603.0 6.6 %all-to-all-done.18 = f32[32,2,128]{2,1,0:T(2,128)S(1)} async-done(((f32[32,2,128]{2,1,0:T(2,128)}), f32[32,2,128]{2,1,0:T(2,128)S(1)}, u32[]{:S(2)}, u32[]{:S(2)}) %all-to-all-start.18) | async-done | bytes 32800 | tf_op jit(solution)/shard_map/all_to_all | solution.py:152
  (147 shorter events, 16.6 us)
Async XLA Ops:
  0.6 29.4 %copy-start.31 = (bf16[1,32,256,128]{3,2,1,0:T(8,128)(2,1)S(1)}, bf16[1,32,256,128]{3,2,1,0:T(8,128)(2,1)}, u32[]{:S(2)}) copy-start(bf16[1,32,256,128]{3,2,1,0:T(8,128)(2,1)} %param.10) | copy-start | bytes 6291460
  30.0 2.0 copy-start.40
  30.0 51.9 %collective-permute-start = (bf16[32,256,128]{2,1,0:T(8,128)(2,1)S(1)}, bf16[32,256,128]{2,1,0:T(8,128)(2,1)}, u32[]{:S(2)}, u32[]{:S(2)}) collective-permute-start(bf16[32,256,128]{2,1,0:T(8,128)(2,1)S(1)} %bitcast.53), channel_id=1, source_target_pairs={{4,10},{5,11},{6,8},{7,9},{8,6},{9,7},{10,4},{11,5},{20,26},{21,27... | collective-permute-start | bytes 6291464 | tf_op jit(solution)/shard_map/ppermute | solution.py:1002
  32.0 5.4 copy-start.51
  33.1 20.5 %all-to-all-start.1 = ((bf16[2,2432,128]{2,1,0:T(8,128)(2,1)}), bf16[2,2432,128]{2,1,0:T(8,128)(2,1)S(1)}, u32[]{:S(2)}, u32[]{:S(2)}) async-start(bf16[2,2432,128]{2,1,0:T(8,128)(2,1)} %broadcast_in_dim.59), calls=%async_computation.1 | async-start | bytes 2490368 | tf_op jit(solution)/shard_map/all_to_all | solution.py:152
  37.4 23.2 %copy-start.50 = (f32[1,256]{1,0:T(1,128)}, f32[1,256]{1,0:T(1,128)S(1)}, u32[]{:S(2)}) copy-start(f32[1,256]{1,0:T(1,128)S(1)} %convert_element_type.27.keep) | copy-start | bytes 3076
  70.5 11.3 %all-to-all-start.3 = ((bf16[16,32,128]{2,1,0:T(8,128)(2,1)}), bf16[16,32,128]{2,1,0:T(8,128)(2,1)S(1)}, u32[]{:S(2)}, u32[]{:S(2)}) async-start(bf16[16,32,128]{2,1,0:T(8,128)(2,1)} %get-tuple-element.151), calls=%async_computation.3 | async-start | bytes 262144 | tf_op jit(solution)/shard_map/all_to_all | solution.py:152
  81.9 12.8 %collective-permute-start.1 = (bf16[16,256,128]{2,1,0:T(8,128)(2,1)}, bf16[16,256,128]{2,1,0:T(8,128)(2,1)S(1)}, u32[]{:S(2)}, u32[]{:S(2)}) collective-permute-start(bf16[16,256,128]{2,1,0:T(8,128)(2,1)} %get-tuple-element.160), channel_id=1, source_target_pairs={{6,8},{7,9},{8,6},{9,7},{22,24},{23,25},{24,22},{25,23}} | collective-permute-start | bytes 3145736 | tf_op jit(solution)/shard_map/ppermute | solution.py:980
  94.6 7.8 %copy-start.38 = (bf16[1,32,256,128]{3,2,1,0:T(8,128)(2,1)S(1)}, bf16[1,32,256,128]{3,2,1,0:T(8,128)(2,1)}, u32[]{:S(2)}) copy-start(bf16[1,32,256,128]{3,2,1,0:T(8,128)(2,1)} %param.14) | copy-start | bytes 6291460
  94.6 56.6 %all-to-all-start.4 = ((bf16[8,32,32,256]{3,2,1,0:T(8,128)(2,1)}), bf16[8,32,32,256]{3,2,1,0:T(8,128)(2,1)}, u32[]{:S(2)}, u32[]{:S(2)}) async-start(bf16[8,32,32,256]{3,2,1,0:T(8,128)(2,1)} %get-tuple-element.161), calls=%async_computation.4 | async-start | bytes 8388608 | tf_op jit(solution)/shard_map/all_to_all | solution.py:152
  102.5 2.0 collective-permute-start.2
  154.9 30.7 %copy-start.43 = (bf16[16,256,128]{2,1,0:T(8,128)(2,1)S(1)}, bf16[16,256,128]{2,1,0:T(8,128)(2,1)}, u32[]{:S(2)}) copy-start(bf16[16,256,128]{2,1,0:T(8,128)(2,1)} %get-tuple-element.170) | copy-start | bytes 3145732
  185.6 11.6 %collective-permute-start.3 = (bf16[16,256,128]{2,1,0:T(8,128)(2,1)S(1)}, bf16[16,256,128]{2,1,0:T(8,128)(2,1)}, u32[]{:S(2)}, u32[]{:S(2)}) collective-permute-start(bf16[16,256,128]{2,1,0:T(8,128)(2,1)S(1)} %copy-done.43), channel_id=1, source_target_pairs={{6,8},{7,9},{8,6},{9,7},{22,24},{23,25},{24,22},{25,23}} | collective-permute-start | bytes 3145736 | tf_op jit(solution)/shard_map/ppermute | solution.py:980
  197.2 56.8 %all-to-all-start.6 = ((bf16[8,32,32,256]{3,2,1,0:T(8,128)(2,1)}), bf16[8,32,32,256]{3,2,1,0:T(8,128)(2,1)}, u32[]{:S(2)}, u32[]{:S(2)}) async-start(bf16[8,32,32,256]{3,2,1,0:T(8,128)(2,1)} %get-tuple-element.171), calls=%async_computation.6 | async-start | bytes 8388608 | tf_op jit(solution)/shard_map/all_to_all | solution.py:152
  276.9 18.4 %all-to-all-start.9 = ((bf16[8,16,16,256]{3,2,1,0:T(8,128)(2,1)}), bf16[8,16,16,256]{3,2,1,0:T(8,128)(2,1)S(1)}, u32[]{:S(2)}, u32[]{:S(2)}) async-start(bf16[8,16,16,256]{3,2,1,0:T(8,128)(2,1)} %get-tuple-element.184), calls=%async_computation.9 | async-start | bytes 2097152 | tf_op jit(solution)/shard_map/all_to_all | solution.py:152
  295.3 4.2 copy-start.35
  295.3 18.8 %all-to-all-start.8 = ((bf16[8,16,16,256]{3,2,1,0:T(8,128)(2,1)}), bf16[8,16,16,256]{3,2,1,0:T(8,128)(2,1)S(1)}, u32[]{:S(2)}, u32[]{:S(2)}) async-start(bf16[8,16,16,256]{3,2,1,0:T(8,128)(2,1)} %bitcast.70), calls=%async_computation.8 | async-start | bytes 2097152 | tf_op jit(solution)/shard_map/all_to_all | solution.py:152
  314.1 19.3 %copy-start.39 = (bf16[8,16,16,256]{3,2,1,0:T(8,128)(2,1)}, bf16[8,16,16,256]{3,2,1,0:T(8,128)(2,1)S(1)}, u32[]{:S(2)}) copy-start(bf16[8,16,16,256]{3,2,1,0:T(8,128)(2,1)S(1)} %all-to-all-done.8.refs_0_) | copy-start | bytes 3145732
  338.3 5.1 copy-start.33
  338.3 7.1 %copy-start.36 = (bf16[8,16,16,256]{3,2,1,0:T(8,128)(2,1)S(1)}, bf16[8,16,16,256]{3,2,1,0:T(8,128)(2,1)}, u32[]{:S(2)}) copy-start(bf16[8,16,16,256]{3,2,1,0:T(8,128)(2,1)} %copy-done.35) | copy-start | bytes 3145732
  338.3 52.8 %all-to-all-start.11 = ((bf16[8,32,32,256]{3,2,1,0:T(8,128)(2,1)}), bf16[8,32,32,256]{3,2,1,0:T(8,128)(2,1)}, u32[]{:S(2)}, u32[]{:S(2)}) async-start(bf16[8,32,32,256]{3,2,1,0:T(8,128)(2,1)} %bitcast.56), calls=%async_computation.11 | async-start | bytes 8388608 | tf_op jit(solution)/shard_map/all_to_all | solution.py:152
  343.4 47.8 %collective-permute-start.4 = (bf16[32,256,128]{2,1,0:T(8,128)(2,1)S(1)}, bf16[32,256,128]{2,1,0:T(8,128)(2,1)}, u32[]{:S(2)}, u32[]{:S(2)}) collective-permute-start(bf16[32,256,128]{2,1,0:T(8,128)(2,1)S(1)} %copy-done.33), channel_id=1, source_target_pairs={{4,10},{5,11},{10,4},{11,5},{20,26},{21,27},{26,20},{27,21}} | collective-permute-start | bytes 6291464 | tf_op jit(solution)/shard_map/ppermute | solution.py:979
  391.1 14.5 %collective-permute-start.5 = (bf16[16,256,128]{2,1,0:T(8,128)(2,1)}, bf16[16,256,128]{2,1,0:T(8,128)(2,1)}, u32[]{:S(2)}, u32[]{:S(2)}) collective-permute-start(bf16[16,256,128]{2,1,0:T(8,128)(2,1)} %get-tuple-element.205), channel_id=1, source_target_pairs={{6,8},{7,9},{8,6},{9,7},{22,24},{23,25},{24,22},{25,23}} | collective-permute-start | bytes 3145736 | tf_op jit(solution)/shard_map/ppermute | solution.py:980
  405.6 34.2 %all-to-all-start.12 = ((bf16[8,16,32,256]{3,2,1,0:T(8,128)(2,1)}), bf16[8,16,32,256]{3,2,1,0:T(8,128)(2,1)S(1)}, u32[]{:S(2)}, u32[]{:S(2)}) async-start(bf16[8,16,32,256]{3,2,1,0:T(8,128)(2,1)} %bitcast.67), calls=%async_computation.12 | async-start | bytes 4194304 | tf_op jit(solution)/shard_map/all_to_all | solution.py:152
  499.3 14.4 %collective-permute-start.6 = (bf16[16,256,128]{2,1,0:T(8,128)(2,1)S(1)}, bf16[16,256,128]{2,1,0:T(8,128)(2,1)S(1)}, u32[]{:S(2)}, u32[]{:S(2)}) collective-permute-start(bf16[16,256,128]{2,1,0:T(8,128)(2,1)S(1)} %get-tuple-element.221), channel_id=1, source_target_pairs={{6,8},{7,9},{8,6},{9,7},{22,24},{23,25},{24,22},{25,23}} | collective-permute-start | bytes 3145736 | tf_op jit(solution)/shard_map/ppermute | solution.py:980
  510.4 26.6 %copy-start.32 = (bf16[1,32,256,128]{3,2,1,0:T(8,128)(2,1)S(1)}, bf16[1,32,256,128]{3,2,1,0:T(8,128)(2,1)}, u32[]{:S(2)}) copy-start(bf16[1,32,256,128]{3,2,1,0:T(8,128)(2,1)} %param.10) | copy-start | bytes 6291460
  513.7 19.1 %copy-start.42 = (bf16[16,256,128]{2,1,0:T(8,128)(2,1)}, bf16[16,256,128]{2,1,0:T(8,128)(2,1)S(1)}, u32[]{:S(2)}) copy-start(bf16[16,256,128]{2,1,0:T(8,128)(2,1)S(1)} %collective-permute-done.6) | copy-start | bytes 3145732
  530.0 48.7 %collective-permute-start.7 = (bf16[32,256,128]{2,1,0:T(8,128)(2,1)}, bf16[32,256,128]{2,1,0:T(8,128)(2,1)}, u32[]{:S(2)}, u32[]{:S(2)}) collective-permute-start(bf16[32,256,128]{2,1,0:T(8,128)(2,1)} %get-tuple-element.268), channel_id=1, source_target_pairs={{4,10},{5,11},{6,8},{7,9},{8,6},{9,7},{10,4},{11,5},{20,26},{21,27... | collective-permute-start | bytes 6291464 | tf_op jit(solution)/shard_map/ppermute | solution.py:1169
  532.8 5.9 copy-start
  532.8 5.9 copy-start.1
  532.8 5.9 copy-start.2
  532.8 5.9 copy-start.3
  532.8 5.9 copy-start.4
  532.8 5.9 copy-start.5
  532.9 5.9 copy-start.7
  532.9 5.9 copy-start.8
  532.9 5.9 copy-start.9
  532.9 5.9 copy-start.11
  532.9 5.9 copy-start.13
  532.9 5.9 copy-start.14
  532.9 5.9 copy-start.15
  532.9 5.9 copy-start.16
  532.9 5.9 copy-start.17
  532.9 5.9 copy-start.18
  533.0 5.9 copy-start.19
  533.0 5.9 copy-start.20
  533.0 5.9 copy-start.22
  533.0 5.9 copy-start.23
  537.0 1.9 copy-start.6
  537.0 1.9 copy-start.10
  537.0 1.9 copy-start.12
  537.0 1.9 copy-start.21
  537.0 1.9 copy-start.24
  537.0 1.9 copy-start.25
  551.0 4.6 copy-start.34
  551.1 21.0 %all-to-all-start.16 = ((bf16[2,8,304,128]{3,2,1,0:T(8,128)(2,1)}), bf16[2,8,304,128]{3,2,1,0:T(8,128)(2,1)}, u32[]{:S(2)}, u32[]{:S(2)}) async-start(bf16[2,8,304,128]{3,2,1,0:T(8,128)(2,1)} %reduce_sum.51), calls=%async_computation.16 | async-start | bytes 2490368 | tf_op jit(solution)/shard_map/all_to_all | solution.py:152
  559.5 19.3 %copy-start.41 = (bf16[32,256,128]{2,1,0:T(8,128)(2,1)S(1)}, bf16[32,256,128]{2,1,0:T(8,128)(2,1)}, u32[]{:S(2)}) copy-start(bf16[32,256,128]{2,1,0:T(8,128)(2,1)} %get-tuple-element.268) | copy-start | bytes 6291460
  559.5 19.3 %copy-start.46 = (bf16[256,256]{1,0:T(8,128)(2,1)S(1)}, bf16[256,256]{1,0:T(8,128)(2,1)}, u32[]{:S(2)}) copy-start(bf16[256,256]{1,0:T(8,128)(2,1)} %get-tuple-element.232) | copy-start | bytes 393220
  574.6 23.0 %all-to-all-start.17 = ((bf16[8,368,128]{2,1,0:T(8,128)(2,1)}), bf16[8,368,128]{2,1,0:T(8,128)(2,1)S(1)}, u32[]{:S(2)}, u32[]{:S(2)}) async-start(bf16[8,368,128]{2,1,0:T(8,128)(2,1)} %pad_maximum_fusion.1), calls=%async_computation.17 | async-start | bytes 1507328 | tf_op jit(solution)/shard_map/all_to_all | solution.py:152
  578.7 32.7 %copy-start.44 = (f32[37488]{0:T(1024)S(1)}, f32[37488]{0:T(1024)}, u32[]{:S(2)}) copy-start(f32[37488]{0:T(1024)} %param.15) | copy-start | bytes 449860
  578.7 32.7 %copy-start.48 = (f32[37488]{0:T(1024)S(1)}, f32[37488]{0:T(1024)}, u32[]{:S(2)}) copy-start(f32[37488]{0:T(1024)} %param.16) | copy-start | bytes 449860
  578.7 32.7 %copy-start.49 = (f32[37488]{0:T(1024)S(1)}, f32[37488]{0:T(1024)}, u32[]{:S(2)}) copy-start(f32[37488]{0:T(1024)} %param.17) | copy-start | bytes 449860
  598.4 13.9 %copy-start.45 = (f32[37488]{0:T(1024)}, f32[37488]{0:T(1024)S(1)}, u32[]{:S(2)}) copy-start(f32[37488]{0:T(1024)S(1)} %get-tuple-element.276) | copy-start | bytes 449860
  599.7 9.9 %all-to-all-start.18 = ((f32[32,2,128]{2,1,0:T(2,128)}), f32[32,2,128]{2,1,0:T(2,128)S(1)}, u32[]{:S(2)}, u32[]{:S(2)}) async-start(f32[32,2,128]{2,1,0:T(2,128)} %broadcast_in_dim.70), calls=%async_computation.18 | async-start | bytes 65536 | tf_op jit(solution)/shard_map/all_to_all | solution.py:152
  (7 other events, 8.6 us)

commit v7 on v6

--- a/solution.py
+++ b/solution.py
@@ -1147,7 +1147,9 @@
     factor_grads, out_last = lax.optimization_barrier((factor_grads, far(out_last)))
     pair_out = settled(pair_final, out_near, out_first, out_last)
     factor_grads = exchange(factor_grads.reshape(slab, local_rows, LANES), BOTH, layout.slabs)
-    factor_grads, pair_one_grad = lax.optimization_barrier((factor_grads, pair_one_grad))
+    factor_grads, pair_one_grad, pair_out = lax.optimization_barrier(
+        (factor_grads, pair_one_grad, pair_out)
+    )
 
     workers = layout.work_place(crop_at * ranks + everyone)
     sources = jnp.concatenate([partner[None], workers]).astype(jnp.int32) % slab
@@ -1195,7 +1197,7 @@
     )
     total = lambda got: low_of(jnp.sum(got.astype(WIDE), axis=0))
     blocks = total(exchange(blocks, BOTH, layout.cores))
-    blocks, pair_out = lax.optimization_barrier((exchange(blocks, BOTH, layout.chips), pair_out))
+    blocks = exchange(blocks, BOTH, layout.chips)
     blocks = total(blocks)
     blocks = exchange(jnp.concatenate([blocks, node_blocks], axis=1), "row")
     pair_grad = jnp.where(stays, pair_one_grad, pair_one_away).astype(WIDE) + jnp.einsum(

time: 624 us -> 622 us (level)
  waiting for transfers between devices: 156 us -> 146 us
    all_to_all x11, waiting for transfers between devices: 156 us -> 146 us  [exchange(): lax.all_to_all(blocks, axes, 0, 0, axis_index_groups=groups, tiled=True)]
where the time goes in v7:
time: 622 us; the launch traced here: 612 us
  blocking collectives  182 us (29%)
  Pallas kernels  165 us (27%)
  waiting for transfers between devices  146 us (23%)
  starting transfers between devices  73.2 us (12%)
  other arithmetic  17.7 us (3%)
  local copies, waits for them, and re-layouts  15.8 us (3%)
  matrix products  7.62 us (1%)
    all_to_all x8, blocking collectives, exchange(): lax.all_to_all(blocks, axes, 0, 0, axis_index_groups=groups, tiled=True)  182 us
    all_to_all x11, waiting for transfers between devices, exchange(): lax.all_to_all(blocks, axes, 0, 0, axis_index_groups=groups, tiled=True)  146 us
    pallas_call x8, Pallas kernels, run(): pl.pallas_call(body, grid=(extent[1] // step[1], extent[0] // step[0]), i...  129 us
    all_to_all x11, starting transfers between devices, exchange(): lax.all_to_all(blocks, axes, 0, 0, axis_index_groups=groups, tiled=True)  60.3 us
    pallas_call x6, Pallas kernels, one_call(): pl.pallas_call(body, in_specs=[pl.BlockSpec(memory_space=pltpu.SMEM)] * l...  18.9 us
  transfers between devices with their start and end apart: 19, of which 9 were waited for; matrix products, arithmetic and copies ran while one was open for 5% of the time, Pallas kernels for 24%

profile of v7, /device:TPU:0, one launch (start us, length us, event | category | flops | bytes accessed | tf_op | source)
XLA Modules:
  0.0 612.2 jit_solution(8828061567307267430)
XLA Ops:
  3.5 26.5 %all_to_all.95 = bf16[8,368,128]{2,1,0:T(8,128)(2,1)S(1)} all-to-all(bf16[8,368,128]{2,1,0:T(8,128)(2,1)S(1)} %broadcast_in_dim.57), channel_id=1, replica_groups=mesh['crop'=4,'row'=8] {'row'}, dimensions={0} | all-to-all | bytes 1507328 | tf_op jit(solution)/shard_map/all_to_all | solution.py:152
  30.0 2.0 collective-permute-start
  32.0 1.1 broadcast_in_dim.59
  33.1 3.6 all-to-all-start.1
  38.2 1.6 slice.24
  39.8 13.8 %all-to-all-done.1 = bf16[2,2432,128]{2,1,0:T(8,128)(2,1)S(1)} async-done(((bf16[2,2432,128]{2,1,0:T(8,128)(2,1)}), bf16[2,2432,128]{2,1,0:T(8,128)(2,1)S(1)}, u32[]{:S(2)}, u32[]{:S(2)}) %all-to-all-start.1) | async-done | bytes 1245216 | tf_op jit(solution)/shard_map/all_to_all | solution.py:152
  54.0 6.7 %all_to_all.96 = bf16[2,2,2432,128]{3,2,1,0:T(8,128)(2,1)} all-to-all(bf16[2,2,2432,128]{3,2,1,0:T(8,128)(2,1)S(1)} %broadcast_in_dim.60), channel_id=1, replica_groups={{0,8},{1,9},{2,10},{3,11},{4,12},{5,13},{6,14},{7,15},{16,24},{17,25},{..., dimensions={0} | all-to-all | bytes 4980736 | tf_op jit(solution)/shard_map/all_to_all | solution.py:152
  60.6 3.5 shard_map.176
  64.1 1.4 fusion.10
  66.3 4.2 shard_map.177
  70.6 3.5 all-to-all-start.3
  74.1 3.1 slice_bitcast_fusion
  77.2 4.6 all-to-all-done.3.factors
  83.4 2.2 shard_map.178
  85.6 9.0 %shard_map.179 = (bf16[32,128,256]{2,1,0:T(8,128)(2,1)}, f32[32,1,256]{2,1,0:T(1,128)}, f32[32,1,256]{2,1,0:T(1,128)}, bf16[32,128,256]{2,1,0:T(8,128)(2,1)}, bf16[8,32,32,256]{3,2,1,0:T(8,128)(2,1)}) custom-call(s32[1]{0:T(128)} %bitcast.10.stays, bf16[32,256,128]{2,1,0:T(8,128)(2,1)} %collective-permute-done.pair, bf16[32,256,128]{2,1,0:T(8,128)(2,1)} %bitcast.52, ...), custom_call_target="tpu_custom_call" | custom-call | flops 1073741824 | bytes 4616196 | tf_op jit(solution)/shard_map/pallas_call | solution.py:327
  94.6 7.9 %all-to-all-start.4 = ((bf16[8,32,32,256]{3,2,1,0:T(8,128)(2,1)}), bf16[8,32,32,256]{3,2,1,0:T(8,128)(2,1)}, u32[]{:S(2)}, u32[]{:S(2)}) async-start(bf16[8,32,32,256]{3,2,1,0:T(8,128)(2,1)} %get-tuple-element.160), calls=%async_computation.4 | async-start | bytes 8388608 | tf_op jit(solution)/shard_map/all_to_all | solution.py:152
  102.5 2.0 collective-permute-start.2
  104.4 46.8 %all-to-all-done.4.refs_0_.refs_1_.refs_2_ = bf16[8,32,32,256]{3,2,1,0:T(8,128)(2,1)} async-done(((bf16[8,32,32,256]{3,2,1,0:T(8,128)(2,1)}), bf16[8,32,32,256]{3,2,1,0:T(8,128)(2,1)}, u32[]{:S(2)}, u32[]{:S(2)}) %all-to-all-start.4) | async-done | bytes 4194336 | tf_op jit(solution)/shard_map/all_to_all | solution.py:152
  151.3 3.6 shard_map.180
  154.9 30.7 %all_to_all.97 = bf16[8,16,32,256]{3,2,1,0:T(8,128)(2,1)} all-to-all(bf16[8,16,32,256]{3,2,1,0:T(8,128)(2,1)} %shard_map.180), channel_id=1, replica_groups={{0,1,2,3,10,11,8,9},{6,7,4,5,12,13,14,15},{16,17,18,19,26,27,24,25},{22..., dimensions={0} | all-to-all | bytes 4194304 | tf_op jit(solution)/shard_map/all_to_all | solution.py:152
  185.6 1.7 collective-permute-start.3
  187.3 9.9 %shard_map.181 = (bf16[32,128,256]{2,1,0:T(8,128)(2,1)}, f32[32,1,256]{2,1,0:T(1,128)}, f32[32,1,256]{2,1,0:T(1,128)}, bf16[32,128,256]{2,1,0:T(8,128)(2,1)}, bf16[8,32,32,256]{3,2,1,0:T(8,128)(2,1)}) custom-call(bf16[128,32,256]{2,1,0:T(8,128)(2,1)} %bitcast.49, bf16[32,128,256]{2,1,0:T(8,128)(2,1)} %get-tuple-element.164.x_in.x_after, ...), custom_call_target="tpu_custom_call" | custom-call | flops 1342177280 | bytes 6467584 | tf_op jit(solution)/shard_map/pallas_call | solution.py:327
  197.2 8.0 %all-to-all-start.6 = ((bf16[8,32,32,256]{3,2,1,0:T(8,128)(2,1)}), bf16[8,32,32,256]{3,2,1,0:T(8,128)(2,1)}, u32[]{:S(2)}, u32[]{:S(2)}) async-start(bf16[8,32,32,256]{3,2,1,0:T(8,128)(2,1)} %get-tuple-element.170), calls=%async_computation.6 | async-start | bytes 8388608 | tf_op jit(solution)/shard_map/all_to_all | solution.py:152
  205.2 3.5 fusion.cot
  208.7 45.3 %all-to-all-done.6.refs_0_.refs_1_.refs_2_.refs_3_ = bf16[8,32,32,256]{3,2,1,0:T(8,128)(2,1)} async-done(((bf16[8,32,32,256]{3,2,1,0:T(8,128)(2,1)}), bf16[8,32,32,256]{3,2,1,0:T(8,128)(2,1)}, u32[]{:S(2)}, u32[]{:S(2)}) %all-to-all-start.6) | async-done | bytes 4194336 | tf_op jit(solution)/shard_map/all_to_all | solution.py:152
  254.0 3.7 shard_map.182
  257.7 19.2 %all_to_all.98 = bf16[8,16,16,256]{3,2,1,0:T(8,128)(2,1)} all-to-all(bf16[8,16,16,256]{3,2,1,0:T(8,128)(2,1)} %get-tuple-element.175), channel_id=1, replica_groups={{0,1,2,3,10,11,8,9},{6,7,4,5,12,13,14,15},{16,17,18,19,26,27,24,25},{22..., dimensions={0} | all-to-all | bytes 2097152 | tf_op jit(solution)/shard_map/all_to_all | solution.py:152
  276.9 3.7 all-to-all-start.9
  280.6 14.6 %shard_map.183 = (bf16[32,256,128]{2,1,0:T(8,128)(2,1)}, bf16[32,128,256]{2,1,0:T(8,128)(2,1)}, bf16[32,128,256]{2,1,0:T(8,128)(2,1)}, bf16[128,16,256]{2,1,0:T(8,128)(2,1)}) custom-call(bf16[128,16,256]{2,1,0:T(8,128)(2,1)} %bitcast.63, bf16[32,128,256]{2,1,0:T(8,128)(2,1)} %get-tuple-element.176.x_in.x_after, ...), custom_call_target="tpu_custom_call" | custom-call | flops 3221225472 | bytes 7647232 | tf_op jit(solution)/shard_map/pallas_call | solution.py:327
  295.2 4.2 all-to-all-start.8
  299.4 14.7 %shard_map.184 = (bf16[32,256,128]{2,1,0:T(8,128)(2,1)}, bf16[32,128,256]{2,1,0:T(8,128)(2,1)}, bf16[32,128,256]{2,1,0:T(8,128)(2,1)}, bf16[128,16,256]{2,1,0:T(8,128)(2,1)}) custom-call(bf16[128,16,256]{2,1,0:T(8,128)(2,1)} %bitcast.59, ...), custom_call_target="tpu_custom_call", output_to_operand_aliasing={{0}: (8, {}), {1}: (9, {}), {2}: (10, {})} | custom-call | flops 3221225472 | bytes 13938688 | tf_op jit(solution)/shard_map/pallas_call | solution.py:327
  314.1 19.3 %all_to_all.99.refs_1_ = bf16[8,16,16,256]{3,2,1,0:T(8,128)(2,1)} all-to-all(bf16[8,16,16,256]{3,2,1,0:T(8,128)(2,1)} %bitcast.71), channel_id=1, replica_groups={{0,1,2,3,10,11,8,9},{6,7,4,5,12,13,14,15},{16,17,18,19,26,27,24,25},{22..., dimensions={0} | all-to-all | bytes 2097152 | tf_op jit(solution)/shard_map/all_to_all | solution.py:152
  333.4 4.9 shard_map.185
  338.3 5.1 all-to-all-start.11
  343.4 2.0 collective-permute-start.4
  345.4 2.9 pad_maximum_fusion.mixed
  348.3 1.4 fusion.22
  349.7 39.5 %shard_map.186 = (f32[128,128]{1,0:T(8,128)}, f32[128,1]{1,0:T(8,128)}, f32[128,512]{1,0:T(8,128)}, f32[512,128]{1,0:T(8,128)}, f32[128,1]{1,0:T(8,128)}, /*index=5*/f32[128,1]{1,0:T(8,128)}) custom-call(bf16[128,32,256]{2,1,0:T(8,128)(2,1)} %pad_maximum_fusion.mixed, bf16[32,128,256]{2,1,0:T(8,128)(2,1)} %get-tuple-element.176.x_in.x_after, ...), custom_call_target="tpu_custom_call" | custom-call | flops 7516192768 | bytes 8695808 | tf_op jit(solution)/shard_map/pallas_call | solution.py:327
  389.2 1.9 all-to-all-done.11.sides_grad
  391.9 13.0 %shard_map.187 = (bf16[32,128,256]{2,1,0:T(8,128)(2,1)}, bf16[32,128,256]{2,1,0:T(8,128)(2,1)}, bf16[128,32,256]{2,1,0:T(8,128)(2,1)}) custom-call(bf16[8,32,32,256]{3,2,1,0:T(8,128)(2,1)} %all-to-all-done.11.sides_grad, bf16[32,128,256]{2,1,0:T(8,128)(2,1)} %get-tuple-element.176.x_in.x_after, f32[32,1,256]{2,1,0:T(1,128)} %get-tuple-element.199.mean_after, ...), custom_call_target="tpu_custom_call" | custom-call | flops 2147483648 | bytes 14921728 | tf_op jit(solution)/shard_map/pallas_call | solution.py:327
  404.8 9.1 %all-to-all-start.12 = ((bf16[8,16,32,256]{3,2,1,0:T(8,128)(2,1)}), bf16[8,16,32,256]{3,2,1,0:T(8,128)(2,1)}, u32[]{:S(2)}, u32[]{:S(2)}) async-start(bf16[8,16,32,256]{3,2,1,0:T(8,128)(2,1)} %bitcast.67), calls=%async_computation.12 | async-start | bytes 4194304 | tf_op jit(solution)/shard_map/all_to_all | solution.py:152
  414.0 18.0 %shard_map.188 = (f32[128,384]{1,0:T(8,128)}, f32[128,1]{1,0:T(8,128)}, f32[128,128]{1,0:T(8,128)}, f32[128,1]{1,0:T(8,128)}) custom-call(bf16[8,32,32,256]{3,2,1,0:T(8,128)(2,1)} %all-to-all-done.11.sides_grad, bf16[32,128,256]{2,1,0:T(8,128)(2,1)} %get-tuple-element.176.x_in.x_after, f32[32,1,256]{2,1,0:T(1,128)} %get-tuple-element.199.mean_after, ...), custom_call_target="tpu_custom_call" | custom-call | flops 3221225472 | bytes 14921728 | tf_op jit(solution)/shard_map/pallas_call | solution.py:327
  432.0 8.3 %all-to-all-done.12.refs_0_ = bf16[8,16,32,256]{3,2,1,0:T(8,128)(2,1)} async-done(((bf16[8,16,32,256]{3,2,1,0:T(8,128)(2,1)}), bf16[8,16,32,256]{3,2,1,0:T(8,128)(2,1)}, u32[]{:S(2)}, u32[]{:S(2)}) %all-to-all-start.12) | async-done | bytes 2097184 | tf_op jit(solution)/shard_map/all_to_all | solution.py:152
  440.3 4.9 shard_map.189
  445.2 53.3 %all_to_all.100.sides_grad = bf16[8,32,32,256]{3,2,1,0:T(8,128)(2,1)} all-to-all(bf16[8,32,32,256]{3,2,1,0:T(8,128)(2,1)} %bitcast.57), channel_id=1, replica_groups={{0,1,2,3,10,11,8,9},{6,7,4,5,12,13,14,15},{16,17,18,19,26,27,24,25},{22..., dimensions={0} | all-to-all | bytes 8388608 | tf_op jit(solution)/shard_map/all_to_all | solution.py:152
  498.5 1.7 collective-permute-start.6
  500.2 10.4 %shard_map.190 = (bf16[32,256,128]{2,1,0:T(8,128)(2,1)}, f32[2,32,32,128]{3,2,1,0:T(8,128)}, f32[32,256]{1,0:T(8,128)}, f32[128,384]{1,0:T(8,128)}, f32[128,1]{1,0:T(8,128)}) custom-call(bf16[8,32,32,256]{3,2,1,0:T(8,128)(2,1)} %all_to_all.100.sides_grad, bf16[32,128,256]{2,1,0:T(8,128)(2,1)} %get-tuple-element.164.x_in.x_after, ...), custom_call_target="tpu_custom_call" | custom-call | flops 2147483648 | bytes 10973184 | tf_op jit(solution)/shard_map/pallas_call | solution.py:327
  510.6 3.1 shard_map.191
  513.7 8.3 %all-to-all-start.14 = ((bf16[16,32,128]{2,1,0:T(8,128)(2,1)}), bf16[16,32,128]{2,1,0:T(8,128)(2,1)S(1)}, u32[]{:S(2)}, u32[]{:S(2)}) async-start(bf16[16,32,128]{2,1,0:T(8,128)(2,1)} %bitcast.76), calls=%async_computation.14 | async-start | bytes 262144 | tf_op jit(solution)/shard_map/all_to_all | solution.py:152
  522.0 3.5 fusion.1
  525.5 4.2 all-to-all-done.14.factor_ref
  529.7 2.2 collective-permute-start.7
  532.6 4.0 shard_map.192
  536.7 2.1 convolution_bitcast_fusion
  541.3 1.9 shard_map.193
  543.2 6.5 %all_to_all.101 = bf16[2,2,8,304,128]{4,3,2,1,0:T(8,128)(2,1)S(1)} all-to-all(bf16[2,2,8,304,128]{4,3,2,1,0:T(8,128)(2,1)S(1)} %get-tuple-element.264), channel_id=1, replica_groups={{0,8},{1,9},{2,10},{3,11},{4,12},{5,13},{6,14},{7,15},{16,24},{17,25},{..., dimensions={0} | all-to-all | bytes 4980736 | tf_op jit(solution)/shard_map/all_to_all | solution.py:152
  549.6 1.8 reduce_sum.51
  551.4 19.9 %all_to_all.102 = bf16[2,8,304,128]{3,2,1,0:T(8,128)(2,1)S(1)} all-to-all(bf16[2,8,304,128]{3,2,1,0:T(8,128)(2,1)} %reduce_sum.51), channel_id=1, replica_groups={{0,16},{1,17},{2,18},{3,19},{4,20},{5,21},{6,22},{7,23},{8,24},{9,25},{..., dimensions={0} | all-to-all | bytes 2490368 | tf_op jit(solution)/shard_map/all_to_all | solution.py:152
  571.8 0.9 pad_maximum_fusion.1
  572.7 4.0 all-to-all-start.17
  576.9 4.1 add_convert_fusion
  581.1 14.7 %all-to-all-done.17 = bf16[8,368,128]{2,1,0:T(8,128)(2,1)S(1)} async-done(((bf16[8,368,128]{2,1,0:T(8,128)(2,1)}), bf16[8,368,128]{2,1,0:T(8,128)(2,1)S(1)}, u32[]{:S(2)}, u32[]{:S(2)}) %all-to-all-start.17) | async-done | bytes 753696 | tf_op jit(solution)/shard_map/all_to_all | solution.py:152
  597.9 2.9 all-to-all-start.18
  601.4 6.6 %all-to-all-done.18 = f32[32,2,128]{2,1,0:T(2,128)S(1)} async-done(((f32[32,2,128]{2,1,0:T(2,128)}), f32[32,2,128]{2,1,0:T(2,128)S(1)}, u32[]{:S(2)}, u32[]{:S(2)}) %all-to-all-start.18) | async-done | bytes 32800 | tf_op jit(solution)/shard_map/all_to_all | solution.py:152
  (143 shorter events, 15.0 us)
Async XLA Ops:
  0.6 29.4 %copy-start.31 = (bf16[1,32,256,128]{3,2,1,0:T(8,128)(2,1)S(1)}, bf16[1,32,256,128]{3,2,1,0:T(8,128)(2,1)}, u32[]{:S(2)}) copy-start(bf16[1,32,256,128]{3,2,1,0:T(8,128)(2,1)} %param.10) | copy-start | bytes 6291460
  30.0 51.9 %collective-permute-start = (bf16[32,256,128]{2,1,0:T(8,128)(2,1)S(1)}, bf16[32,256,128]{2,1,0:T(8,128)(2,1)}, u32[]{:S(2)}, u32[]{:S(2)}) collective-permute-start(bf16[32,256,128]{2,1,0:T(8,128)(2,1)S(1)} %bitcast.54), channel_id=1, source_target_pairs={{4,10},{5,11},{6,8},{7,9},{8,6},{9,7},{10,4},{11,5},{20,26},{21,27... | collective-permute-start | bytes 6291464 | tf_op jit(solution)/shard_map/ppermute | solution.py:1002
  32.0 5.4 copy-start.49
  33.1 20.5 %all-to-all-start.1 = ((bf16[2,2432,128]{2,1,0:T(8,128)(2,1)}), bf16[2,2432,128]{2,1,0:T(8,128)(2,1)S(1)}, u32[]{:S(2)}, u32[]{:S(2)}) async-start(bf16[2,2432,128]{2,1,0:T(8,128)(2,1)} %broadcast_in_dim.59), calls=%async_computation.1 | async-start | bytes 2490368 | tf_op jit(solution)/shard_map/all_to_all | solution.py:152
  37.4 23.2 %copy-start.48 = (f32[1,256]{1,0:T(1,128)}, f32[1,256]{1,0:T(1,128)S(1)}, u32[]{:S(2)}) copy-start(f32[1,256]{1,0:T(1,128)S(1)} %convert_element_type.27.keep) | copy-start | bytes 3076
  70.6 11.3 %all-to-all-start.3 = ((bf16[16,32,128]{2,1,0:T(8,128)(2,1)}), bf16[16,32,128]{2,1,0:T(8,128)(2,1)S(1)}, u32[]{:S(2)}, u32[]{:S(2)}) async-start(bf16[16,32,128]{2,1,0:T(8,128)(2,1)} %get-tuple-element.150), calls=%async_computation.3 | async-start | bytes 262144 | tf_op jit(solution)/shard_map/all_to_all | solution.py:152
  81.9 12.7 %collective-permute-start.1 = (bf16[16,256,128]{2,1,0:T(8,128)(2,1)}, bf16[16,256,128]{2,1,0:T(8,128)(2,1)S(1)}, u32[]{:S(2)}, u32[]{:S(2)}) collective-permute-start(bf16[16,256,128]{2,1,0:T(8,128)(2,1)} %get-tuple-element.159), channel_id=1, source_target_pairs={{6,8},{7,9},{8,6},{9,7},{22,24},{23,25},{24,22},{25,23}} | collective-permute-start | bytes 3145736 | tf_op jit(solution)/shard_map/ppermute | solution.py:980
  94.6 7.9 %copy-start.35 = (bf16[1,32,256,128]{3,2,1,0:T(8,128)(2,1)S(1)}, bf16[1,32,256,128]{3,2,1,0:T(8,128)(2,1)}, u32[]{:S(2)}) copy-start(bf16[1,32,256,128]{3,2,1,0:T(8,128)(2,1)} %param.14) | copy-start | bytes 6291460
  94.6 56.7 %all-to-all-start.4 = ((bf16[8,32,32,256]{3,2,1,0:T(8,128)(2,1)}), bf16[8,32,32,256]{3,2,1,0:T(8,128)(2,1)}, u32[]{:S(2)}, u32[]{:S(2)}) async-start(bf16[8,32,32,256]{3,2,1,0:T(8,128)(2,1)} %get-tuple-element.160), calls=%async_computation.4 | async-start | bytes 8388608 | tf_op jit(solution)/shard_map/all_to_all | solution.py:152
  102.5 2.0 collective-permute-start.2
  154.9 30.7 %copy-start.38 = (bf16[16,256,128]{2,1,0:T(8,128)(2,1)S(1)}, bf16[16,256,128]{2,1,0:T(8,128)(2,1)}, u32[]{:S(2)}) copy-start(bf16[16,256,128]{2,1,0:T(8,128)(2,1)} %get-tuple-element.169) | copy-start | bytes 3145732
  185.6 11.6 %collective-permute-start.3 = (bf16[16,256,128]{2,1,0:T(8,128)(2,1)S(1)}, bf16[16,256,128]{2,1,0:T(8,128)(2,1)}, u32[]{:S(2)}, u32[]{:S(2)}) collective-permute-start(bf16[16,256,128]{2,1,0:T(8,128)(2,1)S(1)} %copy-done.38), channel_id=1, source_target_pairs={{6,8},{7,9},{8,6},{9,7},{22,24},{23,25},{24,22},{25,23}} | collective-permute-start | bytes 3145736 | tf_op jit(solution)/shard_map/ppermute | solution.py:980
  197.2 56.8 %all-to-all-start.6 = ((bf16[8,32,32,256]{3,2,1,0:T(8,128)(2,1)}), bf16[8,32,32,256]{3,2,1,0:T(8,128)(2,1)}, u32[]{:S(2)}, u32[]{:S(2)}) async-start(bf16[8,32,32,256]{3,2,1,0:T(8,128)(2,1)} %get-tuple-element.170), calls=%async_computation.6 | async-start | bytes 8388608 | tf_op jit(solution)/shard_map/all_to_all | solution.py:152
  276.9 18.3 %all-to-all-start.9 = ((bf16[8,16,16,256]{3,2,1,0:T(8,128)(2,1)}), bf16[8,16,16,256]{3,2,1,0:T(8,128)(2,1)S(1)}, u32[]{:S(2)}, u32[]{:S(2)}) async-start(bf16[8,16,16,256]{3,2,1,0:T(8,128)(2,1)} %get-tuple-element.183), calls=%async_computation.9 | async-start | bytes 2097152 | tf_op jit(solution)/shard_map/all_to_all | solution.py:152
  295.2 4.2 copy-start.33
  295.2 18.8 %all-to-all-start.8 = ((bf16[8,16,16,256]{3,2,1,0:T(8,128)(2,1)}), bf16[8,16,16,256]{3,2,1,0:T(8,128)(2,1)S(1)}, u32[]{:S(2)}, u32[]{:S(2)}) async-start(bf16[8,16,16,256]{3,2,1,0:T(8,128)(2,1)} %bitcast.70), calls=%async_computation.8 | async-start | bytes 2097152 | tf_op jit(solution)/shard_map/all_to_all | solution.py:152
  314.1 19.3 %copy-start.36 = (bf16[8,16,16,256]{3,2,1,0:T(8,128)(2,1)}, bf16[8,16,16,256]{3,2,1,0:T(8,128)(2,1)S(1)}, u32[]{:S(2)}) copy-start(bf16[8,16,16,256]{3,2,1,0:T(8,128)(2,1)S(1)} %all-to-all-done.8.refs_0_) | copy-start | bytes 3145732
  338.3 5.1 copy-start.32
  338.3 7.1 %copy-start.34 = (bf16[8,16,16,256]{3,2,1,0:T(8,128)(2,1)S(1)}, bf16[8,16,16,256]{3,2,1,0:T(8,128)(2,1)}, u32[]{:S(2)}) copy-start(bf16[8,16,16,256]{3,2,1,0:T(8,128)(2,1)} %copy-done.33) | copy-start | bytes 3145732
  338.3 52.8 %all-to-all-start.11 = ((bf16[8,32,32,256]{3,2,1,0:T(8,128)(2,1)}), bf16[8,32,32,256]{3,2,1,0:T(8,128)(2,1)}, u32[]{:S(2)}, u32[]{:S(2)}) async-start(bf16[8,32,32,256]{3,2,1,0:T(8,128)(2,1)} %bitcast.56), calls=%async_computation.11 | async-start | bytes 8388608 | tf_op jit(solution)/shard_map/all_to_all | solution.py:152
  343.4 47.8 %collective-permute-start.4 = (bf16[32,256,128]{2,1,0:T(8,128)(2,1)S(1)}, bf16[32,256,128]{2,1,0:T(8,128)(2,1)}, u32[]{:S(2)}, u32[]{:S(2)}) collective-permute-start(bf16[32,256,128]{2,1,0:T(8,128)(2,1)S(1)} %copy-done.32), channel_id=1, source_target_pairs={{4,10},{5,11},{10,4},{11,5},{20,26},{21,27},{26,20},{27,21}} | collective-permute-start | bytes 6291464 | tf_op jit(solution)/shard_map/ppermute | solution.py:979
  391.1 13.7 %collective-permute-start.5 = (bf16[16,256,128]{2,1,0:T(8,128)(2,1)}, bf16[16,256,128]{2,1,0:T(8,128)(2,1)S(1)}, u32[]{:S(2)}, u32[]{:S(2)}) collective-permute-start(bf16[16,256,128]{2,1,0:T(8,128)(2,1)} %get-tuple-element.204), channel_id=1, source_target_pairs={{6,8},{7,9},{8,6},{9,7},{22,24},{23,25},{24,22},{25,23}} | collective-permute-start | bytes 3145736 | tf_op jit(solution)/shard_map/ppermute | solution.py:980
  404.8 35.5 %all-to-all-start.12 = ((bf16[8,16,32,256]{3,2,1,0:T(8,128)(2,1)}), bf16[8,16,32,256]{3,2,1,0:T(8,128)(2,1)}, u32[]{:S(2)}, u32[]{:S(2)}) async-start(bf16[8,16,32,256]{3,2,1,0:T(8,128)(2,1)} %bitcast.67), calls=%async_computation.12 | async-start | bytes 4194304 | tf_op jit(solution)/shard_map/all_to_all | solution.py:152
  445.2 53.3 %copy-start.39 = (bf16[16,256,128]{2,1,0:T(8,128)(2,1)S(1)}, bf16[16,256,128]{2,1,0:T(8,128)(2,1)}, u32[]{:S(2)}) copy-start(bf16[16,256,128]{2,1,0:T(8,128)(2,1)} %get-tuple-element.220) | copy-start | bytes 3145732
  498.5 15.2 %collective-permute-start.6 = (bf16[16,256,128]{2,1,0:T(8,128)(2,1)S(1)}, bf16[16,256,128]{2,1,0:T(8,128)(2,1)}, u32[]{:S(2)}, u32[]{:S(2)}) collective-permute-start(bf16[16,256,128]{2,1,0:T(8,128)(2,1)S(1)} %copy-done.39), channel_id=1, source_target_pairs={{6,8},{7,9},{8,6},{9,7},{22,24},{23,25},{24,22},{25,23}} | collective-permute-start | bytes 3145736 | tf_op jit(solution)/shard_map/ppermute | solution.py:980
  513.7 15.9 %all-to-all-start.14 = ((bf16[16,32,128]{2,1,0:T(8,128)(2,1)}), bf16[16,32,128]{2,1,0:T(8,128)(2,1)S(1)}, u32[]{:S(2)}, u32[]{:S(2)}) async-start(bf16[16,32,128]{2,1,0:T(8,128)(2,1)} %bitcast.76), calls=%async_computation.14 | async-start | bytes 262144 | tf_op jit(solution)/shard_map/all_to_all | solution.py:152
  529.7 2.8 copy-start.43
  529.7 47.2 %collective-permute-start.7 = (bf16[32,256,128]{2,1,0:T(8,128)(2,1)}, bf16[32,256,128]{2,1,0:T(8,128)(2,1)}, u32[]{:S(2)}, u32[]{:S(2)}) collective-permute-start(bf16[32,256,128]{2,1,0:T(8,128)(2,1)} %get-tuple-element.266), channel_id=1, source_target_pairs={{4,10},{5,11},{6,8},{7,9},{8,6},{9,7},{10,4},{11,5},{20,26},{21,27... | collective-permute-start | bytes 6291464 | tf_op jit(solution)/shard_map/ppermute | solution.py:1171
  532.5 6.5 %copy-start = (bf16[256,768]{1,0:T(8,128)(2,1)S(1)}, bf16[256,768]{1,0:T(8,128)(2,1)}, u32[]{:S(2)}) copy-start(bf16[256,768]{1,0:T(8,128)(2,1)} %get-tuple-element.144.w_projections.refs_23_) | copy-start | bytes 1179652
  532.5 6.5 %copy-start.1 = (f32[24,128]{1,0:T(8,128)S(1)}, f32[24,128]{1,0:T(8,128)}, u32[]{:S(2)}) copy-start(f32[24,128]{1,0:T(8,128)} %get-tuple-element.143.vectors.refs_22_) | copy-start | bytes 36868
  532.5 6.6 %copy-start.2 = (f32[1024,128]{1,0:T(8,128)S(1)}, f32[1024,128]{1,0:T(8,128)}, u32[]{:S(2)}) copy-start(f32[1024,128]{1,0:T(8,128)} %get-tuple-element.239.refs_3_) | copy-start | bytes 1572868
  532.5 6.6 %copy-start.3 = (f32[256,256]{1,0:T(8,128)S(1)}, f32[256,256]{1,0:T(8,128)}, u32[]{:S(2)}) copy-start(f32[256,256]{1,0:T(8,128)} %get-tuple-element.254.refs_18_) | copy-start | bytes 786436
  532.5 6.6 %copy-start.4 = (f32[128,512]{1,0:T(8,128)S(1)}, f32[128,512]{1,0:T(8,128)}, u32[]{:S(2)}) copy-start(f32[128,512]{1,0:T(8,128)} %get-tuple-element.241.refs_5_) | copy-start | bytes 786436
  532.5 6.6 %copy-start.5 = (f32[512,128]{1,0:T(8,128)S(1)}, f32[512,128]{1,0:T(8,128)}, u32[]{:S(2)}) copy-start(f32[512,128]{1,0:T(8,128)} %get-tuple-element.242.refs_6_) | copy-start | bytes 786436
  532.5 6.6 %copy-start.7 = (f32[128,1]{1,0:T(8,128)S(1)}, f32[128,1]{1,0:T(8,128)}, u32[]{:S(2)}) copy-start(f32[128,1]{1,0:T(8,128)} %get-tuple-element.243.refs_7_) | copy-start | bytes 1540
  532.5 6.6 %copy-start.8 = (f32[128,384]{1,0:T(8,128)S(1)}, f32[128,384]{1,0:T(8,128)}, u32[]{:S(2)}) copy-start(f32[128,384]{1,0:T(8,128)} %get-tuple-element.249.refs_13_) | copy-start | bytes 589828
  532.5 6.6 %copy-start.9 = (f32[128,384]{1,0:T(8,128)S(1)}, f32[128,384]{1,0:T(8,128)}, u32[]{:S(2)}) copy-start(f32[128,384]{1,0:T(8,128)} %get-tuple-element.245.refs_9_) | copy-start | bytes 589828
  532.5 6.6 %copy-start.11 = (bf16[256,256]{1,0:T(8,128)(2,1)S(1)}, bf16[256,256]{1,0:T(8,128)(2,1)}, u32[]{:S(2)}) copy-start(bf16[256,256]{1,0:T(8,128)(2,1)} %get-tuple-element.256.refs_20_) | copy-start | bytes 393220
  532.5 6.6 %copy-start.13 = (bf16[32,1024]{1,0:T(8,128)(2,1)S(1)}, bf16[32,1024]{1,0:T(8,128)(2,1)}, u32[]{:S(2)}) copy-start(bf16[32,1024]{1,0:T(8,128)(2,1)} %get-tuple-element.257.refs_24_) | copy-start | bytes 196612
  532.5 6.6 %copy-start.14 = (f32[128,128]{1,0:T(8,128)S(1)}, f32[128,128]{1,0:T(8,128)}, u32[]{:S(2)}) copy-start(f32[128,128]{1,0:T(8,128)} %get-tuple-element.251.refs_15_) | copy-start | bytes 196612
  532.6 6.6 %copy-start.15 = (f32[128,1]{1,0:T(8,128)S(1)}, f32[128,1]{1,0:T(8,128)}, u32[]{:S(2)}) copy-start(f32[128,1]{1,0:T(8,128)} %get-tuple-element.250.refs_14_) | copy-start | bytes 1540
  532.6 6.6 %copy-start.16 = (f32[128,1]{1,0:T(8,128)S(1)}, f32[128,1]{1,0:T(8,128)}, u32[]{:S(2)}) copy-start(f32[128,1]{1,0:T(8,128)} %get-tuple-element.240.refs_4_) | copy-start | bytes 1540
  532.6 6.6 %copy-start.17 = (f32[128,1]{1,0:T(8,128)S(1)}, f32[128,1]{1,0:T(8,128)}, u32[]{:S(2)}) copy-start(f32[128,1]{1,0:T(8,128)} %get-tuple-element.248.refs_12_) | copy-start | bytes 1540
  532.6 6.6 %copy-start.18 = (f32[128,128]{1,0:T(8,128)S(1)}, f32[128,128]{1,0:T(8,128)}, u32[]{:S(2)}) copy-start(f32[128,128]{1,0:T(8,128)} %get-tuple-element.247.refs_11_) | copy-start | bytes 196612
  532.6 6.6 %copy-start.19 = (f32[128,1]{1,0:T(8,128)S(1)}, f32[128,1]{1,0:T(8,128)}, u32[]{:S(2)}) copy-start(f32[128,1]{1,0:T(8,128)} %get-tuple-element.246.refs_10_) | copy-start | bytes 1540
  532.6 6.6 %copy-start.20 = (f32[128,1]{1,0:T(8,128)S(1)}, f32[128,1]{1,0:T(8,128)}, u32[]{:S(2)}) copy-start(f32[128,1]{1,0:T(8,128)} %get-tuple-element.244.refs_8_) | copy-start | bytes 1540
  532.6 6.6 %copy-start.22 = (bf16[32,256]{1,0:T(8,128)(2,1)S(1)}, bf16[32,256]{1,0:T(8,128)(2,1)}, u32[]{:S(2)}) copy-start(bf16[32,256]{1,0:T(8,128)(2,1)} %get-tuple-element.255.refs_19_) | copy-start | bytes 49156
  532.6 6.6 %copy-start.23 = (bf16[32,256]{1,0:T(8,128)(2,1)S(1)}, bf16[32,256]{1,0:T(8,128)(2,1)}, u32[]{:S(2)}) copy-start(bf16[32,256]{1,0:T(8,128)(2,1)} %get-tuple-element.261.refs_28_) | copy-start | bytes 49156
  536.6 2.6 copy-start.6
  536.6 2.6 copy-start.10
  536.6 2.6 copy-start.12
  536.7 2.6 copy-start.21
  536.7 2.6 copy-start.24
  536.7 2.6 copy-start.25
  536.7 2.6 copy-start.26
  536.7 2.6 copy-start.27
  571.3 5.6 copy-start.42
  571.3 5.6 copy-start.47
  572.7 23.0 %all-to-all-start.17 = ((bf16[8,368,128]{2,1,0:T(8,128)(2,1)}), bf16[8,368,128]{2,1,0:T(8,128)(2,1)S(1)}, u32[]{:S(2)}, u32[]{:S(2)}) async-start(bf16[8,368,128]{2,1,0:T(8,128)(2,1)} %pad_maximum_fusion.1), calls=%async_computation.17 | async-start | bytes 1507328 | tf_op jit(solution)/shard_map/all_to_all | solution.py:152
  576.9 32.9 %copy-start.40 = (f32[37488]{0:T(1024)S(1)}, f32[37488]{0:T(1024)}, u32[]{:S(2)}) copy-start(f32[37488]{0:T(1024)} %param.15) | copy-start | bytes 449860
  576.9 32.9 %copy-start.45 = (f32[37488]{0:T(1024)S(1)}, f32[37488]{0:T(1024)}, u32[]{:S(2)}) copy-start(f32[37488]{0:T(1024)} %param.16) | copy-start | bytes 449860
  576.9 32.9 %copy-start.46 = (f32[37488]{0:T(1024)S(1)}, f32[37488]{0:T(1024)}, u32[]{:S(2)}) copy-start(f32[37488]{0:T(1024)} %param.17) | copy-start | bytes 449860
  596.6 14.0 %copy-start.41 = (f32[37488]{0:T(1024)}, f32[37488]{0:T(1024)S(1)}, u32[]{:S(2)}) copy-start(f32[37488]{0:T(1024)S(1)} %get-tuple-element.274) | copy-start | bytes 449860
  597.9 10.1 %all-to-all-start.18 = ((f32[32,2,128]{2,1,0:T(2,128)}), f32[32,2,128]{2,1,0:T(2,128)S(1)}, u32[]{:S(2)}, u32[]{:S(2)}) async-start(f32[32,2,128]{2,1,0:T(2,128)} %broadcast_in_dim.70), calls=%async_computation.18 | async-start | bytes 65536 | tf_op jit(solution)/shard_map/all_to_all | solution.py:152
  (5 other events, 5.5 us)
